TPU v7x, 256 devices: a whole 4x4x8 slice. The times are simulated.
256 devices in a mesh: src: 64 (over x, z, y_lo), rcv: 4 (over y_hi, core).
Axes of the slice: x: 4, y: 4 (y_hi: 2, y_lo: 2; y = y_hi * 2 + y_lo), z: 8, core: 2. Of those that a mesh axis runs over, the one named last changes fastest.
Arguments:
- spectra: float32 [2, 4, 4096, 4096], P(None, None, 'src', 'rcv'), may hold values from -6 to 6
- panels: int32 [2], replicated, may hold values from 0 to 63, as said below
- filters: float32 [4096, 64], P('src'), may hold values from -0.036 to 0.036
- offsets: int32 [4096], P('src'), may hold values from 63 to 2040
Outputs:
- primaries: bfloat16 [8, 4096, 4096], P(None, 'src', 'rcv')
Inputs may be any that keep to these rules, and one draw needn't show every extreme that they name: `panels`: 2 different panel numbers, one of them 64 - 1.
All inputs are finite; a program needn't handle non-finite values.
Results may differ from a plain program's by a relative error of at most 0.001.
Values sent between devices are 32-bit elements; how exact they have to be, the bound alone decides.
No kernel may reach another device: no remote copies, remote signals or barrier semaphores. Data moves between devices by JAX's collectives and lax.ppermute only.
A program may use at most 64 MiB of HBM per device.

v0:
```python
import math

import jax
import jax.numpy as jnp
from jax import lax
from jax.sharding import PartitionSpec as P

TWIN = 8
NPAN = 2
NT = 2048
FIRST_BIN = 64


def spread(shard, axis, root):
    mine = lax.axis_index(axis) == root
    return lax.psum(jnp.where(mine, shard, jnp.zeros_like(shard)), axis)


def complex_product(column_band, row_group_block):
    upper_limit = lax.Precision.HIGHEST
    real_component = jnp.einsum(
        "xcy,xye->xce", column_band[0], row_group_block[0], precision=upper_limit
    ) - jnp.einsum("xcy,xye->xce", column_band[1], row_group_block[1], precision=upper_limit)
    imaginary_component = jnp.einsum(
        "xcy,xye->xce", column_band[0], row_group_block[1], precision=upper_limit
    ) + jnp.einsum("xcy,xye->xce", column_band[1], row_group_block[0], precision=upper_limit)
    return jnp.stack([real_component, imaginary_component])


def phase_tables(offsets, sample_count, shift, freq_count):
    sample_times = offsets[:, None] + shift + jnp.arange(sample_count, dtype=jnp.int32)[None, :]
    bin_numbers = FIRST_BIN + jnp.arange(freq_count, dtype=jnp.int32)
    phase_index = sample_times[:, :, None] * bin_numbers[None, None, :] % NT
    angles = phase_index.astype(jnp.float32) * (2.0 * math.pi / NT)
    return (jnp.cos(angles), jnp.sin(angles))


def tap_matrix(filters, out_count):
    taps = filters.shape[1]
    out_time = jnp.arange(out_count, dtype=jnp.int32)[:, None]
    sample_lag = jnp.arange(out_count + taps - 1, dtype=jnp.int32)[None, :]
    tap_index = out_time + taps - 1 - sample_lag
    one_hot = (tap_index[:, :, None] == jnp.arange(taps, dtype=jnp.int32)[None, None, :]).astype(
        jnp.float32
    )
    return jnp.einsum("sj,tlj->stl", filters, one_hot, precision=lax.Precision.HIGHEST)


def time_rows(frequency_spectrum, gather_record, filters, offsets):
    upper_limit = lax.Precision.HIGHEST
    freq_count = frequency_spectrum.shape[1]
    taps = filters.shape[1]
    cosine_predicted, sine_predicted = phase_tables(offsets, TWIN + taps - 1, 1 - taps, freq_count)
    cosine_recorded, sine_recorded = phase_tables(offsets, TWIN, 0, freq_count)
    recorded_data = jnp.einsum(
        "phk,hmp->mhk", gather_record[0], cosine_recorded, precision=upper_limit
    ) - jnp.einsum("phk,hmp->mhk", gather_record[1], sine_recorded, precision=upper_limit)
    tap_table = tap_matrix(filters, TWIN)
    predicted_multiples = jnp.einsum(
        "tvu,vnt->vnu", frequency_spectrum[0], cosine_predicted, precision=upper_limit
    ) - jnp.einsum("tvu,vnt->vnu", frequency_spectrum[1], sine_predicted, precision=upper_limit)
    filtered = jnp.einsum("stl,slr->tsr", tap_table, predicted_multiples, precision=upper_limit)
    return recorded_data - filtered


def time_output(frequency_spectrum, gather_record, filters, offsets):
    row_count = frequency_spectrum.shape[2]
    block_rows = math.gcd(16, row_count)

    def one_block(block_index):
        first_row = block_index * block_rows
        spec_rows = lax.dynamic_slice_in_dim(frequency_spectrum, first_row, block_rows, 2)
        rec_rows = lax.dynamic_slice_in_dim(gather_record, first_row, block_rows, 2)
        filt_rows = lax.dynamic_slice_in_dim(filters, first_row, block_rows, 0)
        off_rows = lax.dynamic_slice_in_dim(offsets, first_row, block_rows, 0)
        return time_rows(spec_rows, rec_rows, filt_rows, off_rows)

    stacked = lax.map(one_block, jnp.arange(row_count // block_rows, dtype=jnp.int32))
    return jnp.transpose(stacked, (1, 0, 2, 3)).reshape(
        TWIN, row_count, frequency_spectrum.shape[3]
    )


def shards(spectra, panels, filters, offsets):
    row_count = spectra.shape[2]
    col_count = spectra.shape[3]
    frequency_spectrum = jnp.zeros((2, spectra.shape[1], row_count, col_count), jnp.float32)
    for panel_step in range(NPAN):
        panel_id = panels[panel_step]
        owner_col = panel_id * row_count // col_count
        strip_start = panel_id * row_count % col_count
        column_band = lax.dynamic_slice_in_dim(spectra, strip_start, row_count, 3)
        column_band = spread(column_band, "rcv", owner_col)
        row_group_block = spread(spectra, "src", panel_id)
        frequency_spectrum = frequency_spectrum + complex_product(column_band, row_group_block)
    primaries = time_output(frequency_spectrum, spectra, filters, offsets)
    return primaries.astype(jnp.bfloat16)


def solution(mesh):
    return jax.shard_map(
        shards,
        mesh=mesh,
        in_specs=(P(None, None, "src", "rcv"), P(), P("src", None), P("src")),
        out_specs=P(None, "src", "rcv"),
        check_vma=False,
    )
```

profile of v0, /device:TPU:16, one launch (start us, length us, event | category | flops | bytes accessed | tf_op | source)
XLA Modules:
  0.0 786.2 jit_solution(17039019366314087306)
XLA Ops:
  6.5 1.3 fusion.64
  9.1 2.1 dynamic-slice_select_fusion
  12.4 4.3 broadcast_select_fusion
  16.8 42.4 %all-reduce.7.cloned.1.call-done = (f32[2,4,64,64]{3,2,1,0:T(8,128)}, f32[2,4,64,64]{3,2,1,0:T(8,128)}) async-done(((f32[2,4,64,64]{3,2,1,0:T(8,128)}, f32[2,4,64,64]{3,2,1,0:T(8,128)}), (f32[2,4,64,64]{3,2,1,0:T(8,128)}, f32[2,4,64,64]{3,2,1,0:T(8,128)})) %all-reduce.7.cloned.1.call-update) | async-done | bytes 262160 | tf_op jit(solution)/shard_map/psum | solution.py:16
  59.1 623.4 %all-reduce.5.cloned.1.call-done = (f32[2,4,64,1024]{3,2,1,0:T(8,128)}, f32[2,4,64,1024]{3,2,1,0:T(8,128)}) async-done(((f32[2,4,64,1024]{3,2,1,0:T(8,128)}, f32[2,4,64,1024]{3,2,1,0:T(8,128)}), (f32[2,4,64,1024]{3,2,1,0:T(8,128)}, f32[2,4,64,1024]{3,2,1,0:T(8,128)})) %all-reduce.5.cloned.1.call-update) | async-done | bytes 4194320 | tf_op jit(solution)/shard_map/psum | solution.py:16
  682.6 2.4 fusion.62
  685.0 1.9 fusion.63
  693.6 84.2 %while.14 = (s32[]{:T(128)}, bf16[4,8,16,1024]{3,1,2,0:T(8,128)(2,1)S(1)}, s32[4]{0:T(128)S(1)}, s32[64]{0:T(128)S(1)}, f32[2,4,64,1024]{3,2,1,0:T(8,128)}, /*in...) while((s32[]{:T(128)}, ...), condition=%wide.region_5.6_spmd, body=%wide.region_4.5_spmd.sunk | while | flops 244514368 | bytes 24640936 | solution.py:78
  695.1 5.9 fusion.91
  701.0 5.9 fusion.92
  708.1 1.1 fusion.89
  709.2 1.1 fusion.90
  710.3 1.2 fusion.93
  711.5 3.1 fusion.94
  716.1 5.9 fusion.91
  722.0 5.9 fusion.92
  729.1 1.1 fusion.89
  730.2 1.1 fusion.90
  731.4 1.2 fusion.93
  732.6 3.1 fusion.94
  737.2 5.9 fusion.91
  743.1 5.9 fusion.92
  750.2 1.1 fusion.89
  751.3 1.1 fusion.90
  752.5 1.2 fusion.93
  753.6 3.1 fusion.94
  758.2 5.9 fusion.91
  764.2 5.9 fusion.92
  771.2 1.1 fusion.89
  773.5 1.2 fusion.93
  774.7 3.1 fusion.94
  777.8 1.5 copy.6
  (60 shorter events, 15.8 us)
Async XLA Ops:
  6.5 52.6 %all-reduce.7.cloned.1.call-start = ((), (), s32[]{:S(2)}) async-start(), calls=%async_computation.1 | async-start | bytes 1048576 | tf_op jit(solution)/shard_map/psum | solution.py:16
  11.2 671.3 %all-reduce.5.cloned.1.call-start = ((), (), s32[]{:S(2)}) async-start(), calls=%async_computation | async-start | bytes 8388608 | tf_op jit(solution)/shard_map/psum | solution.py:16
  682.6 2.4 copy-start.1
  682.6 4.4 copy-start
  682.6 4.4 copy-start.2
  686.9 2.0 copy-start.3
  693.0 0.7 copy-start.4
Sparse Core Ops, SparseCore 0:
  11.3 47.7 all-reduce.6
  61.8 620.7 all-reduce.4
where the time goes:
time: 787 us; the launch traced here: 786 us
  waiting for transfers between devices  666 us (85%)
  matrix products  83.6 us (11%)
  between operations  16 us (2%)
  local copies, waits for them, and re-layouts  9.96 us (1%)
  other arithmetic  7.94 us (1%)
    psum x2, waiting for transfers between devices, spread(): return lax.psum(jnp.where(mine, shard, jnp.zeros_like(shard)), axis)  666 us
    dot_general x4, matrix products, time_rows(): jnp.einsum('tvu,vnt->vnu', frequency_spectrum[1], sine_predicted, precisi...  23.6 us
    dot_general x4, matrix products, time_rows(): jnp.einsum('tvu,vnt->vnu', frequency_spectrum[0], cosine_predicted, preci...  23.6 us
  transfers between devices with their start and end apart: 2, of which 2 were waited for; matrix products, arithmetic and copies ran while one was open for 1% of the time, Pallas kernels for 0%

commit v1 on v0

v1 whole, which is shorter than its diff:
```python
import math

import jax
import jax.numpy as jnp
import numpy as np
from jax import lax
from jax.experimental import pallas as pl
from jax.experimental.pallas import tpu as pltpu
from jax.sharding import Mesh
from jax.sharding import PartitionSpec as P

TWIN = 8
NT = 2048
FIRST_BIN = 64
FREQ = 4
ROWS = 64
COLS = 1024
LAST = 63
HI = lax.Precision.HIGHEST


def place_of(panel):
    return panel // 16, (panel // 2) % 8, panel % 2


def line_broadcast(v, root, z):
    def at(k):
        return (root + k) % 8

    held = jnp.where(z == root, v, jnp.zeros_like(v))
    up = lax.ppermute(v, "z", [(root, at(3))])
    down = lax.ppermute(v, "z", [(root, at(-3))])
    held = held + up + down
    near = lax.ppermute(held, "z", [(root, at(1)), (at(3), at(2)), (at(-3), at(-2))])
    far = lax.ppermute(held, "z", [(root, at(-1)), (at(3), at(4))])
    return held + near + far


def strips(spectra, panels):
    flat = spectra.reshape(2 * FREQ, ROWS, COLS)
    lane_panel = lax.broadcasted_iota(jnp.int32, (1, 1, 2 * ROWS), 2) // ROWS
    picked = [
        lax.dynamic_slice_in_dim(flat, (panels[i] % 16) * ROWS, ROWS, 2) for i in range(2)
    ]
    block = jnp.concatenate(picked, axis=2)
    owners = panels // 16
    for axis, bit in (("c", owners % 2), ("yh", owners // 2)):
        other = lax.ppermute(block, axis, [(0, 1), (1, 0)])
        keep = jnp.where(lane_panel == 0, bit[0], bit[1]) == lax.axis_index(axis)
        block = jnp.where(keep, block, other)
    return block.reshape(2, FREQ, ROWS, 2 * ROWS)


def kernel(bins, x_ref, l_ref, coef_ref, *refs):
    block_refs, o_ref = refs[:-1], refs[-1]
    total = [None] * TWIN
    for i in range(4):
        own, partner = block_refs[2 * i], block_refs[2 * i + 1]
        cols = own.shape[-1]
        b = jnp.concatenate(
            [own[...].reshape(2 * ROWS, cols), partner[...].reshape(2 * ROWS, cols)], axis=0
        )
        high = b.astype(jnp.bfloat16)
        low = (b - high.astype(jnp.float32)).astype(jnp.bfloat16)
        left = l_ref[bins[i]]
        left_high = left.astype(jnp.bfloat16)
        left_low = (left - left_high.astype(jnp.float32)).astype(jnp.bfloat16)
        product = (
            jnp.dot(left_low, high, preferred_element_type=jnp.float32)
            + jnp.dot(left_high, low, preferred_element_type=jnp.float32)
            + jnp.dot(left_high, high, preferred_element_type=jnp.float32)
        )
        f = bins[i]
        real = x_ref[0, f] - product[:ROWS]
        imag = x_ref[1, f] - product[ROWS:]
        for u in range(TWIN):
            at = u * 8 + i * 2
            term = real * coef_ref[:, at : at + 1] - imag * coef_ref[:, at + 1 : at + 2]
            total[u] = term if total[u] is None else total[u] + term
    for u in range(TWIN):
        o_ref[u] = total[u].astype(o_ref.dtype)


def synthesise(bins, spectra, left, coefs, blocks):
    width = 256
    block_spec = pl.BlockSpec((2, ROWS, width), lambda j, bins: (0, 0, j))
    grid_spec = pltpu.PrefetchScalarGridSpec(
        num_scalar_prefetch=1,
        grid=(COLS // width,),
        in_specs=[
            pl.BlockSpec((2, FREQ, ROWS, width), lambda j, bins: (0, 0, 0, j)),
            pl.BlockSpec((4, 128, 256), lambda j, bins: (0, 0, 0)),
            pl.BlockSpec((ROWS, 64), lambda j, bins: (0, 0)),
            *[block_spec] * 8,
        ],
        out_specs=pl.BlockSpec((TWIN, ROWS, width), lambda j, bins: (0, 0, j)),
    )
    return pl.pallas_call(
        kernel,
        grid_spec=grid_spec,
        out_shape=jax.ShapeDtypeStruct((TWIN, ROWS, COLS), jnp.bfloat16),
        compiler_params=pltpu.CompilerParams(vmem_limit_bytes=40 * 1024 * 1024),
        cost_estimate=pl.CostEstimate(
            flops=2 * 3 * 4 * 128 * 256 * COLS, bytes_accessed=8 * 2**20, transcendentals=0
        ),
    )(bins, spectra, left, coefs, *blocks)


def tables(filters, offsets, strip, bins, yl):
    lag = np.arange(64, dtype=np.int64)[:, None] * (FIRST_BIN + np.arange(FREQ))[None, :] % NT
    lag_angle = lag * (2.0 * math.pi / NT)
    response_cos = jnp.dot(filters, jnp.asarray(np.cos(lag_angle), jnp.float32), precision=HI)
    response_sin = jnp.dot(filters, jnp.asarray(np.sin(lag_angle), jnp.float32), precision=HI)
    a_real, a_imag = strip[0], strip[1]
    rc, rs = response_cos.T[:, :, None], response_sin.T[:, :, None]
    real = a_real * rc + a_imag * rs
    imag = a_imag * rc - a_real * rs
    re_first = jnp.concatenate([real, -imag], axis=2)
    im_first = jnp.concatenate([imag, real], axis=2)
    re_last = jnp.concatenate([-imag, real], axis=2)
    im_last = jnp.concatenate([real, imag], axis=2)
    left = jnp.where(
        yl == 0,
        jnp.concatenate([re_first, im_first], axis=1),
        jnp.concatenate([re_last, im_last], axis=1),
    )
    times = offsets[:, None] + jnp.arange(TWIN, dtype=jnp.int32)[None, :]
    phase = times[:, :, None] * (FIRST_BIN + bins)[None, None, :] % NT
    angle = phase.astype(jnp.float32) * (2.0 * math.pi / NT)
    coefs = jnp.stack([jnp.cos(angle), jnp.sin(angle)], axis=3).reshape(ROWS, 64)
    return left, coefs


def shards(spectra, panels, filters, offsets):
    x, z, yl = lax.axis_index("x"), lax.axis_index("z"), lax.axis_index("yl")
    strip = strips(spectra, panels)
    slot = jnp.where(panels[0] == LAST, 0, 1)
    other = jnp.where(panels[0] == LAST, panels[1], panels[0])
    members = [(f - 2 * c) % 4 * 2 + c for c in range(2) for f in range(4)]
    flat = spectra.reshape(2 * FREQ, ROWS, COLS)
    arrived = lax.all_to_all(
        flat, ("x", "yl"), 0, 0, axis_index_groups=[members], tiled=True
    )
    ox, oz, oy = place_of(other)
    lx, lz, ly = place_of(LAST)
    mine = lax.dynamic_index_in_dim(arrived, oy * 4 + (ox + 2 * oy) % 4, 0, keepdims=False)
    last = arrived[ly * 4 + (lx + 2 * ly) % 4]

    def branch(root):
        return lambda a, b: (line_broadcast(a, root, z), line_broadcast(b, lz, z))

    mine, last = lax.switch(oz, [branch(r) for r in range(8)], mine, last)
    own = jnp.where(slot == 0, jnp.stack([last, mine]), jnp.stack([mine, last]))
    plane = [(i, j) for i in range(4) for j in range(2)]
    across = [(i * 2 + j, ((i + 2) % 4) * 2 + 1 - j) for i, j in plane]
    partner = lax.ppermute(own, ("x", "yl"), across)
    blocks = [own, partner]
    turn = [(i, (i + 1) % 4) for i in range(4)]
    back = [(i, (i - 1) % 4) for i in range(4)]
    for axis, pairs in (("yl", [(0, 1), (1, 0)]), ("x", turn), ("x", back)):
        for v in (own, partner):
            blocks.append(lax.ppermute(v, axis, pairs))
    blocks[2], blocks[3] = blocks[3], blocks[2]
    mine_bin = (x + 2 * yl) % 4
    bins = (mine_bin + jnp.array([0, 2, 3, 1], jnp.int32)) % 4
    left, coefs = tables(filters, offsets, strip, bins, yl)
    return synthesise(bins, spectra, left, coefs, blocks)


def solution(mesh):
    fine = Mesh(mesh.devices.reshape(4, 8, 2, 2, 2), ("x", "z", "yl", "yh", "c"))
    src, rcv = ("x", "z", "yl"), ("yh", "c")
    return jax.shard_map(
        shards,
        mesh=fine,
        in_specs=(P(None, None, src, rcv), P(), P(src, None), P(src)),
        out_specs=P(None, src, rcv),
        check_vma=False,
    )
```

time: 787 us -> 181 us (0.23)
  waiting for transfers between devices: 666 us -> 35.6 us
  starting transfers between devices: 0.04 us -> 118 us
  matrix products: 83.6 us -> 0.39 us
  between operations: 16 us -> 6.14 us
    psum x2 -> x0, waiting for transfers between devices: 666 us -> none  [spread(): return lax.psum(jnp.where(mine, shard, jnp.zeros_like(shard)), axis)]
    ppermute x0 -> x17, starting transfers between devices: none -> 112 us  [the longest x6 67.6 us: shards(): blocks.append(lax.ppermute(v, axis, pairs))]
    dot_general x32 -> x2, matrix products: 83.6 us -> 0.39 us  [the longest x1 0.2 us: tables(): jnp.dot(filters, jnp.asarray(np.sin(lag_angle), jnp.float32), precision=HI)]
    ppermute x0 -> x17, waiting for transfers between devices: none -> 32.5 us  [the longest x2 15.3 us: line_broadcast(): lax.ppermute(held, 'z', [(root, at(1)), (at(3), at(2)), (at(-3), at(-2))])]
  transfers between devices with their start and end apart: 2 -> 18, of which waited for: 2 -> 5; matrix products, arithmetic and copies ran while one was open for 1% -> 7% of each run, Pallas kernels for 0% -> 0%
where the time goes in v1:
time: 181 us; the launch traced here: 178 us
  starting transfers between devices  118 us (65%)
  waiting for transfers between devices  35.6 us (20%)
  other arithmetic  8 us (4%)
  between operations  6.14 us (3%)
  Pallas kernels  5.88 us (3%)
  local copies, waits for them, and re-layouts  3.92 us (2%)
    ppermute x6, starting transfers between devices, shards(): blocks.append(lax.ppermute(v, axis, pairs))  67.6 us
    ppermute x2, starting transfers between devices, strips(): other = lax.ppermute(block, axis, [(0, 1), (1, 0)])  25 us
    ppermute x2, waiting for transfers between devices, line_broadcast(): lax.ppermute(held, 'z', [(root, at(1)), (at(3), at(2)), (at(-3), at(-2))])  15.3 us
    ppermute x6, waiting for transfers between devices, shards(): blocks.append(lax.ppermute(v, axis, pairs))  12.4 us
    ppermute x1, starting transfers between devices, shards(): partner = lax.ppermute(own, ('x', 'yl'), across)  11.8 us
    pallas_call x1, Pallas kernels, synthesise(): pl.pallas_call(kernel, grid_spec=grid_spec, out_shape=jax.ShapeDtypeStruc...  5.88 us
    all_to_all x1, starting transfers between devices, shards(): lax.all_to_all(flat, ('x', 'yl'), 0, 0, axis_index_groups=[members], tile...  5.29 us
    ppermute x2, waiting for transfers between devices, line_broadcast(): far = lax.ppermute(held, 'z', [(root, at(-1)), (at(3), at(4))])  4.84 us
  transfers between devices with their start and end apart: 18, of which 5 were waited for; matrix products, arithmetic and copies ran while one was open for 7% of the time, Pallas kernels for 0%

profile of v1, /device:TPU:16, one launch (start us, length us, event | category | flops | bytes accessed | tf_op | source)
XLA Modules:
  0.0 177.8 jit_solution(2411396574096364765)
XLA Ops:
  0.0 5.3 %all-to-all-start = ((f32[8,64,1024]{2,1,0:T(8,128)}), f32[8,64,1024]{2,1,0:T(8,128)}, u32[]{:S(2)}, u32[]{:S(2)}) async-start(f32[8,64,1024]{2,1,0:T(8,128)} %bitcast.92), calls=%async_computation | async-start | bytes 4194304 | tf_op jit(solution)/shard_map/all_to_all | solution.py:141
  10.1 0.7 copy-done.2
  10.8 0.8 pad_maximum_fusion
  11.6 13.1 %collective-permute-start.64 = (f32[8,64,128]{2,1,0:T(8,128)}, f32[8,64,128]{2,1,0:T(8,128)}, u32[]{:S(2)}, u32[]{:S(2)}) collective-permute-start(f32[8,64,128]{2,1,0:T(8,128)} %pad_maximum_fusion), channel_id=1, source_target_pairs={{0,1},{1,0},{2,3},{3,2},{4,5},{5,4},{6,7},{7,6},{8,9},{9,8},{10,11... | collective-permute-start | bytes 786440 | tf_op jit(solution)/shard_map/ppermute | solution.py:48
  26.4 1.3 fusion.7
  29.7 3.1 %all-to-all-done = f32[8,64,1024]{2,1,0:T(8,128)} async-done(((f32[8,64,1024]{2,1,0:T(8,128)}), f32[8,64,1024]{2,1,0:T(8,128)}, u32[]{:S(2)}, u32[]{:S(2)}) %all-to-all-start) | async-done | bytes 2097184 | tf_op jit(solution)/shard_map/all_to_all | solution.py:141
  32.8 30.6 %conditional.1 = (f32[1,64,1024]{2,1,0:T(8,128)S(1)}, f32[1,64,1024]{2,1,0:T(8,128)S(1)}) conditional(s32[]{:T(128)} %clamp.3, (s32[]{:T(128)}, s32[]{:T(128)}, f32[8,64,1024]{2,1,0:T(8,128)}) %tuple.53, (s32[]{:T(128)}, s32[]{:T(128)}, f32[8,64,1024]{2,1,0:T(8,128)}) %tuple.53, (s32[]{:T(128)}, s32[]{:T(128)}, ...), branch_computations={%region_0.1_spmd, %region_1.2_spmd, %region_2.3_spmd, %region_3.4_... | conditional | flops 655365 | bytes 13631882 | solution.py:152
  32.8 1.1 slice_bitcast_fusion.4
  33.8 1.4 collective-permute-start.36
  35.2 1.4 collective-permute-start.37
  37.3 0.7 collective-permute-start.32
  38.0 1.2 add_add_fusion.8
  39.1 0.7 collective-permute-start.39
  39.8 1.3 collective-permute-start.38
  41.2 1.3 collective-permute-start.35
  42.5 0.7 collective-permute-start.34
  43.2 15.3 %collective-permute-done.38 = f32[64,1024]{1,0:T(8,128)S(1)} collective-permute-done((f32[64,1024]{1,0:T(8,128)S(1)}, f32[64,1024]{1,0:T(8,128)S(1)}, u32[]{:S(2)}, u32[]{:S(2)}) %collective-permute-start.38) | collective-permute-done | bytes 262176 | tf_op jit(solution)/shard_map/cond/branch_4_fun/ppermute | solution.py:34
  58.5 4.8 %collective-permute-done.35 = f32[64,1024]{1,0:T(8,128)S(1)} collective-permute-done((f32[64,1024]{1,0:T(8,128)S(1)}, f32[64,1024]{1,0:T(8,128)S(1)}, u32[]{:S(2)}, u32[]{:S(2)}) %collective-permute-start.35) | collective-permute-done | bytes 262176 | tf_op jit(solution)/shard_map/cond/branch_4_fun/ppermute | solution.py:35
  63.5 8.2 %collective-permute-start.71 = (f32[2,64,1024]{2,1,0:T(8,128)S(1)}, f32[2,64,1024]{2,1,0:T(8,128)S(1)}, u32[]{:S(2)}, u32[]{:S(2)}) collective-permute-start(f32[2,64,1024]{2,1,0:T(8,128)S(1)} %maximum_select_fusion.1.refs_0_), channel_id=1, source_target_pairs={{0,192},{64,0},{128,64},{192,128},{1,193},{65,1},{129,65},{193,129... | collective-permute-start | bytes 1572872 | tf_op jit(solution)/shard_map/ppermute | solution.py:162
  71.7 11.8 %collective-permute-start.66 = (f32[2,64,1024]{2,1,0:T(8,128)S(1)}, f32[2,64,1024]{2,1,0:T(8,128)}, u32[]{:S(2)}, u32[]{:S(2)}) collective-permute-start(f32[2,64,1024]{2,1,0:T(8,128)S(1)} %maximum_select_fusion.1.refs_0_), channel_id=1, source_target_pairs={{0,132},{4,128},{64,196},{68,192},{128,4},{132,0},{192,68},{196,64... | collective-permute-start | bytes 1572872 | tf_op jit(solution)/shard_map/ppermute | solution.py:156
  83.5 1.9 %broadcast_select_fusion = f32[8,64,128]{2,1,0:T(8,128)} fusion(f32[8,64,128]{2,1,0:T(8,128)} %collective-permute-done.64, pred[128]{0:T(512)(128)(4,1)S(1)} %fusion.7, f32[8,64,64]{2,1,0:T(8,128)} %copy-done.2, f32[8,64,64]{2,1,0:T(8,128)S(1)} %get-tuple-element.209), kind=kLoop, calls=%fused_computation.53 | loop fusion | flops 131072 | bytes 786560 | tf_op jit(solution)/shard_map/jit(_where)/select_n | solution.py:50
  85.4 11.8 %collective-permute-start.65 = (f32[8,64,128]{2,1,0:T(8,128)}, f32[8,64,128]{2,1,0:T(8,128)}, u32[]{:S(2)}, u32[]{:S(2)}) collective-permute-start(f32[8,64,128]{2,1,0:T(8,128)} %broadcast_select_fusion), channel_id=1, source_target_pairs={{0,2},{2,0},{1,3},{3,1},{4,6},{6,4},{5,7},{7,5},{8,10},{10,8},{9,1... | collective-permute-start | bytes 786440 | tf_op jit(solution)/shard_map/ppermute | solution.py:48
  97.2 1.3 fusion.6
  98.8 12.0 %collective-permute-start.69 = (f32[2,64,1024]{2,1,0:T(8,128)S(1)}, f32[2,64,1024]{2,1,0:T(8,128)S(1)}, u32[]{:S(2)}, u32[]{:S(2)}) collective-permute-start(f32[2,64,1024]{2,1,0:T(8,128)S(1)} %maximum_select_fusion.1.refs_0_), channel_id=1, source_target_pairs={{0,64},{64,128},{128,192},{192,0},{1,65},{65,129},{129,193},{193,1... | collective-permute-start | bytes 1572872 | tf_op jit(solution)/shard_map/ppermute | solution.py:162
  110.9 11.8 %collective-permute-start.68 = (f32[2,64,1024]{2,1,0:T(8,128)S(1)}, f32[2,64,1024]{2,1,0:T(8,128)S(1)}, u32[]{:S(2)}, u32[]{:S(2)}) collective-permute-start(f32[2,64,1024]{2,1,0:T(8,128)S(1)} %maximum_select_fusion.1.refs_0_), channel_id=1, source_target_pairs={{0,4},{4,0},{1,5},{5,1},{2,6},{6,2},{3,7},{7,3},{8,12},{12,8},{9,1... | collective-permute-start | bytes 1572872 | tf_op jit(solution)/shard_map/ppermute | solution.py:162
  122.7 11.8 %collective-permute-start.72 = (f32[2,64,1024]{2,1,0:T(8,128)}, f32[2,64,1024]{2,1,0:T(8,128)S(1)}, u32[]{:S(2)}, u32[]{:S(2)}) collective-permute-start(f32[2,64,1024]{2,1,0:T(8,128)} %collective-permute-done.66.refs_1_), channel_id=1, source_target_pairs={{0,192},{64,0},{128,64},{192,128},{1,193},{65,1},{129,65},{193,129... | collective-permute-start | bytes 1572872 | tf_op jit(solution)/shard_map/ppermute | solution.py:162
  134.5 11.8 %collective-permute-start.70 = (f32[2,64,1024]{2,1,0:T(8,128)}, f32[2,64,1024]{2,1,0:T(8,128)S(1)}, u32[]{:S(2)}, u32[]{:S(2)}) collective-permute-start(f32[2,64,1024]{2,1,0:T(8,128)} %collective-permute-done.66.refs_1_), channel_id=1, source_target_pairs={{0,64},{64,128},{128,192},{192,0},{1,65},{65,129},{129,193},{193,1... | collective-permute-start | bytes 1572872 | tf_op jit(solution)/shard_map/ppermute | solution.py:162
  146.4 11.8 %collective-permute-start.67 = (f32[2,64,1024]{2,1,0:T(8,128)}, f32[2,64,1024]{2,1,0:T(8,128)S(1)}, u32[]{:S(2)}, u32[]{:S(2)}) collective-permute-start(f32[2,64,1024]{2,1,0:T(8,128)} %collective-permute-done.66.refs_1_), channel_id=1, source_target_pairs={{0,4},{4,0},{1,5},{5,1},{2,6},{6,2},{3,7},{7,3},{8,12},{12,8},{9,1... | collective-permute-start | bytes 1572872 | tf_op jit(solution)/shard_map/ppermute | solution.py:162
  158.2 1.1 broadcast_select_fusion.1
  159.5 2.0 %collective-permute-done.70.refs_5_ = f32[2,64,1024]{2,1,0:T(8,128)S(1)} collective-permute-done((f32[2,64,1024]{2,1,0:T(8,128)}, f32[2,64,1024]{2,1,0:T(8,128)S(1)}, u32[]{:S(2)}, u32[]{:S(2)}) %collective-permute-start.70) | collective-permute-done | bytes 524320 | tf_op jit(solution)/shard_map/ppermute | solution.py:162
  161.5 10.4 %collective-permute-done.67.refs_2_ = f32[2,64,1024]{2,1,0:T(8,128)S(1)} collective-permute-done((f32[2,64,1024]{2,1,0:T(8,128)}, f32[2,64,1024]{2,1,0:T(8,128)S(1)}, u32[]{:S(2)}, u32[]{:S(2)}) %collective-permute-start.67) | collective-permute-done | bytes 524320 | tf_op jit(solution)/shard_map/ppermute | solution.py:162
  171.9 5.9 %shard_map.73 = bf16[8,64,1024]{2,1,0:T(8,128)(2,1)} custom-call(s32[4]{0:T(128)S(1)} %get-tuple-element.188.bins, f32[2,4,64,1024]{3,2,1,0:T(8,128)S(1)} %copy-done.1, f32[4,128,256]{2,1,0:T(8,128)S(1)} %maximum_select_fusion.l_ref, f32[64,64]{1,0:T(8,128)S(1)} %copy.10.coef_ref, f32[2,64,1024]{2,1,0:T(8,128)S(1)} %maximum_select_fusion.1.refs_0_, ...), custom_call_target="tpu_custom_call" | custom-call | flops 805306368 | bytes 8388608 | tf_op jit(solution)/shard_map/pallas_call | solution.py:98
  (49 shorter events, 3.8 us)
Async XLA Ops:
  0.0 26.2 %copy-start = (f32[64,64]{1,0:T(8,128)S(1)}, f32[64,64]{1,0:T(8,128)}, u32[]{:S(2)}) copy-start(f32[64,64]{1,0:T(8,128)} %param.17) | copy-start | bytes 49156
  0.0 5.3 %copy-start.5 = (s32[2]{0:T(128)S(1)}, s32[2]{0:T(128)}, u32[]{:S(2)}) copy-start(s32[2]{0:T(128)} %param.16) | copy-start | bytes 28
  0.0 9.8 %copy-start.1 = (f32[2,4,64,1024]{3,2,1,0:T(8,128)S(1)}, f32[2,4,64,1024]{3,2,1,0:T(8,128)}, u32[]{:S(2)}) copy-start(f32[2,4,64,1024]{3,2,1,0:T(8,128)} %x_ref.1) | copy-start | bytes 6291460
  0.0 26.0 %copy-start.7 = (s32[4]{0:T(128)S(1)}, s32[4]{0:T(128)}, u32[]{:S(2)}) copy-start(s32[4]{0:T(128)} %constant.250.clone) | copy-start | bytes 52
  0.0 26.0 %copy-start.6 = (s32[64]{0:T(128)S(1)}, s32[64]{0:T(128)}, u32[]{:S(2)}) copy-start(s32[64]{0:T(128)} %param.18) | copy-start | bytes 772
  0.0 26.1 %copy-start.4 = (f32[64,4]{1,0:T(8,128)S(1)}, f32[64,4]{1,0:T(8,128)}, u32[]{:S(2)}) copy-start(f32[64,4]{1,0:T(8,128)} %constant.251.clone) | copy-start | bytes 3076
  0.0 32.7 %all-to-all-start = ((f32[8,64,1024]{2,1,0:T(8,128)}), f32[8,64,1024]{2,1,0:T(8,128)}, u32[]{:S(2)}, u32[]{:S(2)}) async-start(f32[8,64,1024]{2,1,0:T(8,128)} %bitcast.92), calls=%async_computation | async-start | bytes 4194304 | tf_op jit(solution)/shard_map/all_to_all | solution.py:141
  10.1 0.7 copy-start.2
  11.6 71.9 %collective-permute-start.64 = (f32[8,64,128]{2,1,0:T(8,128)}, f32[8,64,128]{2,1,0:T(8,128)}, u32[]{:S(2)}, u32[]{:S(2)}) collective-permute-start(f32[8,64,128]{2,1,0:T(8,128)} %pad_maximum_fusion), channel_id=1, source_target_pairs={{0,1},{1,0},{2,3},{3,2},{4,5},{5,4},{6,7},{7,6},{8,9},{9,8},{10,11... | collective-permute-start | bytes 786440 | tf_op jit(solution)/shard_map/ppermute | solution.py:48
  33.8 4.1 %collective-permute-start.36 = (f32[64,1024]{1,0:T(8,128)S(1)}, f32[64,1024]{1,0:T(8,128)}, u32[]{:S(2)}, u32[]{:S(2)}) collective-permute-start(f32[64,1024]{1,0:T(8,128)S(1)} %get-tuple-element.201), channel_id=1, source_target_pairs={{56,16},{57,17},{58,18},{59,19},{60,20},{61,21},{62,22},{63,23},{1... | collective-permute-start | bytes 786440 | tf_op jit(solution)/shard_map/cond/branch_4_fun/ppermute | solution.py:31
  35.2 2.7 %collective-permute-start.37 = (f32[64,1024]{1,0:T(8,128)S(1)}, f32[64,1024]{1,0:T(8,128)}, u32[]{:S(2)}, u32[]{:S(2)}) collective-permute-start(f32[64,1024]{1,0:T(8,128)S(1)} %get-tuple-element.201), channel_id=1, source_target_pairs={{56,32},{57,33},{58,34},{59,35},{60,36},{61,37},{62,38},{63,39},{1... | collective-permute-start | bytes 786440 | tf_op jit(solution)/shard_map/cond/branch_4_fun/ppermute | solution.py:32
  36.6 4.5 %collective-permute-start.33 = (f32[64,1024]{1,0:T(8,128)S(1)}, f32[64,1024]{1,0:T(8,128)S(1)}, u32[]{:S(2)}, u32[]{:S(2)}) collective-permute-start(f32[64,1024]{1,0:T(8,128)S(1)} %get-tuple-element.202), channel_id=1, source_target_pairs={{32,8},{33,9},{34,10},{35,11},{36,12},{37,13},{38,14},{39,15},{96,... | collective-permute-start | bytes 786440 | tf_op jit(solution)/shard_map/cond/branch_4_fun/ppermute | solution.py:32
  37.3 3.9 %collective-permute-start.32 = (f32[64,1024]{1,0:T(8,128)S(1)}, f32[64,1024]{1,0:T(8,128)S(1)}, u32[]{:S(2)}, u32[]{:S(2)}) collective-permute-start(f32[64,1024]{1,0:T(8,128)S(1)} %get-tuple-element.202), channel_id=1, source_target_pairs={{32,56},{33,57},{34,58},{35,59},{36,60},{37,61},{38,62},{39,63},{9... | collective-permute-start | bytes 786440 | tf_op jit(solution)/shard_map/cond/branch_4_fun/ppermute | solution.py:31
  39.1 4.0 %collective-permute-start.39 = (f32[64,1024]{1,0:T(8,128)S(1)}, f32[64,1024]{1,0:T(8,128)S(1)}, u32[]{:S(2)}, u32[]{:S(2)}) collective-permute-start(f32[64,1024]{1,0:T(8,128)S(1)} %add_add_fusion.8), channel_id=1, source_target_pairs={{56,48},{16,24},{57,49},{17,25},{58,50},{18,26},{59,51},{19,27},{6... | collective-permute-start | bytes 786440 | tf_op jit(solution)/shard_map/cond/branch_4_fun/ppermute | solution.py:35
  39.8 18.6 %collective-permute-start.38 = (f32[64,1024]{1,0:T(8,128)S(1)}, f32[64,1024]{1,0:T(8,128)S(1)}, u32[]{:S(2)}, u32[]{:S(2)}) collective-permute-start(f32[64,1024]{1,0:T(8,128)S(1)} %add_add_fusion.8), channel_id=1, source_target_pairs={{56,0},{16,8},{32,40},{57,1},{17,9},{33,41},{58,2},{18,10},{34,42}... | collective-permute-start | bytes 786440 | tf_op jit(solution)/shard_map/cond/branch_4_fun/ppermute | solution.py:34
  41.2 22.1 %collective-permute-start.35 = (f32[64,1024]{1,0:T(8,128)S(1)}, f32[64,1024]{1,0:T(8,128)S(1)}, u32[]{:S(2)}, u32[]{:S(2)}) collective-permute-start(f32[64,1024]{1,0:T(8,128)S(1)} %add_add_fusion.9), channel_id=1, source_target_pairs={{32,24},{56,0},{33,25},{57,1},{34,26},{58,2},{35,27},{59,3},{36,28... | collective-permute-start | bytes 786440 | tf_op jit(solution)/shard_map/cond/branch_4_fun/ppermute | solution.py:35
  42.5 20.8 %collective-permute-start.34 = (f32[64,1024]{1,0:T(8,128)S(1)}, f32[64,1024]{1,0:T(8,128)S(1)}, u32[]{:S(2)}, u32[]{:S(2)}) collective-permute-start(f32[64,1024]{1,0:T(8,128)S(1)} %add_add_fusion.9), channel_id=1, source_target_pairs={{32,40},{56,48},{8,16},{33,41},{57,49},{9,17},{34,42},{58,50},{10,... | collective-permute-start | bytes 786440 | tf_op jit(solution)/shard_map/cond/branch_4_fun/ppermute | solution.py:34
  63.4 35.2 %copy-start.3 = (f32[64,4]{1,0:T(8,128)S(1)}, f32[64,4]{1,0:T(8,128)}, u32[]{:S(2)}) copy-start(f32[64,4]{1,0:T(8,128)} %constant.252.clone) | copy-start | bytes 3076
  63.5 82.9 %collective-permute-start.71 = (f32[2,64,1024]{2,1,0:T(8,128)S(1)}, f32[2,64,1024]{2,1,0:T(8,128)S(1)}, u32[]{:S(2)}, u32[]{:S(2)}) collective-permute-start(f32[2,64,1024]{2,1,0:T(8,128)S(1)} %maximum_select_fusion.1.refs_0_), channel_id=1, source_target_pairs={{0,192},{64,0},{128,64},{192,128},{1,193},{65,1},{129,65},{193,129... | collective-permute-start | bytes 1572872 | tf_op jit(solution)/shard_map/ppermute | solution.py:162
  71.7 51.0 %collective-permute-start.66 = (f32[2,64,1024]{2,1,0:T(8,128)S(1)}, f32[2,64,1024]{2,1,0:T(8,128)}, u32[]{:S(2)}, u32[]{:S(2)}) collective-permute-start(f32[2,64,1024]{2,1,0:T(8,128)S(1)} %maximum_select_fusion.1.refs_0_), channel_id=1, source_target_pairs={{0,132},{4,128},{64,196},{68,192},{128,4},{132,0},{192,68},{196,64... | collective-permute-start | bytes 1572872 | tf_op jit(solution)/shard_map/ppermute | solution.py:156
  85.4 49.1 %collective-permute-start.65 = (f32[8,64,128]{2,1,0:T(8,128)}, f32[8,64,128]{2,1,0:T(8,128)}, u32[]{:S(2)}, u32[]{:S(2)}) collective-permute-start(f32[8,64,128]{2,1,0:T(8,128)} %broadcast_select_fusion), channel_id=1, source_target_pairs={{0,2},{2,0},{1,3},{3,1},{4,6},{6,4},{5,7},{7,5},{8,10},{10,8},{9,1... | collective-permute-start | bytes 786440 | tf_op jit(solution)/shard_map/ppermute | solution.py:48
  98.8 60.6 %collective-permute-start.69 = (f32[2,64,1024]{2,1,0:T(8,128)S(1)}, f32[2,64,1024]{2,1,0:T(8,128)S(1)}, u32[]{:S(2)}, u32[]{:S(2)}) collective-permute-start(f32[2,64,1024]{2,1,0:T(8,128)S(1)} %maximum_select_fusion.1.refs_0_), channel_id=1, source_target_pairs={{0,64},{64,128},{128,192},{192,0},{1,65},{65,129},{129,193},{193,1... | collective-permute-start | bytes 1572872 | tf_op jit(solution)/shard_map/ppermute | solution.py:162
  110.9 48.6 %collective-permute-start.68 = (f32[2,64,1024]{2,1,0:T(8,128)S(1)}, f32[2,64,1024]{2,1,0:T(8,128)S(1)}, u32[]{:S(2)}, u32[]{:S(2)}) collective-permute-start(f32[2,64,1024]{2,1,0:T(8,128)S(1)} %maximum_select_fusion.1.refs_0_), channel_id=1, source_target_pairs={{0,4},{4,0},{1,5},{5,1},{2,6},{6,2},{3,7},{7,3},{8,12},{12,8},{9,1... | collective-permute-start | bytes 1572872 | tf_op jit(solution)/shard_map/ppermute | solution.py:162
  122.7 36.8 %collective-permute-start.72 = (f32[2,64,1024]{2,1,0:T(8,128)}, f32[2,64,1024]{2,1,0:T(8,128)S(1)}, u32[]{:S(2)}, u32[]{:S(2)}) collective-permute-start(f32[2,64,1024]{2,1,0:T(8,128)} %collective-permute-done.66.refs_1_), channel_id=1, source_target_pairs={{0,192},{64,0},{128,64},{192,128},{1,193},{65,1},{129,65},{193,129... | collective-permute-start | bytes 1572872 | tf_op jit(solution)/shard_map/ppermute | solution.py:162
  134.5 27.0 %collective-permute-start.70 = (f32[2,64,1024]{2,1,0:T(8,128)}, f32[2,64,1024]{2,1,0:T(8,128)S(1)}, u32[]{:S(2)}, u32[]{:S(2)}) collective-permute-start(f32[2,64,1024]{2,1,0:T(8,128)} %collective-permute-done.66.refs_1_), channel_id=1, source_target_pairs={{0,64},{64,128},{128,192},{192,0},{1,65},{65,129},{129,193},{193,1... | collective-permute-start | bytes 1572872 | tf_op jit(solution)/shard_map/ppermute | solution.py:162
  146.4 25.5 %collective-permute-start.67 = (f32[2,64,1024]{2,1,0:T(8,128)}, f32[2,64,1024]{2,1,0:T(8,128)S(1)}, u32[]{:S(2)}, u32[]{:S(2)}) collective-permute-start(f32[2,64,1024]{2,1,0:T(8,128)} %collective-permute-done.66.refs_1_), channel_id=1, source_target_pairs={{0,4},{4,0},{1,5},{5,1},{2,6},{6,2},{3,7},{7,3},{8,12},{12,8},{9,1... | collective-permute-start | bytes 1572872 | tf_op jit(solution)/shard_map/ppermute | solution.py:162

commit v2 on v1

--- a/solution.py
+++ b/solution.py
@@ -23,17 +23,35 @@
     return panel // 16, (panel // 2) % 8, panel % 2
 
 
-def line_broadcast(v, root, z):
-    def at(k):
-        return (root + k) % 8
+def leap(v, group):
+    roots = (group, group + 4)
+    up = lax.ppermute(v, "z", [(r, (r + 3) % 8) for r in roots])
+    down = lax.ppermute(v, "z", [(r, (r - 3) % 8) for r in roots])
+    return up, down
 
-    held = jnp.where(z == root, v, jnp.zeros_like(v))
-    up = lax.ppermute(v, "z", [(root, at(3))])
-    down = lax.ppermute(v, "z", [(root, at(-3))])
-    held = held + up + down
-    near = lax.ppermute(held, "z", [(root, at(1)), (at(3), at(2)), (at(-3), at(-2))])
-    far = lax.ppermute(held, "z", [(root, at(-1)), (at(3), at(4))])
-    return held + near + far
+
+def line_broadcast(blocks, roots, z):
+    def branch(group):
+        return lambda a, b: (leap(a, group), leap(b, LAST // 2 % 4))
+
+    leaps = lax.switch(roots[0] % 4, [branch(g) for g in range(4)], *blocks)
+    steps = [(z - root) % 8 for root in roots]
+    held = jnp.stack(
+        [
+            jnp.where(d == 0, v, jnp.where(d == 3, up, down))
+            for d, v, (up, down) in zip(steps, blocks, leaps)
+        ]
+    )
+    after = lax.ppermute(held, "z", [(k, (k + 1) % 8) for k in range(8)])
+    before = lax.ppermute(held, "z", [(k, (k - 1) % 8) for k in range(8)])
+    whole = []
+    for i, d in enumerate(steps):
+        from_after = (d == 1) | (d == 4) | (d == 6)
+        from_before = (d == 2) | (d == 7)
+        whole.append(
+            jnp.where(from_after, after[i], jnp.where(from_before, before[i], held[i]))
+        )
+    return whole
 
 
 def strips(spectra, panels):
@@ -146,10 +164,7 @@
     mine = lax.dynamic_index_in_dim(arrived, oy * 4 + (ox + 2 * oy) % 4, 0, keepdims=False)
     last = arrived[ly * 4 + (lx + 2 * ly) % 4]
 
-    def branch(root):
-        return lambda a, b: (line_broadcast(a, root, z), line_broadcast(b, lz, z))
-
-    mine, last = lax.switch(oz, [branch(r) for r in range(8)], mine, last)
+    mine, last = line_broadcast((mine, last), (oz, lz), z)
     own = jnp.where(slot == 0, jnp.stack([last, mine]), jnp.stack([mine, last]))
     plane = [(i, j) for i in range(4) for j in range(2)]
     across = [(i * 2 + j, ((i + 2) % 4) * 2 + 1 - j) for i, j in plane]

time: 181 us -> 123 us (0.68)
  the two profiles are of different devices: /device:TPU:16 before, /device:TPU:6 now
where the time goes in v2:
time: 123 us; the launch traced here: 122 us
  waiting for transfers between devices  72.4 us (59%)
  starting transfers between devices  26.7 us (22%)
  other arithmetic  7.84 us (6%)
  Pallas kernels  5.84 us (5%)
  between operations  5.8 us (5%)
  local copies, waits for them, and re-layouts  3.17 us (3%)
    all_to_all x1, waiting for transfers between devices, shards(): lax.all_to_all(flat, ('x', 'yl'), 0, 0, axis_index_groups=[members], tile...  15 us
    ppermute x6, waiting for transfers between devices, shards(): blocks.append(lax.ppermute(v, axis, pairs))  14.7 us
    ppermute x2, waiting for transfers between devices, leap(): down = lax.ppermute(v, 'z', [(r, (r - 3) % 8) for r in roots])  13.6 us
    ppermute x1, waiting for transfers between devices, shards(): partner = lax.ppermute(own, ('x', 'yl'), across)  13.3 us
    ppermute x1, waiting for transfers between devices, line_broadcast(): before = lax.ppermute(held, 'z', [(k, (k - 1) % 8) for k in range(8)])  9.51 us
    all_to_all x1, starting transfers between devices, shards(): lax.all_to_all(flat, ('x', 'yl'), 0, 0, axis_index_groups=[members], tile...  6.58 us
    ppermute x6, starting transfers between devices, shards(): blocks.append(lax.ppermute(v, axis, pairs))  5.89 us
    pallas_call x1, Pallas kernels, synthesise(): pl.pallas_call(kernel, grid_spec=grid_spec, out_shape=jax.ShapeDtypeStruc...  5.84 us
  transfers between devices with their start and end apart: 16, of which 9 were waited for; matrix products, arithmetic and copies ran while one was open for 9% of the time, Pallas kernels for 0%

profile of v2, /device:TPU:6, one launch (start us, length us, event | category | flops | bytes accessed | tf_op | source)
XLA Modules:
  0.0 122.2 jit_solution(4854519350299262968)
XLA Ops:
  0.0 6.6 %all-to-all-start = ((f32[8,64,1024]{2,1,0:T(8,128)}), f32[8,64,1024]{2,1,0:T(8,128)}, u32[]{:S(2)}, u32[]{:S(2)}) async-start(f32[8,64,1024]{2,1,0:T(8,128)} %bitcast.48), calls=%async_computation | async-start | bytes 4194304 | tf_op jit(solution)/shard_map/all_to_all | solution.py:159
  6.6 0.6 fusion.17
  11.0 0.8 pad_maximum_fusion.1
  14.5 1.2 fusion.13
  15.7 0.6 fusion.15
  16.3 15.0 %all-to-all-done = f32[8,64,1024]{2,1,0:T(8,128)} async-done(((f32[8,64,1024]{2,1,0:T(8,128)}), f32[8,64,1024]{2,1,0:T(8,128)}, u32[]{:S(2)}, u32[]{:S(2)}) %all-to-all-start) | async-done | bytes 2097184 | tf_op jit(solution)/shard_map/all_to_all | solution.py:159
  31.3 1.1 slice_bitcast_fusion.4
  32.4 19.0 %conditional.1 = (f32[64,1024]{1,0:T(8,128)}, f32[64,1024]{1,0:T(8,128)}, f32[64,1024]{1,0:T(8,128)}, f32[64,1024]{1,0:T(8,128)}) conditional(s32[]{:T(128)} %clamp.3, (f32[64,1024]{1,0:T(8,128)S(1)}, f32[64,1024]{1,0:T(8,128)S(1)}) %tuple.21, (f32[64,1024]{1,0:T(8,128)S(1)}, f32[64,1024]{1,0:T(8,128)S(1)}) %tuple.21, ...), branch_computations={%region_0.1_spmd, %region_1.2_spmd, %region_2.3_spmd, %region_3.4_... | conditional | bytes 4194496 | solution.py:37
  32.4 1.3 %collective-permute-start.13 = (f32[64,1024]{1,0:T(8,128)S(1)}, f32[64,1024]{1,0:T(8,128)}, u32[]{:S(2)}, u32[]{:S(2)}) collective-permute-start(f32[64,1024]{1,0:T(8,128)S(1)} %get-tuple-element.27), channel_id=1, source_target_pairs={{24,0},{56,32},{25,1},{57,33},{26,2},{58,34},{27,3},{59,35},{28,4}... | collective-permute-start | bytes 786440 | tf_op jit(solution)/shard_map/cond/branch_3_fun/ppermute | solution.py:29
  33.7 1.4 %collective-permute-start.12 = (f32[64,1024]{1,0:T(8,128)S(1)}, f32[64,1024]{1,0:T(8,128)}, u32[]{:S(2)}, u32[]{:S(2)}) collective-permute-start(f32[64,1024]{1,0:T(8,128)S(1)} %get-tuple-element.27), channel_id=1, source_target_pairs={{24,48},{56,16},{25,49},{57,17},{26,50},{58,18},{27,51},{59,19},{2... | collective-permute-start | bytes 786440 | tf_op jit(solution)/shard_map/cond/branch_3_fun/ppermute | solution.py:28
  35.1 1.3 %collective-permute-start.15 = (f32[64,1024]{1,0:T(8,128)S(1)}, f32[64,1024]{1,0:T(8,128)}, u32[]{:S(2)}, u32[]{:S(2)}) collective-permute-start(f32[64,1024]{1,0:T(8,128)S(1)} %get-tuple-element.28), channel_id=1, source_target_pairs={{24,0},{56,32},{25,1},{57,33},{26,2},{58,34},{27,3},{59,35},{28,4}... | collective-permute-start | bytes 786440 | tf_op jit(solution)/shard_map/cond/branch_3_fun/ppermute | solution.py:29
  36.4 1.4 %collective-permute-start.14 = (f32[64,1024]{1,0:T(8,128)S(1)}, f32[64,1024]{1,0:T(8,128)}, u32[]{:S(2)}, u32[]{:S(2)}) collective-permute-start(f32[64,1024]{1,0:T(8,128)S(1)} %get-tuple-element.28), channel_id=1, source_target_pairs={{24,48},{56,16},{25,49},{57,17},{26,50},{58,18},{27,51},{59,19},{2... | collective-permute-start | bytes 786440 | tf_op jit(solution)/shard_map/cond/branch_3_fun/ppermute | solution.py:28
  37.7 5.9 %collective-permute-done.13 = f32[64,1024]{1,0:T(8,128)} collective-permute-done((f32[64,1024]{1,0:T(8,128)S(1)}, f32[64,1024]{1,0:T(8,128)}, u32[]{:S(2)}, u32[]{:S(2)}) %collective-permute-start.13) | collective-permute-done | bytes 262176 | tf_op jit(solution)/shard_map/cond/branch_3_fun/ppermute | solution.py:29
  43.6 7.7 %collective-permute-done.15 = f32[64,1024]{1,0:T(8,128)} collective-permute-done((f32[64,1024]{1,0:T(8,128)S(1)}, f32[64,1024]{1,0:T(8,128)}, u32[]{:S(2)}, u32[]{:S(2)}) %collective-permute-start.15) | collective-permute-done | bytes 262176 | tf_op jit(solution)/shard_map/cond/branch_3_fun/ppermute | solution.py:29
  51.4 1.2 select_select_fusion
  52.7 2.8 %collective-permute-start.19 = (f32[2,64,1024]{2,1,0:T(8,128)S(1)}, f32[2,64,1024]{2,1,0:T(8,128)S(1)}, u32[]{:S(2)}, u32[]{:S(2)}) collective-permute-start(f32[2,64,1024]{2,1,0:T(8,128)S(1)} %pad_maximum_fusion), channel_id=1, source_target_pairs={{0,56},{8,0},{16,8},{24,16},{32,24},{40,32},{48,40},{56,48},{1,57}... | collective-permute-start | bytes 1572872 | tf_op jit(solution)/shard_map/ppermute | solution.py:46
  55.9 9.5 %collective-permute-done.19 = f32[2,64,1024]{2,1,0:T(8,128)S(1)} collective-permute-done((f32[2,64,1024]{2,1,0:T(8,128)S(1)}, f32[2,64,1024]{2,1,0:T(8,128)S(1)}, u32[]{:S(2)}, u32[]{:S(2)}) %collective-permute-start.19) | collective-permute-done | bytes 524320 | tf_op jit(solution)/shard_map/ppermute | solution.py:46
  65.4 4.5 %collective-permute-done.18 = f32[2,64,1024]{2,1,0:T(8,128)S(1)} collective-permute-done((f32[2,64,1024]{2,1,0:T(8,128)S(1)}, f32[2,64,1024]{2,1,0:T(8,128)S(1)}, u32[]{:S(2)}, u32[]{:S(2)}) %collective-permute-start.18) | collective-permute-done | bytes 524320 | tf_op jit(solution)/shard_map/ppermute | solution.py:45
  70.4 3.2 %collective-permute-start.20 = (f32[2,64,1024]{2,1,0:T(8,128)S(1)}, f32[2,64,1024]{2,1,0:T(8,128)}, u32[]{:S(2)}, u32[]{:S(2)}) collective-permute-start(f32[2,64,1024]{2,1,0:T(8,128)S(1)} %maximum_select_fusion.1.refs_0_), channel_id=1, source_target_pairs={{0,132},{4,128},{64,196},{68,192},{128,4},{132,0},{192,68},{196,64... | collective-permute-start | bytes 1572872 | tf_op jit(solution)/shard_map/ppermute | solution.py:171
  73.6 1.8 %broadcast_select_fusion = f32[8,64,128]{2,1,0:T(8,128)} fusion(f32[8,64,128]{2,1,0:T(8,128)} %collective-permute-done.16, pred[128]{0:T(512)(128)(4,1)S(1)} %fusion.13, f32[8,64,64]{2,1,0:T(8,128)S(1)} %copy-done.3, f32[8,64,64]{2,1,0:T(8,128)S(1)} %get-tuple-element.45), kind=kLoop, calls=%fused_computation.20 | loop fusion | flops 131072 | bytes 786560 | tf_op jit(solution)/shard_map/jit(_where)/select_n | solution.py:68
  75.4 2.9 %collective-permute-start.17 = (f32[8,64,128]{2,1,0:T(8,128)}, f32[8,64,128]{2,1,0:T(8,128)S(1)}, u32[]{:S(2)}, u32[]{:S(2)}) collective-permute-start(f32[8,64,128]{2,1,0:T(8,128)} %broadcast_select_fusion), channel_id=1, source_target_pairs={{0,2},{2,0},{1,3},{3,1},{4,6},{6,4},{5,7},{7,5},{8,10},{10,8},{9,1... | collective-permute-start | bytes 786440 | tf_op jit(solution)/shard_map/ppermute | solution.py:66
  78.3 1.3 %fusion.12 = pred[128]{0:T(512)(128)(4,1)S(1)} fusion(s32[]{:T(128)S(6)} %axis_index.59, s32[]{:T(128)} %bitcast.1, s32[]{:T(128)} %bitcast), kind=kLoop, calls=%fused_computation.55 | loop fusion | flops 1408 | bytes 140 | tf_op jit(solution)/shard_map/eq | solution.py:67
  79.9 1.1 collective-permute-start.23
  81.0 0.9 collective-permute-start.22
  81.9 13.3 %collective-permute-done.20.refs_1_ = f32[2,64,1024]{2,1,0:T(8,128)} collective-permute-done((f32[2,64,1024]{2,1,0:T(8,128)S(1)}, f32[2,64,1024]{2,1,0:T(8,128)}, u32[]{:S(2)}, u32[]{:S(2)}) %collective-permute-start.20) | collective-permute-done | bytes 524320 | tf_op jit(solution)/shard_map/ppermute | solution.py:171
  95.1 1.8 %collective-permute-done.17 = f32[8,64,128]{2,1,0:T(8,128)S(1)} collective-permute-done((f32[8,64,128]{2,1,0:T(8,128)}, f32[8,64,128]{2,1,0:T(8,128)S(1)}, u32[]{:S(2)}, u32[]{:S(2)}) %collective-permute-start.17) | collective-permute-done | bytes 262176 | tf_op jit(solution)/shard_map/ppermute | solution.py:66
  96.9 1.5 %collective-permute-start.24 = (f32[2,64,1024]{2,1,0:T(8,128)}, f32[2,64,1024]{2,1,0:T(8,128)S(1)}, u32[]{:S(2)}, u32[]{:S(2)}) collective-permute-start(f32[2,64,1024]{2,1,0:T(8,128)} %collective-permute-done.20.refs_1_), channel_id=1, source_target_pairs={{0,64},{64,128},{128,192},{192,0},{1,65},{65,129},{129,193},{193,1... | collective-permute-start | bytes 1572872 | tf_op jit(solution)/shard_map/ppermute | solution.py:177
  98.4 2.1 %collective-permute-start.21 = (f32[2,64,1024]{2,1,0:T(8,128)}, f32[2,64,1024]{2,1,0:T(8,128)S(1)}, u32[]{:S(2)}, u32[]{:S(2)}) collective-permute-start(f32[2,64,1024]{2,1,0:T(8,128)} %collective-permute-done.20.refs_1_), channel_id=1, source_target_pairs={{0,4},{4,0},{1,5},{5,1},{2,6},{6,2},{3,7},{7,3},{8,12},{12,8},{9,1... | collective-permute-start | bytes 1572872 | tf_op jit(solution)/shard_map/ppermute | solution.py:177
  100.5 1.0 broadcast_select_fusion.1
  101.7 6.7 %collective-permute-done.22.refs_3_ = f32[2,64,1024]{2,1,0:T(8,128)S(1)} collective-permute-done((f32[2,64,1024]{2,1,0:T(8,128)S(1)}, f32[2,64,1024]{2,1,0:T(8,128)S(1)}, u32[]{:S(2)}, u32[]{:S(2)}) %collective-permute-start.22) | collective-permute-done | bytes 524320 | tf_op jit(solution)/shard_map/ppermute | solution.py:177
  108.3 8.0 %collective-permute-done.21.refs_2_ = f32[2,64,1024]{2,1,0:T(8,128)S(1)} collective-permute-done((f32[2,64,1024]{2,1,0:T(8,128)}, f32[2,64,1024]{2,1,0:T(8,128)S(1)}, u32[]{:S(2)}, u32[]{:S(2)}) %collective-permute-start.21) | collective-permute-done | bytes 524320 | tf_op jit(solution)/shard_map/ppermute | solution.py:177
  116.4 5.8 %shard_map.73 = bf16[8,64,1024]{2,1,0:T(8,128)(2,1)} custom-call(s32[4]{0:T(128)S(1)} %get-tuple-element.38.bins, f32[2,4,64,1024]{3,2,1,0:T(8,128)S(1)} %copy-done.1, f32[4,128,256]{2,1,0:T(8,128)S(1)} %maximum_select_fusion.l_ref, f32[64,64]{1,0:T(8,128)S(1)} %copy.10.coef_ref, f32[2,64,1024]{2,1,0:T(8,128)S(1)} %maximum_select_fusion.1.refs_0_, ...), custom_call_target="tpu_custom_call" | custom-call | flops 805306368 | bytes 8388608 | tf_op jit(solution)/shard_map/pallas_call | solution.py:116
  (46 shorter events, 2.3 us)
Async XLA Ops:
  0.0 55.7 %copy-start = (f32[64,64]{1,0:T(8,128)S(1)}, f32[64,64]{1,0:T(8,128)}, u32[]{:S(2)}) copy-start(f32[64,64]{1,0:T(8,128)} %param.13) | copy-start | bytes 49156
  0.0 6.6 %copy-start.6 = (s32[2]{0:T(128)S(1)}, s32[2]{0:T(128)}, u32[]{:S(2)}) copy-start(s32[2]{0:T(128)} %param.12) | copy-start | bytes 28
  0.0 10.8 %copy-start.1 = (f32[2,4,64,1024]{3,2,1,0:T(8,128)S(1)}, f32[2,4,64,1024]{3,2,1,0:T(8,128)}, u32[]{:S(2)}) copy-start(f32[2,4,64,1024]{3,2,1,0:T(8,128)} %x_ref.1) | copy-start | bytes 6291460
  0.0 31.3 %all-to-all-start = ((f32[8,64,1024]{2,1,0:T(8,128)}), f32[8,64,1024]{2,1,0:T(8,128)}, u32[]{:S(2)}, u32[]{:S(2)}) async-start(f32[8,64,1024]{2,1,0:T(8,128)} %bitcast.48), calls=%async_computation | async-start | bytes 4194304 | tf_op jit(solution)/shard_map/all_to_all | solution.py:159
  6.6 9.7 %copy-start.8 = (s32[4]{0:T(128)S(1)}, s32[4]{0:T(128)}, u32[]{:S(2)}) copy-start(s32[4]{0:T(128)} %constant.189.clone) | copy-start | bytes 52
  6.6 9.7 %copy-start.7 = (s32[64]{0:T(128)S(1)}, s32[64]{0:T(128)}, u32[]{:S(2)}) copy-start(s32[64]{0:T(128)} %param.14) | copy-start | bytes 772
  11.0 41.6 %copy-start.2 = (f32[8,64,64]{2,1,0:T(8,128)}, f32[8,64,64]{2,1,0:T(8,128)S(1)}, u32[]{:S(2)}) copy-start(f32[8,64,64]{2,1,0:T(8,128)S(1)} %get-tuple-element.46) | copy-start | bytes 393220
  11.9 61.7 %collective-permute-start.16 = (f32[8,64,128]{2,1,0:T(8,128)}, f32[8,64,128]{2,1,0:T(8,128)}, u32[]{:S(2)}, u32[]{:S(2)}) collective-permute-start(f32[8,64,128]{2,1,0:T(8,128)} %pad_maximum_fusion.1), channel_id=1, source_target_pairs={{0,1},{1,0},{2,3},{3,2},{4,5},{5,4},{6,7},{7,6},{8,9},{9,8},{10,11... | collective-permute-start | bytes 786440 | tf_op jit(solution)/shard_map/ppermute | solution.py:66
  16.3 39.4 %copy-start.5 = (f32[64,4]{1,0:T(8,128)S(1)}, f32[64,4]{1,0:T(8,128)}, u32[]{:S(2)}) copy-start(f32[64,4]{1,0:T(8,128)} %constant.190.clone) | copy-start | bytes 3076
  32.4 11.3 %collective-permute-start.13 = (f32[64,1024]{1,0:T(8,128)S(1)}, f32[64,1024]{1,0:T(8,128)}, u32[]{:S(2)}, u32[]{:S(2)}) collective-permute-start(f32[64,1024]{1,0:T(8,128)S(1)} %get-tuple-element.27), channel_id=1, source_target_pairs={{24,0},{56,32},{25,1},{57,33},{26,2},{58,34},{27,3},{59,35},{28,4}... | collective-permute-start | bytes 786440 | tf_op jit(solution)/shard_map/cond/branch_3_fun/ppermute | solution.py:29
  33.7 10.0 %collective-permute-start.12 = (f32[64,1024]{1,0:T(8,128)S(1)}, f32[64,1024]{1,0:T(8,128)}, u32[]{:S(2)}, u32[]{:S(2)}) collective-permute-start(f32[64,1024]{1,0:T(8,128)S(1)} %get-tuple-element.27), channel_id=1, source_target_pairs={{24,48},{56,16},{25,49},{57,17},{26,50},{58,18},{27,51},{59,19},{2... | collective-permute-start | bytes 786440 | tf_op jit(solution)/shard_map/cond/branch_3_fun/ppermute | solution.py:28
  35.1 16.3 %collective-permute-start.15 = (f32[64,1024]{1,0:T(8,128)S(1)}, f32[64,1024]{1,0:T(8,128)}, u32[]{:S(2)}, u32[]{:S(2)}) collective-permute-start(f32[64,1024]{1,0:T(8,128)S(1)} %get-tuple-element.28), channel_id=1, source_target_pairs={{24,0},{56,32},{25,1},{57,33},{26,2},{58,34},{27,3},{59,35},{28,4}... | collective-permute-start | bytes 786440 | tf_op jit(solution)/shard_map/cond/branch_3_fun/ppermute | solution.py:29
  36.4 15.0 %collective-permute-start.14 = (f32[64,1024]{1,0:T(8,128)S(1)}, f32[64,1024]{1,0:T(8,128)}, u32[]{:S(2)}, u32[]{:S(2)}) collective-permute-start(f32[64,1024]{1,0:T(8,128)S(1)} %get-tuple-element.28), channel_id=1, source_target_pairs={{24,48},{56,16},{25,49},{57,17},{26,50},{58,18},{27,51},{59,19},{2... | collective-permute-start | bytes 786440 | tf_op jit(solution)/shard_map/cond/branch_3_fun/ppermute | solution.py:28
  52.6 21.0 %copy-start.3 = (f32[8,64,64]{2,1,0:T(8,128)S(1)}, f32[8,64,64]{2,1,0:T(8,128)}, u32[]{:S(2)}) copy-start(f32[8,64,64]{2,1,0:T(8,128)} %copy-done.2) | copy-start | bytes 393220
  52.7 12.7 %collective-permute-start.19 = (f32[2,64,1024]{2,1,0:T(8,128)S(1)}, f32[2,64,1024]{2,1,0:T(8,128)S(1)}, u32[]{:S(2)}, u32[]{:S(2)}) collective-permute-start(f32[2,64,1024]{2,1,0:T(8,128)S(1)} %pad_maximum_fusion), channel_id=1, source_target_pairs={{0,56},{8,0},{16,8},{24,16},{32,24},{40,32},{48,40},{56,48},{1,57}... | collective-permute-start | bytes 1572872 | tf_op jit(solution)/shard_map/ppermute | solution.py:46
  55.5 14.4 %collective-permute-start.18 = (f32[2,64,1024]{2,1,0:T(8,128)S(1)}, f32[2,64,1024]{2,1,0:T(8,128)S(1)}, u32[]{:S(2)}, u32[]{:S(2)}) collective-permute-start(f32[2,64,1024]{2,1,0:T(8,128)S(1)} %pad_maximum_fusion), channel_id=1, source_target_pairs={{0,8},{8,16},{16,24},{24,32},{32,40},{40,48},{48,56},{56,0},{1,9},... | collective-permute-start | bytes 1572872 | tf_op jit(solution)/shard_map/ppermute | solution.py:45
  55.9 23.8 %copy-start.4 = (f32[64,4]{1,0:T(8,128)S(1)}, f32[64,4]{1,0:T(8,128)}, u32[]{:S(2)}) copy-start(f32[64,4]{1,0:T(8,128)} %constant.191.clone) | copy-start | bytes 3076
  70.1 28.3 %collective-permute-start.25 = (f32[2,64,1024]{2,1,0:T(8,128)S(1)}, f32[2,64,1024]{2,1,0:T(8,128)S(1)}, u32[]{:S(2)}, u32[]{:S(2)}) collective-permute-start(f32[2,64,1024]{2,1,0:T(8,128)S(1)} %maximum_select_fusion.1.refs_0_), channel_id=1, source_target_pairs={{0,192},{64,0},{128,64},{192,128},{1,193},{65,1},{129,65},{193,129... | collective-permute-start | bytes 1572872 | tf_op jit(solution)/shard_map/ppermute | solution.py:177
  70.4 24.7 %collective-permute-start.20 = (f32[2,64,1024]{2,1,0:T(8,128)S(1)}, f32[2,64,1024]{2,1,0:T(8,128)}, u32[]{:S(2)}, u32[]{:S(2)}) collective-permute-start(f32[2,64,1024]{2,1,0:T(8,128)S(1)} %maximum_select_fusion.1.refs_0_), channel_id=1, source_target_pairs={{0,132},{4,128},{64,196},{68,192},{128,4},{132,0},{192,68},{196,64... | collective-permute-start | bytes 1572872 | tf_op jit(solution)/shard_map/ppermute | solution.py:171
  75.4 21.5 %collective-permute-start.17 = (f32[8,64,128]{2,1,0:T(8,128)}, f32[8,64,128]{2,1,0:T(8,128)S(1)}, u32[]{:S(2)}, u32[]{:S(2)}) collective-permute-start(f32[8,64,128]{2,1,0:T(8,128)} %broadcast_select_fusion), channel_id=1, source_target_pairs={{0,2},{2,0},{1,3},{3,1},{4,6},{6,4},{5,7},{7,5},{8,10},{10,8},{9,1... | collective-permute-start | bytes 786440 | tf_op jit(solution)/shard_map/ppermute | solution.py:66
  79.9 21.8 %collective-permute-start.23 = (f32[2,64,1024]{2,1,0:T(8,128)S(1)}, f32[2,64,1024]{2,1,0:T(8,128)S(1)}, u32[]{:S(2)}, u32[]{:S(2)}) collective-permute-start(f32[2,64,1024]{2,1,0:T(8,128)S(1)} %maximum_select_fusion.1.refs_0_), channel_id=1, source_target_pairs={{0,64},{64,128},{128,192},{192,0},{1,65},{65,129},{129,193},{193,1... | collective-permute-start | bytes 1572872 | tf_op jit(solution)/shard_map/ppermute | solution.py:177
  81.0 27.3 %collective-permute-start.22 = (f32[2,64,1024]{2,1,0:T(8,128)S(1)}, f32[2,64,1024]{2,1,0:T(8,128)S(1)}, u32[]{:S(2)}, u32[]{:S(2)}) collective-permute-start(f32[2,64,1024]{2,1,0:T(8,128)S(1)} %maximum_select_fusion.1.refs_0_), channel_id=1, source_target_pairs={{0,4},{4,0},{1,5},{5,1},{2,6},{6,2},{3,7},{7,3},{8,12},{12,8},{9,1... | collective-permute-start | bytes 1572872 | tf_op jit(solution)/shard_map/ppermute | solution.py:177
  95.1 13.2 %collective-permute-start.26 = (f32[2,64,1024]{2,1,0:T(8,128)}, f32[2,64,1024]{2,1,0:T(8,128)S(1)}, u32[]{:S(2)}, u32[]{:S(2)}) collective-permute-start(f32[2,64,1024]{2,1,0:T(8,128)} %collective-permute-done.20.refs_1_), channel_id=1, source_target_pairs={{0,192},{64,0},{128,64},{192,128},{1,193},{65,1},{129,65},{193,129... | collective-permute-start | bytes 1572872 | tf_op jit(solution)/shard_map/ppermute | solution.py:177
  96.9 11.4 %collective-permute-start.24 = (f32[2,64,1024]{2,1,0:T(8,128)}, f32[2,64,1024]{2,1,0:T(8,128)S(1)}, u32[]{:S(2)}, u32[]{:S(2)}) collective-permute-start(f32[2,64,1024]{2,1,0:T(8,128)} %collective-permute-done.20.refs_1_), channel_id=1, source_target_pairs={{0,64},{64,128},{128,192},{192,0},{1,65},{65,129},{129,193},{193,1... | collective-permute-start | bytes 1572872 | tf_op jit(solution)/shard_map/ppermute | solution.py:177
  98.4 18.0 %collective-permute-start.21 = (f32[2,64,1024]{2,1,0:T(8,128)}, f32[2,64,1024]{2,1,0:T(8,128)S(1)}, u32[]{:S(2)}, u32[]{:S(2)}) collective-permute-start(f32[2,64,1024]{2,1,0:T(8,128)} %collective-permute-done.20.refs_1_), channel_id=1, source_target_pairs={{0,4},{4,0},{1,5},{5,1},{2,6},{6,2},{3,7},{7,3},{8,12},{12,8},{9,1... | collective-permute-start | bytes 1572872 | tf_op jit(solution)/shard_map/ppermute | solution.py:177

commit v3 on v2

--- a/solution.py
+++ b/solution.py
@@ -15,6 +15,8 @@
 FREQ = 4
 ROWS = 64
 COLS = 1024
+WIDTH = 256
+PARTS = 2
 LAST = 63
 HI = lax.Precision.HIGHEST
 
@@ -30,22 +32,24 @@
     return up, down
 
 
-def line_broadcast(blocks, roots, z):
+def leaps(blocks, roots, z):
     def branch(group):
         return lambda a, b: (leap(a, group), leap(b, LAST // 2 % 4))
 
-    leaps = lax.switch(roots[0] % 4, [branch(g) for g in range(4)], *blocks)
-    steps = [(z - root) % 8 for root in roots]
-    held = jnp.stack(
+    leapt = lax.switch(roots[0] % 4, [branch(g) for g in range(4)], *blocks)
+    return jnp.stack(
         [
             jnp.where(d == 0, v, jnp.where(d == 3, up, down))
-            for d, v, (up, down) in zip(steps, blocks, leaps)
+            for d, v, (up, down) in zip([(z - r) % 8 for r in roots], blocks, leapt)
         ]
     )
+
+
+def steps(held, roots, z):
     after = lax.ppermute(held, "z", [(k, (k + 1) % 8) for k in range(8)])
     before = lax.ppermute(held, "z", [(k, (k - 1) % 8) for k in range(8)])
     whole = []
-    for i, d in enumerate(steps):
+    for i, d in enumerate([(z - r) % 8 for r in roots]):
         from_after = (d == 1) | (d == 4) | (d == 6)
         from_before = (d == 2) | (d == 7)
         whole.append(
@@ -70,7 +74,7 @@
 
 
 def kernel(bins, x_ref, l_ref, coef_ref, *refs):
-    block_refs, o_ref = refs[:-1], refs[-1]
+    block_refs, o_ref = refs[:8], refs[-1]
     total = [None] * TWIN
     for i in range(4):
         own, partner = block_refs[2 * i], block_refs[2 * i + 1]
@@ -99,29 +103,38 @@
         o_ref[u] = total[u].astype(o_ref.dtype)
 
 
-def synthesise(bins, spectra, left, coefs, blocks):
-    width = 256
-    block_spec = pl.BlockSpec((2, ROWS, width), lambda j, bins: (0, 0, j))
+def synthesise(bins, spectra, left, coefs, blocks, first, count, before=None):
+    block_spec = pl.BlockSpec((2, ROWS, WIDTH), lambda j, bins: (0, 0, j))
+    in_specs = [
+        pl.BlockSpec((2, FREQ, ROWS, WIDTH), lambda j, bins: (0, 0, 0, first + j)),
+        pl.BlockSpec((4, 128, 256), lambda j, bins: (0, 0, 0)),
+        pl.BlockSpec((ROWS, 64), lambda j, bins: (0, 0)),
+        *[block_spec] * 8,
+    ]
+    operands = [bins, spectra, left, coefs, *blocks]
+    aliases = {}
+    if before is not None:
+        in_specs.append(pl.BlockSpec(memory_space=pl.ANY))
+        operands.append(before)
+        aliases = {len(operands) - 1: 0}
     grid_spec = pltpu.PrefetchScalarGridSpec(
         num_scalar_prefetch=1,
-        grid=(COLS // width,),
-        in_specs=[
-            pl.BlockSpec((2, FREQ, ROWS, width), lambda j, bins: (0, 0, 0, j)),
-            pl.BlockSpec((4, 128, 256), lambda j, bins: (0, 0, 0)),
-            pl.BlockSpec((ROWS, 64), lambda j, bins: (0, 0)),
-            *[block_spec] * 8,
-        ],
-        out_specs=pl.BlockSpec((TWIN, ROWS, width), lambda j, bins: (0, 0, j)),
+        grid=(count,),
+        in_specs=in_specs,
+        out_specs=pl.BlockSpec((TWIN, ROWS, WIDTH), lambda j, bins: (0, 0, first + j)),
     )
     return pl.pallas_call(
         kernel,
         grid_spec=grid_spec,
         out_shape=jax.ShapeDtypeStruct((TWIN, ROWS, COLS), jnp.bfloat16),
+        input_output_aliases=aliases,
         compiler_params=pltpu.CompilerParams(vmem_limit_bytes=40 * 1024 * 1024),
         cost_estimate=pl.CostEstimate(
-            flops=2 * 3 * 4 * 128 * 256 * COLS, bytes_accessed=8 * 2**20, transcendentals=0
+            flops=2 * 3 * 4 * 128 * 256 * WIDTH * count,
+            bytes_accessed=2 * 2**20 * count,
+            transcendentals=0,
         ),
-    )(bins, spectra, left, coefs, *blocks)
+    )(*operands)
 
 
 def tables(filters, offsets, strip, bins, yl):
@@ -149,23 +162,12 @@
     return left, coefs
 
 
-def shards(spectra, panels, filters, offsets):
-    x, z, yl = lax.axis_index("x"), lax.axis_index("z"), lax.axis_index("yl")
-    strip = strips(spectra, panels)
-    slot = jnp.where(panels[0] == LAST, 0, 1)
-    other = jnp.where(panels[0] == LAST, panels[1], panels[0])
+def scatter(rows):
     members = [(f - 2 * c) % 4 * 2 + c for c in range(2) for f in range(4)]
-    flat = spectra.reshape(2 * FREQ, ROWS, COLS)
-    arrived = lax.all_to_all(
-        flat, ("x", "yl"), 0, 0, axis_index_groups=[members], tiled=True
-    )
-    ox, oz, oy = place_of(other)
-    lx, lz, ly = place_of(LAST)
-    mine = lax.dynamic_index_in_dim(arrived, oy * 4 + (ox + 2 * oy) % 4, 0, keepdims=False)
-    last = arrived[ly * 4 + (lx + 2 * ly) % 4]
-
-    mine, last = line_broadcast((mine, last), (oz, lz), z)
-    own = jnp.where(slot == 0, jnp.stack([last, mine]), jnp.stack([mine, last]))
+    return lax.all_to_all(rows, ("x", "yl"), 0, 0, axis_index_groups=[members], tiled=True)
+
+
+def exchange(own):
     plane = [(i, j) for i in range(4) for j in range(2)]
     across = [(i * 2 + j, ((i + 2) % 4) * 2 + 1 - j) for i, j in plane]
     partner = lax.ppermute(own, ("x", "yl"), across)
@@ -176,10 +178,39 @@
         for v in (own, partner):
             blocks.append(lax.ppermute(v, axis, pairs))
     blocks[2], blocks[3] = blocks[3], blocks[2]
-    mine_bin = (x + 2 * yl) % 4
-    bins = (mine_bin + jnp.array([0, 2, 3, 1], jnp.int32)) % 4
+    return blocks
+
+
+def shards(spectra, panels, filters, offsets):
+    x, z, yl = lax.axis_index("x"), lax.axis_index("z"), lax.axis_index("yl")
+    slot = jnp.where(panels[0] == LAST, 0, 1)
+    other = jnp.where(panels[0] == LAST, panels[1], panels[0])
+    ox, oz, oy = place_of(other)
+    lx, lz, ly = place_of(LAST)
+    flat = spectra.reshape(2 * FREQ, ROWS, COLS)
+    strip = strips(spectra, panels)
+    bins = ((x + 2 * yl) % 4 + jnp.array([0, 2, 3, 1], jnp.int32)) % 4
+    half = COLS // PARTS
+    owns, held = [], None
+    for part in range(PARTS):
+        arrived = scatter(flat[:, :, part * half : (part + 1) * half])
+        if part:
+            held, arrived = lax.optimization_barrier((held, arrived))
+            owns.append(steps(held, (oz, lz), z))
+        mine = lax.dynamic_index_in_dim(arrived, oy * 4 + (ox + 2 * oy) % 4, 0, keepdims=False)
+        last = arrived[ly * 4 + (lx + 2 * ly) % 4]
+        held = leaps((mine, last), (oz, lz), z)
+    owns.append(steps(held, (oz, lz), z))
+    owns = [jnp.where(slot == 0, jnp.stack([b, a]), jnp.stack([a, b])) for a, b in owns]
+    owns[0], strip = lax.optimization_barrier((owns[0], strip))
     left, coefs = tables(filters, offsets, strip, bins, yl)
-    return synthesise(bins, spectra, left, coefs, blocks)
+    result = None
+    for part in range(PARTS):
+        count = half // WIDTH
+        result = synthesise(
+            bins, spectra, left, coefs, exchange(owns[part]), part * count, count, result
+        )
+    return result
 
 
 def solution(mesh):

time: 123 us -> 128 us (1.041)
  the two profiles are of different devices: /device:TPU:6 before, /device:TPU:16 now
where the time goes in v3:
time: 128 us; the launch traced here: 130 us
  starting transfers between devices  60.2 us (47%)
  waiting for transfers between devices  38.3 us (30%)
  local copies, waits for them, and re-layouts  8.72 us (7%)
  Pallas kernels  8.14 us (6%)
  other arithmetic  7.95 us (6%)
  between operations  6.11 us (5%)
    ppermute x12, starting transfers between devices, exchange(): blocks.append(lax.ppermute(v, axis, pairs))  18.6 us
    ppermute x4, waiting for transfers between devices, leap(): down = lax.ppermute(v, 'z', [(r, (r - 3) % 8) for r in roots])  16.4 us
    ppermute x4, starting transfers between devices, leap(): up = lax.ppermute(v, 'z', [(r, (r + 3) % 8) for r in roots])  15.9 us
    all_to_all x2, waiting for transfers between devices, scatter(): lax.all_to_all(rows, ('x', 'yl'), 0, 0, axis_index_groups=[members], tile...  10.9 us
    all_to_all x2, starting transfers between devices, scatter(): lax.all_to_all(rows, ('x', 'yl'), 0, 0, axis_index_groups=[members], tile...  8.72 us
    pallas_call x2, Pallas kernels, synthesise(): pl.pallas_call(kernel, grid_spec=grid_spec, out_shape=jax.ShapeDtypeStruc...  8.14 us
    ppermute x4, starting transfers between devices, leap(): down = lax.ppermute(v, 'z', [(r, (r - 3) % 8) for r in roots])  7.93 us
    ppermute x12, waiting for transfers between devices, exchange(): blocks.append(lax.ppermute(v, axis, pairs))  6.34 us
  transfers between devices with their start and end apart: 30, of which 7 were waited for; matrix products, arithmetic and copies ran while one was open for 10% of the time, Pallas kernels for 3%

profile of v3, /device:TPU:16, one launch (start us, length us, event | category | flops | bytes accessed | tf_op | source)
XLA Modules:
  0.0 130.0 jit_solution(3271208442281289964)
XLA Ops:
  0.0 1.3 %fusion.23 = (s32[1]{0:T(128)}, s32[1]{0:T(128)}) fusion(s32[2]{0:T(128)} %param.16), kind=kLoop, calls=%fused_computation.76 | loop fusion | bytes 16 | tf_op jit(solution)/shard_map/slice | solution.py:187
  6.5 3.1 %fusion.20 = (f32[8,64,512]{2,1,0:T(8,128)}, f32[8,64,512]{2,1,0:T(8,128)}) fusion(f32[8,64,1024]{2,1,0:T(8,128)} %bitcast.76), kind=kLoop, calls=%fused_computation.73 | loop fusion | bytes 4194304 | tf_op jit(solution)/shard_map/slice | solution.py:196
  9.7 5.2 %all-to-all-start = ((f32[8,64,512]{2,1,0:T(8,128)}), f32[8,64,512]{2,1,0:T(8,128)S(1)}, u32[]{:S(2)}, u32[]{:S(2)}) async-start(f32[8,64,512]{2,1,0:T(8,128)} %get-tuple-element.86), calls=%async_computation | async-start | bytes 2097152 | tf_op jit(solution)/shard_map/all_to_all | solution.py:167
  20.7 10.9 %all-to-all-done = f32[8,64,512]{2,1,0:T(8,128)S(1)} async-done(((f32[8,64,512]{2,1,0:T(8,128)}), f32[8,64,512]{2,1,0:T(8,128)S(1)}, u32[]{:S(2)}, u32[]{:S(2)}) %all-to-all-start) | async-done | bytes 1048608 | tf_op jit(solution)/shard_map/all_to_all | solution.py:167
  31.6 3.6 %all-to-all-start.1 = ((f32[8,64,512]{2,1,0:T(8,128)}), f32[8,64,512]{2,1,0:T(8,128)S(1)}, u32[]{:S(2)}, u32[]{:S(2)}) async-start(f32[8,64,512]{2,1,0:T(8,128)} %get-tuple-element.85), calls=%async_computation.1 | async-start | bytes 2097152 | tf_op jit(solution)/shard_map/all_to_all | solution.py:167
  35.2 1.2 fusion.16
  37.2 20.7 %conditional.2 = (f32[64,512]{1,0:T(8,128)}, f32[64,512]{1,0:T(8,128)}, f32[64,512]{1,0:T(8,128)}, f32[64,512]{1,0:T(8,128)}) conditional(s32[]{:T(128)} %clamp.4, (f32[64,512]{1,0:T(8,128)S(1)}, f32[64,512]{1,0:T(8,128)S(1)}) %tuple.39, (f32[64,512]{1,0:T(8,128)S(1)}, f32[64,512]{1,0:T(8,128)S(1)}) %tuple.39, ...), branch_computations={%region_0.1_spmd, %region_1.2_spmd, %region_2.3_spmd, %region_3.4_... | conditional | bytes 2097344 | solution.py:39
  37.2 7.2 %collective-permute-start = (f32[64,512]{1,0:T(8,128)S(1)}, f32[64,512]{1,0:T(8,128)}, u32[]{:S(2)}, u32[]{:S(2)}) collective-permute-start(f32[64,512]{1,0:T(8,128)S(1)} %get-tuple-element.37), channel_id=1, source_target_pairs={{0,24},{32,56},{1,25},{33,57},{2,26},{34,58},{3,27},{35,59},{4,28}... | collective-permute-start | bytes 393224 | tf_op jit(solution)/shard_map/cond/branch_0_fun/ppermute | solution.py:30
  44.4 3.4 %collective-permute-start.1 = (f32[64,512]{1,0:T(8,128)S(1)}, f32[64,512]{1,0:T(8,128)}, u32[]{:S(2)}, u32[]{:S(2)}) collective-permute-start(f32[64,512]{1,0:T(8,128)S(1)} %get-tuple-element.37), channel_id=1, source_target_pairs={{0,40},{32,8},{1,41},{33,9},{2,42},{34,10},{3,43},{35,11},{4,44},{... | collective-permute-start | bytes 393224 | tf_op jit(solution)/shard_map/cond/branch_0_fun/ppermute | solution.py:31
  47.8 1.3 %collective-permute-start.2 = (f32[64,512]{1,0:T(8,128)S(1)}, f32[64,512]{1,0:T(8,128)}, u32[]{:S(2)}, u32[]{:S(2)}) collective-permute-start(f32[64,512]{1,0:T(8,128)S(1)} %get-tuple-element.38), channel_id=1, source_target_pairs={{24,48},{56,16},{25,49},{57,17},{26,50},{58,18},{27,51},{59,19},{2... | collective-permute-start | bytes 393224 | tf_op jit(solution)/shard_map/cond/branch_0_fun/ppermute | solution.py:30
  49.1 1.3 collective-permute-start.3
  50.4 7.4 %collective-permute-done.3 = f32[64,512]{1,0:T(8,128)} collective-permute-done((f32[64,512]{1,0:T(8,128)S(1)}, f32[64,512]{1,0:T(8,128)}, u32[]{:S(2)}, u32[]{:S(2)}) %collective-permute-start.3) | collective-permute-done | bytes 131104 | tf_op jit(solution)/shard_map/cond/branch_0_fun/ppermute | solution.py:31
  59.1 19.6 %conditional.3 = (f32[64,512]{1,0:T(8,128)}, f32[64,512]{1,0:T(8,128)}, f32[64,512]{1,0:T(8,128)}, f32[64,512]{1,0:T(8,128)}) conditional(s32[]{:T(128)} %clamp.4, (f32[64,512]{1,0:T(8,128)S(1)}, f32[64,512]{1,0:T(8,128)S(1)}) %tuple.42, (f32[64,512]{1,0:T(8,128)S(1)}, f32[64,512]{1,0:T(8,128)S(1)}) %tuple.42, ...), branch_computations={%region_4.5_spmd, %region_5.6_spmd, %region_6.7_spmd, %region_7.8_... | conditional | bytes 2097344 | solution.py:39
  59.1 6.1 %collective-permute-start.16 = (f32[64,512]{1,0:T(8,128)S(1)}, f32[64,512]{1,0:T(8,128)}, u32[]{:S(2)}, u32[]{:S(2)}) collective-permute-start(f32[64,512]{1,0:T(8,128)S(1)} %get-tuple-element.45), channel_id=1, source_target_pairs={{0,24},{32,56},{1,25},{33,57},{2,26},{34,58},{3,27},{35,59},{4,28}... | collective-permute-start | bytes 393224 | tf_op jit(solution)/shard_map/cond/branch_0_fun/ppermute | solution.py:30
  65.2 1.9 %collective-permute-start.17 = (f32[64,512]{1,0:T(8,128)S(1)}, f32[64,512]{1,0:T(8,128)}, u32[]{:S(2)}, u32[]{:S(2)}) collective-permute-start(f32[64,512]{1,0:T(8,128)S(1)} %get-tuple-element.45), channel_id=1, source_target_pairs={{0,40},{32,8},{1,41},{33,9},{2,42},{34,10},{3,43},{35,11},{4,44},{... | collective-permute-start | bytes 393224 | tf_op jit(solution)/shard_map/cond/branch_0_fun/ppermute | solution.py:31
  67.1 1.3 %collective-permute-start.18 = (f32[64,512]{1,0:T(8,128)S(1)}, f32[64,512]{1,0:T(8,128)}, u32[]{:S(2)}, u32[]{:S(2)}) collective-permute-start(f32[64,512]{1,0:T(8,128)S(1)} %get-tuple-element.46), channel_id=1, source_target_pairs={{24,48},{56,16},{25,49},{57,17},{26,50},{58,18},{27,51},{59,19},{2... | collective-permute-start | bytes 393224 | tf_op jit(solution)/shard_map/cond/branch_0_fun/ppermute | solution.py:30
  68.4 1.3 collective-permute-start.19
  69.8 9.0 %collective-permute-done.19 = f32[64,512]{1,0:T(8,128)} collective-permute-done((f32[64,512]{1,0:T(8,128)S(1)}, f32[64,512]{1,0:T(8,128)}, u32[]{:S(2)}, u32[]{:S(2)}) %collective-permute-start.19) | collective-permute-done | bytes 131104 | tf_op jit(solution)/shard_map/cond/branch_0_fun/ppermute | solution.py:31
  80.7 2.1 %collective-permute-start.36 = (f32[2,64,512]{2,1,0:T(8,128)S(1)}, f32[2,64,512]{2,1,0:T(8,128)S(1)}, u32[]{:S(2)}, u32[]{:S(2)}) collective-permute-start(f32[2,64,512]{2,1,0:T(8,128)S(1)} %pad_maximum_fusion.2), channel_id=1, source_target_pairs={{0,8},{8,16},{16,24},{24,32},{32,40},{40,48},{48,56},{56,0},{1,9},... | collective-permute-start | bytes 786440 | tf_op jit(solution)/shard_map/ppermute | solution.py:49
  84.0 1.9 %collective-permute-done.33 = f32[2,64,512]{2,1,0:T(8,128)S(1)} collective-permute-done((f32[2,64,512]{2,1,0:T(8,128)S(1)}, f32[2,64,512]{2,1,0:T(8,128)S(1)}, u32[]{:S(2)}, u32[]{:S(2)}) %collective-permute-start.33) | collective-permute-done | bytes 262176 | tf_op jit(solution)/shard_map/ppermute | solution.py:50
  86.0 4.4 %collective-permute-start.45 = (f32[2,64,512]{2,1,0:T(8,128)S(1)}, f32[2,64,512]{2,1,0:T(8,128)S(1)}, u32[]{:S(2)}, u32[]{:S(2)}) collective-permute-start(f32[2,64,512]{2,1,0:T(8,128)S(1)} %maximum_select_fusion.1.refs_0_), channel_id=1, source_target_pairs={{0,132},{4,128},{64,196},{68,192},{128,4},{132,0},{192,68},{196,64... | collective-permute-start | bytes 786440 | tf_op jit(solution)/shard_map/ppermute | solution.py:173
  91.6 2.7 %collective-permute-start.50 = (f32[2,64,512]{2,1,0:T(8,128)S(1)}, f32[2,64,512]{2,1,0:T(8,128)S(1)}, u32[]{:S(2)}, u32[]{:S(2)}) collective-permute-start(f32[2,64,512]{2,1,0:T(8,128)S(1)} %maximum_select_fusion.1.refs_0_), channel_id=1, source_target_pairs={{0,192},{64,0},{128,64},{192,128},{1,193},{65,1},{129,65},{193,129... | collective-permute-start | bytes 786440 | tf_op jit(solution)/shard_map/ppermute | solution.py:179
  94.7 2.7 %collective-permute-done.45.refs_1_ = f32[2,64,512]{2,1,0:T(8,128)S(1)} collective-permute-done((f32[2,64,512]{2,1,0:T(8,128)S(1)}, f32[2,64,512]{2,1,0:T(8,128)S(1)}, u32[]{:S(2)}, u32[]{:S(2)}) %collective-permute-start.45) | collective-permute-done | bytes 262176 | tf_op jit(solution)/shard_map/ppermute | solution.py:173
  97.5 2.3 %collective-permute-start.40 = (f32[2,64,512]{2,1,0:T(8,128)S(1)}, f32[2,64,512]{2,1,0:T(8,128)}, u32[]{:S(2)}, u32[]{:S(2)}) collective-permute-start(f32[2,64,512]{2,1,0:T(8,128)S(1)} %maximum_select_fusion.2.refs_0_), channel_id=1, source_target_pairs={{0,4},{4,0},{1,5},{5,1},{2,6},{6,2},{3,7},{7,3},{8,12},{12,8},{9,1... | collective-permute-start | bytes 786440 | tf_op jit(solution)/shard_map/ppermute | solution.py:179
  99.8 5.3 %collective-permute-done.47.refs_3_ = f32[2,64,512]{2,1,0:T(8,128)S(1)} collective-permute-done((f32[2,64,512]{2,1,0:T(8,128)S(1)}, f32[2,64,512]{2,1,0:T(8,128)S(1)}, u32[]{:S(2)}, u32[]{:S(2)}) %collective-permute-start.47) | collective-permute-done | bytes 262176 | tf_op jit(solution)/shard_map/ppermute | solution.py:179
  105.4 3.1 %collective-permute-start.49 = (f32[2,64,512]{2,1,0:T(8,128)S(1)}, f32[2,64,512]{2,1,0:T(8,128)}, u32[]{:S(2)}, u32[]{:S(2)}) collective-permute-start(f32[2,64,512]{2,1,0:T(8,128)S(1)} %collective-permute-done.45.refs_1_), channel_id=1, source_target_pairs={{0,64},{64,128},{128,192},{192,0},{1,65},{65,129},{129,193},{193,1... | collective-permute-start | bytes 786440 | tf_op jit(solution)/shard_map/ppermute | solution.py:179
  109.6 2.0 %collective-permute-start.41 = (f32[2,64,512]{2,1,0:T(8,128)S(1)}, f32[2,64,512]{2,1,0:T(8,128)S(1)}, u32[]{:S(2)}, u32[]{:S(2)}) collective-permute-start(f32[2,64,512]{2,1,0:T(8,128)S(1)} %maximum_select_fusion.2.refs_0_), channel_id=1, source_target_pairs={{0,64},{64,128},{128,192},{192,0},{1,65},{65,129},{129,193},{193,1... | collective-permute-start | bytes 786440 | tf_op jit(solution)/shard_map/ppermute | solution.py:179
  111.6 1.9 %collective-permute-start.43 = (f32[2,64,512]{2,1,0:T(8,128)S(1)}, f32[2,64,512]{2,1,0:T(8,128)S(1)}, u32[]{:S(2)}, u32[]{:S(2)}) collective-permute-start(f32[2,64,512]{2,1,0:T(8,128)S(1)} %maximum_select_fusion.2.refs_0_), channel_id=1, source_target_pairs={{0,192},{64,0},{128,64},{192,128},{1,193},{65,1},{129,65},{193,129... | collective-permute-start | bytes 786440 | tf_op jit(solution)/shard_map/ppermute | solution.py:179
  114.6 1.9 %collective-permute-start.39 = (f32[2,64,512]{2,1,0:T(8,128)}, f32[2,64,512]{2,1,0:T(8,128)S(1)}, u32[]{:S(2)}, u32[]{:S(2)}) collective-permute-start(f32[2,64,512]{2,1,0:T(8,128)} %collective-permute-done.38.refs_1_), channel_id=1, source_target_pairs={{0,4},{4,0},{1,5},{5,1},{2,6},{6,2},{3,7},{7,3},{8,12},{12,8},{9,1... | collective-permute-start | bytes 786440 | tf_op jit(solution)/shard_map/ppermute | solution.py:179
  116.8 2.9 %collective-permute-start.44 = (f32[2,64,512]{2,1,0:T(8,128)}, f32[2,64,512]{2,1,0:T(8,128)S(1)}, u32[]{:S(2)}, u32[]{:S(2)}) collective-permute-start(f32[2,64,512]{2,1,0:T(8,128)} %collective-permute-done.38.refs_1_), channel_id=1, source_target_pairs={{0,192},{64,0},{128,64},{192,128},{1,193},{65,1},{129,65},{193,129... | collective-permute-start | bytes 786440 | tf_op jit(solution)/shard_map/ppermute | solution.py:179
  121.8 4.1 %shard_map.73.refs_8_ = bf16[8,64,1024]{2,1,0:T(8,128)(2,1)} custom-call(s32[4]{0:T(128)S(1)} %get-tuple-element.78.bins, f32[2,4,64,1024]{3,2,1,0:T(8,128)S(1)} %copy-done.1, f32[4,128,256]{2,1,0:T(8,128)S(1)} %maximum_select_fusion.l_ref, f32[64,64]{1,0:T(8,128)S(1)} %copy.13.coef_ref, f32[2,64,512]{2,1,0:T(8,128)S(1)} %maximum_select_fusion.1.refs_0_, ...), custom_call_target="tpu_custom_call" | custom-call | flops 402653184 | bytes 4194304 | tf_op jit(solution)/shard_map/pallas_call | solution.py:126
  125.9 4.0 %shard_map.74 = bf16[8,64,1024]{2,1,0:T(8,128)(2,1)} custom-call(s32[4]{0:T(128)S(1)} %get-tuple-element.78.bins, f32[2,4,64,1024]{3,2,1,0:T(8,128)S(1)} %copy-done.1, f32[4,128,256]{2,1,0:T(8,128)S(1)} %maximum_select_fusion.l_ref, f32[64,64]{1,0:T(8,128)S(1)} %copy.13.coef_ref, ...), custom_call_target="tpu_custom_call", output_to_operand_aliasing={{}: (12, {})} | custom-call | flops 402653184 | bytes 4194304 | tf_op jit(solution)/shard_map/pallas_call | solution.py:126
  (83 shorter events, 16.9 us)
Async XLA Ops:
  6.4 10.5 %collective-permute-start.34 = (f32[8,64,128]{2,1,0:T(8,128)S(1)}, f32[8,64,128]{2,1,0:T(8,128)S(1)}, u32[]{:S(2)}, u32[]{:S(2)}) collective-permute-start(f32[8,64,128]{2,1,0:T(8,128)S(1)} %pad_maximum_fusion.1), channel_id=1, source_target_pairs={{0,1},{1,0},{2,3},{3,2},{4,5},{5,4},{6,7},{7,6},{8,9},{9,8},{10,11... | collective-permute-start | bytes 786440 | tf_op jit(solution)/shard_map/ppermute | solution.py:70
  9.7 21.9 %all-to-all-start = ((f32[8,64,512]{2,1,0:T(8,128)}), f32[8,64,512]{2,1,0:T(8,128)S(1)}, u32[]{:S(2)}, u32[]{:S(2)}) async-start(f32[8,64,512]{2,1,0:T(8,128)} %get-tuple-element.86), calls=%async_computation | async-start | bytes 2097152 | tf_op jit(solution)/shard_map/all_to_all | solution.py:167
  17.2 19.2 %collective-permute-start.35 = (f32[8,64,128]{2,1,0:T(8,128)S(1)}, f32[8,64,128]{2,1,0:T(8,128)S(1)}, u32[]{:S(2)}, u32[]{:S(2)}) collective-permute-start(f32[8,64,128]{2,1,0:T(8,128)S(1)} %broadcast_select_fusion), channel_id=1, source_target_pairs={{0,2},{2,0},{1,3},{3,1},{4,6},{6,4},{5,7},{7,5},{8,10},{10,8},{9,1... | collective-permute-start | bytes 786440 | tf_op jit(solution)/shard_map/ppermute | solution.py:70
  31.6 27.4 %all-to-all-start.1 = ((f32[8,64,512]{2,1,0:T(8,128)}), f32[8,64,512]{2,1,0:T(8,128)S(1)}, u32[]{:S(2)}, u32[]{:S(2)}) async-start(f32[8,64,512]{2,1,0:T(8,128)} %get-tuple-element.85), calls=%async_computation.1 | async-start | bytes 2097152 | tf_op jit(solution)/shard_map/all_to_all | solution.py:167
  37.2 13.2 %collective-permute-start = (f32[64,512]{1,0:T(8,128)S(1)}, f32[64,512]{1,0:T(8,128)}, u32[]{:S(2)}, u32[]{:S(2)}) collective-permute-start(f32[64,512]{1,0:T(8,128)S(1)} %get-tuple-element.37), channel_id=1, source_target_pairs={{0,24},{32,56},{1,25},{33,57},{2,26},{34,58},{3,27},{35,59},{4,28}... | collective-permute-start | bytes 393224 | tf_op jit(solution)/shard_map/cond/branch_0_fun/ppermute | solution.py:30
  44.4 6.0 %collective-permute-start.1 = (f32[64,512]{1,0:T(8,128)S(1)}, f32[64,512]{1,0:T(8,128)}, u32[]{:S(2)}, u32[]{:S(2)}) collective-permute-start(f32[64,512]{1,0:T(8,128)S(1)} %get-tuple-element.37), channel_id=1, source_target_pairs={{0,40},{32,8},{1,41},{33,9},{2,42},{34,10},{3,43},{35,11},{4,44},{... | collective-permute-start | bytes 393224 | tf_op jit(solution)/shard_map/cond/branch_0_fun/ppermute | solution.py:31
  47.8 2.6 %collective-permute-start.2 = (f32[64,512]{1,0:T(8,128)S(1)}, f32[64,512]{1,0:T(8,128)}, u32[]{:S(2)}, u32[]{:S(2)}) collective-permute-start(f32[64,512]{1,0:T(8,128)S(1)} %get-tuple-element.38), channel_id=1, source_target_pairs={{24,48},{56,16},{25,49},{57,17},{26,50},{58,18},{27,51},{59,19},{2... | collective-permute-start | bytes 393224 | tf_op jit(solution)/shard_map/cond/branch_0_fun/ppermute | solution.py:30
  49.1 8.8 %collective-permute-start.3 = (f32[64,512]{1,0:T(8,128)S(1)}, f32[64,512]{1,0:T(8,128)}, u32[]{:S(2)}, u32[]{:S(2)}) collective-permute-start(f32[64,512]{1,0:T(8,128)S(1)} %get-tuple-element.38), channel_id=1, source_target_pairs={{24,0},{56,32},{25,1},{57,33},{26,2},{58,34},{27,3},{59,35},{28,4}... | collective-permute-start | bytes 393224 | tf_op jit(solution)/shard_map/cond/branch_0_fun/ppermute | solution.py:31
  59.0 25.0 %collective-permute-start.32 = (f32[2,64,512]{2,1,0:T(8,128)S(1)}, f32[2,64,512]{2,1,0:T(8,128)S(1)}, u32[]{:S(2)}, u32[]{:S(2)}) collective-permute-start(f32[2,64,512]{2,1,0:T(8,128)S(1)} %pad_maximum_fusion), channel_id=1, source_target_pairs={{0,8},{8,16},{16,24},{24,32},{32,40},{40,48},{48,56},{56,0},{1,9},... | collective-permute-start | bytes 786440 | tf_op jit(solution)/shard_map/ppermute | solution.py:49
  59.1 10.6 %collective-permute-start.16 = (f32[64,512]{1,0:T(8,128)S(1)}, f32[64,512]{1,0:T(8,128)}, u32[]{:S(2)}, u32[]{:S(2)}) collective-permute-start(f32[64,512]{1,0:T(8,128)S(1)} %get-tuple-element.45), channel_id=1, source_target_pairs={{0,24},{32,56},{1,25},{33,57},{2,26},{34,58},{3,27},{35,59},{4,28}... | collective-permute-start | bytes 393224 | tf_op jit(solution)/shard_map/cond/branch_0_fun/ppermute | solution.py:30
  65.2 4.5 %collective-permute-start.17 = (f32[64,512]{1,0:T(8,128)S(1)}, f32[64,512]{1,0:T(8,128)}, u32[]{:S(2)}, u32[]{:S(2)}) collective-permute-start(f32[64,512]{1,0:T(8,128)S(1)} %get-tuple-element.45), channel_id=1, source_target_pairs={{0,40},{32,8},{1,41},{33,9},{2,42},{34,10},{3,43},{35,11},{4,44},{... | collective-permute-start | bytes 393224 | tf_op jit(solution)/shard_map/cond/branch_0_fun/ppermute | solution.py:31
  67.1 2.6 %collective-permute-start.18 = (f32[64,512]{1,0:T(8,128)S(1)}, f32[64,512]{1,0:T(8,128)}, u32[]{:S(2)}, u32[]{:S(2)}) collective-permute-start(f32[64,512]{1,0:T(8,128)S(1)} %get-tuple-element.46), channel_id=1, source_target_pairs={{24,48},{56,16},{25,49},{57,17},{26,50},{58,18},{27,51},{59,19},{2... | collective-permute-start | bytes 393224 | tf_op jit(solution)/shard_map/cond/branch_0_fun/ppermute | solution.py:30
  68.4 10.3 %collective-permute-start.19 = (f32[64,512]{1,0:T(8,128)S(1)}, f32[64,512]{1,0:T(8,128)}, u32[]{:S(2)}, u32[]{:S(2)}) collective-permute-start(f32[64,512]{1,0:T(8,128)S(1)} %get-tuple-element.46), channel_id=1, source_target_pairs={{24,0},{56,32},{25,1},{57,33},{26,2},{58,34},{27,3},{59,35},{28,4}... | collective-permute-start | bytes 393224 | tf_op jit(solution)/shard_map/cond/branch_0_fun/ppermute | solution.py:31
  78.7 7.2 %collective-permute-start.33 = (f32[2,64,512]{2,1,0:T(8,128)S(1)}, f32[2,64,512]{2,1,0:T(8,128)S(1)}, u32[]{:S(2)}, u32[]{:S(2)}) collective-permute-start(f32[2,64,512]{2,1,0:T(8,128)S(1)} %pad_maximum_fusion), channel_id=1, source_target_pairs={{0,56},{8,0},{16,8},{24,16},{32,24},{40,32},{48,40},{56,48},{1,57}... | collective-permute-start | bytes 786440 | tf_op jit(solution)/shard_map/ppermute | solution.py:50
  79.7 29.7 %copy-start.4 = (f32[64,4]{1,0:T(8,128)S(1)}, f32[64,4]{1,0:T(8,128)}, u32[]{:S(2)}) copy-start(f32[64,4]{1,0:T(8,128)} %constant.209.clone) | copy-start | bytes 3076
  80.7 10.9 %collective-permute-start.36 = (f32[2,64,512]{2,1,0:T(8,128)S(1)}, f32[2,64,512]{2,1,0:T(8,128)S(1)}, u32[]{:S(2)}, u32[]{:S(2)}) collective-permute-start(f32[2,64,512]{2,1,0:T(8,128)S(1)} %pad_maximum_fusion.2), channel_id=1, source_target_pairs={{0,8},{8,16},{16,24},{24,32},{32,40},{40,48},{48,56},{56,0},{1,9},... | collective-permute-start | bytes 786440 | tf_op jit(solution)/shard_map/ppermute | solution.py:49
  82.8 11.5 %collective-permute-start.37 = (f32[2,64,512]{2,1,0:T(8,128)S(1)}, f32[2,64,512]{2,1,0:T(8,128)S(1)}, u32[]{:S(2)}, u32[]{:S(2)}) collective-permute-start(f32[2,64,512]{2,1,0:T(8,128)S(1)} %pad_maximum_fusion.2), channel_id=1, source_target_pairs={{0,56},{8,0},{16,8},{24,16},{32,24},{40,32},{48,40},{56,48},{1,57}... | collective-permute-start | bytes 786440 | tf_op jit(solution)/shard_map/ppermute | solution.py:50
  86.0 34.9 %copy-start.1 = (f32[2,4,64,1024]{3,2,1,0:T(8,128)S(1)}, f32[2,4,64,1024]{3,2,1,0:T(8,128)}, u32[]{:S(2)}) copy-start(f32[2,4,64,1024]{3,2,1,0:T(8,128)} %x_ref.3) | copy-start | bytes 6291460
  86.0 11.5 %collective-permute-start.45 = (f32[2,64,512]{2,1,0:T(8,128)S(1)}, f32[2,64,512]{2,1,0:T(8,128)S(1)}, u32[]{:S(2)}, u32[]{:S(2)}) collective-permute-start(f32[2,64,512]{2,1,0:T(8,128)S(1)} %maximum_select_fusion.1.refs_0_), channel_id=1, source_target_pairs={{0,132},{4,128},{64,196},{68,192},{128,4},{132,0},{192,68},{196,64... | collective-permute-start | bytes 786440 | tf_op jit(solution)/shard_map/ppermute | solution.py:173
  90.4 14.6 %collective-permute-start.47 = (f32[2,64,512]{2,1,0:T(8,128)S(1)}, f32[2,64,512]{2,1,0:T(8,128)S(1)}, u32[]{:S(2)}, u32[]{:S(2)}) collective-permute-start(f32[2,64,512]{2,1,0:T(8,128)S(1)} %maximum_select_fusion.1.refs_0_), channel_id=1, source_target_pairs={{0,4},{4,0},{1,5},{5,1},{2,6},{6,2},{3,7},{7,3},{8,12},{12,8},{9,1... | collective-permute-start | bytes 786440 | tf_op jit(solution)/shard_map/ppermute | solution.py:179
  91.0 14.4 %collective-permute-start.48 = (f32[2,64,512]{2,1,0:T(8,128)S(1)}, f32[2,64,512]{2,1,0:T(8,128)S(1)}, u32[]{:S(2)}, u32[]{:S(2)}) collective-permute-start(f32[2,64,512]{2,1,0:T(8,128)S(1)} %maximum_select_fusion.1.refs_0_), channel_id=1, source_target_pairs={{0,64},{64,128},{128,192},{192,0},{1,65},{65,129},{129,193},{193,1... | collective-permute-start | bytes 786440 | tf_op jit(solution)/shard_map/ppermute | solution.py:179
  91.6 17.0 %collective-permute-start.50 = (f32[2,64,512]{2,1,0:T(8,128)S(1)}, f32[2,64,512]{2,1,0:T(8,128)S(1)}, u32[]{:S(2)}, u32[]{:S(2)}) collective-permute-start(f32[2,64,512]{2,1,0:T(8,128)S(1)} %maximum_select_fusion.1.refs_0_), channel_id=1, source_target_pairs={{0,192},{64,0},{128,64},{192,128},{1,193},{65,1},{129,65},{193,129... | collective-permute-start | bytes 786440 | tf_op jit(solution)/shard_map/ppermute | solution.py:179
  94.3 15.3 %collective-permute-start.38 = (f32[2,64,512]{2,1,0:T(8,128)S(1)}, f32[2,64,512]{2,1,0:T(8,128)}, u32[]{:S(2)}, u32[]{:S(2)}) collective-permute-start(f32[2,64,512]{2,1,0:T(8,128)S(1)} %maximum_select_fusion.2.refs_0_), channel_id=1, source_target_pairs={{0,132},{4,128},{64,196},{68,192},{128,4},{132,0},{192,68},{196,64... | collective-permute-start | bytes 786440 | tf_op jit(solution)/shard_map/ppermute | solution.py:173
  97.5 14.1 %collective-permute-start.40 = (f32[2,64,512]{2,1,0:T(8,128)S(1)}, f32[2,64,512]{2,1,0:T(8,128)}, u32[]{:S(2)}, u32[]{:S(2)}) collective-permute-start(f32[2,64,512]{2,1,0:T(8,128)S(1)} %maximum_select_fusion.2.refs_0_), channel_id=1, source_target_pairs={{0,4},{4,0},{1,5},{5,1},{2,6},{6,2},{3,7},{7,3},{8,12},{12,8},{9,1... | collective-permute-start | bytes 786440 | tf_op jit(solution)/shard_map/ppermute | solution.py:179
  105.1 9.5 %collective-permute-start.46 = (f32[2,64,512]{2,1,0:T(8,128)S(1)}, f32[2,64,512]{2,1,0:T(8,128)}, u32[]{:S(2)}, u32[]{:S(2)}) collective-permute-start(f32[2,64,512]{2,1,0:T(8,128)S(1)} %collective-permute-done.45.refs_1_), channel_id=1, source_target_pairs={{0,4},{4,0},{1,5},{5,1},{2,6},{6,2},{3,7},{7,3},{8,12},{12,8},{9,1... | collective-permute-start | bytes 786440 | tf_op jit(solution)/shard_map/ppermute | solution.py:179
  105.4 11.0 %collective-permute-start.49 = (f32[2,64,512]{2,1,0:T(8,128)S(1)}, f32[2,64,512]{2,1,0:T(8,128)}, u32[]{:S(2)}, u32[]{:S(2)}) collective-permute-start(f32[2,64,512]{2,1,0:T(8,128)S(1)} %collective-permute-done.45.refs_1_), channel_id=1, source_target_pairs={{0,64},{64,128},{128,192},{192,0},{1,65},{65,129},{129,193},{193,1... | collective-permute-start | bytes 786440 | tf_op jit(solution)/shard_map/ppermute | solution.py:179
  109.2 7.5 %collective-permute-start.51 = (f32[2,64,512]{2,1,0:T(8,128)S(1)}, f32[2,64,512]{2,1,0:T(8,128)}, u32[]{:S(2)}, u32[]{:S(2)}) collective-permute-start(f32[2,64,512]{2,1,0:T(8,128)S(1)} %collective-permute-done.45.refs_1_), channel_id=1, source_target_pairs={{0,192},{64,0},{128,64},{192,128},{1,193},{65,1},{129,65},{193,129... | collective-permute-start | bytes 786440 | tf_op jit(solution)/shard_map/ppermute | solution.py:179
  109.6 16.3 %collective-permute-start.41 = (f32[2,64,512]{2,1,0:T(8,128)S(1)}, f32[2,64,512]{2,1,0:T(8,128)S(1)}, u32[]{:S(2)}, u32[]{:S(2)}) collective-permute-start(f32[2,64,512]{2,1,0:T(8,128)S(1)} %maximum_select_fusion.2.refs_0_), channel_id=1, source_target_pairs={{0,64},{64,128},{128,192},{192,0},{1,65},{65,129},{129,193},{193,1... | collective-permute-start | bytes 786440 | tf_op jit(solution)/shard_map/ppermute | solution.py:179
  111.6 14.3 %collective-permute-start.43 = (f32[2,64,512]{2,1,0:T(8,128)S(1)}, f32[2,64,512]{2,1,0:T(8,128)S(1)}, u32[]{:S(2)}, u32[]{:S(2)}) collective-permute-start(f32[2,64,512]{2,1,0:T(8,128)S(1)} %maximum_select_fusion.2.refs_0_), channel_id=1, source_target_pairs={{0,192},{64,0},{128,64},{192,128},{1,193},{65,1},{129,65},{193,129... | collective-permute-start | bytes 786440 | tf_op jit(solution)/shard_map/ppermute | solution.py:179
  114.6 11.3 %collective-permute-start.39 = (f32[2,64,512]{2,1,0:T(8,128)}, f32[2,64,512]{2,1,0:T(8,128)S(1)}, u32[]{:S(2)}, u32[]{:S(2)}) collective-permute-start(f32[2,64,512]{2,1,0:T(8,128)} %collective-permute-done.38.refs_1_), channel_id=1, source_target_pairs={{0,4},{4,0},{1,5},{5,1},{2,6},{6,2},{3,7},{7,3},{8,12},{12,8},{9,1... | collective-permute-start | bytes 786440 | tf_op jit(solution)/shard_map/ppermute | solution.py:179
  116.4 9.5 %collective-permute-start.42 = (f32[2,64,512]{2,1,0:T(8,128)}, f32[2,64,512]{2,1,0:T(8,128)S(1)}, u32[]{:S(2)}, u32[]{:S(2)}) collective-permute-start(f32[2,64,512]{2,1,0:T(8,128)} %collective-permute-done.38.refs_1_), channel_id=1, source_target_pairs={{0,64},{64,128},{128,192},{192,0},{1,65},{65,129},{129,193},{193,1... | collective-permute-start | bytes 786440 | tf_op jit(solution)/shard_map/ppermute | solution.py:179
  116.8 9.1 %collective-permute-start.44 = (f32[2,64,512]{2,1,0:T(8,128)}, f32[2,64,512]{2,1,0:T(8,128)S(1)}, u32[]{:S(2)}, u32[]{:S(2)}) collective-permute-start(f32[2,64,512]{2,1,0:T(8,128)} %collective-permute-done.38.refs_1_), channel_id=1, source_target_pairs={{0,192},{64,0},{128,64},{192,128},{1,193},{65,1},{129,65},{193,129... | collective-permute-start | bytes 786440 | tf_op jit(solution)/shard_map/ppermute | solution.py:179
  (7 other events, 42.5 us)

commit v4 on v3

--- a/solution.py
+++ b/solution.py
@@ -22,34 +22,42 @@
 
 
 def place_of(panel):
-    return panel // 16, (panel // 2) % 8, panel % 2
-
-
-def leap(v, group):
-    roots = (group, group + 4)
+    return panel >> 4, (panel >> 1) & 7, panel & 1
+
+
+def leap(v, groups):
+    roots = [g + k for g in groups for k in (0, 4)]
     up = lax.ppermute(v, "z", [(r, (r + 3) % 8) for r in roots])
     down = lax.ppermute(v, "z", [(r, (r - 3) % 8) for r in roots])
     return up, down
 
 
-def leaps(blocks, roots, z):
+def leaps(mine, last, root, z):
+    fixed = LAST // 2 % 4
+
     def branch(group):
-        return lambda a, b: (leap(a, group), leap(b, LAST // 2 % 4))
-
-    leapt = lax.switch(roots[0] % 4, [branch(g) for g in range(4)], *blocks)
-    return jnp.stack(
-        [
-            jnp.where(d == 0, v, jnp.where(d == 3, up, down))
-            for d, v, (up, down) in zip([(z - r) % 8 for r in roots], blocks, leapt)
-        ]
-    )
+        def both(a, b):
+            up, down = leap(jnp.where(z & 3 == fixed, b, a), (group, fixed))
+            return up, down, up, down
+
+        def apart(a, b):
+            return (*leap(a, (fixed,)), *leap(b, (fixed,)))
+
+        return apart if group == fixed else both
+
+    leapt = lax.switch(root & 3, [branch(g) for g in range(4)], mine, last)
+    held = []
+    for i, (v, d) in enumerate(((mine, (z - root) & 7), (last, (z - LAST // 2 % 8) & 7))):
+        up, down = leapt[2 * i], leapt[2 * i + 1]
+        held.append(jnp.where(d == 0, v, jnp.where(d == 3, up, down)))
+    return jnp.stack(held)
 
 
 def steps(held, roots, z):
     after = lax.ppermute(held, "z", [(k, (k + 1) % 8) for k in range(8)])
     before = lax.ppermute(held, "z", [(k, (k - 1) % 8) for k in range(8)])
     whole = []
-    for i, d in enumerate([(z - r) % 8 for r in roots]):
+    for i, d in enumerate([(z - r) & 7 for r in roots]):
         from_after = (d == 1) | (d == 4) | (d == 6)
         from_before = (d == 2) | (d == 7)
         whole.append(
@@ -62,11 +70,12 @@
     flat = spectra.reshape(2 * FREQ, ROWS, COLS)
     lane_panel = lax.broadcasted_iota(jnp.int32, (1, 1, 2 * ROWS), 2) // ROWS
     picked = [
-        lax.dynamic_slice_in_dim(flat, (panels[i] % 16) * ROWS, ROWS, 2) for i in range(2)
+        lax.dynamic_slice_in_dim(flat, (panels[i].astype(jnp.uint32) & 15) * ROWS, ROWS, 2)
+        for i in range(2)
     ]
     block = jnp.concatenate(picked, axis=2)
-    owners = panels // 16
-    for axis, bit in (("c", owners % 2), ("yh", owners // 2)):
+    owners = panels >> 4
+    for axis, bit in (("c", owners & 1), ("yh", owners >> 1)):
         other = lax.ppermute(block, axis, [(0, 1), (1, 0)])
         keep = jnp.where(lane_panel == 0, bit[0], bit[1]) == lax.axis_index(axis)
         block = jnp.where(keep, block, other)
@@ -156,7 +165,7 @@
         jnp.concatenate([re_last, im_last], axis=1),
     )
     times = offsets[:, None] + jnp.arange(TWIN, dtype=jnp.int32)[None, :]
-    phase = times[:, :, None] * (FIRST_BIN + bins)[None, None, :] % NT
+    phase = times[:, :, None] * (FIRST_BIN + bins)[None, None, :] & (NT - 1)
     angle = phase.astype(jnp.float32) * (2.0 * math.pi / NT)
     coefs = jnp.stack([jnp.cos(angle), jnp.sin(angle)], axis=3).reshape(ROWS, 64)
     return left, coefs
@@ -187,19 +196,26 @@
     other = jnp.where(panels[0] == LAST, panels[1], panels[0])
     ox, oz, oy = place_of(other)
     lx, lz, ly = place_of(LAST)
-    flat = spectra.reshape(2 * FREQ, ROWS, COLS)
-    strip = strips(spectra, panels)
-    bins = ((x + 2 * yl) % 4 + jnp.array([0, 2, 3, 1], jnp.int32)) % 4
     half = COLS // PARTS
+    later, pieces = spectra, []
+    for part in range(PARTS):
+        flat = later.reshape(2 * FREQ, ROWS, COLS)
+        later, piece = lax.optimization_barrier(
+            (later, flat[:, :, part * half : (part + 1) * half])
+        )
+        pieces.append(piece)
+    strip = strips(later, panels)
+    bins = (x + 2 * yl + jnp.array([0, 2, 3, 1], jnp.int32)) & 3
+    spot = (oy * 4 + ((ox + 2 * oy) & 3)).astype(jnp.uint32)
     owns, held = [], None
     for part in range(PARTS):
-        arrived = scatter(flat[:, :, part * half : (part + 1) * half])
+        arrived = scatter(pieces[part])
         if part:
             held, arrived = lax.optimization_barrier((held, arrived))
             owns.append(steps(held, (oz, lz), z))
-        mine = lax.dynamic_index_in_dim(arrived, oy * 4 + (ox + 2 * oy) % 4, 0, keepdims=False)
+        mine = lax.dynamic_index_in_dim(arrived, spot, 0, keepdims=False)
         last = arrived[ly * 4 + (lx + 2 * ly) % 4]
-        held = leaps((mine, last), (oz, lz), z)
+        held = leaps(mine, last, oz, z)
     owns.append(steps(held, (oz, lz), z))
     owns = [jnp.where(slot == 0, jnp.stack([b, a]), jnp.stack([a, b])) for a, b in owns]
     owns[0], strip = lax.optimization_barrier((owns[0], strip))

time: 128 us -> 124 us (0.969)
  the two profiles are of different devices: /device:TPU:16 before, /device:TPU:32 now
where the time goes in v4:
time: 124 us; the launch traced here: 123 us
  starting transfers between devices  61.7 us (50%)
  waiting for transfers between devices  25.1 us (20%)
  local copies, waits for them, and re-layouts  14 us (11%)
  other arithmetic  10.7 us (9%)
  Pallas kernels  8.14 us (7%)
  between operations  3.37 us (3%)
    ppermute x12, starting transfers between devices, exchange(): blocks.append(lax.ppermute(v, axis, pairs))  19 us
    ppermute x2, starting transfers between devices, leap(): up = lax.ppermute(v, 'z', [(r, (r + 3) % 8) for r in roots])  14.2 us
    all_to_all x2, starting transfers between devices, scatter(): lax.all_to_all(rows, ('x', 'yl'), 0, 0, axis_index_groups=[members], tile...  8.87 us
    pallas_call x2, Pallas kernels, synthesise(): pl.pallas_call(kernel, grid_spec=grid_spec, out_shape=jax.ShapeDtypeStruc...  8.14 us
    cond x4, local copies, waits for them, and re-layouts  6.24 us
    ppermute x2, starting transfers between devices, steps(): before = lax.ppermute(held, 'z', [(k, (k - 1) % 8) for k in range(8)])  6.17 us
    all_to_all x2, waiting for transfers between devices, scatter(): lax.all_to_all(rows, ('x', 'yl'), 0, 0, axis_index_groups=[members], tile...  5.45 us
    ppermute x12, waiting for transfers between devices, exchange(): blocks.append(lax.ppermute(v, axis, pairs))  5.28 us
  transfers between devices with their start and end apart: 26, of which 12 were waited for; matrix products, arithmetic and copies ran while one was open for 17% of the time, Pallas kernels for 3%

profile of v4, /device:TPU:32, one launch (start us, length us, event | category | flops | bytes accessed | tf_op | source)
XLA Modules:
  0.0 123.3 jit_solution(12084023726913902695)
XLA Ops:
  0.0 2.4 %slice.92 = f32[8,64,512]{2,1,0:T(8,128)} slice(f32[8,64,1024]{2,1,0:T(8,128)} %bitcast.77), slice={[0:8], [0:64], [0:512]} | slice | bytes 2097152 | tf_op jit(solution)/shard_map/slice | solution.py:204
  2.4 5.3 %all-to-all-start = ((f32[8,64,512]{2,1,0:T(8,128)}), f32[8,64,512]{2,1,0:T(8,128)}, u32[]{:S(2)}, u32[]{:S(2)}) async-start(f32[8,64,512]{2,1,0:T(8,128)} %slice.92), calls=%async_computation | async-start | bytes 2097152 | tf_op jit(solution)/shard_map/all_to_all | solution.py:176
  15.3 3.0 %collective-permute-start.23 = (f32[8,64,128]{2,1,0:T(8,128)S(1)}, f32[8,64,128]{2,1,0:T(8,128)}, u32[]{:S(2)}, u32[]{:S(2)}) collective-permute-start(f32[8,64,128]{2,1,0:T(8,128)S(1)} %broadcast_select_fusion.6), channel_id=1, source_target_pairs={{0,2},{2,0},{1,3},{3,1},{4,6},{6,4},{5,7},{7,5},{8,10},{10,8},{9,1... | collective-permute-start | bytes 786440 | tf_op jit(solution)/shard_map/ppermute | solution.py:79
  18.4 5.4 %all-to-all-done = f32[8,64,512]{2,1,0:T(8,128)} async-done(((f32[8,64,512]{2,1,0:T(8,128)}), f32[8,64,512]{2,1,0:T(8,128)}, u32[]{:S(2)}, u32[]{:S(2)}) %all-to-all-start) | async-done | bytes 1048608 | tf_op jit(solution)/shard_map/all_to_all | solution.py:176
  23.9 3.6 %all-to-all-start.1 = ((f32[8,64,512]{2,1,0:T(8,128)}), f32[8,64,512]{2,1,0:T(8,128)S(1)}, u32[]{:S(2)}, u32[]{:S(2)}) async-start(f32[8,64,512]{2,1,0:T(8,128)} %slice.94), calls=%async_computation.1 | async-start | bytes 2097152 | tf_op jit(solution)/shard_map/all_to_all | solution.py:176
  29.8 1.7 %broadcast_select_fusion.7 = f32[8,64,128]{2,1,0:T(8,128)} fusion(f32[8,64,128]{2,1,0:T(8,128)S(1)} %broadcast_select_fusion.6, f32[8,64,128]{2,1,0:T(8,128)} %collective-permute-done.23, pred[128]{0:T(512)(128)(4,1)S(1)} %fusion.12), kind=kLoop, calls=%fused_computation.41 | loop fusion | flops 65536 | bytes 786560 | tf_op jit(solution)/shard_map/jit(_where)/select_n | solution.py:81
  32.5 17.0 %conditional.2 = (f32[64,512]{1,0:T(8,128)}, f32[64,512]{1,0:T(8,128)}, f32[64,512]{1,0:T(8,128)}, f32[64,512]{1,0:T(8,128)}) conditional(s32[]{:T(128)} %clamp.4, (s32[]{:T(128)}, f32[64,512]{1,0:T(8,128)S(1)}, f32[64,512]{1,0:T(8,128)S(1)}) %tuple.42, (s32[]{:T(128)}, f32[64,512]{1,0:T(8,128)S(1)}, ...), branch_computations={%region_0.1_spmd, %region_1.2_spmd, %region_2.3_spmd, %region_3.4_... | conditional | flops 32770 | bytes 2097344 | solution.py:48
  32.6 8.4 %collective-permute-start.10 = (f32[64,512]{1,0:T(8,128)S(1)}, f32[64,512]{1,0:T(8,128)}, u32[]{:S(2)}, u32[]{:S(2)}) collective-permute-start(f32[64,512]{1,0:T(8,128)S(1)} %broadcast_select_fusion.1), channel_id=1, source_target_pairs={{8,32},{40,0},{24,48},{56,16},{9,33},{41,1},{25,49},{57,17},{10,34... | collective-permute-start | bytes 393224 | tf_op jit(solution)/shard_map/cond/branch_1_fun/ppermute | solution.py:30
  40.9 1.9 %collective-permute-start.11 = (f32[64,512]{1,0:T(8,128)S(1)}, f32[64,512]{1,0:T(8,128)}, u32[]{:S(2)}, u32[]{:S(2)}) collective-permute-start(f32[64,512]{1,0:T(8,128)S(1)} %broadcast_select_fusion.1), channel_id=1, source_target_pairs={{8,48},{40,16},{24,0},{56,32},{9,49},{41,17},{25,1},{57,33},{10,50... | collective-permute-start | bytes 393224 | tf_op jit(solution)/shard_map/cond/branch_1_fun/ppermute | solution.py:31
  42.9 2.6 %collective-permute-done.10 = f32[64,512]{1,0:T(8,128)} collective-permute-done((f32[64,512]{1,0:T(8,128)S(1)}, f32[64,512]{1,0:T(8,128)}, u32[]{:S(2)}, u32[]{:S(2)}) %collective-permute-start.10) | collective-permute-done | bytes 131104 | tf_op jit(solution)/shard_map/cond/branch_1_fun/ppermute | solution.py:30
  45.5 1.6 %copy.20 = f32[64,512]{1,0:T(8,128)} copy(f32[64,512]{1,0:T(8,128)} %collective-permute-done.10) | data formatting | bytes 262144 | tf_op jit(solution)/shard_map/cond
  48.0 1.5 %copy.21 = f32[64,512]{1,0:T(8,128)} copy(f32[64,512]{1,0:T(8,128)} %collective-permute-done.11) | data formatting | bytes 262144 | tf_op jit(solution)/shard_map/cond
  51.4 1.5 %collective-permute-start.20 = (f32[2,64,512]{2,1,0:T(8,128)}, f32[2,64,512]{2,1,0:T(8,128)}, u32[]{:S(2)}, u32[]{:S(2)}) collective-permute-start(f32[2,64,512]{2,1,0:T(8,128)} %pad_maximum_fusion), channel_id=1, source_target_pairs={{0,8},{8,16},{16,24},{24,32},{32,40},{40,48},{48,56},{56,0},{1,9},... | collective-permute-start | bytes 786440 | tf_op jit(solution)/shard_map/ppermute | solution.py:57
  52.8 12.1 %conditional.3 = (f32[64,512]{1,0:T(8,128)}, f32[64,512]{1,0:T(8,128)}, f32[64,512]{1,0:T(8,128)}, f32[64,512]{1,0:T(8,128)}) conditional(s32[]{:T(128)} %clamp.4, (s32[]{:T(128)}, f32[64,512]{1,0:T(8,128)S(1)}, f32[64,512]{1,0:T(8,128)S(1)}) %tuple.47, (s32[]{:T(128)}, f32[64,512]{1,0:T(8,128)S(1)}, ...), branch_computations={%region_4.5_spmd, %region_5.6_spmd, %region_6.7_spmd, %region_7.8_... | conditional | flops 32770 | bytes 2097344 | solution.py:48
  52.8 5.9 %collective-permute-start.16 = (f32[64,512]{1,0:T(8,128)S(1)}, f32[64,512]{1,0:T(8,128)}, u32[]{:S(2)}, u32[]{:S(2)}) collective-permute-start(f32[64,512]{1,0:T(8,128)S(1)} %broadcast_select_fusion.4), channel_id=1, source_target_pairs={{8,32},{40,0},{24,48},{56,16},{9,33},{41,1},{25,49},{57,17},{10,34... | collective-permute-start | bytes 393224 | tf_op jit(solution)/shard_map/cond/branch_1_fun/ppermute | solution.py:30
  58.7 2.2 %collective-permute-start.17 = (f32[64,512]{1,0:T(8,128)S(1)}, f32[64,512]{1,0:T(8,128)}, u32[]{:S(2)}, u32[]{:S(2)}) collective-permute-start(f32[64,512]{1,0:T(8,128)S(1)} %broadcast_select_fusion.4), channel_id=1, source_target_pairs={{8,48},{40,16},{24,0},{56,32},{9,49},{41,17},{25,1},{57,33},{10,50... | collective-permute-start | bytes 393224 | tf_op jit(solution)/shard_map/cond/branch_1_fun/ppermute | solution.py:31
  61.0 1.6 %copy.36 = f32[64,512]{1,0:T(8,128)} copy(f32[64,512]{1,0:T(8,128)} %collective-permute-done.16) | data formatting | bytes 262144 | tf_op jit(solution)/shard_map/cond
  63.3 1.6 %copy.37 = f32[64,512]{1,0:T(8,128)} copy(f32[64,512]{1,0:T(8,128)} %collective-permute-done.17) | data formatting | bytes 262144 | tf_op jit(solution)/shard_map/cond
  64.9 6.0 %collective-permute-start.21 = (f32[2,64,512]{2,1,0:T(8,128)}, f32[2,64,512]{2,1,0:T(8,128)S(1)}, u32[]{:S(2)}, u32[]{:S(2)}) collective-permute-start(f32[2,64,512]{2,1,0:T(8,128)} %pad_maximum_fusion), channel_id=1, source_target_pairs={{0,56},{8,0},{16,8},{24,16},{32,24},{40,32},{48,40},{56,48},{1,57}... | collective-permute-start | bytes 786440 | tf_op jit(solution)/shard_map/ppermute | solution.py:58
  72.8 1.9 %collective-permute-start.24 = (f32[2,64,512]{2,1,0:T(8,128)S(1)}, f32[2,64,512]{2,1,0:T(8,128)S(1)}, u32[]{:S(2)}, u32[]{:S(2)}) collective-permute-start(f32[2,64,512]{2,1,0:T(8,128)S(1)} %pad_maximum_fusion.2), channel_id=1, source_target_pairs={{0,8},{8,16},{16,24},{24,32},{32,40},{40,48},{48,56},{56,0},{1,9},... | collective-permute-start | bytes 786440 | tf_op jit(solution)/shard_map/ppermute | solution.py:57
  74.9 5.0 %collective-permute-done.21 = f32[2,64,512]{2,1,0:T(8,128)S(1)} collective-permute-done((f32[2,64,512]{2,1,0:T(8,128)}, f32[2,64,512]{2,1,0:T(8,128)S(1)}, u32[]{:S(2)}, u32[]{:S(2)}) %collective-permute-start.21) | collective-permute-done | bytes 262176 | tf_op jit(solution)/shard_map/ppermute | solution.py:58
  81.1 1.6 %collective-permute-start.33 = (f32[2,64,512]{2,1,0:T(8,128)S(1)}, f32[2,64,512]{2,1,0:T(8,128)S(1)}, u32[]{:S(2)}, u32[]{:S(2)}) collective-permute-start(f32[2,64,512]{2,1,0:T(8,128)S(1)} %maximum_select_fusion.1.refs_0_), channel_id=1, source_target_pairs={{0,132},{4,128},{64,196},{68,192},{128,4},{132,0},{192,68},{196,64... | collective-permute-start | bytes 786440 | tf_op jit(solution)/shard_map/ppermute | solution.py:182
  82.7 2.0 %collective-permute-start.35 = (f32[2,64,512]{2,1,0:T(8,128)S(1)}, f32[2,64,512]{2,1,0:T(8,128)S(1)}, u32[]{:S(2)}, u32[]{:S(2)}) collective-permute-start(f32[2,64,512]{2,1,0:T(8,128)S(1)} %maximum_select_fusion.1.refs_0_), channel_id=1, source_target_pairs={{0,4},{4,0},{1,5},{5,1},{2,6},{6,2},{3,7},{7,3},{8,12},{12,8},{9,1... | collective-permute-start | bytes 786440 | tf_op jit(solution)/shard_map/ppermute | solution.py:188
  84.7 3.2 %collective-permute-start.38 = (f32[2,64,512]{2,1,0:T(8,128)S(1)}, f32[2,64,512]{2,1,0:T(8,128)S(1)}, u32[]{:S(2)}, u32[]{:S(2)}) collective-permute-start(f32[2,64,512]{2,1,0:T(8,128)S(1)} %maximum_select_fusion.1.refs_0_), channel_id=1, source_target_pairs={{0,192},{64,0},{128,64},{192,128},{1,193},{65,1},{129,65},{193,129... | collective-permute-start | bytes 786440 | tf_op jit(solution)/shard_map/ppermute | solution.py:188
  89.2 3.6 %collective-permute-done.33.refs_1_ = f32[2,64,512]{2,1,0:T(8,128)S(1)} collective-permute-done((f32[2,64,512]{2,1,0:T(8,128)S(1)}, f32[2,64,512]{2,1,0:T(8,128)S(1)}, u32[]{:S(2)}, u32[]{:S(2)}) %collective-permute-start.33) | collective-permute-done | bytes 262176 | tf_op jit(solution)/shard_map/ppermute | solution.py:182
  94.2 3.2 %collective-permute-done.35.refs_3_ = f32[2,64,512]{2,1,0:T(8,128)S(1)} collective-permute-done((f32[2,64,512]{2,1,0:T(8,128)S(1)}, f32[2,64,512]{2,1,0:T(8,128)S(1)}, u32[]{:S(2)}, u32[]{:S(2)}) %collective-permute-start.35) | collective-permute-done | bytes 262176 | tf_op jit(solution)/shard_map/ppermute | solution.py:188
  98.7 3.4 %collective-permute-start.37 = (f32[2,64,512]{2,1,0:T(8,128)S(1)}, f32[2,64,512]{2,1,0:T(8,128)}, u32[]{:S(2)}, u32[]{:S(2)}) collective-permute-start(f32[2,64,512]{2,1,0:T(8,128)S(1)} %collective-permute-done.33.refs_1_), channel_id=1, source_target_pairs={{0,64},{64,128},{128,192},{192,0},{1,65},{65,129},{129,193},{193,1... | collective-permute-start | bytes 786440 | tf_op jit(solution)/shard_map/ppermute | solution.py:188
  103.4 1.8 %collective-permute-start.29 = (f32[2,64,512]{2,1,0:T(8,128)S(1)}, f32[2,64,512]{2,1,0:T(8,128)S(1)}, u32[]{:S(2)}, u32[]{:S(2)}) collective-permute-start(f32[2,64,512]{2,1,0:T(8,128)S(1)} %maximum_select_fusion.2.refs_0_), channel_id=1, source_target_pairs={{0,64},{64,128},{128,192},{192,0},{1,65},{65,129},{129,193},{193,1... | collective-permute-start | bytes 786440 | tf_op jit(solution)/shard_map/ppermute | solution.py:188
  106.7 1.8 %collective-permute-done.34.refs_2_ = f32[2,64,512]{2,1,0:T(8,128)} collective-permute-done((f32[2,64,512]{2,1,0:T(8,128)S(1)}, f32[2,64,512]{2,1,0:T(8,128)}, u32[]{:S(2)}, u32[]{:S(2)}) %collective-permute-start.34) | collective-permute-done | bytes 262176 | tf_op jit(solution)/shard_map/ppermute | solution.py:188
  110.4 2.6 %collective-permute-start.32 = (f32[2,64,512]{2,1,0:T(8,128)}, f32[2,64,512]{2,1,0:T(8,128)S(1)}, u32[]{:S(2)}, u32[]{:S(2)}) collective-permute-start(f32[2,64,512]{2,1,0:T(8,128)} %collective-permute-done.26.refs_1_), channel_id=1, source_target_pairs={{0,192},{64,0},{128,64},{192,128},{1,193},{65,1},{129,65},{193,129... | collective-permute-start | bytes 786440 | tf_op jit(solution)/shard_map/ppermute | solution.py:188
  115.1 4.1 %shard_map.73.refs_8_ = bf16[8,64,1024]{2,1,0:T(8,128)(2,1)} custom-call(s32[4]{0:T(128)S(1)} %get-tuple-element.119.bins, f32[2,4,64,1024]{3,2,1,0:T(8,128)S(1)} %copy-done.1, f32[4,128,256]{2,1,0:T(8,128)S(1)} %maximum_select_fusion.l_ref, f32[64,64]{1,0:T(8,128)S(1)} %copy.13.coef_ref, f32[2,64,512]{2,1,0:T(8,128)S(1)} %maximum_select_fusion.1.refs_0_, ...), custom_call_target="tpu_custom_call" | custom-call | flops 402653184 | bytes 4194304 | tf_op jit(solution)/shard_map/pallas_call | solution.py:135
  119.3 4.0 %shard_map.74 = bf16[8,64,1024]{2,1,0:T(8,128)(2,1)} custom-call(s32[4]{0:T(128)S(1)} %get-tuple-element.119.bins, f32[2,4,64,1024]{3,2,1,0:T(8,128)S(1)} %copy-done.1, f32[4,128,256]{2,1,0:T(8,128)S(1)} %maximum_select_fusion.l_ref, f32[64,64]{1,0:T(8,128)S(1)} %copy.13.coef_ref, ...), custom_call_target="tpu_custom_call", output_to_operand_aliasing={{}: (12, {})} | custom-call | flops 402653184 | bytes 4194304 | tf_op jit(solution)/shard_map/pallas_call | solution.py:135
  (80 shorter events, 25.5 us)
Async XLA Ops:
  0.0 14.9 %copy-start = (f32[64,64]{1,0:T(8,128)S(1)}, f32[64,64]{1,0:T(8,128)}, u32[]{:S(2)}) copy-start(f32[64,64]{1,0:T(8,128)} %param.17) | copy-start | bytes 49156
  0.0 7.8 %copy-start.6 = (s32[2]{0:T(128)S(1)}, s32[2]{0:T(128)}, u32[]{:S(2)}) copy-start(s32[2]{0:T(128)} %param.16) | copy-start | bytes 28
  0.0 8.5 %copy-start.1 = (f32[2,4,64,1024]{3,2,1,0:T(8,128)S(1)}, f32[2,4,64,1024]{3,2,1,0:T(8,128)}, u32[]{:S(2)}) copy-start(f32[2,4,64,1024]{3,2,1,0:T(8,128)} %x_ref.3) | copy-start | bytes 6291460
  2.4 21.5 %all-to-all-start = ((f32[8,64,512]{2,1,0:T(8,128)}), f32[8,64,512]{2,1,0:T(8,128)}, u32[]{:S(2)}, u32[]{:S(2)}) async-start(f32[8,64,512]{2,1,0:T(8,128)} %slice.92), calls=%async_computation | async-start | bytes 2097152 | tf_op jit(solution)/shard_map/all_to_all | solution.py:176
  7.8 3.5 %copy-start.8 = (s32[4]{0:T(128)S(1)}, s32[4]{0:T(128)}, u32[]{:S(2)}) copy-start(s32[4]{0:T(128)} %constant.89.clone) | copy-start | bytes 52
  7.8 7.2 %copy-start.5 = (f32[64,4]{1,0:T(8,128)S(1)}, f32[64,4]{1,0:T(8,128)}, u32[]{:S(2)}) copy-start(f32[64,4]{1,0:T(8,128)} %constant.90.clone) | copy-start | bytes 3076
  11.1 4.0 %collective-permute-start.22 = (f32[8,64,128]{2,1,0:T(8,128)S(1)}, f32[8,64,128]{2,1,0:T(8,128)S(1)}, u32[]{:S(2)}, u32[]{:S(2)}) collective-permute-start(f32[8,64,128]{2,1,0:T(8,128)S(1)} %pad_maximum_fusion.1), channel_id=1, source_target_pairs={{0,1},{1,0},{2,3},{3,2},{4,5},{5,4},{6,7},{7,6},{8,9},{9,8},{10,11... | collective-permute-start | bytes 786440 | tf_op jit(solution)/shard_map/ppermute | solution.py:79
  15.3 14.5 %collective-permute-start.23 = (f32[8,64,128]{2,1,0:T(8,128)S(1)}, f32[8,64,128]{2,1,0:T(8,128)}, u32[]{:S(2)}, u32[]{:S(2)}) collective-permute-start(f32[8,64,128]{2,1,0:T(8,128)S(1)} %broadcast_select_fusion.6), channel_id=1, source_target_pairs={{0,2},{2,0},{1,3},{3,1},{4,6},{6,4},{5,7},{7,5},{8,10},{10,8},{9,1... | collective-permute-start | bytes 786440 | tf_op jit(solution)/shard_map/ppermute | solution.py:79
  23.9 27.4 %all-to-all-start.1 = ((f32[8,64,512]{2,1,0:T(8,128)}), f32[8,64,512]{2,1,0:T(8,128)S(1)}, u32[]{:S(2)}, u32[]{:S(2)}) async-start(f32[8,64,512]{2,1,0:T(8,128)} %slice.94), calls=%async_computation.1 | async-start | bytes 2097152 | tf_op jit(solution)/shard_map/all_to_all | solution.py:176
  32.6 12.9 %collective-permute-start.10 = (f32[64,512]{1,0:T(8,128)S(1)}, f32[64,512]{1,0:T(8,128)}, u32[]{:S(2)}, u32[]{:S(2)}) collective-permute-start(f32[64,512]{1,0:T(8,128)S(1)} %broadcast_select_fusion.1), channel_id=1, source_target_pairs={{8,32},{40,0},{24,48},{56,16},{9,33},{41,1},{25,49},{57,17},{10,34... | collective-permute-start | bytes 393224 | tf_op jit(solution)/shard_map/cond/branch_1_fun/ppermute | solution.py:30
  40.9 7.0 %collective-permute-start.11 = (f32[64,512]{1,0:T(8,128)S(1)}, f32[64,512]{1,0:T(8,128)}, u32[]{:S(2)}, u32[]{:S(2)}) collective-permute-start(f32[64,512]{1,0:T(8,128)S(1)} %broadcast_select_fusion.1), channel_id=1, source_target_pairs={{8,48},{40,16},{24,0},{56,32},{9,49},{41,17},{25,1},{57,33},{10,50... | collective-permute-start | bytes 393224 | tf_op jit(solution)/shard_map/cond/branch_1_fun/ppermute | solution.py:31
  51.4 23.6 %collective-permute-start.20 = (f32[2,64,512]{2,1,0:T(8,128)}, f32[2,64,512]{2,1,0:T(8,128)}, u32[]{:S(2)}, u32[]{:S(2)}) collective-permute-start(f32[2,64,512]{2,1,0:T(8,128)} %pad_maximum_fusion), channel_id=1, source_target_pairs={{0,8},{8,16},{16,24},{24,32},{32,40},{40,48},{48,56},{56,0},{1,9},... | collective-permute-start | bytes 786440 | tf_op jit(solution)/shard_map/ppermute | solution.py:57
  52.8 8.2 %collective-permute-start.16 = (f32[64,512]{1,0:T(8,128)S(1)}, f32[64,512]{1,0:T(8,128)}, u32[]{:S(2)}, u32[]{:S(2)}) collective-permute-start(f32[64,512]{1,0:T(8,128)S(1)} %broadcast_select_fusion.4), channel_id=1, source_target_pairs={{8,32},{40,0},{24,48},{56,16},{9,33},{41,1},{25,49},{57,17},{10,34... | collective-permute-start | bytes 393224 | tf_op jit(solution)/shard_map/cond/branch_1_fun/ppermute | solution.py:30
  58.7 4.6 %collective-permute-start.17 = (f32[64,512]{1,0:T(8,128)S(1)}, f32[64,512]{1,0:T(8,128)}, u32[]{:S(2)}, u32[]{:S(2)}) collective-permute-start(f32[64,512]{1,0:T(8,128)S(1)} %broadcast_select_fusion.4), channel_id=1, source_target_pairs={{8,48},{40,16},{24,0},{56,32},{9,49},{41,17},{25,1},{57,33},{10,50... | collective-permute-start | bytes 393224 | tf_op jit(solution)/shard_map/cond/branch_1_fun/ppermute | solution.py:31
  64.9 15.0 %collective-permute-start.21 = (f32[2,64,512]{2,1,0:T(8,128)}, f32[2,64,512]{2,1,0:T(8,128)S(1)}, u32[]{:S(2)}, u32[]{:S(2)}) collective-permute-start(f32[2,64,512]{2,1,0:T(8,128)} %pad_maximum_fusion), channel_id=1, source_target_pairs={{0,56},{8,0},{16,8},{24,16},{32,24},{40,32},{48,40},{56,48},{1,57}... | collective-permute-start | bytes 786440 | tf_op jit(solution)/shard_map/ppermute | solution.py:58
  71.8 31.1 %copy-start.4 = (f32[64,4]{1,0:T(8,128)S(1)}, f32[64,4]{1,0:T(8,128)}, u32[]{:S(2)}) copy-start(f32[64,4]{1,0:T(8,128)} %constant.91.clone) | copy-start | bytes 3076
  72.8 11.9 %collective-permute-start.24 = (f32[2,64,512]{2,1,0:T(8,128)S(1)}, f32[2,64,512]{2,1,0:T(8,128)S(1)}, u32[]{:S(2)}, u32[]{:S(2)}) collective-permute-start(f32[2,64,512]{2,1,0:T(8,128)S(1)} %pad_maximum_fusion.2), channel_id=1, source_target_pairs={{0,8},{8,16},{16,24},{24,32},{32,40},{40,48},{48,56},{56,0},{1,9},... | collective-permute-start | bytes 786440 | tf_op jit(solution)/shard_map/ppermute | solution.py:57
  74.8 13.2 %collective-permute-start.25 = (f32[2,64,512]{2,1,0:T(8,128)S(1)}, f32[2,64,512]{2,1,0:T(8,128)S(1)}, u32[]{:S(2)}, u32[]{:S(2)}) collective-permute-start(f32[2,64,512]{2,1,0:T(8,128)S(1)} %pad_maximum_fusion.2), channel_id=1, source_target_pairs={{0,56},{8,0},{16,8},{24,16},{32,24},{40,32},{48,40},{56,48},{1,57}... | collective-permute-start | bytes 786440 | tf_op jit(solution)/shard_map/ppermute | solution.py:58
  81.1 11.7 %collective-permute-start.33 = (f32[2,64,512]{2,1,0:T(8,128)S(1)}, f32[2,64,512]{2,1,0:T(8,128)S(1)}, u32[]{:S(2)}, u32[]{:S(2)}) collective-permute-start(f32[2,64,512]{2,1,0:T(8,128)S(1)} %maximum_select_fusion.1.refs_0_), channel_id=1, source_target_pairs={{0,132},{4,128},{64,196},{68,192},{128,4},{132,0},{192,68},{196,64... | collective-permute-start | bytes 786440 | tf_op jit(solution)/shard_map/ppermute | solution.py:182
  82.7 14.7 %collective-permute-start.35 = (f32[2,64,512]{2,1,0:T(8,128)S(1)}, f32[2,64,512]{2,1,0:T(8,128)S(1)}, u32[]{:S(2)}, u32[]{:S(2)}) collective-permute-start(f32[2,64,512]{2,1,0:T(8,128)S(1)} %maximum_select_fusion.1.refs_0_), channel_id=1, source_target_pairs={{0,4},{4,0},{1,5},{5,1},{2,6},{6,2},{3,7},{7,3},{8,12},{12,8},{9,1... | collective-permute-start | bytes 786440 | tf_op jit(solution)/shard_map/ppermute | solution.py:188
  84.7 14.0 %collective-permute-start.36 = (f32[2,64,512]{2,1,0:T(8,128)S(1)}, f32[2,64,512]{2,1,0:T(8,128)S(1)}, u32[]{:S(2)}, u32[]{:S(2)}) collective-permute-start(f32[2,64,512]{2,1,0:T(8,128)S(1)} %maximum_select_fusion.1.refs_0_), channel_id=1, source_target_pairs={{0,64},{64,128},{128,192},{192,0},{1,65},{65,129},{129,193},{193,1... | collective-permute-start | bytes 786440 | tf_op jit(solution)/shard_map/ppermute | solution.py:188
  84.7 17.4 %collective-permute-start.38 = (f32[2,64,512]{2,1,0:T(8,128)S(1)}, f32[2,64,512]{2,1,0:T(8,128)S(1)}, u32[]{:S(2)}, u32[]{:S(2)}) collective-permute-start(f32[2,64,512]{2,1,0:T(8,128)S(1)} %maximum_select_fusion.1.refs_0_), channel_id=1, source_target_pairs={{0,192},{64,0},{128,64},{192,128},{1,193},{65,1},{129,65},{193,129... | collective-permute-start | bytes 786440 | tf_op jit(solution)/shard_map/ppermute | solution.py:188
  88.0 15.4 %collective-permute-start.26 = (f32[2,64,512]{2,1,0:T(8,128)S(1)}, f32[2,64,512]{2,1,0:T(8,128)}, u32[]{:S(2)}, u32[]{:S(2)}) collective-permute-start(f32[2,64,512]{2,1,0:T(8,128)S(1)} %maximum_select_fusion.2.refs_0_), channel_id=1, source_target_pairs={{0,132},{4,128},{64,196},{68,192},{128,4},{132,0},{192,68},{196,64... | collective-permute-start | bytes 786440 | tf_op jit(solution)/shard_map/ppermute | solution.py:182
  92.8 12.7 %collective-permute-start.28 = (f32[2,64,512]{2,1,0:T(8,128)S(1)}, f32[2,64,512]{2,1,0:T(8,128)}, u32[]{:S(2)}, u32[]{:S(2)}) collective-permute-start(f32[2,64,512]{2,1,0:T(8,128)S(1)} %maximum_select_fusion.2.refs_0_), channel_id=1, source_target_pairs={{0,4},{4,0},{1,5},{5,1},{2,6},{6,2},{3,7},{7,3},{8,12},{12,8},{9,1... | collective-permute-start | bytes 786440 | tf_op jit(solution)/shard_map/ppermute | solution.py:188
  97.4 11.1 %collective-permute-start.34 = (f32[2,64,512]{2,1,0:T(8,128)S(1)}, f32[2,64,512]{2,1,0:T(8,128)}, u32[]{:S(2)}, u32[]{:S(2)}) collective-permute-start(f32[2,64,512]{2,1,0:T(8,128)S(1)} %collective-permute-done.33.refs_1_), channel_id=1, source_target_pairs={{0,4},{4,0},{1,5},{5,1},{2,6},{6,2},{3,7},{7,3},{8,12},{12,8},{9,1... | collective-permute-start | bytes 786440 | tf_op jit(solution)/shard_map/ppermute | solution.py:188
  98.7 11.0 %collective-permute-start.37 = (f32[2,64,512]{2,1,0:T(8,128)S(1)}, f32[2,64,512]{2,1,0:T(8,128)}, u32[]{:S(2)}, u32[]{:S(2)}) collective-permute-start(f32[2,64,512]{2,1,0:T(8,128)S(1)} %collective-permute-done.33.refs_1_), channel_id=1, source_target_pairs={{0,64},{64,128},{128,192},{192,0},{1,65},{65,129},{129,193},{193,1... | collective-permute-start | bytes 786440 | tf_op jit(solution)/shard_map/ppermute | solution.py:188
  102.8 7.6 %collective-permute-start.39 = (f32[2,64,512]{2,1,0:T(8,128)S(1)}, f32[2,64,512]{2,1,0:T(8,128)}, u32[]{:S(2)}, u32[]{:S(2)}) collective-permute-start(f32[2,64,512]{2,1,0:T(8,128)S(1)} %collective-permute-done.33.refs_1_), channel_id=1, source_target_pairs={{0,192},{64,0},{128,64},{192,128},{1,193},{65,1},{129,65},{193,129... | collective-permute-start | bytes 786440 | tf_op jit(solution)/shard_map/ppermute | solution.py:188
  103.4 15.8 %collective-permute-start.29 = (f32[2,64,512]{2,1,0:T(8,128)S(1)}, f32[2,64,512]{2,1,0:T(8,128)S(1)}, u32[]{:S(2)}, u32[]{:S(2)}) collective-permute-start(f32[2,64,512]{2,1,0:T(8,128)S(1)} %maximum_select_fusion.2.refs_0_), channel_id=1, source_target_pairs={{0,64},{64,128},{128,192},{192,0},{1,65},{65,129},{129,193},{193,1... | collective-permute-start | bytes 786440 | tf_op jit(solution)/shard_map/ppermute | solution.py:188
  105.5 13.7 %collective-permute-start.31 = (f32[2,64,512]{2,1,0:T(8,128)S(1)}, f32[2,64,512]{2,1,0:T(8,128)S(1)}, u32[]{:S(2)}, u32[]{:S(2)}) collective-permute-start(f32[2,64,512]{2,1,0:T(8,128)S(1)} %maximum_select_fusion.2.refs_0_), channel_id=1, source_target_pairs={{0,192},{64,0},{128,64},{192,128},{1,193},{65,1},{129,65},{193,129... | collective-permute-start | bytes 786440 | tf_op jit(solution)/shard_map/ppermute | solution.py:188
  108.5 10.8 %collective-permute-start.27 = (f32[2,64,512]{2,1,0:T(8,128)}, f32[2,64,512]{2,1,0:T(8,128)S(1)}, u32[]{:S(2)}, u32[]{:S(2)}) collective-permute-start(f32[2,64,512]{2,1,0:T(8,128)} %collective-permute-done.26.refs_1_), channel_id=1, source_target_pairs={{0,4},{4,0},{1,5},{5,1},{2,6},{6,2},{3,7},{7,3},{8,12},{12,8},{9,1... | collective-permute-start | bytes 786440 | tf_op jit(solution)/shard_map/ppermute | solution.py:188
  109.8 9.5 %collective-permute-start.30 = (f32[2,64,512]{2,1,0:T(8,128)}, f32[2,64,512]{2,1,0:T(8,128)S(1)}, u32[]{:S(2)}, u32[]{:S(2)}) collective-permute-start(f32[2,64,512]{2,1,0:T(8,128)} %collective-permute-done.26.refs_1_), channel_id=1, source_target_pairs={{0,64},{64,128},{128,192},{192,0},{1,65},{65,129},{129,193},{193,1... | collective-permute-start | bytes 786440 | tf_op jit(solution)/shard_map/ppermute | solution.py:188
  110.4 8.9 %collective-permute-start.32 = (f32[2,64,512]{2,1,0:T(8,128)}, f32[2,64,512]{2,1,0:T(8,128)S(1)}, u32[]{:S(2)}, u32[]{:S(2)}) collective-permute-start(f32[2,64,512]{2,1,0:T(8,128)} %collective-permute-done.26.refs_1_), channel_id=1, source_target_pairs={{0,192},{64,0},{128,64},{192,128},{1,193},{65,1},{129,65},{193,129... | collective-permute-start | bytes 786440 | tf_op jit(solution)/shard_map/ppermute | solution.py:188
  (3 other events, 5.1 us)

commit v5 on v1

v5 whole, which is shorter than its diff:
```python
import math

import jax
import jax.numpy as jnp
import numpy as np
from jax import lax
from jax.experimental import pallas as pl
from jax.experimental.pallas import tpu as pltpu
from jax.sharding import Mesh
from jax.sharding import PartitionSpec as P

TWIN = 8
NT = 2048
FIRST_BIN = 64
FREQ = 4
ROWS = 64
COLS = 1024
WIDTH = 256
LAST = 63
HI = lax.Precision.HIGHEST


def place_of(panel):
    return panel >> 4, (panel >> 1) & 7, panel & 1


def leap(v, roots):
    up = lax.ppermute(v, "z", [(r, (r + 3) % 8) for r in roots])
    down = lax.ppermute(v, "z", [(r, (r - 3) % 8) for r in roots])
    return up, down


def leaps(mine, last, root, z):
    fixed = place_of(LAST)[1]

    def both(group):
        roots = [group, group + 4] + ([3, 7] if group != 3 else [])

        def branch(a, b):
            spare = jnp.zeros_like(a)
            return (*leap(jnp.where(z == fixed, b, a), roots), spare, spare + 1)

        return branch

    def apart(a, b):
        return (*leap(a, [3, 7]), *leap(b, [3, 7]))

    case = jnp.where(root == fixed, 4, root & 3)
    up, down, last_up, last_down = lax.switch(
        case, [both(0), both(1), both(2), both(3), apart], mine, last
    )
    d, e = (z - root) & 7, (z - fixed) & 7
    mine = jnp.where(d == 0, mine, jnp.where(d == 3, up, down))
    last_up = jnp.where(root == fixed, last_up, up)
    last_down = jnp.where(root == fixed, last_down, down)
    last = jnp.where(e == 0, last, jnp.where(e == 3, last_up, last_down))
    return mine, last


def steps(held, root, z):
    after = lax.ppermute(held, "z", [(k, (k + 1) % 8) for k in range(8)])
    before = lax.ppermute(held, "z", [(k, (k - 1) % 8) for k in range(8)])
    d = (z - root) & 7
    from_after = (d == 1) | (d == 4) | (d == 6)
    from_before = (d == 2) | (d == 7)
    return jnp.where(from_after, after, jnp.where(from_before, before, held))


def strips(spectra, panel):
    flat = spectra.reshape(2 * FREQ, ROWS, COLS)
    is_first = lax.broadcasted_iota(jnp.int32, (1, 1, 2 * ROWS), 2) < ROWS
    start = (panel.astype(jnp.uint32) & 15) * ROWS
    block = jnp.concatenate(
        [lax.dynamic_slice_in_dim(flat, start, ROWS, 2), flat[:, :, COLS - ROWS :]], axis=2
    )
    owner = panel >> 4
    for axis, bit in (("c", owner & 1), ("yh", owner >> 1)):
        other = lax.ppermute(block, axis, [(0, 1), (1, 0)])
        keep = jnp.where(is_first, bit, 1) == lax.axis_index(axis)
        block = jnp.where(keep, block, other)
    return block.reshape(2, FREQ, ROWS, 2 * ROWS)


def kernel(bins, x_ref, l_ref, coef_ref, *refs):
    block_refs, o_ref = refs[:16], refs[16]
    total = [None] * TWIN
    for i in range(4):
        b = jnp.concatenate([r[...] for r in block_refs[4 * i : 4 * i + 4]], axis=0)
        high = b.astype(jnp.bfloat16)
        low = (b - high.astype(jnp.float32)).astype(jnp.bfloat16)
        f = bins[i]
        left = l_ref[f]
        left_high = left.astype(jnp.bfloat16)
        left_low = (left - left_high.astype(jnp.float32)).astype(jnp.bfloat16)
        both = jnp.dot(
            jnp.concatenate([left_high, left_low], axis=0),
            high,
            preferred_element_type=jnp.float32,
        )
        rest = jnp.dot(left_high, low, preferred_element_type=jnp.float32)
        product = both[: 2 * ROWS] + (both[2 * ROWS :] + rest)
        real = x_ref[0, f] - product[:ROWS]
        imag = x_ref[1, f] - product[ROWS:]
        for u in range(TWIN):
            at = u * 8 + i * 2
            term = real * coef_ref[:, at : at + 1] - imag * coef_ref[:, at + 1 : at + 2]
            total[u] = term if total[u] is None else total[u] + term
    for u in range(TWIN):
        o_ref[u] = total[u].astype(o_ref.dtype)


def synthesise(bins, spectra, left, coefs, blocks):
    grid_spec = pltpu.PrefetchScalarGridSpec(
        num_scalar_prefetch=1,
        grid=(COLS // WIDTH,),
        in_specs=[
            pl.BlockSpec((2, FREQ, ROWS, WIDTH), lambda j, bins: (0, 0, 0, j)),
            pl.BlockSpec((4, 128, 256), lambda j, bins: (0, 0, 0)),
            pl.BlockSpec((ROWS, 64), lambda j, bins: (0, 0)),
            *[pl.BlockSpec((ROWS, WIDTH), lambda j, bins: (0, j))] * 16,
        ],
        out_specs=pl.BlockSpec((TWIN, ROWS, WIDTH), lambda j, bins: (0, 0, j)),
    )
    return pl.pallas_call(
        kernel,
        grid_spec=grid_spec,
        out_shape=jax.ShapeDtypeStruct((TWIN, ROWS, COLS), jnp.bfloat16),
        compiler_params=pltpu.CompilerParams(vmem_limit_bytes=40 * 1024 * 1024),
        cost_estimate=pl.CostEstimate(
            flops=2 * 3 * 4 * 128 * 256 * COLS, bytes_accessed=8 * 2**20, transcendentals=0
        ),
    )(bins, spectra, left, coefs, *blocks)


def tables(filters, offsets, strip, bins, yl):
    lag = np.arange(64, dtype=np.int64)[:, None] * (FIRST_BIN + np.arange(FREQ))[None, :] % NT
    lag_angle = lag * (2.0 * math.pi / NT)
    response_cos = jnp.dot(filters, jnp.asarray(np.cos(lag_angle), jnp.float32), precision=HI)
    response_sin = jnp.dot(filters, jnp.asarray(np.sin(lag_angle), jnp.float32), precision=HI)
    a_real, a_imag = strip[0], strip[1]
    rc, rs = response_cos.T[:, :, None], response_sin.T[:, :, None]
    real = a_real * rc + a_imag * rs
    imag = a_imag * rc - a_real * rs
    re_first = jnp.concatenate([real, -imag], axis=2)
    im_first = jnp.concatenate([imag, real], axis=2)
    re_last = jnp.concatenate([-imag, real], axis=2)
    im_last = jnp.concatenate([real, imag], axis=2)
    left = jnp.where(
        yl == 0,
        jnp.concatenate([re_first, im_first], axis=1),
        jnp.concatenate([re_last, im_last], axis=1),
    )
    times = offsets[:, None] + jnp.arange(TWIN, dtype=jnp.int32)[None, :]
    phase = times[:, :, None] * (FIRST_BIN + bins)[None, None, :] & (NT - 1)
    angle = phase.astype(jnp.float32) * (2.0 * math.pi / NT)
    coefs = jnp.stack([jnp.cos(angle), jnp.sin(angle)], axis=3).reshape(ROWS, 64)
    return left, coefs


def scatter(rows):
    members = [(f - 2 * c) % 4 * 2 + c for c in range(2) for f in range(4)]
    return lax.all_to_all(rows, ("x", "yl"), 0, 0, axis_index_groups=[members], tiled=True)


def exchange(own):
    plane = [(i, j) for i in range(4) for j in range(2)]
    across = [(i * 2 + j, ((i + 2) % 4) * 2 + 1 - j) for i, j in plane]
    partner = lax.ppermute(own, ("x", "yl"), across)
    blocks = [own, partner]
    turn = [(i, (i + 1) % 4) for i in range(4)]
    back = [(i, (i - 1) % 4) for i in range(4)]
    for axis, pairs in (("yl", [(0, 1), (1, 0)]), ("x", turn), ("x", back)):
        for v in (own, partner):
            blocks.append(lax.ppermute(v, axis, pairs))
    blocks[2], blocks[3] = blocks[3], blocks[2]
    return blocks


def shards(spectra, panels, filters, offsets):
    x, z, yl = lax.axis_index("x"), lax.axis_index("z"), lax.axis_index("yl")
    other_first = panels[1] == LAST
    other = jnp.where(other_first, panels[0], panels[1])
    ox, oz, oy = place_of(other)
    lx, lz, ly = place_of(LAST)
    strip = strips(spectra, other)
    arrived = scatter(spectra.reshape(2 * FREQ, ROWS, COLS))
    arrived, strip = lax.optimization_barrier((arrived, strip))
    spot = (oy * 4 + ((ox + 2 * oy) & 3)).astype(jnp.uint32)
    mine = lax.dynamic_index_in_dim(arrived, spot, 0, keepdims=False)
    last = arrived[ly * 4 + (lx + 2 * ly) % 4]
    mine, last = leaps(mine, last, oz, z)
    last = exchange(steps(last, lz, z))
    mine = exchange(steps(mine, oz, z))
    blocks = [v for pair in zip(mine, last) for v in pair]
    bins = (x + 2 * yl + jnp.array([0, 2, 3, 1], jnp.int32)) & 3
    left, coefs = tables(filters, offsets, strip, bins, yl)
    return synthesise(bins, spectra, left, coefs, blocks)


def solution(mesh):
    fine = Mesh(mesh.devices.reshape(4, 8, 2, 2, 2), ("x", "z", "yl", "yh", "c"))
    src, rcv = ("x", "z", "yl"), ("yh", "c")
    return jax.shard_map(
        shards,
        mesh=fine,
        in_specs=(P(None, None, src, rcv), P(), P(src, None), P(src)),
        out_specs=P(None, src, rcv),
        check_vma=False,
    )
```

time: 181 us -> 126 us (0.70)
  the two profiles are of different devices: /device:TPU:16 before, /device:TPU:8 now
where the time goes in v5:
time: 126 us; the launch traced here: 125 us
  waiting for transfers between devices  57.2 us (45%)
  starting transfers between devices  51.5 us (41%)
  Pallas kernels  6.1 us (5%)
  other arithmetic  4.65 us (4%)
  local copies, waits for them, and re-layouts  3.41 us (3%)
  between operations  2 us (2%)
    ppermute x2, waiting for transfers between devices, strips(): other = lax.ppermute(block, axis, [(0, 1), (1, 0)])  25.1 us
    ppermute x12, starting transfers between devices, exchange(): blocks.append(lax.ppermute(v, axis, pairs))  19.9 us
    ppermute x2, starting transfers between devices, steps(): before = lax.ppermute(held, 'z', [(k, (k - 1) % 8) for k in range(8)])  15.7 us
    ppermute x12, waiting for transfers between devices, exchange(): blocks.append(lax.ppermute(v, axis, pairs))  15.6 us
    ppermute x1, waiting for transfers between devices, leap(): down = lax.ppermute(v, 'z', [(r, (r - 3) % 8) for r in roots])  9.15 us
    ppermute x2, waiting for transfers between devices, steps(): after = lax.ppermute(held, 'z', [(k, (k + 1) % 8) for k in range(8)])  7.02 us
    all_to_all x1, starting transfers between devices, scatter(): lax.all_to_all(rows, ('x', 'yl'), 0, 0, axis_index_groups=[members], tile...  6.56 us
    pallas_call x1, Pallas kernels, synthesise(): pl.pallas_call(kernel, grid_spec=grid_spec, out_shape=jax.ShapeDtypeStruc...  6.1 us
  transfers between devices with their start and end apart: 23, of which 10 were waited for; matrix products, arithmetic and copies ran while one was open for 4% of the time, Pallas kernels for 0%

profile of v5, /device:TPU:8, one launch (start us, length us, event | category | flops | bytes accessed | tf_op | source)
XLA Modules:
  0.0 125.3 jit_solution(1607955989459669949)
XLA Ops:
  0.0 6.6 %all-to-all-start = ((f32[8,64,1024]{2,1,0:T(8,128)}), f32[8,64,1024]{2,1,0:T(8,128)}, u32[]{:S(2)}, u32[]{:S(2)}) async-start(f32[8,64,1024]{2,1,0:T(8,128)} %bitcast.31), calls=%async_computation | async-start | bytes 4194304 | tf_op jit(solution)/shard_map/all_to_all | solution.py:162
  9.4 1.5 %collective-permute-done.12 = f32[8,64,128]{2,1,0:T(8,128)S(1)} collective-permute-done((f32[8,64,128]{2,1,0:T(8,128)S(1)}, f32[8,64,128]{2,1,0:T(8,128)S(1)}, u32[]{:S(2)}, u32[]{:S(2)}) %collective-permute-start.12) | collective-permute-done | bytes 262176 | tf_op jit(solution)/shard_map/ppermute | solution.py:78
  11.1 1.7 %collective-permute-start.13 = (f32[8,64,128]{2,1,0:T(8,128)S(1)}, f32[8,64,128]{2,1,0:T(8,128)S(1)}, u32[]{:S(2)}, u32[]{:S(2)}) collective-permute-start(f32[8,64,128]{2,1,0:T(8,128)S(1)} %broadcast_select_fusion.4), channel_id=1, source_target_pairs={{0,2},{2,0},{1,3},{3,1},{4,6},{6,4},{5,7},{7,5},{8,10},{10,8},{9,1... | collective-permute-start | bytes 786440 | tf_op jit(solution)/shard_map/ppermute | solution.py:78
  13.0 23.6 %collective-permute-done.13 = f32[8,64,128]{2,1,0:T(8,128)S(1)} collective-permute-done((f32[8,64,128]{2,1,0:T(8,128)S(1)}, f32[8,64,128]{2,1,0:T(8,128)S(1)}, u32[]{:S(2)}, u32[]{:S(2)}) %collective-permute-start.13) | collective-permute-done | bytes 262176 | tf_op jit(solution)/shard_map/ppermute | solution.py:78
  37.4 1.1 slice_bitcast_fusion
  38.4 13.4 %conditional.1 = (f32[64,1024]{1,0:T(8,128)}, f32[64,1024]{1,0:T(8,128)}, f32[64,1024]{1,0:T(8,128)}, f32[64,1024]{1,0:T(8,128)}) conditional(s32[]{:T(128)} %clamp.3, (s32[]{:T(128)}, f32[64,1024]{1,0:T(8,128)S(1)}, f32[64,1024]{1,0:T(8,128)S(1)}) %tuple.27, (s32[]{:T(128)}, f32[64,1024]{1,0:T(8,128)S(1)}, ...), branch_computations={%region_0.1_spmd, %region_1.2_spmd, %region_2.3_spmd, %region_3.4_... | conditional | flops 65537 | bytes 4194496 | solution.py:49
  38.5 1.3 %collective-permute-start.9 = (f32[64,1024]{1,0:T(8,128)S(1)}, f32[64,1024]{1,0:T(8,128)}, u32[]{:S(2)}, u32[]{:S(2)}) collective-permute-start(f32[64,1024]{1,0:T(8,128)S(1)} %broadcast_select_fusion.2), channel_id=1, source_target_pairs={{16,56},{48,24},{24,0},{56,32},{17,57},{49,25},{25,1},{57,33},{18,... | collective-permute-start | bytes 786440 | tf_op jit(solution)/shard_map/cond/branch_2_fun/ppermute | solution.py:29
  39.8 1.4 %collective-permute-start.8 = (f32[64,1024]{1,0:T(8,128)S(1)}, f32[64,1024]{1,0:T(8,128)}, u32[]{:S(2)}, u32[]{:S(2)}) collective-permute-start(f32[64,1024]{1,0:T(8,128)S(1)} %broadcast_select_fusion.2), channel_id=1, source_target_pairs={{16,40},{48,8},{24,48},{56,16},{17,41},{49,9},{25,49},{57,17},{18,... | collective-permute-start | bytes 786440 | tf_op jit(solution)/shard_map/cond/branch_2_fun/ppermute | solution.py:28
  41.2 9.2 %collective-permute-done.9 = f32[64,1024]{1,0:T(8,128)} collective-permute-done((f32[64,1024]{1,0:T(8,128)S(1)}, f32[64,1024]{1,0:T(8,128)}, u32[]{:S(2)}, u32[]{:S(2)}) %collective-permute-start.9) | collective-permute-done | bytes 262176 | tf_op jit(solution)/shard_map/cond/branch_2_fun/ppermute | solution.py:29
  51.8 1.3 %select_select_fusion.1 = (f32[64,1024]{1,0:T(8,128)S(1)}, f32[64,1024]{1,0:T(8,128)S(1)}) fusion(f32[64,1024]{1,0:T(8,128)} %get-tuple-element.58, f32[64,1024]{1,0:T(8,128)} %get-tuple-element.56, f32[64,1024]{1,0:T(8,128)} %get-tuple-element.57, f32[64,1024]{1,0:T(8,128)} %get-tuple-element.55, pred[]{:T(512)S(6)} %eq.98, pred[]{:T(512)S(6)} %eq.105, ...), kind=kLoop, calls=%fused_computation.7 | loop fusion | flops 393216 | bytes 2097157 | tf_op jit(solution)/shard_map/jit(_where)/select_n | solution.py:56
  53.1 10.0 %collective-permute-start.17 = (f32[64,1024]{1,0:T(8,128)S(1)}, f32[64,1024]{1,0:T(8,128)S(1)}, u32[]{:S(2)}, u32[]{:S(2)}) collective-permute-start(f32[64,1024]{1,0:T(8,128)S(1)} %get-tuple-element.65), channel_id=1, source_target_pairs={{0,56},{8,0},{16,8},{24,16},{32,24},{40,32},{48,40},{56,48},{1,57}... | collective-permute-start | bytes 786440 | tf_op jit(solution)/shard_map/ppermute | solution.py:62
  63.1 5.7 %collective-permute-start.15 = (f32[64,1024]{1,0:T(8,128)S(1)}, f32[64,1024]{1,0:T(8,128)}, u32[]{:S(2)}, u32[]{:S(2)}) collective-permute-start(f32[64,1024]{1,0:T(8,128)S(1)} %get-tuple-element.66), channel_id=1, source_target_pairs={{0,56},{8,0},{16,8},{24,16},{32,24},{40,32},{48,40},{56,48},{1,57}... | collective-permute-start | bytes 786440 | tf_op jit(solution)/shard_map/ppermute | solution.py:62
  68.8 7.0 %collective-permute-done.16 = f32[64,1024]{1,0:T(8,128)S(1)} collective-permute-done((f32[64,1024]{1,0:T(8,128)S(1)}, f32[64,1024]{1,0:T(8,128)S(1)}, u32[]{:S(2)}, u32[]{:S(2)}) %collective-permute-start.16) | collective-permute-done | bytes 262176 | tf_op jit(solution)/shard_map/ppermute | solution.py:61
  75.9 3.8 %collective-permute-start.29 = (f32[64,1024]{1,0:T(8,128)S(1)}, f32[64,1024]{1,0:T(8,128)S(1)}, u32[]{:S(2)}, u32[]{:S(2)}) collective-permute-start(f32[64,1024]{1,0:T(8,128)S(1)} %select_select_fusion.refs_1_), channel_id=1, source_target_pairs={{0,192},{64,0},{128,64},{192,128},{1,193},{65,1},{129,65},{193,129... | collective-permute-start | bytes 786440 | tf_op jit(solution)/shard_map/ppermute | solution.py:174
  79.7 1.2 collective-permute-start.23
  80.8 3.0 %collective-permute-start.19 = (f32[64,1024]{1,0:T(8,128)S(1)}, f32[64,1024]{1,0:T(8,128)}, u32[]{:S(2)}, u32[]{:S(2)}) collective-permute-start(f32[64,1024]{1,0:T(8,128)S(1)} %select_select_fusion.refs_1_), channel_id=1, source_target_pairs={{0,132},{4,128},{64,196},{68,192},{128,4},{132,0},{192,68},{196,64... | collective-permute-start | bytes 786440 | tf_op jit(solution)/shard_map/ppermute | solution.py:168
  84.0 1.0 select_select_fusion.2.refs_0_
  85.0 1.3 collective-permute-start.28
  86.2 2.3 %collective-permute-done.29.refs_13_ = f32[64,1024]{1,0:T(8,128)S(1)} collective-permute-done((f32[64,1024]{1,0:T(8,128)S(1)}, f32[64,1024]{1,0:T(8,128)S(1)}, u32[]{:S(2)}, u32[]{:S(2)}) %collective-permute-start.29) | collective-permute-done | bytes 262176 | tf_op jit(solution)/shard_map/ppermute | solution.py:174
  88.5 4.1 %collective-permute-done.25.refs_9_ = f32[64,1024]{1,0:T(8,128)S(1)} collective-permute-done((f32[64,1024]{1,0:T(8,128)S(1)}, f32[64,1024]{1,0:T(8,128)S(1)}, u32[]{:S(2)}, u32[]{:S(2)}) %collective-permute-start.25) | collective-permute-done | bytes 262176 | tf_op jit(solution)/shard_map/ppermute | solution.py:174
  92.6 1.2 collective-permute-start.22
  93.8 1.9 %collective-permute-start.18 = (f32[64,1024]{1,0:T(8,128)S(1)}, f32[64,1024]{1,0:T(8,128)}, u32[]{:S(2)}, u32[]{:S(2)}) collective-permute-start(f32[64,1024]{1,0:T(8,128)S(1)} %select_select_fusion.2.refs_0_), channel_id=1, source_target_pairs={{0,132},{4,128},{64,196},{68,192},{128,4},{132,0},{192,68},{196,64... | collective-permute-start | bytes 786440 | tf_op jit(solution)/shard_map/ppermute | solution.py:168
  95.9 3.9 %collective-permute-start.31 = (f32[64,1024]{1,0:T(8,128)}, f32[64,1024]{1,0:T(8,128)}, u32[]{:S(2)}, u32[]{:S(2)}) collective-permute-start(f32[64,1024]{1,0:T(8,128)} %collective-permute-done.19.refs_3_), channel_id=1, source_target_pairs={{0,192},{64,0},{128,64},{192,128},{1,193},{65,1},{129,65},{193,129... | collective-permute-start | bytes 786440 | tf_op jit(solution)/shard_map/ppermute | solution.py:174
  100.2 0.8 collective-permute-start.27
  101.0 3.4 %collective-permute-done.24.refs_8_ = f32[64,1024]{1,0:T(8,128)} collective-permute-done((f32[64,1024]{1,0:T(8,128)S(1)}, f32[64,1024]{1,0:T(8,128)}, u32[]{:S(2)}, u32[]{:S(2)}) %collective-permute-start.24) | collective-permute-done | bytes 262176 | tf_op jit(solution)/shard_map/ppermute | solution.py:174
  104.5 1.1 collective-permute-start.21
  105.6 5.9 %collective-permute-start.30 = (f32[64,1024]{1,0:T(8,128)}, f32[64,1024]{1,0:T(8,128)S(1)}, u32[]{:S(2)}, u32[]{:S(2)}) collective-permute-start(f32[64,1024]{1,0:T(8,128)} %collective-permute-done.18.refs_2_), channel_id=1, source_target_pairs={{0,192},{64,0},{128,64},{192,128},{1,193},{65,1},{129,65},{193,129... | collective-permute-start | bytes 786440 | tf_op jit(solution)/shard_map/ppermute | solution.py:174
  111.5 0.8 collective-permute-start.20
  112.3 1.1 fusion.6
  113.4 2.2 %collective-permute-done.30.refs_14_ = f32[64,1024]{1,0:T(8,128)S(1)} collective-permute-done((f32[64,1024]{1,0:T(8,128)}, f32[64,1024]{1,0:T(8,128)S(1)}, u32[]{:S(2)}, u32[]{:S(2)}) %collective-permute-start.30) | collective-permute-done | bytes 262176 | tf_op jit(solution)/shard_map/ppermute | solution.py:174
  115.7 3.6 %collective-permute-done.26.refs_10_ = f32[64,1024]{1,0:T(8,128)S(1)} collective-permute-done((f32[64,1024]{1,0:T(8,128)}, f32[64,1024]{1,0:T(8,128)S(1)}, u32[]{:S(2)}, u32[]{:S(2)}) %collective-permute-start.26) | collective-permute-done | bytes 262176 | tf_op jit(solution)/shard_map/ppermute | solution.py:174
  119.2 6.1 %shard_map.73 = bf16[8,64,1024]{2,1,0:T(8,128)(2,1)} custom-call(s32[4]{0:T(128)S(1)} %get-tuple-element.71.bins, f32[2,4,64,1024]{3,2,1,0:T(8,128)S(1)} %copy-done.1, f32[4,128,256]{2,1,0:T(8,128)S(1)} %maximum_select_fusion.l_ref, f32[64,64]{1,0:T(8,128)S(1)} %copy.10.coef_ref, f32[64,1024]{1,0:T(8,128)S(1)} %select_select_fusion.2.refs_0_, ...), custom_call_target="tpu_custom_call" | custom-call | flops 805306368 | bytes 8388608 | tf_op jit(solution)/shard_map/pallas_call | solution.py:124
  (56 shorter events, 4.5 us)
Async XLA Ops:
  0.0 12.8 %copy-start = (f32[64,64]{1,0:T(8,128)S(1)}, f32[64,64]{1,0:T(8,128)}, u32[]{:S(2)}) copy-start(f32[64,64]{1,0:T(8,128)} %param.14) | copy-start | bytes 49156
  0.0 6.6 %copy-start.5 = (s32[2]{0:T(128)S(1)}, s32[2]{0:T(128)}, u32[]{:S(2)}) copy-start(s32[2]{0:T(128)} %param.13) | copy-start | bytes 28
  0.0 8.9 %copy-start.1 = (f32[2,4,64,1024]{3,2,1,0:T(8,128)S(1)}, f32[2,4,64,1024]{3,2,1,0:T(8,128)}, u32[]{:S(2)}) copy-start(f32[2,4,64,1024]{3,2,1,0:T(8,128)} %x_ref.1) | copy-start | bytes 6291460
  0.0 37.4 %all-to-all-start = ((f32[8,64,1024]{2,1,0:T(8,128)}), f32[8,64,1024]{2,1,0:T(8,128)}, u32[]{:S(2)}, u32[]{:S(2)}) async-start(f32[8,64,1024]{2,1,0:T(8,128)} %bitcast.31), calls=%async_computation | async-start | bytes 4194304 | tf_op jit(solution)/shard_map/all_to_all | solution.py:162
  6.6 6.2 %copy-start.4 = (f32[64,4]{1,0:T(8,128)S(1)}, f32[64,4]{1,0:T(8,128)}, u32[]{:S(2)}) copy-start(f32[64,4]{1,0:T(8,128)} %constant.83.clone) | copy-start | bytes 3076
  9.3 1.6 %collective-permute-start.12 = (f32[8,64,128]{2,1,0:T(8,128)S(1)}, f32[8,64,128]{2,1,0:T(8,128)S(1)}, u32[]{:S(2)}, u32[]{:S(2)}) collective-permute-start(f32[8,64,128]{2,1,0:T(8,128)S(1)} %pad_maximum_fusion), channel_id=1, source_target_pairs={{0,1},{1,0},{2,3},{3,2},{4,5},{5,4},{6,7},{7,6},{8,9},{9,8},{10,11... | collective-permute-start | bytes 786440 | tf_op jit(solution)/shard_map/ppermute | solution.py:78
  11.1 25.6 %collective-permute-start.13 = (f32[8,64,128]{2,1,0:T(8,128)S(1)}, f32[8,64,128]{2,1,0:T(8,128)S(1)}, u32[]{:S(2)}, u32[]{:S(2)}) collective-permute-start(f32[8,64,128]{2,1,0:T(8,128)S(1)} %broadcast_select_fusion.4), channel_id=1, source_target_pairs={{0,2},{2,0},{1,3},{3,1},{4,6},{6,4},{5,7},{7,5},{8,10},{10,8},{9,1... | collective-permute-start | bytes 786440 | tf_op jit(solution)/shard_map/ppermute | solution.py:78
  38.5 11.8 %collective-permute-start.9 = (f32[64,1024]{1,0:T(8,128)S(1)}, f32[64,1024]{1,0:T(8,128)}, u32[]{:S(2)}, u32[]{:S(2)}) collective-permute-start(f32[64,1024]{1,0:T(8,128)S(1)} %broadcast_select_fusion.2), channel_id=1, source_target_pairs={{16,56},{48,24},{24,0},{56,32},{17,57},{49,25},{25,1},{57,33},{18,... | collective-permute-start | bytes 786440 | tf_op jit(solution)/shard_map/cond/branch_2_fun/ppermute | solution.py:29
  39.8 10.5 %collective-permute-start.8 = (f32[64,1024]{1,0:T(8,128)S(1)}, f32[64,1024]{1,0:T(8,128)}, u32[]{:S(2)}, u32[]{:S(2)}) collective-permute-start(f32[64,1024]{1,0:T(8,128)S(1)} %broadcast_select_fusion.2), channel_id=1, source_target_pairs={{16,40},{48,8},{24,48},{56,16},{17,41},{49,9},{25,49},{57,17},{18,... | collective-permute-start | bytes 786440 | tf_op jit(solution)/shard_map/cond/branch_2_fun/ppermute | solution.py:28
  51.8 11.3 %copy-start.6 = (s32[64]{0:T(128)S(1)}, s32[64]{0:T(128)}, u32[]{:S(2)}) copy-start(s32[64]{0:T(128)} %param.15) | copy-start | bytes 772
  51.8 17.0 %copy-start.7 = (s32[4]{0:T(128)S(1)}, s32[4]{0:T(128)}, u32[]{:S(2)}) copy-start(s32[4]{0:T(128)} %constant.82.clone) | copy-start | bytes 52
  51.8 48.2 %copy-start.3 = (f32[64,4]{1,0:T(8,128)S(1)}, f32[64,4]{1,0:T(8,128)}, u32[]{:S(2)}) copy-start(f32[64,4]{1,0:T(8,128)} %constant.84.clone) | copy-start | bytes 3076
  53.1 30.9 %copy-start.2 = (f32[64,1024]{1,0:T(8,128)}, f32[64,1024]{1,0:T(8,128)S(1)}, u32[]{:S(2)}) copy-start(f32[64,1024]{1,0:T(8,128)S(1)} %get-tuple-element.66) | copy-start | bytes 786436
  53.1 15.7 %collective-permute-start.17 = (f32[64,1024]{1,0:T(8,128)S(1)}, f32[64,1024]{1,0:T(8,128)S(1)}, u32[]{:S(2)}, u32[]{:S(2)}) collective-permute-start(f32[64,1024]{1,0:T(8,128)S(1)} %get-tuple-element.65), channel_id=1, source_target_pairs={{0,56},{8,0},{16,8},{24,16},{32,24},{40,32},{48,40},{56,48},{1,57}... | collective-permute-start | bytes 786440 | tf_op jit(solution)/shard_map/ppermute | solution.py:62
  63.1 12.8 %collective-permute-start.16 = (f32[64,1024]{1,0:T(8,128)S(1)}, f32[64,1024]{1,0:T(8,128)S(1)}, u32[]{:S(2)}, u32[]{:S(2)}) collective-permute-start(f32[64,1024]{1,0:T(8,128)S(1)} %get-tuple-element.65), channel_id=1, source_target_pairs={{0,8},{8,16},{16,24},{24,32},{32,40},{40,48},{48,56},{56,0},{1,9},... | collective-permute-start | bytes 786440 | tf_op jit(solution)/shard_map/ppermute | solution.py:61
  63.1 17.7 %collective-permute-start.15 = (f32[64,1024]{1,0:T(8,128)S(1)}, f32[64,1024]{1,0:T(8,128)}, u32[]{:S(2)}, u32[]{:S(2)}) collective-permute-start(f32[64,1024]{1,0:T(8,128)S(1)} %get-tuple-element.66), channel_id=1, source_target_pairs={{0,56},{8,0},{16,8},{24,16},{32,24},{40,32},{48,40},{56,48},{1,57}... | collective-permute-start | bytes 786440 | tf_op jit(solution)/shard_map/ppermute | solution.py:62
  68.8 15.2 %collective-permute-start.14 = (f32[64,1024]{1,0:T(8,128)S(1)}, f32[64,1024]{1,0:T(8,128)}, u32[]{:S(2)}, u32[]{:S(2)}) collective-permute-start(f32[64,1024]{1,0:T(8,128)S(1)} %get-tuple-element.66), channel_id=1, source_target_pairs={{0,8},{8,16},{16,24},{24,32},{32,40},{40,48},{48,56},{56,0},{1,9},... | collective-permute-start | bytes 786440 | tf_op jit(solution)/shard_map/ppermute | solution.py:61
  75.9 12.6 %collective-permute-start.29 = (f32[64,1024]{1,0:T(8,128)S(1)}, f32[64,1024]{1,0:T(8,128)S(1)}, u32[]{:S(2)}, u32[]{:S(2)}) collective-permute-start(f32[64,1024]{1,0:T(8,128)S(1)} %select_select_fusion.refs_1_), channel_id=1, source_target_pairs={{0,192},{64,0},{128,64},{192,128},{1,193},{65,1},{129,65},{193,129... | collective-permute-start | bytes 786440 | tf_op jit(solution)/shard_map/ppermute | solution.py:174
  79.7 12.9 %collective-permute-start.25 = (f32[64,1024]{1,0:T(8,128)S(1)}, f32[64,1024]{1,0:T(8,128)S(1)}, u32[]{:S(2)}, u32[]{:S(2)}) collective-permute-start(f32[64,1024]{1,0:T(8,128)S(1)} %select_select_fusion.refs_1_), channel_id=1, source_target_pairs={{0,64},{64,128},{128,192},{192,0},{1,65},{65,129},{129,193},{193,1... | collective-permute-start | bytes 786440 | tf_op jit(solution)/shard_map/ppermute | solution.py:174
  79.7 14.1 %collective-permute-start.23 = (f32[64,1024]{1,0:T(8,128)S(1)}, f32[64,1024]{1,0:T(8,128)S(1)}, u32[]{:S(2)}, u32[]{:S(2)}) collective-permute-start(f32[64,1024]{1,0:T(8,128)S(1)} %select_select_fusion.refs_1_), channel_id=1, source_target_pairs={{0,4},{4,0},{1,5},{5,1},{2,6},{6,2},{3,7},{7,3},{8,12},{12,8},{9,1... | collective-permute-start | bytes 786440 | tf_op jit(solution)/shard_map/ppermute | solution.py:174
  80.8 15.1 %collective-permute-start.19 = (f32[64,1024]{1,0:T(8,128)S(1)}, f32[64,1024]{1,0:T(8,128)}, u32[]{:S(2)}, u32[]{:S(2)}) collective-permute-start(f32[64,1024]{1,0:T(8,128)S(1)} %select_select_fusion.refs_1_), channel_id=1, source_target_pairs={{0,132},{4,128},{64,196},{68,192},{128,4},{132,0},{192,68},{196,64... | collective-permute-start | bytes 786440 | tf_op jit(solution)/shard_map/ppermute | solution.py:168
  85.0 15.2 %collective-permute-start.28 = (f32[64,1024]{1,0:T(8,128)S(1)}, f32[64,1024]{1,0:T(8,128)}, u32[]{:S(2)}, u32[]{:S(2)}) collective-permute-start(f32[64,1024]{1,0:T(8,128)S(1)} %select_select_fusion.2.refs_0_), channel_id=1, source_target_pairs={{0,192},{64,0},{128,64},{192,128},{1,193},{65,1},{129,65},{193,129... | collective-permute-start | bytes 786440 | tf_op jit(solution)/shard_map/ppermute | solution.py:174
  88.5 15.9 %collective-permute-start.24 = (f32[64,1024]{1,0:T(8,128)S(1)}, f32[64,1024]{1,0:T(8,128)}, u32[]{:S(2)}, u32[]{:S(2)}) collective-permute-start(f32[64,1024]{1,0:T(8,128)S(1)} %select_select_fusion.2.refs_0_), channel_id=1, source_target_pairs={{0,64},{64,128},{128,192},{192,0},{1,65},{65,129},{129,193},{193,1... | collective-permute-start | bytes 786440 | tf_op jit(solution)/shard_map/ppermute | solution.py:174
  92.6 18.8 %collective-permute-start.22 = (f32[64,1024]{1,0:T(8,128)S(1)}, f32[64,1024]{1,0:T(8,128)}, u32[]{:S(2)}, u32[]{:S(2)}) collective-permute-start(f32[64,1024]{1,0:T(8,128)S(1)} %select_select_fusion.2.refs_0_), channel_id=1, source_target_pairs={{0,4},{4,0},{1,5},{5,1},{2,6},{6,2},{3,7},{7,3},{8,12},{12,8},{9,1... | collective-permute-start | bytes 786440 | tf_op jit(solution)/shard_map/ppermute | solution.py:174
  93.8 11.8 %collective-permute-start.18 = (f32[64,1024]{1,0:T(8,128)S(1)}, f32[64,1024]{1,0:T(8,128)}, u32[]{:S(2)}, u32[]{:S(2)}) collective-permute-start(f32[64,1024]{1,0:T(8,128)S(1)} %select_select_fusion.2.refs_0_), channel_id=1, source_target_pairs={{0,132},{4,128},{64,196},{68,192},{128,4},{132,0},{192,68},{196,64... | collective-permute-start | bytes 786440 | tf_op jit(solution)/shard_map/ppermute | solution.py:168
  95.9 15.5 %collective-permute-start.31 = (f32[64,1024]{1,0:T(8,128)}, f32[64,1024]{1,0:T(8,128)}, u32[]{:S(2)}, u32[]{:S(2)}) collective-permute-start(f32[64,1024]{1,0:T(8,128)} %collective-permute-done.19.refs_3_), channel_id=1, source_target_pairs={{0,192},{64,0},{128,64},{192,128},{1,193},{65,1},{129,65},{193,129... | collective-permute-start | bytes 786440 | tf_op jit(solution)/shard_map/ppermute | solution.py:174
  100.2 13.2 %collective-permute-start.27 = (f32[64,1024]{1,0:T(8,128)}, f32[64,1024]{1,0:T(8,128)S(1)}, u32[]{:S(2)}, u32[]{:S(2)}) collective-permute-start(f32[64,1024]{1,0:T(8,128)} %collective-permute-done.19.refs_3_), channel_id=1, source_target_pairs={{0,64},{64,128},{128,192},{192,0},{1,65},{65,129},{129,193},{193,1... | collective-permute-start | bytes 786440 | tf_op jit(solution)/shard_map/ppermute | solution.py:174
  104.5 9.0 %collective-permute-start.21 = (f32[64,1024]{1,0:T(8,128)}, f32[64,1024]{1,0:T(8,128)S(1)}, u32[]{:S(2)}, u32[]{:S(2)}) collective-permute-start(f32[64,1024]{1,0:T(8,128)} %collective-permute-done.19.refs_3_), channel_id=1, source_target_pairs={{0,4},{4,0},{1,5},{5,1},{2,6},{6,2},{3,7},{7,3},{8,12},{12,8},{9,1... | collective-permute-start | bytes 786440 | tf_op jit(solution)/shard_map/ppermute | solution.py:174
  105.6 10.1 %collective-permute-start.30 = (f32[64,1024]{1,0:T(8,128)}, f32[64,1024]{1,0:T(8,128)S(1)}, u32[]{:S(2)}, u32[]{:S(2)}) collective-permute-start(f32[64,1024]{1,0:T(8,128)} %collective-permute-done.18.refs_2_), channel_id=1, source_target_pairs={{0,192},{64,0},{128,64},{192,128},{1,193},{65,1},{129,65},{193,129... | collective-permute-start | bytes 786440 | tf_op jit(solution)/shard_map/ppermute | solution.py:174
  111.4 7.8 %collective-permute-start.26 = (f32[64,1024]{1,0:T(8,128)}, f32[64,1024]{1,0:T(8,128)S(1)}, u32[]{:S(2)}, u32[]{:S(2)}) collective-permute-start(f32[64,1024]{1,0:T(8,128)} %collective-permute-done.18.refs_2_), channel_id=1, source_target_pairs={{0,64},{64,128},{128,192},{192,0},{1,65},{65,129},{129,193},{193,1... | collective-permute-start | bytes 786440 | tf_op jit(solution)/shard_map/ppermute | solution.py:174
  111.5 7.8 %collective-permute-start.20 = (f32[64,1024]{1,0:T(8,128)}, f32[64,1024]{1,0:T(8,128)S(1)}, u32[]{:S(2)}, u32[]{:S(2)}) collective-permute-start(f32[64,1024]{1,0:T(8,128)} %collective-permute-done.18.refs_2_), channel_id=1, source_target_pairs={{0,4},{4,0},{1,5},{5,1},{2,6},{6,2},{3,7},{7,3},{8,12},{12,8},{9,1... | collective-permute-start | bytes 786440 | tf_op jit(solution)/shard_map/ppermute | solution.py:174

commit v6 on v5

--- a/solution.py
+++ b/solution.py
@@ -24,37 +24,15 @@
     return panel >> 4, (panel >> 1) & 7, panel & 1
 
 
-def leap(v, roots):
-    up = lax.ppermute(v, "z", [(r, (r + 3) % 8) for r in roots])
-    down = lax.ppermute(v, "z", [(r, (r - 3) % 8) for r in roots])
+def leap(v, root):
+    up = lax.ppermute(v, "z", [(root, (root + 3) % 8)])
+    down = lax.ppermute(v, "z", [(root, (root - 3) % 8)])
     return up, down
 
 
-def leaps(mine, last, root, z):
-    fixed = place_of(LAST)[1]
-
-    def both(group):
-        roots = [group, group + 4] + ([3, 7] if group != 3 else [])
-
-        def branch(a, b):
-            spare = jnp.zeros_like(a)
-            return (*leap(jnp.where(z == fixed, b, a), roots), spare, spare + 1)
-
-        return branch
-
-    def apart(a, b):
-        return (*leap(a, [3, 7]), *leap(b, [3, 7]))
-
-    case = jnp.where(root == fixed, 4, root & 3)
-    up, down, last_up, last_down = lax.switch(
-        case, [both(0), both(1), both(2), both(3), apart], mine, last
-    )
-    d, e = (z - root) & 7, (z - fixed) & 7
-    mine = jnp.where(d == 0, mine, jnp.where(d == 3, up, down))
-    last_up = jnp.where(root == fixed, last_up, up)
-    last_down = jnp.where(root == fixed, last_down, down)
-    last = jnp.where(e == 0, last, jnp.where(e == 3, last_up, last_down))
-    return mine, last
+def land(v, leapt, root, z):
+    d = (z - root) & 7
+    return jnp.where(d == 0, v, jnp.where(d == 3, leapt[0], leapt[1]))
 
 
 def steps(held, root, z):
@@ -184,12 +162,14 @@
     lx, lz, ly = place_of(LAST)
     strip = strips(spectra, other)
     arrived = scatter(spectra.reshape(2 * FREQ, ROWS, COLS))
-    arrived, strip = lax.optimization_barrier((arrived, strip))
     spot = (oy * 4 + ((ox + 2 * oy) & 3)).astype(jnp.uint32)
     mine = lax.dynamic_index_in_dim(arrived, spot, 0, keepdims=False)
     last = arrived[ly * 4 + (lx + 2 * ly) % 4]
-    mine, last = leaps(mine, last, oz, z)
-    last = exchange(steps(last, lz, z))
+    last = land(last, leap(last, lz), lz, z)
+    branches = [lambda v, r=r: leap(v, r) for r in range(8)]
+    mine = land(mine, lax.switch(oz, branches, mine), oz, z)
+    last, strip = lax.optimization_barrier((steps(last, lz, z), strip))
+    last = exchange(last)
     mine = exchange(steps(mine, oz, z))
     blocks = [v for pair in zip(mine, last) for v in pair]
     bins = (x + 2 * yl + jnp.array([0, 2, 3, 1], jnp.int32)) & 3

time: 126 us -> 116 us (0.921)
  the two profiles are of different devices: /device:TPU:8 before, /device:TPU:16 now
where the time goes in v6:
time: 116 us; the launch traced here: 115 us
  waiting for transfers between devices  57.6 us (50%)
  starting transfers between devices  37.7 us (33%)
  other arithmetic  7.47 us (6%)
  Pallas kernels  6.15 us (5%)
  local copies, waits for them, and re-layouts  3.41 us (3%)
  between operations  2.18 us (2%)
    all_to_all x1, waiting for transfers between devices, scatter(): lax.all_to_all(rows, ('x', 'yl'), 0, 0, axis_index_groups=[members], tile...  24 us
    ppermute x12, waiting for transfers between devices, exchange(): blocks.append(lax.ppermute(v, axis, pairs))  19.1 us
    ppermute x12, starting transfers between devices, exchange(): blocks.append(lax.ppermute(v, axis, pairs))  11.1 us
    ppermute x2, starting transfers between devices, leap(): down = lax.ppermute(v, 'z', [(root, (root - 3) % 8)])  10 us
    pallas_call x1, Pallas kernels, synthesise(): pl.pallas_call(kernel, grid_spec=grid_spec, out_shape=jax.ShapeDtypeStruc...  6.15 us
    all_to_all x1, starting transfers between devices, scatter(): lax.all_to_all(rows, ('x', 'yl'), 0, 0, axis_index_groups=[members], tile...  5.29 us
    ppermute x2, waiting for transfers between devices, steps(): before = lax.ppermute(held, 'z', [(k, (k - 1) % 8) for k in range(8)])  4.45 us
    ppermute x2, waiting for transfers between devices, leap(): up = lax.ppermute(v, 'z', [(root, (root + 3) % 8)])  3.95 us
  transfers between devices with their start and end apart: 25, of which 12 were waited for; matrix products, arithmetic and copies ran while one was open for 9% of the time, Pallas kernels for 0%

profile of v6, /device:TPU:16, one launch (start us, length us, event | category | flops | bytes accessed | tf_op | source)
XLA Modules:
  0.0 114.9 jit_solution(12420682439846459508)
XLA Ops:
  0.0 5.3 %all-to-all-start = ((f32[8,64,1024]{2,1,0:T(8,128)}), f32[8,64,1024]{2,1,0:T(8,128)}, u32[]{:S(2)}, u32[]{:S(2)}) async-start(f32[8,64,1024]{2,1,0:T(8,128)} %bitcast.31), calls=%async_computation | async-start | bytes 4194304 | tf_op jit(solution)/shard_map/all_to_all | solution.py:140
  8.8 24.0 %all-to-all-done = f32[8,64,1024]{2,1,0:T(8,128)} async-done(((f32[8,64,1024]{2,1,0:T(8,128)}), f32[8,64,1024]{2,1,0:T(8,128)}, u32[]{:S(2)}, u32[]{:S(2)}) %all-to-all-start) | async-done | bytes 2097184 | tf_op jit(solution)/shard_map/all_to_all | solution.py:140
  32.8 1.8 %dynamic-slice_bitcast_fusion = (f32[64,1024]{1,0:T(8,128)S(1)}, f32[64,1024]{1,0:T(8,128)}) fusion(f32[8,64,1024]{2,1,0:T(8,128)} %all-to-all-done, u32[]{:T(128)S(6)} %convert_element_type.22), kind=kLoop, calls=%fused_computation.5 | loop fusion | bytes 1048580 | tf_op jit(solution)/shard_map/jit(dynamic_index_in_dim)/squeeze | solution.py:166
  35.2 1.4 %collective-permute-start.16 = (f32[64,1024]{1,0:T(8,128)}, f32[64,1024]{1,0:T(8,128)}, u32[]{:S(2)}, u32[]{:S(2)}) collective-permute-start(f32[64,1024]{1,0:T(8,128)} %get-tuple-element.24), channel_id=1, source_target_pairs={{56,16},{57,17},{58,18},{59,19},{60,20},{61,21},{62,22},{63,23},{1... | collective-permute-start | bytes 786440 | tf_op jit(solution)/shard_map/ppermute | solution.py:28
  36.6 1.1 broadcast_select_fusion
  38.4 16.8 %conditional.1 = (f32[64,1024]{1,0:T(8,128)}, f32[64,1024]{1,0:T(8,128)}) conditional(s32[]{:T(128)} %clamp.3, f32[64,1024]{1,0:T(8,128)S(1)} %get-tuple-element.23, f32[64,1024]{1,0:T(8,128)S(1)} %get-tuple-element.23, f32[64,1024]{1,0:T(8,128)S(1)} %get-tuple-element.23, ...), branch_computations={%region_0.1_spmd, %region_1.2_spmd, %region_2.3_spmd, %region_3.4_... | conditional | bytes 2097248 | solution.py:170
  38.4 9.3 %collective-permute-start.1 = (f32[64,1024]{1,0:T(8,128)S(1)}, f32[64,1024]{1,0:T(8,128)}, u32[]{:S(2)}, u32[]{:S(2)}) collective-permute-start(f32[64,1024]{1,0:T(8,128)S(1)} %param), channel_id=1, source_target_pairs={{0,40},{1,41},{2,42},{3,43},{4,44},{5,45},{6,46},{7,47},{64,104},{... | collective-permute-start | bytes 786440 | tf_op jit(solution)/shard_map/cond/branch_0_fun/ppermute | solution.py:29
  47.8 2.0 %collective-permute-start = (f32[64,1024]{1,0:T(8,128)S(1)}, f32[64,1024]{1,0:T(8,128)}, u32[]{:S(2)}, u32[]{:S(2)}) collective-permute-start(f32[64,1024]{1,0:T(8,128)S(1)} %param), channel_id=1, source_target_pairs={{0,24},{1,25},{2,26},{3,27},{4,28},{5,29},{6,30},{7,31},{64,88},{6... | collective-permute-start | bytes 786440 | tf_op jit(solution)/shard_map/cond/branch_0_fun/ppermute | solution.py:28
  49.7 1.5 %collective-permute-done.1 = f32[64,1024]{1,0:T(8,128)} collective-permute-done((f32[64,1024]{1,0:T(8,128)S(1)}, f32[64,1024]{1,0:T(8,128)}, u32[]{:S(2)}, u32[]{:S(2)}) %collective-permute-start.1) | collective-permute-done | bytes 262176 | tf_op jit(solution)/shard_map/cond/branch_0_fun/ppermute | solution.py:29
  51.2 3.9 %collective-permute-done = f32[64,1024]{1,0:T(8,128)} collective-permute-done((f32[64,1024]{1,0:T(8,128)S(1)}, f32[64,1024]{1,0:T(8,128)}, u32[]{:S(2)}, u32[]{:S(2)}) %collective-permute-start) | collective-permute-done | bytes 262176 | tf_op jit(solution)/shard_map/cond/branch_0_fun/ppermute | solution.py:28
  55.2 1.0 select_select_fusion.1
  56.3 2.0 %collective-permute-start.22 = (f32[64,1024]{1,0:T(8,128)S(1)}, f32[64,1024]{1,0:T(8,128)}, u32[]{:S(2)}, u32[]{:S(2)}) collective-permute-start(f32[64,1024]{1,0:T(8,128)S(1)} %select_select_fusion.1), channel_id=1, source_target_pairs={{0,8},{8,16},{16,24},{24,32},{32,40},{40,48},{48,56},{56,0},{1,9},... | collective-permute-start | bytes 786440 | tf_op jit(solution)/shard_map/ppermute | solution.py:39
  59.0 1.1 select_select_fusion.3
  60.1 1.4 %collective-permute-start.19 = (f32[64,1024]{1,0:T(8,128)S(1)}, f32[64,1024]{1,0:T(8,128)}, u32[]{:S(2)}, u32[]{:S(2)}) collective-permute-start(f32[64,1024]{1,0:T(8,128)S(1)} %select_select_fusion.3), channel_id=1, source_target_pairs={{0,56},{8,0},{16,8},{24,16},{32,24},{40,32},{48,40},{56,48},{1,57}... | collective-permute-start | bytes 786440 | tf_op jit(solution)/shard_map/ppermute | solution.py:40
  62.2 3.3 %collective-permute-done.23 = f32[64,1024]{1,0:T(8,128)S(1)} collective-permute-done((f32[64,1024]{1,0:T(8,128)S(1)}, f32[64,1024]{1,0:T(8,128)S(1)}, u32[]{:S(2)}, u32[]{:S(2)}) %collective-permute-start.23) | collective-permute-done | bytes 262176 | tf_op jit(solution)/shard_map/ppermute | solution.py:40
  66.5 1.3 %collective-permute-start.34 = (f32[64,1024]{1,0:T(8,128)S(1)}, f32[64,1024]{1,0:T(8,128)S(1)}, u32[]{:S(2)}, u32[]{:S(2)}) collective-permute-start(f32[64,1024]{1,0:T(8,128)S(1)} %select_select_fusion.refs_0_), channel_id=1, source_target_pairs={{0,192},{64,0},{128,64},{192,128},{1,193},{65,1},{129,65},{193,129... | collective-permute-start | bytes 786440 | tf_op jit(solution)/shard_map/ppermute | solution.py:152
  68.6 1.1 collective-permute-done.19
  69.7 1.1 collective-permute-start.24
  70.9 1.8 %broadcast_select_fusion.1 = f32[8,64,128]{2,1,0:T(8,128)} fusion(f32[8,64,128]{2,1,0:T(8,128)} %copy-done.3, f32[8,64,128]{2,1,0:T(8,128)} %collective-permute-done.21, pred[128]{0:T(512)(128)(4,1)S(1)} %fusion.4), kind=kLoop, calls=%fused_computation.15 | loop fusion | flops 65536 | bytes 786560 | tf_op jit(solution)/shard_map/jit(_where)/select_n | solution.py:58
  72.6 1.0 select_select_fusion.2.refs_1_
  73.6 2.4 %collective-permute-start.35 = (f32[64,1024]{1,0:T(8,128)S(1)}, f32[64,1024]{1,0:T(8,128)}, u32[]{:S(2)}, u32[]{:S(2)}) collective-permute-start(f32[64,1024]{1,0:T(8,128)S(1)} %select_select_fusion.2.refs_1_), channel_id=1, source_target_pairs={{0,192},{64,0},{128,64},{192,128},{1,193},{65,1},{129,65},{193,129... | collective-permute-start | bytes 786440 | tf_op jit(solution)/shard_map/ppermute | solution.py:152
  76.0 1.8 %collective-permute-start.25 = (f32[64,1024]{1,0:T(8,128)S(1)}, f32[64,1024]{1,0:T(8,128)}, u32[]{:S(2)}, u32[]{:S(2)}) collective-permute-start(f32[64,1024]{1,0:T(8,128)S(1)} %select_select_fusion.2.refs_1_), channel_id=1, source_target_pairs={{0,132},{4,128},{64,196},{68,192},{128,4},{132,0},{192,68},{196,64... | collective-permute-start | bytes 786440 | tf_op jit(solution)/shard_map/ppermute | solution.py:146
  77.8 3.8 %collective-permute-done.24.refs_2_ = f32[64,1024]{1,0:T(8,128)} collective-permute-done((f32[64,1024]{1,0:T(8,128)S(1)}, f32[64,1024]{1,0:T(8,128)}, u32[]{:S(2)}, u32[]{:S(2)}) %collective-permute-start.24) | collective-permute-done | bytes 262176 | tf_op jit(solution)/shard_map/ppermute | solution.py:146
  81.6 1.3 %collective-permute-start.36 = (f32[64,1024]{1,0:T(8,128)}, f32[64,1024]{1,0:T(8,128)}, u32[]{:S(2)}, u32[]{:S(2)}) collective-permute-start(f32[64,1024]{1,0:T(8,128)} %collective-permute-done.24.refs_2_), channel_id=1, source_target_pairs={{0,192},{64,0},{128,64},{192,128},{1,193},{65,1},{129,65},{193,129... | collective-permute-start | bytes 786440 | tf_op jit(solution)/shard_map/ppermute | solution.py:152
  82.9 3.1 %collective-permute-done.30.refs_8_ = f32[64,1024]{1,0:T(8,128)S(1)} collective-permute-done((f32[64,1024]{1,0:T(8,128)S(1)}, f32[64,1024]{1,0:T(8,128)S(1)}, u32[]{:S(2)}, u32[]{:S(2)}) %collective-permute-start.30) | collective-permute-done | bytes 262176 | tf_op jit(solution)/shard_map/ppermute | solution.py:152
  87.0 8.5 %collective-permute-done.36.refs_14_ = f32[64,1024]{1,0:T(8,128)} collective-permute-done((f32[64,1024]{1,0:T(8,128)}, f32[64,1024]{1,0:T(8,128)}, u32[]{:S(2)}, u32[]{:S(2)}) %collective-permute-start.36) | collective-permute-done | bytes 262176 | tf_op jit(solution)/shard_map/ppermute | solution.py:152
  96.9 2.0 %collective-permute-start.37 = (f32[64,1024]{1,0:T(8,128)}, f32[64,1024]{1,0:T(8,128)S(1)}, u32[]{:S(2)}, u32[]{:S(2)}) collective-permute-start(f32[64,1024]{1,0:T(8,128)} %collective-permute-done.25.refs_3_), channel_id=1, source_target_pairs={{0,192},{64,0},{128,64},{192,128},{1,193},{65,1},{129,65},{193,129... | collective-permute-start | bytes 786440 | tf_op jit(solution)/shard_map/ppermute | solution.py:152
  98.9 2.0 %collective-permute-start.27 = (f32[64,1024]{1,0:T(8,128)}, f32[64,1024]{1,0:T(8,128)S(1)}, u32[]{:S(2)}, u32[]{:S(2)}) collective-permute-start(f32[64,1024]{1,0:T(8,128)} %collective-permute-done.25.refs_3_), channel_id=1, source_target_pairs={{0,4},{4,0},{1,5},{5,1},{2,6},{6,2},{3,7},{7,3},{8,12},{12,8},{9,1... | collective-permute-start | bytes 786440 | tf_op jit(solution)/shard_map/ppermute | solution.py:152
  100.9 1.1 fusion.6
  102.0 3.8 %collective-permute-done.31.refs_9_ = f32[64,1024]{1,0:T(8,128)S(1)} collective-permute-done((f32[64,1024]{1,0:T(8,128)S(1)}, f32[64,1024]{1,0:T(8,128)S(1)}, u32[]{:S(2)}, u32[]{:S(2)}) %collective-permute-start.31) | collective-permute-done | bytes 262176 | tf_op jit(solution)/shard_map/ppermute | solution.py:152
  105.8 3.0 %collective-permute-done.33.refs_11_ = f32[64,1024]{1,0:T(8,128)S(1)} collective-permute-done((f32[64,1024]{1,0:T(8,128)}, f32[64,1024]{1,0:T(8,128)S(1)}, u32[]{:S(2)}, u32[]{:S(2)}) %collective-permute-start.33) | collective-permute-done | bytes 262176 | tf_op jit(solution)/shard_map/ppermute | solution.py:152
  108.8 6.2 %shard_map.73 = bf16[8,64,1024]{2,1,0:T(8,128)(2,1)} custom-call(s32[4]{0:T(128)S(1)} %get-tuple-element.31.bins, f32[2,4,64,1024]{3,2,1,0:T(8,128)S(1)} %copy-done.1, f32[4,128,256]{2,1,0:T(8,128)S(1)} %maximum_select_fusion.l_ref, f32[64,64]{1,0:T(8,128)S(1)} %copy.10.coef_ref, f32[64,1024]{1,0:T(8,128)S(1)} %select_select_fusion.refs_0_, ...), custom_call_target="tpu_custom_call" | custom-call | flops 805306368 | bytes 8388608 | tf_op jit(solution)/shard_map/pallas_call | solution.py:102
  (62 shorter events, 8.6 us)
Async XLA Ops:
  0.0 8.5 %copy-start = (f32[64,64]{1,0:T(8,128)S(1)}, f32[64,64]{1,0:T(8,128)}, u32[]{:S(2)}) copy-start(f32[64,64]{1,0:T(8,128)} %param.17) | copy-start | bytes 49156
  0.0 8.3 %copy-start.9 = (s32[4]{0:T(128)S(1)}, s32[4]{0:T(128)}, u32[]{:S(2)}) copy-start(s32[4]{0:T(128)} %constant.58.clone) | copy-start | bytes 52
  0.0 8.3 %copy-start.8 = (s32[64]{0:T(128)S(1)}, s32[64]{0:T(128)}, u32[]{:S(2)}) copy-start(s32[64]{0:T(128)} %param.18) | copy-start | bytes 772
  0.0 8.5 %copy-start.6 = (f32[64,4]{1,0:T(8,128)S(1)}, f32[64,4]{1,0:T(8,128)}, u32[]{:S(2)}) copy-start(f32[64,4]{1,0:T(8,128)} %constant.59.clone) | copy-start | bytes 3076
  0.0 32.7 %all-to-all-start = ((f32[8,64,1024]{2,1,0:T(8,128)}), f32[8,64,1024]{2,1,0:T(8,128)}, u32[]{:S(2)}, u32[]{:S(2)}) async-start(f32[8,64,1024]{2,1,0:T(8,128)} %bitcast.31), calls=%async_computation | async-start | bytes 4194304 | tf_op jit(solution)/shard_map/all_to_all | solution.py:140
  8.2 28.4 %collective-permute-start.20 = (f32[8,64,128]{2,1,0:T(8,128)S(1)}, f32[8,64,128]{2,1,0:T(8,128)}, u32[]{:S(2)}, u32[]{:S(2)}) collective-permute-start(f32[8,64,128]{2,1,0:T(8,128)S(1)} %pad_maximum_fusion), channel_id=1, source_target_pairs={{0,1},{1,0},{2,3},{3,2},{4,5},{5,4},{6,7},{7,6},{8,9},{9,8},{10,11... | collective-permute-start | bytes 786440 | tf_op jit(solution)/shard_map/ppermute | solution.py:56
  34.5 23.8 %collective-permute-start.17 = (f32[64,1024]{1,0:T(8,128)}, f32[64,1024]{1,0:T(8,128)S(1)}, u32[]{:S(2)}, u32[]{:S(2)}) collective-permute-start(f32[64,1024]{1,0:T(8,128)} %get-tuple-element.24), channel_id=1, source_target_pairs={{56,32},{57,33},{58,34},{59,35},{60,36},{61,37},{62,38},{63,39},{1... | collective-permute-start | bytes 786440 | tf_op jit(solution)/shard_map/ppermute | solution.py:29
  35.2 23.8 %collective-permute-start.16 = (f32[64,1024]{1,0:T(8,128)}, f32[64,1024]{1,0:T(8,128)}, u32[]{:S(2)}, u32[]{:S(2)}) collective-permute-start(f32[64,1024]{1,0:T(8,128)} %get-tuple-element.24), channel_id=1, source_target_pairs={{56,16},{57,17},{58,18},{59,19},{60,20},{61,21},{62,22},{63,23},{1... | collective-permute-start | bytes 786440 | tf_op jit(solution)/shard_map/ppermute | solution.py:28
  37.7 30.9 %copy-start.3 = (f32[8,64,128]{2,1,0:T(8,128)}, f32[8,64,128]{2,1,0:T(8,128)S(1)}, u32[]{:S(2)}) copy-start(f32[8,64,128]{2,1,0:T(8,128)S(1)} %broadcast_select_fusion) | copy-start | bytes 786436
  37.7 30.9 %collective-permute-start.21 = (f32[8,64,128]{2,1,0:T(8,128)S(1)}, f32[8,64,128]{2,1,0:T(8,128)}, u32[]{:S(2)}, u32[]{:S(2)}) collective-permute-start(f32[8,64,128]{2,1,0:T(8,128)S(1)} %broadcast_select_fusion), channel_id=1, source_target_pairs={{0,2},{2,0},{1,3},{3,1},{4,6},{6,4},{5,7},{7,5},{8,10},{10,8},{9,1... | collective-permute-start | bytes 786440 | tf_op jit(solution)/shard_map/ppermute | solution.py:56
  38.4 12.8 %collective-permute-start.1 = (f32[64,1024]{1,0:T(8,128)S(1)}, f32[64,1024]{1,0:T(8,128)}, u32[]{:S(2)}, u32[]{:S(2)}) collective-permute-start(f32[64,1024]{1,0:T(8,128)S(1)} %param), channel_id=1, source_target_pairs={{0,40},{1,41},{2,42},{3,43},{4,44},{5,45},{6,46},{7,47},{64,104},{... | collective-permute-start | bytes 786440 | tf_op jit(solution)/shard_map/cond/branch_0_fun/ppermute | solution.py:29
  47.8 7.4 %collective-permute-start = (f32[64,1024]{1,0:T(8,128)S(1)}, f32[64,1024]{1,0:T(8,128)}, u32[]{:S(2)}, u32[]{:S(2)}) collective-permute-start(f32[64,1024]{1,0:T(8,128)S(1)} %param), channel_id=1, source_target_pairs={{0,24},{1,25},{2,26},{3,27},{4,28},{5,29},{6,30},{7,31},{64,88},{6... | collective-permute-start | bytes 786440 | tf_op jit(solution)/shard_map/cond/branch_0_fun/ppermute | solution.py:28
  56.2 30.6 %copy-start.5 = (f32[64,4]{1,0:T(8,128)S(1)}, f32[64,4]{1,0:T(8,128)}, u32[]{:S(2)}) copy-start(f32[64,4]{1,0:T(8,128)} %constant.60.clone) | copy-start | bytes 3076
  56.2 9.3 %collective-permute-start.23 = (f32[64,1024]{1,0:T(8,128)S(1)}, f32[64,1024]{1,0:T(8,128)S(1)}, u32[]{:S(2)}, u32[]{:S(2)}) collective-permute-start(f32[64,1024]{1,0:T(8,128)S(1)} %select_select_fusion.1), channel_id=1, source_target_pairs={{0,56},{8,0},{16,8},{24,16},{32,24},{40,32},{48,40},{56,48},{1,57}... | collective-permute-start | bytes 786440 | tf_op jit(solution)/shard_map/ppermute | solution.py:40
  56.3 10.1 %collective-permute-start.22 = (f32[64,1024]{1,0:T(8,128)S(1)}, f32[64,1024]{1,0:T(8,128)}, u32[]{:S(2)}, u32[]{:S(2)}) collective-permute-start(f32[64,1024]{1,0:T(8,128)S(1)} %select_select_fusion.1), channel_id=1, source_target_pairs={{0,8},{8,16},{16,24},{24,32},{32,40},{40,48},{48,56},{56,0},{1,9},... | collective-permute-start | bytes 786440 | tf_op jit(solution)/shard_map/ppermute | solution.py:39
  60.1 12.5 %copy-start.2 = (f32[64,1024]{1,0:T(8,128)}, f32[64,1024]{1,0:T(8,128)S(1)}, u32[]{:S(2)}) copy-start(f32[64,1024]{1,0:T(8,128)S(1)} %select_select_fusion.3) | copy-start | bytes 786436
  60.1 9.6 %collective-permute-start.19 = (f32[64,1024]{1,0:T(8,128)S(1)}, f32[64,1024]{1,0:T(8,128)}, u32[]{:S(2)}, u32[]{:S(2)}) collective-permute-start(f32[64,1024]{1,0:T(8,128)S(1)} %select_select_fusion.3), channel_id=1, source_target_pairs={{0,56},{8,0},{16,8},{24,16},{32,24},{40,32},{48,40},{56,48},{1,57}... | collective-permute-start | bytes 786440 | tf_op jit(solution)/shard_map/ppermute | solution.py:40
  61.5 11.1 %collective-permute-start.18 = (f32[64,1024]{1,0:T(8,128)S(1)}, f32[64,1024]{1,0:T(8,128)S(1)}, u32[]{:S(2)}, u32[]{:S(2)}) collective-permute-start(f32[64,1024]{1,0:T(8,128)S(1)} %select_select_fusion.3), channel_id=1, source_target_pairs={{0,8},{8,16},{16,24},{24,32},{32,40},{40,48},{48,56},{56,0},{1,9},... | collective-permute-start | bytes 786440 | tf_op jit(solution)/shard_map/ppermute | solution.py:39
  66.5 9.5 %collective-permute-start.34 = (f32[64,1024]{1,0:T(8,128)S(1)}, f32[64,1024]{1,0:T(8,128)S(1)}, u32[]{:S(2)}, u32[]{:S(2)}) collective-permute-start(f32[64,1024]{1,0:T(8,128)S(1)} %select_select_fusion.refs_0_), channel_id=1, source_target_pairs={{0,192},{64,0},{128,64},{192,128},{1,193},{65,1},{129,65},{193,129... | collective-permute-start | bytes 786440 | tf_op jit(solution)/shard_map/ppermute | solution.py:152
  67.8 18.2 %collective-permute-start.30 = (f32[64,1024]{1,0:T(8,128)S(1)}, f32[64,1024]{1,0:T(8,128)S(1)}, u32[]{:S(2)}, u32[]{:S(2)}) collective-permute-start(f32[64,1024]{1,0:T(8,128)S(1)} %select_select_fusion.refs_0_), channel_id=1, source_target_pairs={{0,64},{64,128},{128,192},{192,0},{1,65},{65,129},{129,193},{193,1... | collective-permute-start | bytes 786440 | tf_op jit(solution)/shard_map/ppermute | solution.py:152
  68.6 18.1 %collective-permute-start.28 = (f32[64,1024]{1,0:T(8,128)S(1)}, f32[64,1024]{1,0:T(8,128)S(1)}, u32[]{:S(2)}, u32[]{:S(2)}) collective-permute-start(f32[64,1024]{1,0:T(8,128)S(1)} %select_select_fusion.refs_0_), channel_id=1, source_target_pairs={{0,4},{4,0},{1,5},{5,1},{2,6},{6,2},{3,7},{7,3},{8,12},{12,8},{9,1... | collective-permute-start | bytes 786440 | tf_op jit(solution)/shard_map/ppermute | solution.py:152
  69.7 11.9 %collective-permute-start.24 = (f32[64,1024]{1,0:T(8,128)S(1)}, f32[64,1024]{1,0:T(8,128)}, u32[]{:S(2)}, u32[]{:S(2)}) collective-permute-start(f32[64,1024]{1,0:T(8,128)S(1)} %select_select_fusion.refs_0_), channel_id=1, source_target_pairs={{0,132},{4,128},{64,196},{68,192},{128,4},{132,0},{192,68},{196,64... | collective-permute-start | bytes 786440 | tf_op jit(solution)/shard_map/ppermute | solution.py:146
  73.6 25.3 %collective-permute-start.35 = (f32[64,1024]{1,0:T(8,128)S(1)}, f32[64,1024]{1,0:T(8,128)}, u32[]{:S(2)}, u32[]{:S(2)}) collective-permute-start(f32[64,1024]{1,0:T(8,128)S(1)} %select_select_fusion.2.refs_1_), channel_id=1, source_target_pairs={{0,192},{64,0},{128,64},{192,128},{1,193},{65,1},{129,65},{193,129... | collective-permute-start | bytes 786440 | tf_op jit(solution)/shard_map/ppermute | solution.py:152
  76.0 20.9 %collective-permute-start.25 = (f32[64,1024]{1,0:T(8,128)S(1)}, f32[64,1024]{1,0:T(8,128)}, u32[]{:S(2)}, u32[]{:S(2)}) collective-permute-start(f32[64,1024]{1,0:T(8,128)S(1)} %select_select_fusion.2.refs_1_), channel_id=1, source_target_pairs={{0,132},{4,128},{64,196},{68,192},{128,4},{132,0},{192,68},{196,64... | collective-permute-start | bytes 786440 | tf_op jit(solution)/shard_map/ppermute | solution.py:146
  81.6 13.9 %collective-permute-start.36 = (f32[64,1024]{1,0:T(8,128)}, f32[64,1024]{1,0:T(8,128)}, u32[]{:S(2)}, u32[]{:S(2)}) collective-permute-start(f32[64,1024]{1,0:T(8,128)} %collective-permute-done.24.refs_2_), channel_id=1, source_target_pairs={{0,192},{64,0},{128,64},{192,128},{1,193},{65,1},{129,65},{193,129... | collective-permute-start | bytes 786440 | tf_op jit(solution)/shard_map/ppermute | solution.py:152
  86.0 10.0 %collective-permute-start.32 = (f32[64,1024]{1,0:T(8,128)}, f32[64,1024]{1,0:T(8,128)}, u32[]{:S(2)}, u32[]{:S(2)}) collective-permute-start(f32[64,1024]{1,0:T(8,128)} %collective-permute-done.24.refs_2_), channel_id=1, source_target_pairs={{0,64},{64,128},{128,192},{192,0},{1,65},{65,129},{129,193},{193,1... | collective-permute-start | bytes 786440 | tf_op jit(solution)/shard_map/ppermute | solution.py:152
  86.6 12.2 %collective-permute-start.26 = (f32[64,1024]{1,0:T(8,128)}, f32[64,1024]{1,0:T(8,128)}, u32[]{:S(2)}, u32[]{:S(2)}) collective-permute-start(f32[64,1024]{1,0:T(8,128)} %collective-permute-done.24.refs_2_), channel_id=1, source_target_pairs={{0,4},{4,0},{1,5},{5,1},{2,6},{6,2},{3,7},{7,3},{8,12},{12,8},{9,1... | collective-permute-start | bytes 786440 | tf_op jit(solution)/shard_map/ppermute | solution.py:152
  95.5 10.3 %collective-permute-start.31 = (f32[64,1024]{1,0:T(8,128)S(1)}, f32[64,1024]{1,0:T(8,128)S(1)}, u32[]{:S(2)}, u32[]{:S(2)}) collective-permute-start(f32[64,1024]{1,0:T(8,128)S(1)} %select_select_fusion.2.refs_1_), channel_id=1, source_target_pairs={{0,64},{64,128},{128,192},{192,0},{1,65},{65,129},{129,193},{193,1... | collective-permute-start | bytes 786440 | tf_op jit(solution)/shard_map/ppermute | solution.py:152
  95.9 9.9 %collective-permute-start.29 = (f32[64,1024]{1,0:T(8,128)S(1)}, f32[64,1024]{1,0:T(8,128)S(1)}, u32[]{:S(2)}, u32[]{:S(2)}) collective-permute-start(f32[64,1024]{1,0:T(8,128)S(1)} %select_select_fusion.2.refs_1_), channel_id=1, source_target_pairs={{0,4},{4,0},{1,5},{5,1},{2,6},{6,2},{3,7},{7,3},{8,12},{12,8},{9,1... | collective-permute-start | bytes 786440 | tf_op jit(solution)/shard_map/ppermute | solution.py:152
  96.9 8.9 %collective-permute-start.37 = (f32[64,1024]{1,0:T(8,128)}, f32[64,1024]{1,0:T(8,128)S(1)}, u32[]{:S(2)}, u32[]{:S(2)}) collective-permute-start(f32[64,1024]{1,0:T(8,128)} %collective-permute-done.25.refs_3_), channel_id=1, source_target_pairs={{0,192},{64,0},{128,64},{192,128},{1,193},{65,1},{129,65},{193,129... | collective-permute-start | bytes 786440 | tf_op jit(solution)/shard_map/ppermute | solution.py:152
  98.8 10.0 %collective-permute-start.33 = (f32[64,1024]{1,0:T(8,128)}, f32[64,1024]{1,0:T(8,128)S(1)}, u32[]{:S(2)}, u32[]{:S(2)}) collective-permute-start(f32[64,1024]{1,0:T(8,128)} %collective-permute-done.25.refs_3_), channel_id=1, source_target_pairs={{0,64},{64,128},{128,192},{192,0},{1,65},{65,129},{129,193},{193,1... | collective-permute-start | bytes 786440 | tf_op jit(solution)/shard_map/ppermute | solution.py:152
  98.9 9.9 %collective-permute-start.27 = (f32[64,1024]{1,0:T(8,128)}, f32[64,1024]{1,0:T(8,128)S(1)}, u32[]{:S(2)}, u32[]{:S(2)}) collective-permute-start(f32[64,1024]{1,0:T(8,128)} %collective-permute-done.25.refs_3_), channel_id=1, source_target_pairs={{0,4},{4,0},{1,5},{5,1},{2,6},{6,2},{3,7},{7,3},{8,12},{12,8},{9,1... | collective-permute-start | bytes 786440 | tf_op jit(solution)/shard_map/ppermute | solution.py:152
  (3 other events, 13.9 us)

commit v7 on v6

--- a/solution.py
+++ b/solution.py
@@ -46,17 +46,19 @@
 
 def strips(spectra, panel):
     flat = spectra.reshape(2 * FREQ, ROWS, COLS)
-    is_first = lax.broadcasted_iota(jnp.int32, (1, 1, 2 * ROWS), 2) < ROWS
     start = (panel.astype(jnp.uint32) & 15) * ROWS
     block = jnp.concatenate(
         [lax.dynamic_slice_in_dim(flat, start, ROWS, 2), flat[:, :, COLS - ROWS :]], axis=2
     )
-    owner = panel >> 4
-    for axis, bit in (("c", owner & 1), ("yh", owner >> 1)):
-        other = lax.ppermute(block, axis, [(0, 1), (1, 0)])
-        keep = jnp.where(is_first, bit, 1) == lax.axis_index(axis)
-        block = jnp.where(keep, block, other)
-    return block.reshape(2, FREQ, ROWS, 2 * ROWS)
+    return block
+
+
+def swap(block, panel, axis):
+    is_first = lax.broadcasted_iota(jnp.int32, (1, 1, 2 * ROWS), 2) < ROWS
+    bit = panel >> 4 & 1 if axis == "c" else panel >> 5
+    other = lax.ppermute(block, axis, [(0, 1), (1, 0)])
+    keep = jnp.where(is_first, bit, 1) == lax.axis_index(axis)
+    return jnp.where(keep, block, other)
 
 
 def kernel(bins, x_ref, l_ref, coef_ref, *refs):
@@ -140,18 +142,24 @@
     return lax.all_to_all(rows, ("x", "yl"), 0, 0, axis_index_groups=[members], tiled=True)
 
 
-def exchange(own):
-    plane = [(i, j) for i in range(4) for j in range(2)]
-    across = [(i * 2 + j, ((i + 2) % 4) * 2 + 1 - j) for i, j in plane]
-    partner = lax.ppermute(own, ("x", "yl"), across)
-    blocks = [own, partner]
-    turn = [(i, (i + 1) % 4) for i in range(4)]
-    back = [(i, (i - 1) % 4) for i in range(4)]
-    for axis, pairs in (("yl", [(0, 1), (1, 0)]), ("x", turn), ("x", back)):
-        for v in (own, partner):
-            blocks.append(lax.ppermute(v, axis, pairs))
-    blocks[2], blocks[3] = blocks[3], blocks[2]
-    return blocks
+def exchange(panels):
+    def send(v, way):
+        axis, pairs = {
+            "on": ("x", [(i, (i + 1) % 4) for i in range(4)]),
+            "back": ("x", [(i, (i - 1) % 4) for i in range(4)]),
+            "y": ("yl", [(0, 1), (1, 0)]),
+        }[way]
+        return lax.ppermute(v, axis, pairs)
+
+    near = [(send(own, "on"), send(own, "back"), send(own, "y")) for own in panels]
+    mid = [(send(a, "on"), send(c, "back"), send(a, "y")) for a, _, c in near]
+    far = [
+        send(d, "y") if i == 0 else send(e, "back") for i, (d, e, _) in enumerate(mid)
+    ]
+    return [
+        [own, g, d, c, a, e, b, f]
+        for own, (a, b, c), (d, e, f), g in zip(panels, near, mid, far)
+    ]
 
 
 def shards(spectra, panels, filters, offsets):
@@ -160,17 +168,18 @@
     other = jnp.where(other_first, panels[0], panels[1])
     ox, oz, oy = place_of(other)
     lx, lz, ly = place_of(LAST)
-    strip = strips(spectra, other)
+    strip = swap(strips(spectra, other), other, "c")
     arrived = scatter(spectra.reshape(2 * FREQ, ROWS, COLS))
+    arrived, strip = lax.optimization_barrier((arrived, strip))
     spot = (oy * 4 + ((ox + 2 * oy) & 3)).astype(jnp.uint32)
     mine = lax.dynamic_index_in_dim(arrived, spot, 0, keepdims=False)
     last = arrived[ly * 4 + (lx + 2 * ly) % 4]
     last = land(last, leap(last, lz), lz, z)
     branches = [lambda v, r=r: leap(v, r) for r in range(8)]
     mine = land(mine, lax.switch(oz, branches, mine), oz, z)
-    last, strip = lax.optimization_barrier((steps(last, lz, z), strip))
-    last = exchange(last)
-    mine = exchange(steps(mine, oz, z))
+    mine, strip = lax.optimization_barrier((mine, strip))
+    strip = swap(strip, other, "yh").reshape(2, FREQ, ROWS, 2 * ROWS)
+    last, mine = exchange([steps(last, lz, z), steps(mine, oz, z)])
     blocks = [v for pair in zip(mine, last) for v in pair]
     bins = (x + 2 * yl + jnp.array([0, 2, 3, 1], jnp.int32)) & 3
     left, coefs = tables(filters, offsets, strip, bins, yl)

time: 116 us -> 106 us (0.914); the launches traced: 115 us -> 107 us
  waiting for transfers between devices: 57.6 us -> 45.5 us
  starting transfers between devices: 37.7 us -> 45.3 us
  other arithmetic: 7.47 us -> 5.59 us
  local copies, waits for them, and re-layouts: 3.41 us -> 1.99 us
    ppermute x2, starting transfers between devices: 1.46 us -> 9.78 us  [steps(): before = lax.ppermute(held, 'z', [(k, (k - 1) % 8) for k in range(8)])]
    ppermute x2, starting transfers between devices: 10 us -> 2.05 us  [leap(): down = lax.ppermute(v, 'z', [(root, (root - 3) % 8)])]
    ppermute x2, starting transfers between devices: 2.74 us -> 10.2 us  [steps(): after = lax.ppermute(held, 'z', [(k, (k + 1) % 8) for k in range(8)])]
    ppermute x16, waiting for transfers between devices: 22.9 us -> 17.5 us  [the longest x14 16.3 us: send(): return lax.ppermute(v, axis, pairs)]
    ppermute x2, waiting for transfers between devices: 3.95 us -> 0.01 us  [leap(): up = lax.ppermute(v, 'z', [(root, (root + 3) % 8)])]
    all_to_all x1, waiting for transfers between devices: 24 us -> 22.1 us  [scatter(): lax.all_to_all(rows, ('x', 'yl'), 0, 0, axis_index_groups=[members], tile...]
    ppermute x2, waiting for transfers between devices: 1.49 us -> 0.01 us  [leap(): down = lax.ppermute(v, 'z', [(root, (root - 3) % 8)])]
    ppermute x2, waiting for transfers between devices: 4.45 us -> 5.91 us  [steps(): before = lax.ppermute(held, 'z', [(k, (k - 1) % 8) for k in range(8)])]
  transfers between devices with their start and end apart: 25 -> 25, of which waited for: 12 -> 10; matrix products, arithmetic and copies ran while one was open for 9% -> 6% of each run, Pallas kernels for 0% -> 0%
where the time goes in v7:
time: 106 us; the launch traced here: 107 us
  waiting for transfers between devices  45.5 us (43%)
  starting transfers between devices  45.3 us (43%)
  Pallas kernels  6.19 us (6%)
  other arithmetic  5.59 us (5%)
  between operations  2.19 us (2%)
  local copies, waits for them, and re-layouts  1.99 us (2%)
    all_to_all x1, waiting for transfers between devices, scatter(): lax.all_to_all(rows, ('x', 'yl'), 0, 0, axis_index_groups=[members], tile...  22.1 us
    ppermute x14, waiting for transfers between devices, send(): return lax.ppermute(v, axis, pairs)  16.3 us
    ppermute x14, starting transfers between devices, send(): return lax.ppermute(v, axis, pairs)  15.2 us
    ppermute x2, starting transfers between devices, steps(): after = lax.ppermute(held, 'z', [(k, (k + 1) % 8) for k in range(8)])  10.2 us
    ppermute x2, starting transfers between devices, steps(): before = lax.ppermute(held, 'z', [(k, (k - 1) % 8) for k in range(8)])  9.78 us
    pallas_call x1, Pallas kernels, synthesise(): pl.pallas_call(kernel, grid_spec=grid_spec, out_shape=jax.ShapeDtypeStruc...  6.19 us
    ppermute x2, waiting for transfers between devices, steps(): before = lax.ppermute(held, 'z', [(k, (k - 1) % 8) for k in range(8)])  5.91 us
    all_to_all x1, starting transfers between devices, scatter(): lax.all_to_all(rows, ('x', 'yl'), 0, 0, axis_index_groups=[members], tile...  5.29 us
  transfers between devices with their start and end apart: 25, of which 10 were waited for; matrix products, arithmetic and copies ran while one was open for 6% of the time, Pallas kernels for 0%

profile of v7, /device:TPU:16, one launch (start us, length us, event | category | flops | bytes accessed | tf_op | source)
XLA Modules:
  0.0 107.2 jit_solution(18233591970096466376)
XLA Ops:
  0.0 5.3 %all-to-all-start = ((f32[8,64,1024]{2,1,0:T(8,128)}), f32[8,64,1024]{2,1,0:T(8,128)}, u32[]{:S(2)}, u32[]{:S(2)}) async-start(f32[8,64,1024]{2,1,0:T(8,128)} %bitcast.14), calls=%async_computation | async-start | bytes 4194304 | tf_op jit(solution)/shard_map/all_to_all | solution.py:142
  8.6 1.2 %collective-permute-done.16 = f32[8,64,128]{2,1,0:T(8,128)S(1)} collective-permute-done((f32[8,64,128]{2,1,0:T(8,128)S(1)}, f32[8,64,128]{2,1,0:T(8,128)S(1)}, u32[]{:S(2)}, u32[]{:S(2)}) %collective-permute-start.16) | collective-permute-done | bytes 262176 | tf_op jit(solution)/shard_map/ppermute | solution.py:59
  9.8 0.8 broadcast_select_fusion
  10.7 22.1 %all-to-all-done = f32[8,64,1024]{2,1,0:T(8,128)} async-done(((f32[8,64,1024]{2,1,0:T(8,128)}), f32[8,64,1024]{2,1,0:T(8,128)}, u32[]{:S(2)}, u32[]{:S(2)}) %all-to-all-start) | async-done | bytes 2097184 | tf_op jit(solution)/shard_map/all_to_all | solution.py:142
  32.8 1.1 slice_bitcast_fusion
  35.2 2.8 %conditional.1 = (f32[64,1024]{1,0:T(8,128)}, f32[64,1024]{1,0:T(8,128)}) conditional(s32[]{:T(128)} %clamp.3, f32[64,1024]{1,0:T(8,128)S(1)} %get-tuple-element.28, f32[64,1024]{1,0:T(8,128)S(1)} %get-tuple-element.28, f32[64,1024]{1,0:T(8,128)S(1)} %get-tuple-element.28, ...), branch_computations={%region_0.1_spmd, %region_1.2_spmd, %region_2.3_spmd, %region_3.4_... | conditional | bytes 2097248 | solution.py:179
  35.3 1.4 %collective-permute-start.3 = (f32[64,1024]{1,0:T(8,128)S(1)}, f32[64,1024]{1,0:T(8,128)}, u32[]{:S(2)}, u32[]{:S(2)}) collective-permute-start(f32[64,1024]{1,0:T(8,128)S(1)} %param.1), channel_id=1, source_target_pairs={{8,48},{9,49},{10,50},{11,51},{12,52},{13,53},{14,54},{15,55},{72,... | collective-permute-start | bytes 786440 | tf_op jit(solution)/shard_map/cond/branch_1_fun/ppermute | solution.py:29
  36.6 1.4 %collective-permute-start.2 = (f32[64,1024]{1,0:T(8,128)S(1)}, f32[64,1024]{1,0:T(8,128)}, u32[]{:S(2)}, u32[]{:S(2)}) collective-permute-start(f32[64,1024]{1,0:T(8,128)S(1)} %param.1), channel_id=1, source_target_pairs={{8,32},{9,33},{10,34},{11,35},{12,36},{13,37},{14,38},{15,39},{72,... | collective-permute-start | bytes 786440 | tf_op jit(solution)/shard_map/cond/branch_1_fun/ppermute | solution.py:28
  38.0 1.0 select_select_fusion.3
  39.0 9.7 %collective-permute-start.19 = (f32[64,1024]{1,0:T(8,128)S(1)}, f32[64,1024]{1,0:T(8,128)S(1)}, u32[]{:S(2)}, u32[]{:S(2)}) collective-permute-start(f32[64,1024]{1,0:T(8,128)S(1)} %select_select_fusion.3), channel_id=1, source_target_pairs={{0,56},{8,0},{16,8},{24,16},{32,24},{40,32},{48,40},{56,48},{1,57}... | collective-permute-start | bytes 786440 | tf_op jit(solution)/shard_map/ppermute | solution.py:40
  48.7 8.2 %collective-permute-start.18 = (f32[64,1024]{1,0:T(8,128)S(1)}, f32[64,1024]{1,0:T(8,128)}, u32[]{:S(2)}, u32[]{:S(2)}) collective-permute-start(f32[64,1024]{1,0:T(8,128)S(1)} %select_select_fusion.3), channel_id=1, source_target_pairs={{0,8},{8,16},{16,24},{24,32},{32,40},{40,48},{48,56},{56,0},{1,9},... | collective-permute-start | bytes 786440 | tf_op jit(solution)/shard_map/ppermute | solution.py:39
  56.9 1.0 select_select_fusion.1
  58.0 2.0 %collective-permute-start.22 = (f32[64,1024]{1,0:T(8,128)S(1)}, f32[64,1024]{1,0:T(8,128)}, u32[]{:S(2)}, u32[]{:S(2)}) collective-permute-start(f32[64,1024]{1,0:T(8,128)S(1)} %select_select_fusion.1), channel_id=1, source_target_pairs={{0,8},{8,16},{16,24},{24,32},{32,40},{40,48},{48,56},{56,0},{1,9},... | collective-permute-start | bytes 786440 | tf_op jit(solution)/shard_map/ppermute | solution.py:39
  60.9 3.0 %collective-permute-done.19 = f32[64,1024]{1,0:T(8,128)S(1)} collective-permute-done((f32[64,1024]{1,0:T(8,128)S(1)}, f32[64,1024]{1,0:T(8,128)S(1)}, u32[]{:S(2)}, u32[]{:S(2)}) %collective-permute-start.19) | collective-permute-done | bytes 262176 | tf_op jit(solution)/shard_map/ppermute | solution.py:40
  64.0 1.3 %collective-permute-start.34 = (f32[64,1024]{1,0:T(8,128)S(1)}, f32[64,1024]{1,0:T(8,128)S(1)}, u32[]{:S(2)}, u32[]{:S(2)}) collective-permute-start(f32[64,1024]{1,0:T(8,128)S(1)} %select_select_fusion.2.refs_0_), channel_id=1, source_target_pairs={{0,192},{64,0},{128,64},{192,128},{1,193},{65,1},{129,65},{193,129... | collective-permute-start | bytes 786440 | tf_op jit(solution)/shard_map/ppermute | solution.py:152
  66.1 2.9 %collective-permute-done.23 = f32[64,1024]{1,0:T(8,128)} collective-permute-done((f32[64,1024]{1,0:T(8,128)S(1)}, f32[64,1024]{1,0:T(8,128)}, u32[]{:S(2)}, u32[]{:S(2)}) %collective-permute-start.23) | collective-permute-done | bytes 262176 | tf_op jit(solution)/shard_map/ppermute | solution.py:40
  69.6 1.1 %select_select_fusion.refs_1_ = f32[64,1024]{1,0:T(8,128)S(1)} fusion(f32[64,1024]{1,0:T(8,128)} %collective-permute-done.22, f32[64,1024]{1,0:T(8,128)} %collective-permute-done.23, f32[64,1024]{1,0:T(8,128)} %copy-done.2, pred[]{:T(512)S(6)} %or.23, pred[]{:T(512)S(6)} %or.22), kind=kLoop, calls=%fused_computation.2 | loop fusion | flops 131072 | bytes 1048578 | tf_op jit(solution)/shard_map/jit(_where)/select_n | solution.py:44
  71.4 2.8 %collective-permute-start.35 = (f32[64,1024]{1,0:T(8,128)S(1)}, f32[64,1024]{1,0:T(8,128)}, u32[]{:S(2)}, u32[]{:S(2)}) collective-permute-start(f32[64,1024]{1,0:T(8,128)S(1)} %select_select_fusion.refs_1_), channel_id=1, source_target_pairs={{0,192},{64,0},{128,64},{192,128},{1,193},{65,1},{129,65},{193,129... | collective-permute-start | bytes 786440 | tf_op jit(solution)/shard_map/ppermute | solution.py:152
  74.2 1.5 %collective-permute-start.32 = (f32[64,1024]{1,0:T(8,128)S(1)}, f32[64,1024]{1,0:T(8,128)}, u32[]{:S(2)}, u32[]{:S(2)}) collective-permute-start(f32[64,1024]{1,0:T(8,128)S(1)} %select_select_fusion.refs_1_), channel_id=1, source_target_pairs={{0,4},{4,0},{1,5},{5,1},{2,6},{6,2},{3,7},{7,3},{8,12},{12,8},{9,1... | collective-permute-start | bytes 786440 | tf_op jit(solution)/shard_map/ppermute | solution.py:152
  76.3 1.7 %collective-permute-done.24.refs_6_ = f32[64,1024]{1,0:T(8,128)S(1)} collective-permute-done((f32[64,1024]{1,0:T(8,128)S(1)}, f32[64,1024]{1,0:T(8,128)S(1)}, u32[]{:S(2)}, u32[]{:S(2)}) %collective-permute-start.24) | collective-permute-done | bytes 262176 | tf_op jit(solution)/shard_map/ppermute | solution.py:152
  77.9 1.6 %collective-permute-start.25 = (f32[64,1024]{1,0:T(8,128)S(1)}, f32[64,1024]{1,0:T(8,128)}, u32[]{:S(2)}, u32[]{:S(2)}) collective-permute-start(f32[64,1024]{1,0:T(8,128)S(1)} %collective-permute-done.24.refs_6_), channel_id=1, source_target_pairs={{0,192},{64,0},{128,64},{192,128},{1,193},{65,1},{129,65},{193,129... | collective-permute-start | bytes 786440 | tf_op jit(solution)/shard_map/ppermute | solution.py:152
  80.1 1.1 broadcast_select_fusion.1
  81.1 0.9 collective-permute-start.31
  82.0 1.6 %collective-permute-done.32.refs_7_ = f32[64,1024]{1,0:T(8,128)} collective-permute-done((f32[64,1024]{1,0:T(8,128)S(1)}, f32[64,1024]{1,0:T(8,128)}, u32[]{:S(2)}, u32[]{:S(2)}) %collective-permute-start.32) | collective-permute-done | bytes 262176 | tf_op jit(solution)/shard_map/ppermute | solution.py:152
  83.6 1.4 %collective-permute-start.37 = (f32[64,1024]{1,0:T(8,128)}, f32[64,1024]{1,0:T(8,128)S(1)}, u32[]{:S(2)}, u32[]{:S(2)}) collective-permute-start(f32[64,1024]{1,0:T(8,128)} %collective-permute-done.27.refs_9_), channel_id=1, source_target_pairs={{0,4},{4,0},{1,5},{5,1},{2,6},{6,2},{3,7},{7,3},{8,12},{12,8},{9,1... | collective-permute-start | bytes 786440 | tf_op jit(solution)/shard_map/ppermute | solution.py:152
  85.1 4.2 %collective-permute-done.36.refs_14_ = f32[64,1024]{1,0:T(8,128)} collective-permute-done((f32[64,1024]{1,0:T(8,128)S(1)}, f32[64,1024]{1,0:T(8,128)}, u32[]{:S(2)}, u32[]{:S(2)}) %collective-permute-start.36) | collective-permute-done | bytes 262176 | tf_op jit(solution)/shard_map/ppermute | solution.py:152
  89.3 1.6 %collective-permute-start.33 = (f32[64,1024]{1,0:T(8,128)}, f32[64,1024]{1,0:T(8,128)S(1)}, u32[]{:S(2)}, u32[]{:S(2)}) collective-permute-start(f32[64,1024]{1,0:T(8,128)} %collective-permute-done.32.refs_7_), channel_id=1, source_target_pairs={{0,192},{64,0},{128,64},{192,128},{1,193},{65,1},{129,65},{193,129... | collective-permute-start | bytes 786440 | tf_op jit(solution)/shard_map/ppermute | solution.py:152
  91.2 0.9 collective-permute-start.29
  92.2 0.8 collective-permute-done.31.refs_4_
  93.0 5.2 %collective-permute-done.33.refs_11_ = f32[64,1024]{1,0:T(8,128)S(1)} collective-permute-done((f32[64,1024]{1,0:T(8,128)}, f32[64,1024]{1,0:T(8,128)S(1)}, u32[]{:S(2)}, u32[]{:S(2)}) %collective-permute-start.33) | collective-permute-done | bytes 262176 | tf_op jit(solution)/shard_map/ppermute | solution.py:152
  98.2 2.8 %collective-permute-done.26.refs_2_ = f32[64,1024]{1,0:T(8,128)S(1)} collective-permute-done((f32[64,1024]{1,0:T(8,128)}, f32[64,1024]{1,0:T(8,128)S(1)}, u32[]{:S(2)}, u32[]{:S(2)}) %collective-permute-start.26) | collective-permute-done | bytes 262176 | tf_op jit(solution)/shard_map/ppermute | solution.py:152
  101.0 6.2 %shard_map.73 = bf16[8,64,1024]{2,1,0:T(8,128)(2,1)} custom-call(s32[4]{0:T(128)S(1)} %get-tuple-element.35.bins, f32[2,4,64,1024]{3,2,1,0:T(8,128)S(1)} %copy-done.1, f32[4,128,256]{2,1,0:T(8,128)S(1)} %maximum_select_fusion.l_ref, f32[64,64]{1,0:T(8,128)S(1)} %copy.10.coef_ref, f32[64,1024]{1,0:T(8,128)S(1)} %select_select_fusion.2.refs_0_, ...), custom_call_target="tpu_custom_call" | custom-call | flops 805306368 | bytes 8388608 | tf_op jit(solution)/shard_map/pallas_call | solution.py:104
  (58 shorter events, 7.3 us)
Async XLA Ops:
  0.0 8.4 %copy-start = (f32[64,64]{1,0:T(8,128)S(1)}, f32[64,64]{1,0:T(8,128)}, u32[]{:S(2)}) copy-start(f32[64,64]{1,0:T(8,128)} %param.17) | copy-start | bytes 49156
  0.0 7.8 %copy-start.1 = (f32[2,4,64,1024]{3,2,1,0:T(8,128)S(1)}, f32[2,4,64,1024]{3,2,1,0:T(8,128)}, u32[]{:S(2)}) copy-start(f32[2,4,64,1024]{3,2,1,0:T(8,128)} %x_ref.1) | copy-start | bytes 6291460
  0.0 8.3 %copy-start.6 = (s32[64]{0:T(128)S(1)}, s32[64]{0:T(128)}, u32[]{:S(2)}) copy-start(s32[64]{0:T(128)} %param.18) | copy-start | bytes 772
  0.0 8.3 %copy-start.4 = (f32[64,4]{1,0:T(8,128)S(1)}, f32[64,4]{1,0:T(8,128)}, u32[]{:S(2)}) copy-start(f32[64,4]{1,0:T(8,128)} %constant.61.clone) | copy-start | bytes 3076
  0.0 32.7 %all-to-all-start = ((f32[8,64,1024]{2,1,0:T(8,128)}), f32[8,64,1024]{2,1,0:T(8,128)}, u32[]{:S(2)}, u32[]{:S(2)}) async-start(f32[8,64,1024]{2,1,0:T(8,128)} %bitcast.14), calls=%async_computation | async-start | bytes 4194304 | tf_op jit(solution)/shard_map/all_to_all | solution.py:142
  5.3 29.9 %copy-start.7 = (s32[4]{0:T(128)S(1)}, s32[4]{0:T(128)}, u32[]{:S(2)}) copy-start(s32[4]{0:T(128)} %constant.60.clone) | copy-start | bytes 52
  8.2 1.6 %collective-permute-start.16 = (f32[8,64,128]{2,1,0:T(8,128)S(1)}, f32[8,64,128]{2,1,0:T(8,128)S(1)}, u32[]{:S(2)}, u32[]{:S(2)}) collective-permute-start(f32[8,64,128]{2,1,0:T(8,128)S(1)} %pad_maximum_fusion), channel_id=1, source_target_pairs={{0,1},{1,0},{2,3},{3,2},{4,5},{5,4},{6,7},{7,6},{8,9},{9,8},{10,11... | collective-permute-start | bytes 786440 | tf_op jit(solution)/shard_map/ppermute | solution.py:59
  33.8 23.1 %collective-permute-start.21 = (f32[64,1024]{1,0:T(8,128)S(1)}, f32[64,1024]{1,0:T(8,128)S(1)}, u32[]{:S(2)}, u32[]{:S(2)}) collective-permute-start(f32[64,1024]{1,0:T(8,128)S(1)} %get-tuple-element.27), channel_id=1, source_target_pairs={{56,32},{57,33},{58,34},{59,35},{60,36},{61,37},{62,38},{63,39},{1... | collective-permute-start | bytes 786440 | tf_op jit(solution)/shard_map/ppermute | solution.py:29
  34.5 22.4 %collective-permute-start.20 = (f32[64,1024]{1,0:T(8,128)S(1)}, f32[64,1024]{1,0:T(8,128)S(1)}, u32[]{:S(2)}, u32[]{:S(2)}) collective-permute-start(f32[64,1024]{1,0:T(8,128)S(1)} %get-tuple-element.27), channel_id=1, source_target_pairs={{56,16},{57,17},{58,18},{59,19},{60,20},{61,21},{62,22},{63,23},{1... | collective-permute-start | bytes 786440 | tf_op jit(solution)/shard_map/ppermute | solution.py:28
  35.3 2.8 %collective-permute-start.3 = (f32[64,1024]{1,0:T(8,128)S(1)}, f32[64,1024]{1,0:T(8,128)}, u32[]{:S(2)}, u32[]{:S(2)}) collective-permute-start(f32[64,1024]{1,0:T(8,128)S(1)} %param.1), channel_id=1, source_target_pairs={{8,48},{9,49},{10,50},{11,51},{12,52},{13,53},{14,54},{15,55},{72,... | collective-permute-start | bytes 786440 | tf_op jit(solution)/shard_map/cond/branch_1_fun/ppermute | solution.py:29
  36.6 1.4 %collective-permute-start.2 = (f32[64,1024]{1,0:T(8,128)S(1)}, f32[64,1024]{1,0:T(8,128)}, u32[]{:S(2)}, u32[]{:S(2)}) collective-permute-start(f32[64,1024]{1,0:T(8,128)S(1)} %param.1), channel_id=1, source_target_pairs={{8,32},{9,33},{10,34},{11,35},{12,36},{13,37},{14,38},{15,39},{72,... | collective-permute-start | bytes 786440 | tf_op jit(solution)/shard_map/cond/branch_1_fun/ppermute | solution.py:28
  38.0 33.2 %copy-start.3 = (f32[64,4]{1,0:T(8,128)S(1)}, f32[64,4]{1,0:T(8,128)}, u32[]{:S(2)}) copy-start(f32[64,4]{1,0:T(8,128)} %constant.62.clone) | copy-start | bytes 3076
  39.0 24.9 %collective-permute-start.19 = (f32[64,1024]{1,0:T(8,128)S(1)}, f32[64,1024]{1,0:T(8,128)S(1)}, u32[]{:S(2)}, u32[]{:S(2)}) collective-permute-start(f32[64,1024]{1,0:T(8,128)S(1)} %select_select_fusion.3), channel_id=1, source_target_pairs={{0,56},{8,0},{16,8},{24,16},{32,24},{40,32},{48,40},{56,48},{1,57}... | collective-permute-start | bytes 786440 | tf_op jit(solution)/shard_map/ppermute | solution.py:40
  48.7 15.2 %collective-permute-start.18 = (f32[64,1024]{1,0:T(8,128)S(1)}, f32[64,1024]{1,0:T(8,128)}, u32[]{:S(2)}, u32[]{:S(2)}) collective-permute-start(f32[64,1024]{1,0:T(8,128)S(1)} %select_select_fusion.3), channel_id=1, source_target_pairs={{0,8},{8,16},{16,24},{24,32},{32,40},{40,48},{48,56},{56,0},{1,9},... | collective-permute-start | bytes 786440 | tf_op jit(solution)/shard_map/ppermute | solution.py:39
  57.9 11.7 %copy-start.2 = (f32[64,1024]{1,0:T(8,128)}, f32[64,1024]{1,0:T(8,128)S(1)}, u32[]{:S(2)}) copy-start(f32[64,1024]{1,0:T(8,128)S(1)} %select_select_fusion.1) | copy-start | bytes 786436
  57.9 11.1 %collective-permute-start.23 = (f32[64,1024]{1,0:T(8,128)S(1)}, f32[64,1024]{1,0:T(8,128)}, u32[]{:S(2)}, u32[]{:S(2)}) collective-permute-start(f32[64,1024]{1,0:T(8,128)S(1)} %select_select_fusion.1), channel_id=1, source_target_pairs={{0,56},{8,0},{16,8},{24,16},{32,24},{40,32},{48,40},{56,48},{1,57}... | collective-permute-start | bytes 786440 | tf_op jit(solution)/shard_map/ppermute | solution.py:40
  58.0 11.6 %collective-permute-start.22 = (f32[64,1024]{1,0:T(8,128)S(1)}, f32[64,1024]{1,0:T(8,128)}, u32[]{:S(2)}, u32[]{:S(2)}) collective-permute-start(f32[64,1024]{1,0:T(8,128)S(1)} %select_select_fusion.1), channel_id=1, source_target_pairs={{0,8},{8,16},{16,24},{24,32},{32,40},{40,48},{48,56},{56,0},{1,9},... | collective-permute-start | bytes 786440 | tf_op jit(solution)/shard_map/ppermute | solution.py:39
  60.2 11.2 %collective-permute-start.17 = (f32[8,64,128]{2,1,0:T(8,128)}, f32[8,64,128]{2,1,0:T(8,128)}, u32[]{:S(2)}, u32[]{:S(2)}) collective-permute-start(f32[8,64,128]{2,1,0:T(8,128)} %broadcast_select_fusion), channel_id=1, source_target_pairs={{0,2},{2,0},{1,3},{3,1},{4,6},{6,4},{5,7},{7,5},{8,10},{10,8},{9,1... | collective-permute-start | bytes 786440 | tf_op jit(solution)/shard_map/ppermute | solution.py:59
  64.0 10.2 %collective-permute-start.34 = (f32[64,1024]{1,0:T(8,128)S(1)}, f32[64,1024]{1,0:T(8,128)S(1)}, u32[]{:S(2)}, u32[]{:S(2)}) collective-permute-start(f32[64,1024]{1,0:T(8,128)S(1)} %select_select_fusion.2.refs_0_), channel_id=1, source_target_pairs={{0,192},{64,0},{128,64},{192,128},{1,193},{65,1},{129,65},{193,129... | collective-permute-start | bytes 786440 | tf_op jit(solution)/shard_map/ppermute | solution.py:152
  65.3 10.4 %collective-permute-start.30 = (f32[64,1024]{1,0:T(8,128)S(1)}, f32[64,1024]{1,0:T(8,128)S(1)}, u32[]{:S(2)}, u32[]{:S(2)}) collective-permute-start(f32[64,1024]{1,0:T(8,128)S(1)} %select_select_fusion.2.refs_0_), channel_id=1, source_target_pairs={{0,64},{64,128},{128,192},{192,0},{1,65},{65,129},{129,193},{193,1... | collective-permute-start | bytes 786440 | tf_op jit(solution)/shard_map/ppermute | solution.py:152
  69.0 8.9 %collective-permute-start.24 = (f32[64,1024]{1,0:T(8,128)S(1)}, f32[64,1024]{1,0:T(8,128)S(1)}, u32[]{:S(2)}, u32[]{:S(2)}) collective-permute-start(f32[64,1024]{1,0:T(8,128)S(1)} %select_select_fusion.2.refs_0_), channel_id=1, source_target_pairs={{0,4},{4,0},{1,5},{5,1},{2,6},{6,2},{3,7},{7,3},{8,12},{12,8},{9,1... | collective-permute-start | bytes 786440 | tf_op jit(solution)/shard_map/ppermute | solution.py:152
  70.7 8.9 %collective-permute-start.27 = (f32[64,1024]{1,0:T(8,128)S(1)}, f32[64,1024]{1,0:T(8,128)}, u32[]{:S(2)}, u32[]{:S(2)}) collective-permute-start(f32[64,1024]{1,0:T(8,128)S(1)} %select_select_fusion.refs_1_), channel_id=1, source_target_pairs={{0,64},{64,128},{128,192},{192,0},{1,65},{65,129},{129,193},{193,1... | collective-permute-start | bytes 786440 | tf_op jit(solution)/shard_map/ppermute | solution.py:152
  71.4 9.7 %collective-permute-start.35 = (f32[64,1024]{1,0:T(8,128)S(1)}, f32[64,1024]{1,0:T(8,128)}, u32[]{:S(2)}, u32[]{:S(2)}) collective-permute-start(f32[64,1024]{1,0:T(8,128)S(1)} %select_select_fusion.refs_1_), channel_id=1, source_target_pairs={{0,192},{64,0},{128,64},{192,128},{1,193},{65,1},{129,65},{193,129... | collective-permute-start | bytes 786440 | tf_op jit(solution)/shard_map/ppermute | solution.py:152
  74.2 9.4 %collective-permute-start.32 = (f32[64,1024]{1,0:T(8,128)S(1)}, f32[64,1024]{1,0:T(8,128)}, u32[]{:S(2)}, u32[]{:S(2)}) collective-permute-start(f32[64,1024]{1,0:T(8,128)S(1)} %select_select_fusion.refs_1_), channel_id=1, source_target_pairs={{0,4},{4,0},{1,5},{5,1},{2,6},{6,2},{3,7},{7,3},{8,12},{12,8},{9,1... | collective-permute-start | bytes 786440 | tf_op jit(solution)/shard_map/ppermute | solution.py:152
  75.7 13.6 %collective-permute-start.36 = (f32[64,1024]{1,0:T(8,128)S(1)}, f32[64,1024]{1,0:T(8,128)}, u32[]{:S(2)}, u32[]{:S(2)}) collective-permute-start(f32[64,1024]{1,0:T(8,128)S(1)} %collective-permute-done.30.refs_8_), channel_id=1, source_target_pairs={{0,4},{4,0},{1,5},{5,1},{2,6},{6,2},{3,7},{7,3},{8,12},{12,8},{9,1... | collective-permute-start | bytes 786440 | tf_op jit(solution)/shard_map/ppermute | solution.py:152
  77.9 13.0 %collective-permute-start.25 = (f32[64,1024]{1,0:T(8,128)S(1)}, f32[64,1024]{1,0:T(8,128)}, u32[]{:S(2)}, u32[]{:S(2)}) collective-permute-start(f32[64,1024]{1,0:T(8,128)S(1)} %collective-permute-done.24.refs_6_), channel_id=1, source_target_pairs={{0,192},{64,0},{128,64},{192,128},{1,193},{65,1},{129,65},{193,129... | collective-permute-start | bytes 786440 | tf_op jit(solution)/shard_map/ppermute | solution.py:152
  79.5 11.6 %collective-permute-start.28 = (f32[64,1024]{1,0:T(8,128)}, f32[64,1024]{1,0:T(8,128)}, u32[]{:S(2)}, u32[]{:S(2)}) collective-permute-start(f32[64,1024]{1,0:T(8,128)} %collective-permute-done.27.refs_9_), channel_id=1, source_target_pairs={{0,64},{64,128},{128,192},{192,0},{1,65},{65,129},{129,193},{193,1... | collective-permute-start | bytes 786440 | tf_op jit(solution)/shard_map/ppermute | solution.py:152
  81.1 11.9 %collective-permute-start.31 = (f32[64,1024]{1,0:T(8,128)S(1)}, f32[64,1024]{1,0:T(8,128)S(1)}, u32[]{:S(2)}, u32[]{:S(2)}) collective-permute-start(f32[64,1024]{1,0:T(8,128)S(1)} %collective-permute-done.30.refs_8_), channel_id=1, source_target_pairs={{0,64},{64,128},{128,192},{192,0},{1,65},{65,129},{129,193},{193,1... | collective-permute-start | bytes 786440 | tf_op jit(solution)/shard_map/ppermute | solution.py:152
  83.6 14.6 %collective-permute-start.37 = (f32[64,1024]{1,0:T(8,128)}, f32[64,1024]{1,0:T(8,128)S(1)}, u32[]{:S(2)}, u32[]{:S(2)}) collective-permute-start(f32[64,1024]{1,0:T(8,128)} %collective-permute-done.27.refs_9_), channel_id=1, source_target_pairs={{0,4},{4,0},{1,5},{5,1},{2,6},{6,2},{3,7},{7,3},{8,12},{12,8},{9,1... | collective-permute-start | bytes 786440 | tf_op jit(solution)/shard_map/ppermute | solution.py:152
  89.3 9.0 %collective-permute-start.33 = (f32[64,1024]{1,0:T(8,128)}, f32[64,1024]{1,0:T(8,128)S(1)}, u32[]{:S(2)}, u32[]{:S(2)}) collective-permute-start(f32[64,1024]{1,0:T(8,128)} %collective-permute-done.32.refs_7_), channel_id=1, source_target_pairs={{0,192},{64,0},{128,64},{192,128},{1,193},{65,1},{129,65},{193,129... | collective-permute-start | bytes 786440 | tf_op jit(solution)/shard_map/ppermute | solution.py:152
  90.9 10.2 %collective-permute-start.26 = (f32[64,1024]{1,0:T(8,128)}, f32[64,1024]{1,0:T(8,128)S(1)}, u32[]{:S(2)}, u32[]{:S(2)}) collective-permute-start(f32[64,1024]{1,0:T(8,128)} %collective-permute-done.25.refs_10_), channel_id=1, source_target_pairs={{0,192},{64,0},{128,64},{192,128},{1,193},{65,1},{129,65},{193,129... | collective-permute-start | bytes 786440 | tf_op jit(solution)/shard_map/ppermute | solution.py:152
  91.2 9.9 %collective-permute-start.29 = (f32[64,1024]{1,0:T(8,128)}, f32[64,1024]{1,0:T(8,128)S(1)}, u32[]{:S(2)}, u32[]{:S(2)}) collective-permute-start(f32[64,1024]{1,0:T(8,128)} %collective-permute-done.28.refs_5_), channel_id=1, source_target_pairs={{0,4},{4,0},{1,5},{5,1},{2,6},{6,2},{3,7},{7,3},{8,12},{12,8},{9,1... | collective-permute-start | bytes 786440 | tf_op jit(solution)/shard_map/ppermute | solution.py:152
  (1 other events, 5.3 us)

commit v8 on v7

--- a/solution.py
+++ b/solution.py
@@ -15,7 +15,7 @@
 FREQ = 4
 ROWS = 64
 COLS = 1024
-WIDTH = 256
+GROUP = 16
 LAST = 63
 HI = lax.Precision.HIGHEST
 
@@ -61,11 +61,9 @@
     return jnp.where(keep, block, other)
 
 
-def kernel(bins, x_ref, l_ref, coef_ref, *refs):
-    block_refs, o_ref = refs[:16], refs[16]
-    total = [None] * TWIN
-    for i in range(4):
-        b = jnp.concatenate([r[...] for r in block_refs[4 * i : 4 * i + 4]], axis=0)
+def partial(sets, bins, x_ref, l_ref, coef_ref, block_refs, before_ref, d_ref, store):
+    for n, i in enumerate(sets):
+        b = jnp.concatenate([r[...] for r in block_refs[4 * n : 4 * n + 4]], axis=0)
         high = b.astype(jnp.bfloat16)
         low = (b - high.astype(jnp.float32)).astype(jnp.bfloat16)
         f = bins[i]
@@ -79,37 +77,60 @@
         )
         rest = jnp.dot(left_high, low, preferred_element_type=jnp.float32)
         product = both[: 2 * ROWS] + (both[2 * ROWS :] + rest)
-        real = x_ref[0, f] - product[:ROWS]
-        imag = x_ref[1, f] - product[ROWS:]
+        d_ref[2 * n] = x_ref[0, f] - product[:ROWS]
+        d_ref[2 * n + 1] = x_ref[1, f] - product[ROWS:]
+    for first in range(0, ROWS, GROUP):
+        rows = slice(first, first + GROUP)
+        spectrum = [d_ref[k, rows, :] for k in range(2 * len(sets))]
         for u in range(TWIN):
-            at = u * 8 + i * 2
-            term = real * coef_ref[:, at : at + 1] - imag * coef_ref[:, at + 1 : at + 2]
-            total[u] = term if total[u] is None else total[u] + term
-    for u in range(TWIN):
-        o_ref[u] = total[u].astype(o_ref.dtype)
+            total = None if before_ref is None else before_ref[u, rows, :]
+            for k, value in enumerate(spectrum):
+                at = u * 8 + 2 * sets[0] + k
+                term = value * coef_ref[rows, at : at + 1]
+                total = term if total is None else total + term
+            store(u, rows, total)
+
+
+def early_kernel(bins, x_ref, l_ref, coef_ref, *refs):
+    block_refs, o_ref, d_ref = refs[:12], refs[12], refs[13]
+
+    def store(u, rows, total):
+        o_ref[u, rows, :] = total
+
+    partial((1, 2, 3), bins, x_ref, l_ref, coef_ref, block_refs, None, d_ref, store)
+
+
+def late_kernel(bins, x_ref, l_ref, coef_ref, *refs):
+    block_refs, before_ref, o_ref, d_ref = refs[:4], refs[4], refs[5], refs[6]
+
+    def store(u, rows, total):
+        o_ref[u, rows, :] = total.astype(o_ref.dtype)
+
+    partial((0,), bins, x_ref, l_ref, coef_ref, block_refs, before_ref, d_ref, store)
 
 
 def synthesise(bins, spectra, left, coefs, blocks):
-    grid_spec = pltpu.PrefetchScalarGridSpec(
-        num_scalar_prefetch=1,
-        grid=(COLS // WIDTH,),
-        in_specs=[
-            pl.BlockSpec((2, FREQ, ROWS, WIDTH), lambda j, bins: (0, 0, 0, j)),
-            pl.BlockSpec((4, 128, 256), lambda j, bins: (0, 0, 0)),
-            pl.BlockSpec((ROWS, 64), lambda j, bins: (0, 0)),
-            *[pl.BlockSpec((ROWS, WIDTH), lambda j, bins: (0, j))] * 16,
-        ],
-        out_specs=pl.BlockSpec((TWIN, ROWS, WIDTH), lambda j, bins: (0, 0, j)),
-    )
-    return pl.pallas_call(
-        kernel,
-        grid_spec=grid_spec,
-        out_shape=jax.ShapeDtypeStruct((TWIN, ROWS, COLS), jnp.bfloat16),
-        compiler_params=pltpu.CompilerParams(vmem_limit_bytes=40 * 1024 * 1024),
-        cost_estimate=pl.CostEstimate(
-            flops=2 * 3 * 4 * 128 * 256 * COLS, bytes_accessed=8 * 2**20, transcendentals=0
-        ),
-    )(bins, spectra, left, coefs, *blocks)
+    vmem = pl.BlockSpec(memory_space=pltpu.VMEM)
+
+    def call(body, sets, dtype, operands):
+        return pl.pallas_call(
+            body,
+            in_specs=[pl.BlockSpec(memory_space=pltpu.SMEM), *[vmem] * len(operands)],
+            out_specs=vmem,
+            out_shape=jax.ShapeDtypeStruct((TWIN, ROWS, COLS), dtype),
+            scratch_shapes=[pltpu.VMEM((2 * sets, ROWS, COLS), jnp.float32)],
+            compiler_params=pltpu.CompilerParams(vmem_limit_bytes=24 * 1024 * 1024),
+            cost_estimate=pl.CostEstimate(
+                flops=2 * 3 * sets * 128 * 256 * COLS,
+                bytes_accessed=2 * 2**20 * sets,
+                transcendentals=0,
+            ),
+        )(bins, *operands)
+
+    early = call(early_kernel, 3, jnp.float32, [spectra, left, coefs, *blocks[4:]])
+    return call(
+        late_kernel, 1, jnp.bfloat16, [spectra, left, coefs, *blocks[:4], early]
+    )
 
 
 def tables(filters, offsets, strip, bins, yl):
@@ -133,7 +154,7 @@
     times = offsets[:, None] + jnp.arange(TWIN, dtype=jnp.int32)[None, :]
     phase = times[:, :, None] * (FIRST_BIN + bins)[None, None, :] & (NT - 1)
     angle = phase.astype(jnp.float32) * (2.0 * math.pi / NT)
-    coefs = jnp.stack([jnp.cos(angle), jnp.sin(angle)], axis=3).reshape(ROWS, 64)
+    coefs = jnp.stack([jnp.cos(angle), -jnp.sin(angle)], axis=3).reshape(ROWS, 64)
     return left, coefs
 
 

time: 106 us -> 104 us (0.981)
  the two profiles are of different devices: /device:TPU:16 before, /device:TPU:102 now
where the time goes in v8:
time: 104 us; the launch traced here: 103 us
  starting transfers between devices  50.6 us (49%)
  waiting for transfers between devices  37.3 us (36%)
  other arithmetic  5.55 us (5%)
  Pallas kernels  5.31 us (5%)
  between operations  2.19 us (2%)
  local copies, waits for them, and re-layouts  1.98 us (2%)
    all_to_all x1, waiting for transfers between devices, scatter(): lax.all_to_all(rows, ('x', 'yl'), 0, 0, axis_index_groups=[members], tile...  20.2 us
    ppermute x14, starting transfers between devices, send(): return lax.ppermute(v, axis, pairs)  18.3 us
    ppermute x2, starting transfers between devices, steps(): before = lax.ppermute(held, 'z', [(k, (k - 1) % 8) for k in range(8)])  15.1 us
    ppermute x14, waiting for transfers between devices, send(): return lax.ppermute(v, axis, pairs)  12.7 us
    all_to_all x1, starting transfers between devices, scatter(): lax.all_to_all(rows, ('x', 'yl'), 0, 0, axis_index_groups=[members], tile...  6.06 us
    pallas_call x2, Pallas kernels, call(): pl.pallas_call(body, in_specs=[pl.BlockSpec(memory_space=pltpu.SMEM), *[v...  5.31 us
    ppermute x2, starting transfers between devices, steps(): after = lax.ppermute(held, 'z', [(k, (k + 1) % 8) for k in range(8)])  3.9 us
    ppermute x2, waiting for transfers between devices, steps(): after = lax.ppermute(held, 'z', [(k, (k + 1) % 8) for k in range(8)])  3.13 us
  transfers between devices with their start and end apart: 25, of which 12 were waited for; matrix products, arithmetic and copies ran while one was open for 7% of the time, Pallas kernels for 3%

profile of v8, /device:TPU:102, one launch (start us, length us, event | category | flops | bytes accessed | tf_op | source)
XLA Modules:
  0.0 103.3 jit_solution(7243223519381860210)
XLA Ops:
  0.0 6.1 %all-to-all-start = ((f32[8,64,1024]{2,1,0:T(8,128)}), f32[8,64,1024]{2,1,0:T(8,128)}, u32[]{:S(2)}, u32[]{:S(2)}) async-start(f32[8,64,1024]{2,1,0:T(8,128)} %bitcast.14), calls=%async_computation | async-start | bytes 4194304 | tf_op jit(solution)/shard_map/all_to_all | solution.py:163
  9.3 1.2 %collective-permute-done.16 = f32[8,64,128]{2,1,0:T(8,128)S(1)} collective-permute-done((f32[8,64,128]{2,1,0:T(8,128)S(1)}, f32[8,64,128]{2,1,0:T(8,128)S(1)}, u32[]{:S(2)}, u32[]{:S(2)}) %collective-permute-start.16) | collective-permute-done | bytes 262176 | tf_op jit(solution)/shard_map/ppermute | solution.py:59
  10.6 0.8 broadcast_select_fusion
  11.4 20.2 %all-to-all-done = f32[8,64,1024]{2,1,0:T(8,128)} async-done(((f32[8,64,1024]{2,1,0:T(8,128)}), f32[8,64,1024]{2,1,0:T(8,128)}, u32[]{:S(2)}, u32[]{:S(2)}) %all-to-all-start) | async-done | bytes 2097184 | tf_op jit(solution)/shard_map/all_to_all | solution.py:163
  31.6 1.1 %slice_bitcast_fusion = (f32[64,1024]{1,0:T(8,128)S(1)}, f32[64,1024]{1,0:T(8,128)S(1)}) fusion(f32[8,64,1024]{2,1,0:T(8,128)} %all-to-all-done, u32[]{:T(128)S(6)} %convert_element_type.21), kind=kLoop, calls=%fused_computation.4 | loop fusion | bytes 1048580 | tf_op jit(solution)/shard_map/squeeze | solution.py:197
  34.1 2.8 %conditional.1 = (f32[64,1024]{1,0:T(8,128)}, f32[64,1024]{1,0:T(8,128)}) conditional(s32[]{:T(128)} %clamp.3, f32[64,1024]{1,0:T(8,128)S(1)} %get-tuple-element.28, f32[64,1024]{1,0:T(8,128)S(1)} %get-tuple-element.28, f32[64,1024]{1,0:T(8,128)S(1)} %get-tuple-element.28, ...), branch_computations={%region_0.1_spmd, %region_1.2_spmd, %region_2.3_spmd, %region_3.4_... | conditional | bytes 2097248 | solution.py:200
  34.1 1.4 %collective-permute-start.10 = (f32[64,1024]{1,0:T(8,128)S(1)}, f32[64,1024]{1,0:T(8,128)}, u32[]{:S(2)}, u32[]{:S(2)}) collective-permute-start(f32[64,1024]{1,0:T(8,128)S(1)} %param.5), channel_id=1, source_target_pairs={{40,0},{41,1},{42,2},{43,3},{44,4},{45,5},{46,6},{47,7},{104,64},{... | collective-permute-start | bytes 786440 | tf_op jit(solution)/shard_map/cond/branch_5_fun/ppermute | solution.py:28
  35.5 1.4 %collective-permute-start.11 = (f32[64,1024]{1,0:T(8,128)S(1)}, f32[64,1024]{1,0:T(8,128)}, u32[]{:S(2)}, u32[]{:S(2)}) collective-permute-start(f32[64,1024]{1,0:T(8,128)S(1)} %param.5), channel_id=1, source_target_pairs={{40,16},{41,17},{42,18},{43,19},{44,20},{45,21},{46,22},{47,23},{1... | collective-permute-start | bytes 786440 | tf_op jit(solution)/shard_map/cond/branch_5_fun/ppermute | solution.py:29
  36.9 1.0 select_select_fusion.3
  37.9 3.8 %collective-permute-start.18 = (f32[64,1024]{1,0:T(8,128)S(1)}, f32[64,1024]{1,0:T(8,128)S(1)}, u32[]{:S(2)}, u32[]{:S(2)}) collective-permute-start(f32[64,1024]{1,0:T(8,128)S(1)} %select_select_fusion.3), channel_id=1, source_target_pairs={{0,8},{8,16},{16,24},{24,32},{32,40},{40,48},{48,56},{56,0},{1,9},... | collective-permute-start | bytes 786440 | tf_op jit(solution)/shard_map/ppermute | solution.py:39
  41.7 13.1 %collective-permute-start.19 = (f32[64,1024]{1,0:T(8,128)S(1)}, f32[64,1024]{1,0:T(8,128)}, u32[]{:S(2)}, u32[]{:S(2)}) collective-permute-start(f32[64,1024]{1,0:T(8,128)S(1)} %select_select_fusion.3), channel_id=1, source_target_pairs={{0,56},{8,0},{16,8},{24,16},{32,24},{40,32},{48,40},{56,48},{1,57}... | collective-permute-start | bytes 786440 | tf_op jit(solution)/shard_map/ppermute | solution.py:40
  54.8 1.0 select_select_fusion.1
  55.9 2.0 %collective-permute-start.23 = (f32[64,1024]{1,0:T(8,128)S(1)}, f32[64,1024]{1,0:T(8,128)}, u32[]{:S(2)}, u32[]{:S(2)}) collective-permute-start(f32[64,1024]{1,0:T(8,128)S(1)} %select_select_fusion.1), channel_id=1, source_target_pairs={{0,56},{8,0},{16,8},{24,16},{32,24},{40,32},{48,40},{56,48},{1,57}... | collective-permute-start | bytes 786440 | tf_op jit(solution)/shard_map/ppermute | solution.py:40
  58.1 3.0 %collective-permute-start.17 = (f32[8,64,128]{2,1,0:T(8,128)}, f32[8,64,128]{2,1,0:T(8,128)}, u32[]{:S(2)}, u32[]{:S(2)}) collective-permute-start(f32[8,64,128]{2,1,0:T(8,128)} %broadcast_select_fusion), channel_id=1, source_target_pairs={{0,2},{2,0},{1,3},{3,1},{4,6},{6,4},{5,7},{7,5},{8,10},{10,8},{9,1... | collective-permute-start | bytes 786440 | tf_op jit(solution)/shard_map/ppermute | solution.py:59
  61.1 0.7 collective-permute-done.18
  62.5 2.0 %collective-permute-start.30 = (f32[64,1024]{1,0:T(8,128)S(1)}, f32[64,1024]{1,0:T(8,128)S(1)}, u32[]{:S(2)}, u32[]{:S(2)}) collective-permute-start(f32[64,1024]{1,0:T(8,128)S(1)} %select_select_fusion.2.refs_0_), channel_id=1, source_target_pairs={{0,64},{64,128},{128,192},{192,0},{1,65},{65,129},{129,193},{193,1... | collective-permute-start | bytes 786440 | tf_op jit(solution)/shard_map/ppermute | solution.py:173
  64.5 2.4 %collective-permute-done.22 = f32[64,1024]{1,0:T(8,128)} collective-permute-done((f32[64,1024]{1,0:T(8,128)S(1)}, f32[64,1024]{1,0:T(8,128)}, u32[]{:S(2)}, u32[]{:S(2)}) %collective-permute-start.22) | collective-permute-done | bytes 262176 | tf_op jit(solution)/shard_map/ppermute | solution.py:39
  67.2 1.1 %select_select_fusion.refs_1_ = f32[64,1024]{1,0:T(8,128)S(1)} fusion(f32[64,1024]{1,0:T(8,128)} %collective-permute-done.22, f32[64,1024]{1,0:T(8,128)} %collective-permute-done.23, f32[64,1024]{1,0:T(8,128)} %copy-done.2, pred[]{:T(512)S(6)} %or.23, pred[]{:T(512)S(6)} %or.22), kind=kLoop, calls=%fused_computation.2 | loop fusion | flops 131072 | bytes 1048578 | tf_op jit(solution)/shard_map/jit(_where)/select_n | solution.py:44
  68.3 3.0 %collective-permute-start.27 = (f32[64,1024]{1,0:T(8,128)S(1)}, f32[64,1024]{1,0:T(8,128)}, u32[]{:S(2)}, u32[]{:S(2)}) collective-permute-start(f32[64,1024]{1,0:T(8,128)S(1)} %select_select_fusion.refs_1_), channel_id=1, source_target_pairs={{0,64},{64,128},{128,192},{192,0},{1,65},{65,129},{129,193},{193,1... | collective-permute-start | bytes 786440 | tf_op jit(solution)/shard_map/ppermute | solution.py:173
  72.5 1.2 %collective-permute-start.35 = (f32[64,1024]{1,0:T(8,128)S(1)}, f32[64,1024]{1,0:T(8,128)}, u32[]{:S(2)}, u32[]{:S(2)}) collective-permute-start(f32[64,1024]{1,0:T(8,128)S(1)} %select_select_fusion.refs_1_), channel_id=1, source_target_pairs={{0,192},{64,0},{128,64},{192,128},{1,193},{65,1},{129,65},{193,129... | collective-permute-start | bytes 786440 | tf_op jit(solution)/shard_map/ppermute | solution.py:173
  73.6 1.9 %collective-permute-start.25 = (f32[64,1024]{1,0:T(8,128)S(1)}, f32[64,1024]{1,0:T(8,128)}, u32[]{:S(2)}, u32[]{:S(2)}) collective-permute-start(f32[64,1024]{1,0:T(8,128)S(1)} %collective-permute-done.24.refs_2_), channel_id=1, source_target_pairs={{0,192},{64,0},{128,64},{192,128},{1,193},{65,1},{129,65},{193,129... | collective-permute-start | bytes 786440 | tf_op jit(solution)/shard_map/ppermute | solution.py:173
  75.6 1.5 %collective-permute-done.34.refs_8_ = f32[64,1024]{1,0:T(8,128)S(1)} collective-permute-done((f32[64,1024]{1,0:T(8,128)S(1)}, f32[64,1024]{1,0:T(8,128)S(1)}, u32[]{:S(2)}, u32[]{:S(2)}) %collective-permute-start.34) | collective-permute-done | bytes 262176 | tf_op jit(solution)/shard_map/ppermute | solution.py:173
  77.0 1.0 %collective-permute-start.31 = (f32[64,1024]{1,0:T(8,128)S(1)}, f32[64,1024]{1,0:T(8,128)}, u32[]{:S(2)}, u32[]{:S(2)}) collective-permute-start(f32[64,1024]{1,0:T(8,128)S(1)} %collective-permute-done.30.refs_4_), channel_id=1, source_target_pairs={{0,64},{64,128},{128,192},{192,0},{1,65},{65,129},{129,193},{193,1... | collective-permute-start | bytes 786440 | tf_op jit(solution)/shard_map/ppermute | solution.py:173
  78.1 2.9 %collective-permute-start.28 = (f32[64,1024]{1,0:T(8,128)}, f32[64,1024]{1,0:T(8,128)}, u32[]{:S(2)}, u32[]{:S(2)}) collective-permute-start(f32[64,1024]{1,0:T(8,128)} %collective-permute-done.27.refs_5_), channel_id=1, source_target_pairs={{0,64},{64,128},{128,192},{192,0},{1,65},{65,129},{129,193},{193,1... | collective-permute-start | bytes 786440 | tf_op jit(solution)/shard_map/ppermute | solution.py:173
  81.1 1.1 %broadcast_select_fusion.1 = f32[8,64,128]{2,1,0:T(8,128)S(1)} fusion(f32[8,64,128]{2,1,0:T(8,128)} %broadcast_select_fusion, f32[8,64,128]{2,1,0:T(8,128)} %collective-permute-done.17, pred[128]{0:T(512)(128)(4,1)S(1)} %fusion.1), kind=kLoop, calls=%fused_computation.11 | loop fusion | flops 65536 | bytes 786560 | tf_op jit(solution)/shard_map/jit(_where)/select_n | solution.py:61
  83.0 1.9 %collective-permute-start.37 = (f32[64,1024]{1,0:T(8,128)}, f32[64,1024]{1,0:T(8,128)S(1)}, u32[]{:S(2)}, u32[]{:S(2)}) collective-permute-start(f32[64,1024]{1,0:T(8,128)} %collective-permute-done.27.refs_5_), channel_id=1, source_target_pairs={{0,4},{4,0},{1,5},{5,1},{2,6},{6,2},{3,7},{7,3},{8,12},{12,8},{9,1... | collective-permute-start | bytes 786440 | tf_op jit(solution)/shard_map/ppermute | solution.py:173
  84.9 2.2 %collective-permute-done.25.refs_6_ = f32[64,1024]{1,0:T(8,128)} collective-permute-done((f32[64,1024]{1,0:T(8,128)S(1)}, f32[64,1024]{1,0:T(8,128)}, u32[]{:S(2)}, u32[]{:S(2)}) %collective-permute-start.25) | collective-permute-done | bytes 262176 | tf_op jit(solution)/shard_map/ppermute | solution.py:173
  88.4 1.6 %collective-permute-start.29 = (f32[64,1024]{1,0:T(8,128)}, f32[64,1024]{1,0:T(8,128)S(1)}, u32[]{:S(2)}, u32[]{:S(2)}) collective-permute-start(f32[64,1024]{1,0:T(8,128)} %collective-permute-done.28.refs_1_), channel_id=1, source_target_pairs={{0,4},{4,0},{1,5},{5,1},{2,6},{6,2},{3,7},{7,3},{8,12},{12,8},{9,1... | collective-permute-start | bytes 786440 | tf_op jit(solution)/shard_map/ppermute | solution.py:173
  90.1 1.4 %collective-permute-done.36.refs_10_ = f32[64,1024]{1,0:T(8,128)S(1)} collective-permute-done((f32[64,1024]{1,0:T(8,128)S(1)}, f32[64,1024]{1,0:T(8,128)S(1)}, u32[]{:S(2)}, u32[]{:S(2)}) %collective-permute-start.36) | collective-permute-done | bytes 262176 | tf_op jit(solution)/shard_map/ppermute | solution.py:173
  91.5 6.4 %collective-permute-done.33.refs_7_ = f32[64,1024]{1,0:T(8,128)S(1)} collective-permute-done((f32[64,1024]{1,0:T(8,128)}, f32[64,1024]{1,0:T(8,128)S(1)}, u32[]{:S(2)}, u32[]{:S(2)}) %collective-permute-start.33) | collective-permute-done | bytes 262176 | tf_op jit(solution)/shard_map/ppermute | solution.py:173
  97.9 3.1 %shard_map.73.refs_4_ = f32[8,64,1024]{2,1,0:T(8,128)S(1)} custom-call(s32[4]{0:T(128)S(1)} %get-tuple-element.35.bins, f32[2,4,64,1024]{3,2,1,0:T(8,128)S(1)} %copy-done.1, f32[4,128,256]{2,1,0:T(8,128)S(1)} %maximum_select_fusion.l_ref, f32[64,64]{1,0:T(8,128)S(1)} %copy.12.coef_ref, f32[64,1024]{1,0:T(8,128)} %collective-permute-done.31.refs_0_, ...), custom_call_target="tpu_custom_call" | custom-call | flops 603979776 | bytes 6291456 | tf_op jit(solution)/shard_map/pallas_call | solution.py:116
  101.1 2.2 %shard_map.74 = bf16[8,64,1024]{2,1,0:T(8,128)(2,1)} custom-call(s32[4]{0:T(128)S(1)} %get-tuple-element.35.bins, f32[2,4,64,1024]{3,2,1,0:T(8,128)S(1)} %copy-done.1, f32[4,128,256]{2,1,0:T(8,128)S(1)} %maximum_select_fusion.l_ref, f32[64,64]{1,0:T(8,128)S(1)} %copy.12.coef_ref, f32[64,1024]{1,0:T(8,128)S(1)} %select_select_fusion.2.refs_0_, ...), custom_call_target="tpu_custom_call" | custom-call | flops 201326592 | bytes 2097152 | tf_op jit(solution)/shard_map/pallas_call | solution.py:116
  (59 shorter events, 7.4 us)
Async XLA Ops:
  0.0 9.1 %copy-start = (f32[64,64]{1,0:T(8,128)S(1)}, f32[64,64]{1,0:T(8,128)}, u32[]{:S(2)}) copy-start(f32[64,64]{1,0:T(8,128)} %param.17) | copy-start | bytes 49156
  0.0 8.6 %copy-start.1 = (f32[2,4,64,1024]{3,2,1,0:T(8,128)S(1)}, f32[2,4,64,1024]{3,2,1,0:T(8,128)}, u32[]{:S(2)}) copy-start(f32[2,4,64,1024]{3,2,1,0:T(8,128)} %x_ref.3) | copy-start | bytes 6291460
  0.0 9.0 %copy-start.6 = (s32[64]{0:T(128)S(1)}, s32[64]{0:T(128)}, u32[]{:S(2)}) copy-start(s32[64]{0:T(128)} %param.18) | copy-start | bytes 772
  0.0 9.1 %copy-start.4 = (f32[64,4]{1,0:T(8,128)S(1)}, f32[64,4]{1,0:T(8,128)}, u32[]{:S(2)}) copy-start(f32[64,4]{1,0:T(8,128)} %constant.61.clone) | copy-start | bytes 3076
  0.0 31.5 %all-to-all-start = ((f32[8,64,1024]{2,1,0:T(8,128)}), f32[8,64,1024]{2,1,0:T(8,128)}, u32[]{:S(2)}, u32[]{:S(2)}) async-start(f32[8,64,1024]{2,1,0:T(8,128)} %bitcast.14), calls=%async_computation | async-start | bytes 4194304 | tf_op jit(solution)/shard_map/all_to_all | solution.py:163
  6.1 27.9 %copy-start.7 = (s32[4]{0:T(128)S(1)}, s32[4]{0:T(128)}, u32[]{:S(2)}) copy-start(s32[4]{0:T(128)} %constant.60.clone) | copy-start | bytes 52
  8.9 1.6 %collective-permute-start.16 = (f32[8,64,128]{2,1,0:T(8,128)S(1)}, f32[8,64,128]{2,1,0:T(8,128)S(1)}, u32[]{:S(2)}, u32[]{:S(2)}) collective-permute-start(f32[8,64,128]{2,1,0:T(8,128)S(1)} %pad_maximum_fusion), channel_id=1, source_target_pairs={{0,1},{1,0},{2,3},{3,2},{4,5},{5,4},{6,7},{7,6},{8,9},{9,8},{10,11... | collective-permute-start | bytes 786440 | tf_op jit(solution)/shard_map/ppermute | solution.py:59
  32.7 22.2 %collective-permute-start.20 = (f32[64,1024]{1,0:T(8,128)S(1)}, f32[64,1024]{1,0:T(8,128)S(1)}, u32[]{:S(2)}, u32[]{:S(2)}) collective-permute-start(f32[64,1024]{1,0:T(8,128)S(1)} %get-tuple-element.27), channel_id=1, source_target_pairs={{56,16},{57,17},{58,18},{59,19},{60,20},{61,21},{62,22},{63,23},{1... | collective-permute-start | bytes 786440 | tf_op jit(solution)/shard_map/ppermute | solution.py:28
  33.3 21.5 %collective-permute-start.21 = (f32[64,1024]{1,0:T(8,128)S(1)}, f32[64,1024]{1,0:T(8,128)S(1)}, u32[]{:S(2)}, u32[]{:S(2)}) collective-permute-start(f32[64,1024]{1,0:T(8,128)S(1)} %get-tuple-element.27), channel_id=1, source_target_pairs={{56,32},{57,33},{58,34},{59,35},{60,36},{61,37},{62,38},{63,39},{1... | collective-permute-start | bytes 786440 | tf_op jit(solution)/shard_map/ppermute | solution.py:29
  34.1 2.8 %collective-permute-start.10 = (f32[64,1024]{1,0:T(8,128)S(1)}, f32[64,1024]{1,0:T(8,128)}, u32[]{:S(2)}, u32[]{:S(2)}) collective-permute-start(f32[64,1024]{1,0:T(8,128)S(1)} %param.5), channel_id=1, source_target_pairs={{40,0},{41,1},{42,2},{43,3},{44,4},{45,5},{46,6},{47,7},{104,64},{... | collective-permute-start | bytes 786440 | tf_op jit(solution)/shard_map/cond/branch_5_fun/ppermute | solution.py:28
  35.5 1.4 %collective-permute-start.11 = (f32[64,1024]{1,0:T(8,128)S(1)}, f32[64,1024]{1,0:T(8,128)}, u32[]{:S(2)}, u32[]{:S(2)}) collective-permute-start(f32[64,1024]{1,0:T(8,128)S(1)} %param.5), channel_id=1, source_target_pairs={{40,16},{41,17},{42,18},{43,19},{44,20},{45,21},{46,22},{47,23},{1... | collective-permute-start | bytes 786440 | tf_op jit(solution)/shard_map/cond/branch_5_fun/ppermute | solution.py:29
  36.8 34.5 %copy-start.3 = (f32[64,4]{1,0:T(8,128)S(1)}, f32[64,4]{1,0:T(8,128)}, u32[]{:S(2)}) copy-start(f32[64,4]{1,0:T(8,128)} %constant.62.clone) | copy-start | bytes 3076
  37.9 24.0 %collective-permute-start.18 = (f32[64,1024]{1,0:T(8,128)S(1)}, f32[64,1024]{1,0:T(8,128)S(1)}, u32[]{:S(2)}, u32[]{:S(2)}) collective-permute-start(f32[64,1024]{1,0:T(8,128)S(1)} %select_select_fusion.3), channel_id=1, source_target_pairs={{0,8},{8,16},{16,24},{24,32},{32,40},{40,48},{48,56},{56,0},{1,9},... | collective-permute-start | bytes 786440 | tf_op jit(solution)/shard_map/ppermute | solution.py:39
  41.7 20.2 %collective-permute-start.19 = (f32[64,1024]{1,0:T(8,128)S(1)}, f32[64,1024]{1,0:T(8,128)}, u32[]{:S(2)}, u32[]{:S(2)}) collective-permute-start(f32[64,1024]{1,0:T(8,128)S(1)} %select_select_fusion.3), channel_id=1, source_target_pairs={{0,56},{8,0},{16,8},{24,16},{32,24},{40,32},{48,40},{56,48},{1,57}... | collective-permute-start | bytes 786440 | tf_op jit(solution)/shard_map/ppermute | solution.py:40
  55.8 11.4 %copy-start.2 = (f32[64,1024]{1,0:T(8,128)}, f32[64,1024]{1,0:T(8,128)S(1)}, u32[]{:S(2)}) copy-start(f32[64,1024]{1,0:T(8,128)S(1)} %select_select_fusion.1) | copy-start | bytes 786436
  55.8 11.1 %collective-permute-start.22 = (f32[64,1024]{1,0:T(8,128)S(1)}, f32[64,1024]{1,0:T(8,128)}, u32[]{:S(2)}, u32[]{:S(2)}) collective-permute-start(f32[64,1024]{1,0:T(8,128)S(1)} %select_select_fusion.1), channel_id=1, source_target_pairs={{0,8},{8,16},{16,24},{24,32},{32,40},{40,48},{48,56},{56,0},{1,9},... | collective-permute-start | bytes 786440 | tf_op jit(solution)/shard_map/ppermute | solution.py:39
  55.9 11.3 %collective-permute-start.23 = (f32[64,1024]{1,0:T(8,128)S(1)}, f32[64,1024]{1,0:T(8,128)}, u32[]{:S(2)}, u32[]{:S(2)}) collective-permute-start(f32[64,1024]{1,0:T(8,128)S(1)} %select_select_fusion.1), channel_id=1, source_target_pairs={{0,56},{8,0},{16,8},{24,16},{32,24},{40,32},{48,40},{56,48},{1,57}... | collective-permute-start | bytes 786440 | tf_op jit(solution)/shard_map/ppermute | solution.py:40
  58.1 13.4 %collective-permute-start.17 = (f32[8,64,128]{2,1,0:T(8,128)}, f32[8,64,128]{2,1,0:T(8,128)}, u32[]{:S(2)}, u32[]{:S(2)}) collective-permute-start(f32[8,64,128]{2,1,0:T(8,128)} %broadcast_select_fusion), channel_id=1, source_target_pairs={{0,2},{2,0},{1,3},{3,1},{4,6},{6,4},{5,7},{7,5},{8,10},{10,8},{9,1... | collective-permute-start | bytes 786440 | tf_op jit(solution)/shard_map/ppermute | solution.py:59
  61.9 10.6 %collective-permute-start.24 = (f32[64,1024]{1,0:T(8,128)S(1)}, f32[64,1024]{1,0:T(8,128)S(1)}, u32[]{:S(2)}, u32[]{:S(2)}) collective-permute-start(f32[64,1024]{1,0:T(8,128)S(1)} %select_select_fusion.2.refs_0_), channel_id=1, source_target_pairs={{0,4},{4,0},{1,5},{5,1},{2,6},{6,2},{3,7},{7,3},{8,12},{12,8},{9,1... | collective-permute-start | bytes 786440 | tf_op jit(solution)/shard_map/ppermute | solution.py:173
  62.5 11.1 %collective-permute-start.30 = (f32[64,1024]{1,0:T(8,128)S(1)}, f32[64,1024]{1,0:T(8,128)S(1)}, u32[]{:S(2)}, u32[]{:S(2)}) collective-permute-start(f32[64,1024]{1,0:T(8,128)S(1)} %select_select_fusion.2.refs_0_), channel_id=1, source_target_pairs={{0,64},{64,128},{128,192},{192,0},{1,65},{65,129},{129,193},{193,1... | collective-permute-start | bytes 786440 | tf_op jit(solution)/shard_map/ppermute | solution.py:173
  66.9 10.1 %collective-permute-start.34 = (f32[64,1024]{1,0:T(8,128)S(1)}, f32[64,1024]{1,0:T(8,128)S(1)}, u32[]{:S(2)}, u32[]{:S(2)}) collective-permute-start(f32[64,1024]{1,0:T(8,128)S(1)} %select_select_fusion.2.refs_0_), channel_id=1, source_target_pairs={{0,192},{64,0},{128,64},{192,128},{1,193},{65,1},{129,65},{193,129... | collective-permute-start | bytes 786440 | tf_op jit(solution)/shard_map/ppermute | solution.py:173
  68.3 9.8 %collective-permute-start.27 = (f32[64,1024]{1,0:T(8,128)S(1)}, f32[64,1024]{1,0:T(8,128)}, u32[]{:S(2)}, u32[]{:S(2)}) collective-permute-start(f32[64,1024]{1,0:T(8,128)S(1)} %select_select_fusion.refs_1_), channel_id=1, source_target_pairs={{0,64},{64,128},{128,192},{192,0},{1,65},{65,129},{129,193},{193,1... | collective-permute-start | bytes 786440 | tf_op jit(solution)/shard_map/ppermute | solution.py:173
  71.6 10.6 %collective-permute-start.32 = (f32[64,1024]{1,0:T(8,128)S(1)}, f32[64,1024]{1,0:T(8,128)}, u32[]{:S(2)}, u32[]{:S(2)}) collective-permute-start(f32[64,1024]{1,0:T(8,128)S(1)} %select_select_fusion.refs_1_), channel_id=1, source_target_pairs={{0,4},{4,0},{1,5},{5,1},{2,6},{6,2},{3,7},{7,3},{8,12},{12,8},{9,1... | collective-permute-start | bytes 786440 | tf_op jit(solution)/shard_map/ppermute | solution.py:173
  72.5 10.6 %collective-permute-start.35 = (f32[64,1024]{1,0:T(8,128)S(1)}, f32[64,1024]{1,0:T(8,128)}, u32[]{:S(2)}, u32[]{:S(2)}) collective-permute-start(f32[64,1024]{1,0:T(8,128)S(1)} %select_select_fusion.refs_1_), channel_id=1, source_target_pairs={{0,192},{64,0},{128,64},{192,128},{1,193},{65,1},{129,65},{193,129... | collective-permute-start | bytes 786440 | tf_op jit(solution)/shard_map/ppermute | solution.py:173
  73.6 13.6 %collective-permute-start.25 = (f32[64,1024]{1,0:T(8,128)S(1)}, f32[64,1024]{1,0:T(8,128)}, u32[]{:S(2)}, u32[]{:S(2)}) collective-permute-start(f32[64,1024]{1,0:T(8,128)S(1)} %collective-permute-done.24.refs_2_), channel_id=1, source_target_pairs={{0,192},{64,0},{128,64},{192,128},{1,193},{65,1},{129,65},{193,129... | collective-permute-start | bytes 786440 | tf_op jit(solution)/shard_map/ppermute | solution.py:173
  77.0 10.2 %collective-permute-start.31 = (f32[64,1024]{1,0:T(8,128)S(1)}, f32[64,1024]{1,0:T(8,128)}, u32[]{:S(2)}, u32[]{:S(2)}) collective-permute-start(f32[64,1024]{1,0:T(8,128)S(1)} %collective-permute-done.30.refs_4_), channel_id=1, source_target_pairs={{0,64},{64,128},{128,192},{192,0},{1,65},{65,129},{129,193},{193,1... | collective-permute-start | bytes 786440 | tf_op jit(solution)/shard_map/ppermute | solution.py:173
  78.1 10.3 %collective-permute-start.28 = (f32[64,1024]{1,0:T(8,128)}, f32[64,1024]{1,0:T(8,128)}, u32[]{:S(2)}, u32[]{:S(2)}) collective-permute-start(f32[64,1024]{1,0:T(8,128)} %collective-permute-done.27.refs_5_), channel_id=1, source_target_pairs={{0,64},{64,128},{128,192},{192,0},{1,65},{65,129},{129,193},{193,1... | collective-permute-start | bytes 786440 | tf_op jit(solution)/shard_map/ppermute | solution.py:173
  82.2 9.3 %collective-permute-start.36 = (f32[64,1024]{1,0:T(8,128)S(1)}, f32[64,1024]{1,0:T(8,128)S(1)}, u32[]{:S(2)}, u32[]{:S(2)}) collective-permute-start(f32[64,1024]{1,0:T(8,128)S(1)} %collective-permute-done.30.refs_4_), channel_id=1, source_target_pairs={{0,4},{4,0},{1,5},{5,1},{2,6},{6,2},{3,7},{7,3},{8,12},{12,8},{9,1... | collective-permute-start | bytes 786440 | tf_op jit(solution)/shard_map/ppermute | solution.py:173
  83.0 14.8 %collective-permute-start.37 = (f32[64,1024]{1,0:T(8,128)}, f32[64,1024]{1,0:T(8,128)S(1)}, u32[]{:S(2)}, u32[]{:S(2)}) collective-permute-start(f32[64,1024]{1,0:T(8,128)} %collective-permute-done.27.refs_5_), channel_id=1, source_target_pairs={{0,4},{4,0},{1,5},{5,1},{2,6},{6,2},{3,7},{7,3},{8,12},{12,8},{9,1... | collective-permute-start | bytes 786440 | tf_op jit(solution)/shard_map/ppermute | solution.py:173
  87.2 10.7 %collective-permute-start.33 = (f32[64,1024]{1,0:T(8,128)}, f32[64,1024]{1,0:T(8,128)S(1)}, u32[]{:S(2)}, u32[]{:S(2)}) collective-permute-start(f32[64,1024]{1,0:T(8,128)} %collective-permute-done.32.refs_3_), channel_id=1, source_target_pairs={{0,192},{64,0},{128,64},{192,128},{1,193},{65,1},{129,65},{193,129... | collective-permute-start | bytes 786440 | tf_op jit(solution)/shard_map/ppermute | solution.py:173
  87.2 13.9 %collective-permute-start.26 = (f32[64,1024]{1,0:T(8,128)}, f32[64,1024]{1,0:T(8,128)S(1)}, u32[]{:S(2)}, u32[]{:S(2)}) collective-permute-start(f32[64,1024]{1,0:T(8,128)} %collective-permute-done.25.refs_6_), channel_id=1, source_target_pairs={{0,192},{64,0},{128,64},{192,128},{1,193},{65,1},{129,65},{193,129... | collective-permute-start | bytes 786440 | tf_op jit(solution)/shard_map/ppermute | solution.py:173
  88.4 12.8 %collective-permute-start.29 = (f32[64,1024]{1,0:T(8,128)}, f32[64,1024]{1,0:T(8,128)S(1)}, u32[]{:S(2)}, u32[]{:S(2)}) collective-permute-start(f32[64,1024]{1,0:T(8,128)} %collective-permute-done.28.refs_1_), channel_id=1, source_target_pairs={{0,4},{4,0},{1,5},{5,1},{2,6},{6,2},{3,7},{7,3},{8,12},{12,8},{9,1... | collective-permute-start | bytes 786440 | tf_op jit(solution)/shard_map/ppermute | solution.py:173
  (1 other events, 6.1 us)

commit v9 on v8

--- a/solution.py
+++ b/solution.py
@@ -35,9 +35,13 @@
     return jnp.where(d == 0, v, jnp.where(d == 3, leapt[0], leapt[1]))
 
 
-def steps(held, root, z):
-    after = lax.ppermute(held, "z", [(k, (k + 1) % 8) for k in range(8)])
-    before = lax.ppermute(held, "z", [(k, (k - 1) % 8) for k in range(8)])
+def steps(held, root, z, exact):
+    def pairs(step, away):
+        senders = [(root + k) % 8 for k in away] if exact else range(8)
+        return [(k, (k + step) % 8) for k in senders]
+
+    after = lax.ppermute(held, "z", pairs(1, (0, 3, 5)))
+    before = lax.ppermute(held, "z", pairs(-1, (0, 3)))
     d = (z - root) & 7
     from_after = (d == 1) | (d == 4) | (d == 6)
     from_before = (d == 2) | (d == 7)
@@ -200,7 +204,7 @@
     mine = land(mine, lax.switch(oz, branches, mine), oz, z)
     mine, strip = lax.optimization_barrier((mine, strip))
     strip = swap(strip, other, "yh").reshape(2, FREQ, ROWS, 2 * ROWS)
-    last, mine = exchange([steps(last, lz, z), steps(mine, oz, z)])
+    last, mine = exchange([steps(last, lz, z, True), steps(mine, oz, z, False)])
     blocks = [v for pair in zip(mine, last) for v in pair]
     bins = (x + 2 * yl + jnp.array([0, 2, 3, 1], jnp.int32)) & 3
     left, coefs = tables(filters, offsets, strip, bins, yl)

time: 104 us -> 103 us (level)
  the two profiles are of different devices: /device:TPU:102 before, /device:TPU:72 now
where the time goes in v9:
time: 103 us; the launch traced here: 104 us
  waiting for transfers between devices  53.6 us (52%)
  starting transfers between devices  35 us (34%)
  other arithmetic  5.49 us (5%)
  Pallas kernels  5.33 us (5%)
  between operations  2.25 us (2%)
  local copies, waits for them, and re-layouts  1.99 us (2%)
    all_to_all x1, waiting for transfers between devices, scatter(): lax.all_to_all(rows, ('x', 'yl'), 0, 0, axis_index_groups=[members], tile...  20.6 us
    ppermute x14, waiting for transfers between devices, send(): return lax.ppermute(v, axis, pairs)  16.8 us
    ppermute x2, waiting for transfers between devices, leap(): up = lax.ppermute(v, 'z', [(root, (root + 3) % 8)])  12.9 us
    ppermute x14, starting transfers between devices, send(): return lax.ppermute(v, axis, pairs)  12.8 us
    all_to_all x1, starting transfers between devices, scatter(): lax.all_to_all(rows, ('x', 'yl'), 0, 0, axis_index_groups=[members], tile...  6.04 us
    pallas_call x2, Pallas kernels, call(): pl.pallas_call(body, in_specs=[pl.BlockSpec(memory_space=pltpu.SMEM), *[v...  5.33 us
    ppermute x2, starting transfers between devices, steps(): after = lax.ppermute(held, 'z', pairs(1, (0, 3, 5)))  5.12 us
    ppermute x2, starting transfers between devices, steps(): before = lax.ppermute(held, 'z', pairs(-1, (0, 3)))  4 us
  transfers between devices with their start and end apart: 25, of which 8 were waited for; matrix products, arithmetic and copies ran while one was open for 7% of the time, Pallas kernels for 3%

profile of v9, /device:TPU:72, one launch (start us, length us, event | category | flops | bytes accessed | tf_op | source)
XLA Modules:
  0.0 104.1 jit_solution(286580965972206681)
XLA Ops:
  0.0 6.0 %all-to-all-start = ((f32[8,64,1024]{2,1,0:T(8,128)}), f32[8,64,1024]{2,1,0:T(8,128)}, u32[]{:S(2)}, u32[]{:S(2)}) async-start(f32[8,64,1024]{2,1,0:T(8,128)} %bitcast.14), calls=%async_computation | async-start | bytes 4194304 | tf_op jit(solution)/shard_map/all_to_all | solution.py:167
  9.3 1.2 %collective-permute-done.16 = f32[8,64,128]{2,1,0:T(8,128)S(1)} collective-permute-done((f32[8,64,128]{2,1,0:T(8,128)S(1)}, f32[8,64,128]{2,1,0:T(8,128)S(1)}, u32[]{:S(2)}, u32[]{:S(2)}) %collective-permute-start.16) | collective-permute-done | bytes 262176 | tf_op jit(solution)/shard_map/ppermute | solution.py:63
  10.5 0.8 broadcast_select_fusion
  11.4 20.6 %all-to-all-done = f32[8,64,1024]{2,1,0:T(8,128)} async-done(((f32[8,64,1024]{2,1,0:T(8,128)}), f32[8,64,1024]{2,1,0:T(8,128)}, u32[]{:S(2)}, u32[]{:S(2)}) %all-to-all-start) | async-done | bytes 2097184 | tf_op jit(solution)/shard_map/all_to_all | solution.py:167
  32.0 1.1 %slice_bitcast_fusion = (f32[64,1024]{1,0:T(8,128)S(1)}, f32[64,1024]{1,0:T(8,128)S(1)}) fusion(f32[8,64,1024]{2,1,0:T(8,128)} %all-to-all-done, u32[]{:T(128)S(6)} %convert_element_type.21), kind=kLoop, calls=%fused_computation.4 | loop fusion | bytes 1048580 | tf_op jit(solution)/shard_map/squeeze | solution.py:201
  33.1 1.3 %collective-permute-start.20 = (f32[64,1024]{1,0:T(8,128)S(1)}, f32[64,1024]{1,0:T(8,128)S(1)}, u32[]{:S(2)}, u32[]{:S(2)}) collective-permute-start(f32[64,1024]{1,0:T(8,128)S(1)} %get-tuple-element.27), channel_id=1, source_target_pairs={{56,16},{57,17},{58,18},{59,19},{60,20},{61,21},{62,22},{63,23},{1... | collective-permute-start | bytes 786440 | tf_op jit(solution)/shard_map/ppermute | solution.py:28
  35.1 15.6 %conditional.1 = (f32[64,1024]{1,0:T(8,128)}, f32[64,1024]{1,0:T(8,128)}) conditional(s32[]{:T(128)} %clamp.3, f32[64,1024]{1,0:T(8,128)S(1)} %get-tuple-element.28, f32[64,1024]{1,0:T(8,128)S(1)} %get-tuple-element.28, f32[64,1024]{1,0:T(8,128)S(1)} %get-tuple-element.28, ...), branch_computations={%region_0.1_spmd, %region_1.2_spmd, %region_2.3_spmd, %region_3.4_... | conditional | bytes 2097248 | solution.py:204
  35.2 1.3 %collective-permute-start.14 = (f32[64,1024]{1,0:T(8,128)S(1)}, f32[64,1024]{1,0:T(8,128)}, u32[]{:S(2)}, u32[]{:S(2)}) collective-permute-start(f32[64,1024]{1,0:T(8,128)S(1)} %param.7), channel_id=1, source_target_pairs={{56,16},{57,17},{58,18},{59,19},{60,20},{61,21},{62,22},{63,23},{1... | collective-permute-start | bytes 786440 | tf_op jit(solution)/shard_map/cond/branch_7_fun/ppermute | solution.py:28
  36.5 1.4 %collective-permute-start.15 = (f32[64,1024]{1,0:T(8,128)S(1)}, f32[64,1024]{1,0:T(8,128)}, u32[]{:S(2)}, u32[]{:S(2)}) collective-permute-start(f32[64,1024]{1,0:T(8,128)S(1)} %param.7), channel_id=1, source_target_pairs={{56,32},{57,33},{58,34},{59,35},{60,36},{61,37},{62,38},{63,39},{1... | collective-permute-start | bytes 786440 | tf_op jit(solution)/shard_map/cond/branch_7_fun/ppermute | solution.py:29
  37.8 12.9 %collective-permute-done.14 = f32[64,1024]{1,0:T(8,128)} collective-permute-done((f32[64,1024]{1,0:T(8,128)S(1)}, f32[64,1024]{1,0:T(8,128)}, u32[]{:S(2)}, u32[]{:S(2)}) %collective-permute-start.14) | collective-permute-done | bytes 262176 | tf_op jit(solution)/shard_map/cond/branch_7_fun/ppermute | solution.py:28
  50.7 1.0 select_select_fusion.3
  51.9 2.0 %collective-permute-start.19 = (f32[64,1024]{1,0:T(8,128)S(1)}, f32[64,1024]{1,0:T(8,128)}, u32[]{:S(2)}, u32[]{:S(2)}) collective-permute-start(f32[64,1024]{1,0:T(8,128)S(1)} %select_select_fusion.3), channel_id=1, source_target_pairs={{0,56},{8,0},{16,8},{24,16},{32,24},{40,32},{48,40},{56,48},{1,57}... | collective-permute-start | bytes 786440 | tf_op jit(solution)/shard_map/ppermute | solution.py:44
  53.9 1.0 select_select_fusion.1
  54.9 5.0 %collective-permute-start.22 = (f32[64,1024]{1,0:T(8,128)S(1)}, f32[64,1024]{1,0:T(8,128)}, u32[]{:S(2)}, u32[]{:S(2)}) collective-permute-start(f32[64,1024]{1,0:T(8,128)S(1)} %select_select_fusion.1), channel_id=1, source_target_pairs={{56,0},{16,24},{32,40},{57,1},{17,25},{33,41},{58,2},{18,26},{34,4... | collective-permute-start | bytes 786440 | tf_op jit(solution)/shard_map/ppermute | solution.py:43
  59.9 2.0 %collective-permute-start.23 = (f32[64,1024]{1,0:T(8,128)S(1)}, f32[64,1024]{1,0:T(8,128)}, u32[]{:S(2)}, u32[]{:S(2)}) collective-permute-start(f32[64,1024]{1,0:T(8,128)S(1)} %select_select_fusion.1), channel_id=1, source_target_pairs={{56,48},{16,8},{57,49},{17,9},{58,50},{18,10},{59,51},{19,11},{60,... | collective-permute-start | bytes 786440 | tf_op jit(solution)/shard_map/ppermute | solution.py:44
  62.1 2.4 %collective-permute-start.17 = (f32[8,64,128]{2,1,0:T(8,128)}, f32[8,64,128]{2,1,0:T(8,128)}, u32[]{:S(2)}, u32[]{:S(2)}) collective-permute-start(f32[8,64,128]{2,1,0:T(8,128)} %broadcast_select_fusion), channel_id=1, source_target_pairs={{0,2},{2,0},{1,3},{3,1},{4,6},{6,4},{5,7},{7,5},{8,10},{10,8},{9,1... | collective-permute-start | bytes 786440 | tf_op jit(solution)/shard_map/ppermute | solution.py:63
  64.5 2.2 %collective-permute-start.24 = (f32[64,1024]{1,0:T(8,128)S(1)}, f32[64,1024]{1,0:T(8,128)S(1)}, u32[]{:S(2)}, u32[]{:S(2)}) collective-permute-start(f32[64,1024]{1,0:T(8,128)S(1)} %select_select_fusion.2.refs_0_), channel_id=1, source_target_pairs={{0,4},{4,0},{1,5},{5,1},{2,6},{6,2},{3,7},{7,3},{8,12},{12,8},{9,1... | collective-permute-start | bytes 786440 | tf_op jit(solution)/shard_map/ppermute | solution.py:177
  67.2 2.8 %collective-permute-start.34 = (f32[64,1024]{1,0:T(8,128)S(1)}, f32[64,1024]{1,0:T(8,128)S(1)}, u32[]{:S(2)}, u32[]{:S(2)}) collective-permute-start(f32[64,1024]{1,0:T(8,128)S(1)} %select_select_fusion.2.refs_0_), channel_id=1, source_target_pairs={{0,192},{64,0},{128,64},{192,128},{1,193},{65,1},{129,65},{193,129... | collective-permute-start | bytes 786440 | tf_op jit(solution)/shard_map/ppermute | solution.py:177
  69.9 1.0 select_select_fusion.refs_1_
  71.3 2.0 %collective-permute-done.17 = f32[8,64,128]{2,1,0:T(8,128)} collective-permute-done((f32[8,64,128]{2,1,0:T(8,128)}, f32[8,64,128]{2,1,0:T(8,128)}, u32[]{:S(2)}, u32[]{:S(2)}) %collective-permute-start.17) | collective-permute-done | bytes 262176 | tf_op jit(solution)/shard_map/ppermute | solution.py:63
  73.2 1.5 %collective-permute-start.32 = (f32[64,1024]{1,0:T(8,128)S(1)}, f32[64,1024]{1,0:T(8,128)}, u32[]{:S(2)}, u32[]{:S(2)}) collective-permute-start(f32[64,1024]{1,0:T(8,128)S(1)} %select_select_fusion.refs_1_), channel_id=1, source_target_pairs={{0,4},{4,0},{1,5},{5,1},{2,6},{6,2},{3,7},{7,3},{8,12},{12,8},{9,1... | collective-permute-start | bytes 786440 | tf_op jit(solution)/shard_map/ppermute | solution.py:177
  74.7 4.0 %collective-permute-done.24.refs_2_ = f32[64,1024]{1,0:T(8,128)S(1)} collective-permute-done((f32[64,1024]{1,0:T(8,128)S(1)}, f32[64,1024]{1,0:T(8,128)S(1)}, u32[]{:S(2)}, u32[]{:S(2)}) %collective-permute-start.24) | collective-permute-done | bytes 262176 | tf_op jit(solution)/shard_map/ppermute | solution.py:177
  78.7 1.2 %collective-permute-start.35 = (f32[64,1024]{1,0:T(8,128)S(1)}, f32[64,1024]{1,0:T(8,128)}, u32[]{:S(2)}, u32[]{:S(2)}) collective-permute-start(f32[64,1024]{1,0:T(8,128)S(1)} %select_select_fusion.refs_1_), channel_id=1, source_target_pairs={{0,192},{64,0},{128,64},{192,128},{1,193},{65,1},{129,65},{193,129... | collective-permute-start | bytes 786440 | tf_op jit(solution)/shard_map/ppermute | solution.py:177
  80.2 1.8 %collective-permute-start.31 = (f32[64,1024]{1,0:T(8,128)S(1)}, f32[64,1024]{1,0:T(8,128)}, u32[]{:S(2)}, u32[]{:S(2)}) collective-permute-start(f32[64,1024]{1,0:T(8,128)S(1)} %collective-permute-done.30.refs_4_), channel_id=1, source_target_pairs={{0,64},{64,128},{128,192},{192,0},{1,65},{65,129},{129,193},{193,1... | collective-permute-start | bytes 786440 | tf_op jit(solution)/shard_map/ppermute | solution.py:177
  82.0 0.8 collective-permute-start.28
  82.8 1.1 %broadcast_select_fusion.1 = f32[8,64,128]{2,1,0:T(8,128)S(1)} fusion(f32[8,64,128]{2,1,0:T(8,128)} %broadcast_select_fusion, f32[8,64,128]{2,1,0:T(8,128)} %collective-permute-done.17, pred[128]{0:T(512)(128)(4,1)S(1)} %fusion.1), kind=kLoop, calls=%fused_computation.11 | loop fusion | flops 65536 | bytes 786560 | tf_op jit(solution)/shard_map/jit(_where)/select_n | solution.py:65
  84.2 2.4 %collective-permute-done.35.refs_9_ = f32[64,1024]{1,0:T(8,128)} collective-permute-done((f32[64,1024]{1,0:T(8,128)S(1)}, f32[64,1024]{1,0:T(8,128)}, u32[]{:S(2)}, u32[]{:S(2)}) %collective-permute-start.35) | collective-permute-done | bytes 262176 | tf_op jit(solution)/shard_map/ppermute | solution.py:177
  86.6 5.6 %collective-permute-done.25.refs_6_ = f32[64,1024]{1,0:T(8,128)} collective-permute-done((f32[64,1024]{1,0:T(8,128)S(1)}, f32[64,1024]{1,0:T(8,128)}, u32[]{:S(2)}, u32[]{:S(2)}) %collective-permute-start.25) | collective-permute-done | bytes 262176 | tf_op jit(solution)/shard_map/ppermute | solution.py:177
  92.2 1.4 %collective-permute-start.33 = (f32[64,1024]{1,0:T(8,128)}, f32[64,1024]{1,0:T(8,128)S(1)}, u32[]{:S(2)}, u32[]{:S(2)}) collective-permute-start(f32[64,1024]{1,0:T(8,128)} %collective-permute-done.32.refs_3_), channel_id=1, source_target_pairs={{0,192},{64,0},{128,64},{192,128},{1,193},{65,1},{129,65},{193,129... | collective-permute-start | bytes 786440 | tf_op jit(solution)/shard_map/ppermute | solution.py:177
  93.9 4.9 %collective-permute-done.33.refs_7_ = f32[64,1024]{1,0:T(8,128)S(1)} collective-permute-done((f32[64,1024]{1,0:T(8,128)}, f32[64,1024]{1,0:T(8,128)S(1)}, u32[]{:S(2)}, u32[]{:S(2)}) %collective-permute-start.33) | collective-permute-done | bytes 262176 | tf_op jit(solution)/shard_map/ppermute | solution.py:177
  98.8 3.1 %shard_map.73.refs_4_ = f32[8,64,1024]{2,1,0:T(8,128)S(1)} custom-call(s32[4]{0:T(128)S(1)} %get-tuple-element.35.bins, f32[2,4,64,1024]{3,2,1,0:T(8,128)S(1)} %copy-done.1, f32[4,128,256]{2,1,0:T(8,128)S(1)} %maximum_select_fusion.l_ref, f32[64,64]{1,0:T(8,128)S(1)} %copy.12.coef_ref, f32[64,1024]{1,0:T(8,128)} %collective-permute-done.31.refs_0_, ...), custom_call_target="tpu_custom_call" | custom-call | flops 603979776 | bytes 6291456 | tf_op jit(solution)/shard_map/pallas_call | solution.py:120
  101.9 2.2 %shard_map.74 = bf16[8,64,1024]{2,1,0:T(8,128)(2,1)} custom-call(s32[4]{0:T(128)S(1)} %get-tuple-element.35.bins, f32[2,4,64,1024]{3,2,1,0:T(8,128)S(1)} %copy-done.1, f32[4,128,256]{2,1,0:T(8,128)S(1)} %maximum_select_fusion.l_ref, f32[64,64]{1,0:T(8,128)S(1)} %copy.12.coef_ref, f32[64,1024]{1,0:T(8,128)S(1)} %select_select_fusion.2.refs_0_, ...), custom_call_target="tpu_custom_call" | custom-call | flops 201326592 | bytes 2097152 | tf_op jit(solution)/shard_map/pallas_call | solution.py:120
  (59 shorter events, 4.0 us)
Async XLA Ops:
  0.0 9.1 %copy-start = (f32[64,64]{1,0:T(8,128)S(1)}, f32[64,64]{1,0:T(8,128)}, u32[]{:S(2)}) copy-start(f32[64,64]{1,0:T(8,128)} %param.17) | copy-start | bytes 49156
  0.0 8.6 %copy-start.1 = (f32[2,4,64,1024]{3,2,1,0:T(8,128)S(1)}, f32[2,4,64,1024]{3,2,1,0:T(8,128)}, u32[]{:S(2)}) copy-start(f32[2,4,64,1024]{3,2,1,0:T(8,128)} %x_ref.3) | copy-start | bytes 6291460
  0.0 9.0 %copy-start.6 = (s32[64]{0:T(128)S(1)}, s32[64]{0:T(128)}, u32[]{:S(2)}) copy-start(s32[64]{0:T(128)} %param.18) | copy-start | bytes 772
  0.0 9.1 %copy-start.4 = (f32[64,4]{1,0:T(8,128)S(1)}, f32[64,4]{1,0:T(8,128)}, u32[]{:S(2)}) copy-start(f32[64,4]{1,0:T(8,128)} %constant.61.clone) | copy-start | bytes 3076
  0.0 32.0 %all-to-all-start = ((f32[8,64,1024]{2,1,0:T(8,128)}), f32[8,64,1024]{2,1,0:T(8,128)}, u32[]{:S(2)}, u32[]{:S(2)}) async-start(f32[8,64,1024]{2,1,0:T(8,128)} %bitcast.14), calls=%async_computation | async-start | bytes 4194304 | tf_op jit(solution)/shard_map/all_to_all | solution.py:167
  6.1 29.0 %copy-start.7 = (s32[4]{0:T(128)S(1)}, s32[4]{0:T(128)}, u32[]{:S(2)}) copy-start(s32[4]{0:T(128)} %constant.60.clone) | copy-start | bytes 52
  8.9 1.6 %collective-permute-start.16 = (f32[8,64,128]{2,1,0:T(8,128)S(1)}, f32[8,64,128]{2,1,0:T(8,128)S(1)}, u32[]{:S(2)}, u32[]{:S(2)}) collective-permute-start(f32[8,64,128]{2,1,0:T(8,128)S(1)} %pad_maximum_fusion), channel_id=1, source_target_pairs={{0,1},{1,0},{2,3},{3,2},{4,5},{5,4},{6,7},{7,6},{8,9},{9,8},{10,11... | collective-permute-start | bytes 786440 | tf_op jit(solution)/shard_map/ppermute | solution.py:63
  33.1 20.8 %collective-permute-start.20 = (f32[64,1024]{1,0:T(8,128)S(1)}, f32[64,1024]{1,0:T(8,128)S(1)}, u32[]{:S(2)}, u32[]{:S(2)}) collective-permute-start(f32[64,1024]{1,0:T(8,128)S(1)} %get-tuple-element.27), channel_id=1, source_target_pairs={{56,16},{57,17},{58,18},{59,19},{60,20},{61,21},{62,22},{63,23},{1... | collective-permute-start | bytes 786440 | tf_op jit(solution)/shard_map/ppermute | solution.py:28
  34.4 19.5 %collective-permute-start.21 = (f32[64,1024]{1,0:T(8,128)S(1)}, f32[64,1024]{1,0:T(8,128)S(1)}, u32[]{:S(2)}, u32[]{:S(2)}) collective-permute-start(f32[64,1024]{1,0:T(8,128)S(1)} %get-tuple-element.27), channel_id=1, source_target_pairs={{56,32},{57,33},{58,34},{59,35},{60,36},{61,37},{62,38},{63,39},{1... | collective-permute-start | bytes 786440 | tf_op jit(solution)/shard_map/ppermute | solution.py:29
  35.2 15.6 %collective-permute-start.14 = (f32[64,1024]{1,0:T(8,128)S(1)}, f32[64,1024]{1,0:T(8,128)}, u32[]{:S(2)}, u32[]{:S(2)}) collective-permute-start(f32[64,1024]{1,0:T(8,128)S(1)} %param.7), channel_id=1, source_target_pairs={{56,16},{57,17},{58,18},{59,19},{60,20},{61,21},{62,22},{63,23},{1... | collective-permute-start | bytes 786440 | tf_op jit(solution)/shard_map/cond/branch_7_fun/ppermute | solution.py:28
  36.5 14.3 %collective-permute-start.15 = (f32[64,1024]{1,0:T(8,128)S(1)}, f32[64,1024]{1,0:T(8,128)}, u32[]{:S(2)}, u32[]{:S(2)}) collective-permute-start(f32[64,1024]{1,0:T(8,128)S(1)} %param.7), channel_id=1, source_target_pairs={{56,32},{57,33},{58,34},{59,35},{60,36},{61,37},{62,38},{63,39},{1... | collective-permute-start | bytes 786440 | tf_op jit(solution)/shard_map/cond/branch_7_fun/ppermute | solution.py:29
  50.7 20.3 %copy-start.3 = (f32[64,4]{1,0:T(8,128)S(1)}, f32[64,4]{1,0:T(8,128)}, u32[]{:S(2)}) copy-start(f32[64,4]{1,0:T(8,128)} %constant.62.clone) | copy-start | bytes 3076
  51.8 12.7 %collective-permute-start.18 = (f32[64,1024]{1,0:T(8,128)S(1)}, f32[64,1024]{1,0:T(8,128)S(1)}, u32[]{:S(2)}, u32[]{:S(2)}) collective-permute-start(f32[64,1024]{1,0:T(8,128)S(1)} %select_select_fusion.3), channel_id=1, source_target_pairs={{0,8},{8,16},{16,24},{24,32},{32,40},{40,48},{48,56},{56,0},{1,9},... | collective-permute-start | bytes 786440 | tf_op jit(solution)/shard_map/ppermute | solution.py:43
  51.9 12.6 %collective-permute-start.19 = (f32[64,1024]{1,0:T(8,128)S(1)}, f32[64,1024]{1,0:T(8,128)}, u32[]{:S(2)}, u32[]{:S(2)}) collective-permute-start(f32[64,1024]{1,0:T(8,128)S(1)} %select_select_fusion.3), channel_id=1, source_target_pairs={{0,56},{8,0},{16,8},{24,16},{32,24},{40,32},{48,40},{56,48},{1,57}... | collective-permute-start | bytes 786440 | tf_op jit(solution)/shard_map/ppermute | solution.py:44
  54.9 15.1 %copy-start.2 = (f32[64,1024]{1,0:T(8,128)}, f32[64,1024]{1,0:T(8,128)S(1)}, u32[]{:S(2)}) copy-start(f32[64,1024]{1,0:T(8,128)S(1)} %select_select_fusion.1) | copy-start | bytes 786436
  54.9 12.3 %collective-permute-start.22 = (f32[64,1024]{1,0:T(8,128)S(1)}, f32[64,1024]{1,0:T(8,128)}, u32[]{:S(2)}, u32[]{:S(2)}) collective-permute-start(f32[64,1024]{1,0:T(8,128)S(1)} %select_select_fusion.1), channel_id=1, source_target_pairs={{56,0},{16,24},{32,40},{57,1},{17,25},{33,41},{58,2},{18,26},{34,4... | collective-permute-start | bytes 786440 | tf_op jit(solution)/shard_map/ppermute | solution.py:43
  59.9 10.0 %collective-permute-start.23 = (f32[64,1024]{1,0:T(8,128)S(1)}, f32[64,1024]{1,0:T(8,128)}, u32[]{:S(2)}, u32[]{:S(2)}) collective-permute-start(f32[64,1024]{1,0:T(8,128)S(1)} %select_select_fusion.1), channel_id=1, source_target_pairs={{56,48},{16,8},{57,49},{17,9},{58,50},{18,10},{59,51},{19,11},{60,... | collective-permute-start | bytes 786440 | tf_op jit(solution)/shard_map/ppermute | solution.py:44
  62.1 11.1 %collective-permute-start.17 = (f32[8,64,128]{2,1,0:T(8,128)}, f32[8,64,128]{2,1,0:T(8,128)}, u32[]{:S(2)}, u32[]{:S(2)}) collective-permute-start(f32[8,64,128]{2,1,0:T(8,128)} %broadcast_select_fusion), channel_id=1, source_target_pairs={{0,2},{2,0},{1,3},{3,1},{4,6},{6,4},{5,7},{7,5},{8,10},{10,8},{9,1... | collective-permute-start | bytes 786440 | tf_op jit(solution)/shard_map/ppermute | solution.py:63
  64.5 14.1 %collective-permute-start.24 = (f32[64,1024]{1,0:T(8,128)S(1)}, f32[64,1024]{1,0:T(8,128)S(1)}, u32[]{:S(2)}, u32[]{:S(2)}) collective-permute-start(f32[64,1024]{1,0:T(8,128)S(1)} %select_select_fusion.2.refs_0_), channel_id=1, source_target_pairs={{0,4},{4,0},{1,5},{5,1},{2,6},{6,2},{3,7},{7,3},{8,12},{12,8},{9,1... | collective-permute-start | bytes 786440 | tf_op jit(solution)/shard_map/ppermute | solution.py:177
  66.7 13.2 %collective-permute-start.30 = (f32[64,1024]{1,0:T(8,128)S(1)}, f32[64,1024]{1,0:T(8,128)S(1)}, u32[]{:S(2)}, u32[]{:S(2)}) collective-permute-start(f32[64,1024]{1,0:T(8,128)S(1)} %select_select_fusion.2.refs_0_), channel_id=1, source_target_pairs={{0,64},{64,128},{128,192},{192,0},{1,65},{65,129},{129,193},{193,1... | collective-permute-start | bytes 786440 | tf_op jit(solution)/shard_map/ppermute | solution.py:177
  67.2 13.0 %collective-permute-start.34 = (f32[64,1024]{1,0:T(8,128)S(1)}, f32[64,1024]{1,0:T(8,128)S(1)}, u32[]{:S(2)}, u32[]{:S(2)}) collective-permute-start(f32[64,1024]{1,0:T(8,128)S(1)} %select_select_fusion.2.refs_0_), channel_id=1, source_target_pairs={{0,192},{64,0},{128,64},{192,128},{1,193},{65,1},{129,65},{193,129... | collective-permute-start | bytes 786440 | tf_op jit(solution)/shard_map/ppermute | solution.py:177
  70.9 11.0 %collective-permute-start.27 = (f32[64,1024]{1,0:T(8,128)S(1)}, f32[64,1024]{1,0:T(8,128)}, u32[]{:S(2)}, u32[]{:S(2)}) collective-permute-start(f32[64,1024]{1,0:T(8,128)S(1)} %select_select_fusion.refs_1_), channel_id=1, source_target_pairs={{0,64},{64,128},{128,192},{192,0},{1,65},{65,129},{129,193},{193,1... | collective-permute-start | bytes 786440 | tf_op jit(solution)/shard_map/ppermute | solution.py:177
  73.2 10.7 %collective-permute-start.32 = (f32[64,1024]{1,0:T(8,128)S(1)}, f32[64,1024]{1,0:T(8,128)}, u32[]{:S(2)}, u32[]{:S(2)}) collective-permute-start(f32[64,1024]{1,0:T(8,128)S(1)} %select_select_fusion.refs_1_), channel_id=1, source_target_pairs={{0,4},{4,0},{1,5},{5,1},{2,6},{6,2},{3,7},{7,3},{8,12},{12,8},{9,1... | collective-permute-start | bytes 786440 | tf_op jit(solution)/shard_map/ppermute | solution.py:177
  78.7 7.9 %collective-permute-start.35 = (f32[64,1024]{1,0:T(8,128)S(1)}, f32[64,1024]{1,0:T(8,128)}, u32[]{:S(2)}, u32[]{:S(2)}) collective-permute-start(f32[64,1024]{1,0:T(8,128)S(1)} %select_select_fusion.refs_1_), channel_id=1, source_target_pairs={{0,192},{64,0},{128,64},{192,128},{1,193},{65,1},{129,65},{193,129... | collective-permute-start | bytes 786440 | tf_op jit(solution)/shard_map/ppermute | solution.py:177
  79.9 12.2 %collective-permute-start.25 = (f32[64,1024]{1,0:T(8,128)S(1)}, f32[64,1024]{1,0:T(8,128)}, u32[]{:S(2)}, u32[]{:S(2)}) collective-permute-start(f32[64,1024]{1,0:T(8,128)S(1)} %collective-permute-done.24.refs_2_), channel_id=1, source_target_pairs={{0,192},{64,0},{128,64},{192,128},{1,193},{65,1},{129,65},{193,129... | collective-permute-start | bytes 786440 | tf_op jit(solution)/shard_map/ppermute | solution.py:177
  80.2 13.4 %collective-permute-start.31 = (f32[64,1024]{1,0:T(8,128)S(1)}, f32[64,1024]{1,0:T(8,128)}, u32[]{:S(2)}, u32[]{:S(2)}) collective-permute-start(f32[64,1024]{1,0:T(8,128)S(1)} %collective-permute-done.30.refs_4_), channel_id=1, source_target_pairs={{0,64},{64,128},{128,192},{192,0},{1,65},{65,129},{129,193},{193,1... | collective-permute-start | bytes 786440 | tf_op jit(solution)/shard_map/ppermute | solution.py:177
  82.0 11.7 %collective-permute-start.28 = (f32[64,1024]{1,0:T(8,128)}, f32[64,1024]{1,0:T(8,128)}, u32[]{:S(2)}, u32[]{:S(2)}) collective-permute-start(f32[64,1024]{1,0:T(8,128)} %collective-permute-done.27.refs_5_), channel_id=1, source_target_pairs={{0,64},{64,128},{128,192},{192,0},{1,65},{65,129},{129,193},{193,1... | collective-permute-start | bytes 786440 | tf_op jit(solution)/shard_map/ppermute | solution.py:177
  83.9 10.0 %collective-permute-start.36 = (f32[64,1024]{1,0:T(8,128)S(1)}, f32[64,1024]{1,0:T(8,128)S(1)}, u32[]{:S(2)}, u32[]{:S(2)}) collective-permute-start(f32[64,1024]{1,0:T(8,128)S(1)} %collective-permute-done.30.refs_4_), channel_id=1, source_target_pairs={{0,4},{4,0},{1,5},{5,1},{2,6},{6,2},{3,7},{7,3},{8,12},{12,8},{9,1... | collective-permute-start | bytes 786440 | tf_op jit(solution)/shard_map/ppermute | solution.py:177
  86.6 12.2 %collective-permute-start.37 = (f32[64,1024]{1,0:T(8,128)}, f32[64,1024]{1,0:T(8,128)S(1)}, u32[]{:S(2)}, u32[]{:S(2)}) collective-permute-start(f32[64,1024]{1,0:T(8,128)} %collective-permute-done.27.refs_5_), channel_id=1, source_target_pairs={{0,4},{4,0},{1,5},{5,1},{2,6},{6,2},{3,7},{7,3},{8,12},{12,8},{9,1... | collective-permute-start | bytes 786440 | tf_op jit(solution)/shard_map/ppermute | solution.py:177
  92.2 6.6 %collective-permute-start.33 = (f32[64,1024]{1,0:T(8,128)}, f32[64,1024]{1,0:T(8,128)S(1)}, u32[]{:S(2)}, u32[]{:S(2)}) collective-permute-start(f32[64,1024]{1,0:T(8,128)} %collective-permute-done.32.refs_3_), channel_id=1, source_target_pairs={{0,192},{64,0},{128,64},{192,128},{1,193},{65,1},{129,65},{193,129... | collective-permute-start | bytes 786440 | tf_op jit(solution)/shard_map/ppermute | solution.py:177
  93.6 8.3 %collective-permute-start.26 = (f32[64,1024]{1,0:T(8,128)}, f32[64,1024]{1,0:T(8,128)S(1)}, u32[]{:S(2)}, u32[]{:S(2)}) collective-permute-start(f32[64,1024]{1,0:T(8,128)} %collective-permute-done.25.refs_6_), channel_id=1, source_target_pairs={{0,192},{64,0},{128,64},{192,128},{1,193},{65,1},{129,65},{193,129... | collective-permute-start | bytes 786440 | tf_op jit(solution)/shard_map/ppermute | solution.py:177
  93.6 8.3 %collective-permute-start.29 = (f32[64,1024]{1,0:T(8,128)}, f32[64,1024]{1,0:T(8,128)S(1)}, u32[]{:S(2)}, u32[]{:S(2)}) collective-permute-start(f32[64,1024]{1,0:T(8,128)} %collective-permute-done.28.refs_1_), channel_id=1, source_target_pairs={{0,4},{4,0},{1,5},{5,1},{2,6},{6,2},{3,7},{7,3},{8,12},{12,8},{9,1... | collective-permute-start | bytes 786440 | tf_op jit(solution)/shard_map/ppermute | solution.py:177
  (1 other events, 6.1 us)

commit v10 on v9

--- a/solution.py
+++ b/solution.py
@@ -199,12 +199,14 @@
     spot = (oy * 4 + ((ox + 2 * oy) & 3)).astype(jnp.uint32)
     mine = lax.dynamic_index_in_dim(arrived, spot, 0, keepdims=False)
     last = arrived[ly * 4 + (lx + 2 * ly) % 4]
+    branches = [lambda v, r=r: leap(v, r) for r in range(8)]
+    leapt = lax.switch(oz, branches, mine)
+    leapt, last = lax.optimization_barrier((leapt, last))
+    mine = land(mine, leapt, oz, z)
     last = land(last, leap(last, lz), lz, z)
-    branches = [lambda v, r=r: leap(v, r) for r in range(8)]
-    mine = land(mine, lax.switch(oz, branches, mine), oz, z)
     mine, strip = lax.optimization_barrier((mine, strip))
     strip = swap(strip, other, "yh").reshape(2, FREQ, ROWS, 2 * ROWS)
-    last, mine = exchange([steps(last, lz, z, True), steps(mine, oz, z, False)])
+    mine, last = exchange([steps(mine, oz, z, False), steps(last, lz, z, True)])
     blocks = [v for pair in zip(mine, last) for v in pair]
     bins = (x + 2 * yl + jnp.array([0, 2, 3, 1], jnp.int32)) & 3
     left, coefs = tables(filters, offsets, strip, bins, yl)

time: 103 us -> 105 us (1.019)
  the two profiles are of different devices: /device:TPU:72 before, /device:TPU:70 now
where the time goes in v10:
time: 105 us; the launch traced here: 107 us
  starting transfers between devices  57 us (54%)
  waiting for transfers between devices  33.8 us (32%)
  other arithmetic  5.47 us (5%)
  Pallas kernels  5.33 us (5%)
  local copies, waits for them, and re-layouts  2.73 us (3%)
  between operations  2.17 us (2%)
    ppermute x2, starting transfers between devices, steps(): after = lax.ppermute(held, 'z', pairs(1, (0, 3, 5)))  24.2 us
    all_to_all x1, waiting for transfers between devices, scatter(): lax.all_to_all(rows, ('x', 'yl'), 0, 0, axis_index_groups=[members], tile...  20.1 us
    ppermute x14, starting transfers between devices, send(): return lax.ppermute(v, axis, pairs)  16.4 us
    ppermute x14, waiting for transfers between devices, send(): return lax.ppermute(v, axis, pairs)  10.9 us
    all_to_all x1, starting transfers between devices, scatter(): lax.all_to_all(rows, ('x', 'yl'), 0, 0, axis_index_groups=[members], tile...  6.06 us
    pallas_call x2, Pallas kernels, call(): pl.pallas_call(body, in_specs=[pl.BlockSpec(memory_space=pltpu.SMEM), *[v...  5.33 us
    ppermute x2, starting transfers between devices, swap(): other = lax.ppermute(block, axis, [(0, 1), (1, 0)])  3.08 us
    ppermute x2, waiting for transfers between devices, swap(): other = lax.ppermute(block, axis, [(0, 1), (1, 0)])  2.82 us
  transfers between devices with their start and end apart: 25, of which 8 were waited for; matrix products, arithmetic and copies ran while one was open for 6% of the time, Pallas kernels for 3%

profile of v10, /device:TPU:70, one launch (start us, length us, event | category | flops | bytes accessed | tf_op | source)
XLA Modules:
  0.0 107.0 jit_solution(8499019051695191165)
XLA Ops:
  0.0 6.1 %all-to-all-start = ((f32[8,64,1024]{2,1,0:T(8,128)}), f32[8,64,1024]{2,1,0:T(8,128)}, u32[]{:S(2)}, u32[]{:S(2)}) async-start(f32[8,64,1024]{2,1,0:T(8,128)} %bitcast.12), calls=%async_computation | async-start | bytes 4194304 | tf_op jit(solution)/shard_map/all_to_all | solution.py:167
  9.4 1.2 %collective-permute-done.16 = f32[8,64,128]{2,1,0:T(8,128)S(1)} collective-permute-done((f32[8,64,128]{2,1,0:T(8,128)S(1)}, f32[8,64,128]{2,1,0:T(8,128)S(1)}, u32[]{:S(2)}, u32[]{:S(2)}) %collective-permute-start.16) | collective-permute-done | bytes 262176 | tf_op jit(solution)/shard_map/ppermute | solution.py:63
  11.5 20.1 %all-to-all-done = f32[8,64,1024]{2,1,0:T(8,128)} async-done(((f32[8,64,1024]{2,1,0:T(8,128)}), f32[8,64,1024]{2,1,0:T(8,128)}, u32[]{:S(2)}, u32[]{:S(2)}) %all-to-all-start) | async-done | bytes 2097184 | tf_op jit(solution)/shard_map/all_to_all | solution.py:167
  31.6 1.1 slice_bitcast_fusion
  32.7 2.8 %conditional.1 = (f32[64,1024]{1,0:T(8,128)}, f32[64,1024]{1,0:T(8,128)}) conditional(s32[]{:T(128)} %clamp.3, f32[64,1024]{1,0:T(8,128)S(1)} %get-tuple-element.34, f32[64,1024]{1,0:T(8,128)S(1)} %get-tuple-element.34, f32[64,1024]{1,0:T(8,128)S(1)} %get-tuple-element.34, ...), branch_computations={%region_0.1_spmd, %region_1.2_spmd, %region_2.3_spmd, %region_3.4_... | conditional | bytes 2097248 | solution.py:203
  32.7 1.4 %collective-permute-start.12 = (f32[64,1024]{1,0:T(8,128)S(1)}, f32[64,1024]{1,0:T(8,128)}, u32[]{:S(2)}, u32[]{:S(2)}) collective-permute-start(f32[64,1024]{1,0:T(8,128)S(1)} %param.6), channel_id=1, source_target_pairs={{48,8},{49,9},{50,10},{51,11},{52,12},{53,13},{54,14},{55,15},{112... | collective-permute-start | bytes 786440 | tf_op jit(solution)/shard_map/cond/branch_6_fun/ppermute | solution.py:28
  34.1 1.3 %collective-permute-start.13 = (f32[64,1024]{1,0:T(8,128)S(1)}, f32[64,1024]{1,0:T(8,128)}, u32[]{:S(2)}, u32[]{:S(2)}) collective-permute-start(f32[64,1024]{1,0:T(8,128)S(1)} %param.6), channel_id=1, source_target_pairs={{48,24},{49,25},{50,26},{51,27},{52,28},{53,29},{54,30},{55,31},{1... | collective-permute-start | bytes 786440 | tf_op jit(solution)/shard_map/cond/branch_6_fun/ppermute | solution.py:29
  35.4 1.3 %collective-permute-start.20 = (f32[64,1024]{1,0:T(8,128)S(1)}, f32[64,1024]{1,0:T(8,128)S(1)}, u32[]{:S(2)}, u32[]{:S(2)}) collective-permute-start(f32[64,1024]{1,0:T(8,128)S(1)} %get-tuple-element.30), channel_id=1, source_target_pairs={{56,16},{57,17},{58,18},{59,19},{60,20},{61,21},{62,22},{63,23},{1... | collective-permute-start | bytes 786440 | tf_op jit(solution)/shard_map/ppermute | solution.py:28
  36.7 1.4 %collective-permute-start.21 = (f32[64,1024]{1,0:T(8,128)S(1)}, f32[64,1024]{1,0:T(8,128)}, u32[]{:S(2)}, u32[]{:S(2)}) collective-permute-start(f32[64,1024]{1,0:T(8,128)S(1)} %get-tuple-element.30), channel_id=1, source_target_pairs={{56,32},{57,33},{58,34},{59,35},{60,36},{61,37},{62,38},{63,39},{1... | collective-permute-start | bytes 786440 | tf_op jit(solution)/shard_map/ppermute | solution.py:29
  38.1 1.0 select_select_fusion.3
  39.1 19.5 %collective-permute-start.18 = (f32[64,1024]{1,0:T(8,128)S(1)}, f32[64,1024]{1,0:T(8,128)S(1)}, u32[]{:S(2)}, u32[]{:S(2)}) collective-permute-start(f32[64,1024]{1,0:T(8,128)S(1)} %select_select_fusion.3), channel_id=1, source_target_pairs={{0,8},{8,16},{16,24},{24,32},{32,40},{40,48},{48,56},{56,0},{1,9},... | collective-permute-start | bytes 786440 | tf_op jit(solution)/shard_map/ppermute | solution.py:43
  59.3 1.0 select_select_fusion.1
  60.4 4.6 %collective-permute-start.22 = (f32[64,1024]{1,0:T(8,128)S(1)}, f32[64,1024]{1,0:T(8,128)}, u32[]{:S(2)}, u32[]{:S(2)}) collective-permute-start(f32[64,1024]{1,0:T(8,128)S(1)} %select_select_fusion.1), channel_id=1, source_target_pairs={{56,0},{16,24},{32,40},{57,1},{17,25},{33,41},{58,2},{18,26},{34,4... | collective-permute-start | bytes 786440 | tf_op jit(solution)/shard_map/ppermute | solution.py:43
  65.0 2.0 %collective-permute-start.23 = (f32[64,1024]{1,0:T(8,128)S(1)}, f32[64,1024]{1,0:T(8,128)}, u32[]{:S(2)}, u32[]{:S(2)}) collective-permute-start(f32[64,1024]{1,0:T(8,128)S(1)} %select_select_fusion.1), channel_id=1, source_target_pairs={{56,48},{16,8},{57,49},{17,9},{58,50},{18,10},{59,51},{19,11},{60,... | collective-permute-start | bytes 786440 | tf_op jit(solution)/shard_map/ppermute | solution.py:44
  67.1 3.0 %collective-permute-start.17 = (f32[8,64,128]{2,1,0:T(8,128)}, f32[8,64,128]{2,1,0:T(8,128)}, u32[]{:S(2)}, u32[]{:S(2)}) collective-permute-start(f32[8,64,128]{2,1,0:T(8,128)} %broadcast_select_fusion), channel_id=1, source_target_pairs={{0,2},{2,0},{1,3},{3,1},{4,6},{6,4},{5,7},{7,5},{8,10},{10,8},{9,1... | collective-permute-start | bytes 786440 | tf_op jit(solution)/shard_map/ppermute | solution.py:63
  70.2 2.1 %collective-permute-start.24 = (f32[64,1024]{1,0:T(8,128)S(1)}, f32[64,1024]{1,0:T(8,128)S(1)}, u32[]{:S(2)}, u32[]{:S(2)}) collective-permute-start(f32[64,1024]{1,0:T(8,128)S(1)} %select_select_fusion.2.refs_0_), channel_id=1, source_target_pairs={{0,64},{64,128},{128,192},{192,0},{1,65},{65,129},{129,193},{193,1... | collective-permute-start | bytes 786440 | tf_op jit(solution)/shard_map/ppermute | solution.py:177
  72.3 1.0 select_select_fusion.refs_1_
  73.3 2.1 %collective-permute-start.27 = (f32[64,1024]{1,0:T(8,128)S(1)}, f32[64,1024]{1,0:T(8,128)}, u32[]{:S(2)}, u32[]{:S(2)}) collective-permute-start(f32[64,1024]{1,0:T(8,128)S(1)} %select_select_fusion.refs_1_), channel_id=1, source_target_pairs={{0,4},{4,0},{1,5},{5,1},{2,6},{6,2},{3,7},{7,3},{8,12},{12,8},{9,1... | collective-permute-start | bytes 786440 | tf_op jit(solution)/shard_map/ppermute | solution.py:177
  75.6 1.6 %collective-permute-done.17 = f32[8,64,128]{2,1,0:T(8,128)} collective-permute-done((f32[8,64,128]{2,1,0:T(8,128)}, f32[8,64,128]{2,1,0:T(8,128)}, u32[]{:S(2)}, u32[]{:S(2)}) %collective-permute-start.17) | collective-permute-done | bytes 262176 | tf_op jit(solution)/shard_map/ppermute | solution.py:63
  77.2 1.7 %collective-permute-start.30 = (f32[64,1024]{1,0:T(8,128)S(1)}, f32[64,1024]{1,0:T(8,128)}, u32[]{:S(2)}, u32[]{:S(2)}) collective-permute-start(f32[64,1024]{1,0:T(8,128)S(1)} %select_select_fusion.refs_1_), channel_id=1, source_target_pairs={{0,64},{64,128},{128,192},{192,0},{1,65},{65,129},{129,193},{193,1... | collective-permute-start | bytes 786440 | tf_op jit(solution)/shard_map/ppermute | solution.py:177
  79.2 2.8 %collective-permute-done.32.refs_2_ = f32[64,1024]{1,0:T(8,128)S(1)} collective-permute-done((f32[64,1024]{1,0:T(8,128)S(1)}, f32[64,1024]{1,0:T(8,128)S(1)}, u32[]{:S(2)}, u32[]{:S(2)}) %collective-permute-start.32) | collective-permute-done | bytes 262176 | tf_op jit(solution)/shard_map/ppermute | solution.py:177
  82.0 0.9 collective-permute-start.25
  83.0 1.1 %collective-permute-start.33 = (f32[64,1024]{1,0:T(8,128)S(1)}, f32[64,1024]{1,0:T(8,128)}, u32[]{:S(2)}, u32[]{:S(2)}) collective-permute-start(f32[64,1024]{1,0:T(8,128)S(1)} %collective-permute-done.32.refs_2_), channel_id=1, source_target_pairs={{0,192},{64,0},{128,64},{192,128},{1,193},{65,1},{129,65},{193,129... | collective-permute-start | bytes 786440 | tf_op jit(solution)/shard_map/ppermute | solution.py:177
  84.1 3.6 %collective-permute-done.27.refs_3_ = f32[64,1024]{1,0:T(8,128)} collective-permute-done((f32[64,1024]{1,0:T(8,128)S(1)}, f32[64,1024]{1,0:T(8,128)}, u32[]{:S(2)}, u32[]{:S(2)}) %collective-permute-start.27) | collective-permute-done | bytes 262176 | tf_op jit(solution)/shard_map/ppermute | solution.py:177
  87.8 1.1 broadcast_select_fusion.1
  88.9 2.9 %collective-permute-start.36 = (f32[64,1024]{1,0:T(8,128)S(1)}, f32[64,1024]{1,0:T(8,128)S(1)}, u32[]{:S(2)}, u32[]{:S(2)}) collective-permute-start(f32[64,1024]{1,0:T(8,128)S(1)} %collective-permute-done.24.refs_4_), channel_id=1, source_target_pairs={{0,4},{4,0},{1,5},{5,1},{2,6},{6,2},{3,7},{7,3},{8,12},{12,8},{9,1... | collective-permute-start | bytes 786440 | tf_op jit(solution)/shard_map/ppermute | solution.py:177
  91.7 3.2 %collective-permute-start.31 = (f32[64,1024]{1,0:T(8,128)}, f32[64,1024]{1,0:T(8,128)S(1)}, u32[]{:S(2)}, u32[]{:S(2)}) collective-permute-start(f32[64,1024]{1,0:T(8,128)} %collective-permute-done.30.refs_5_), channel_id=1, source_target_pairs={{0,64},{64,128},{128,192},{192,0},{1,65},{65,129},{129,193},{193,1... | collective-permute-start | bytes 786440 | tf_op jit(solution)/shard_map/ppermute | solution.py:177
  95.0 1.9 %collective-permute-start.26 = (f32[64,1024]{1,0:T(8,128)}, f32[64,1024]{1,0:T(8,128)S(1)}, u32[]{:S(2)}, u32[]{:S(2)}) collective-permute-start(f32[64,1024]{1,0:T(8,128)} %collective-permute-done.25.refs_0_), channel_id=1, source_target_pairs={{0,4},{4,0},{1,5},{5,1},{2,6},{6,2},{3,7},{7,3},{8,12},{12,8},{9,1... | collective-permute-start | bytes 786440 | tf_op jit(solution)/shard_map/ppermute | solution.py:177
  97.2 2.0 %collective-permute-done.31.refs_1_ = f32[64,1024]{1,0:T(8,128)S(1)} collective-permute-done((f32[64,1024]{1,0:T(8,128)}, f32[64,1024]{1,0:T(8,128)S(1)}, u32[]{:S(2)}, u32[]{:S(2)}) %collective-permute-start.31) | collective-permute-done | bytes 262176 | tf_op jit(solution)/shard_map/ppermute | solution.py:177
  99.1 2.4 %collective-permute-done.37.refs_11_ = f32[64,1024]{1,0:T(8,128)S(1)} collective-permute-done((f32[64,1024]{1,0:T(8,128)}, f32[64,1024]{1,0:T(8,128)S(1)}, u32[]{:S(2)}, u32[]{:S(2)}) %collective-permute-start.37) | collective-permute-done | bytes 262176 | tf_op jit(solution)/shard_map/ppermute | solution.py:177
  101.5 3.1 %shard_map.73.refs_4_ = f32[8,64,1024]{2,1,0:T(8,128)S(1)} custom-call(s32[4]{0:T(128)S(1)} %get-tuple-element.41.bins, f32[2,4,64,1024]{3,2,1,0:T(8,128)S(1)} %copy-done.1, f32[4,128,256]{2,1,0:T(8,128)S(1)} %maximum_select_fusion.l_ref, f32[64,64]{1,0:T(8,128)S(1)} %copy.12.coef_ref, f32[64,1024]{1,0:T(8,128)} %collective-permute-done.25.refs_0_, ...), custom_call_target="tpu_custom_call" | custom-call | flops 603979776 | bytes 6291456 | tf_op jit(solution)/shard_map/pallas_call | solution.py:120
  104.8 2.2 %shard_map.74 = bf16[8,64,1024]{2,1,0:T(8,128)(2,1)} custom-call(s32[4]{0:T(128)S(1)} %get-tuple-element.41.bins, f32[2,4,64,1024]{3,2,1,0:T(8,128)S(1)} %copy-done.1, f32[4,128,256]{2,1,0:T(8,128)S(1)} %maximum_select_fusion.l_ref, f32[64,64]{1,0:T(8,128)S(1)} %copy.12.coef_ref, f32[64,1024]{1,0:T(8,128)S(1)} %select_select_fusion.2.refs_0_, ...), custom_call_target="tpu_custom_call" | custom-call | flops 201326592 | bytes 2097152 | tf_op jit(solution)/shard_map/pallas_call | solution.py:120
  (61 shorter events, 4.2 us)
Async XLA Ops:
  0.0 9.2 %copy-start = (f32[64,64]{1,0:T(8,128)S(1)}, f32[64,64]{1,0:T(8,128)}, u32[]{:S(2)}) copy-start(f32[64,64]{1,0:T(8,128)} %param.17) | copy-start | bytes 49156
  0.0 8.6 %copy-start.1 = (f32[2,4,64,1024]{3,2,1,0:T(8,128)S(1)}, f32[2,4,64,1024]{3,2,1,0:T(8,128)}, u32[]{:S(2)}) copy-start(f32[2,4,64,1024]{3,2,1,0:T(8,128)} %x_ref.3) | copy-start | bytes 6291460
  0.0 9.1 %copy-start.7 = (s32[64]{0:T(128)S(1)}, s32[64]{0:T(128)}, u32[]{:S(2)}) copy-start(s32[64]{0:T(128)} %param.18) | copy-start | bytes 772
  0.0 9.2 %copy-start.5 = (f32[64,4]{1,0:T(8,128)S(1)}, f32[64,4]{1,0:T(8,128)}, u32[]{:S(2)}) copy-start(f32[64,4]{1,0:T(8,128)} %constant.61.clone) | copy-start | bytes 3076
  0.0 31.5 %all-to-all-start = ((f32[8,64,1024]{2,1,0:T(8,128)}), f32[8,64,1024]{2,1,0:T(8,128)}, u32[]{:S(2)}, u32[]{:S(2)}) async-start(f32[8,64,1024]{2,1,0:T(8,128)} %bitcast.12), calls=%async_computation | async-start | bytes 4194304 | tf_op jit(solution)/shard_map/all_to_all | solution.py:167
  6.1 32.0 %copy-start.8 = (s32[4]{0:T(128)S(1)}, s32[4]{0:T(128)}, u32[]{:S(2)}) copy-start(s32[4]{0:T(128)} %constant.60.clone) | copy-start | bytes 52
  9.0 1.6 %collective-permute-start.16 = (f32[8,64,128]{2,1,0:T(8,128)S(1)}, f32[8,64,128]{2,1,0:T(8,128)S(1)}, u32[]{:S(2)}, u32[]{:S(2)}) collective-permute-start(f32[8,64,128]{2,1,0:T(8,128)S(1)} %pad_maximum_fusion), channel_id=1, source_target_pairs={{0,1},{1,0},{2,3},{3,2},{4,5},{5,4},{6,7},{7,6},{8,9},{9,8},{10,11... | collective-permute-start | bytes 786440 | tf_op jit(solution)/shard_map/ppermute | solution.py:63
  32.7 2.7 %collective-permute-start.12 = (f32[64,1024]{1,0:T(8,128)S(1)}, f32[64,1024]{1,0:T(8,128)}, u32[]{:S(2)}, u32[]{:S(2)}) collective-permute-start(f32[64,1024]{1,0:T(8,128)S(1)} %param.6), channel_id=1, source_target_pairs={{48,8},{49,9},{50,10},{51,11},{52,12},{53,13},{54,14},{55,15},{112... | collective-permute-start | bytes 786440 | tf_op jit(solution)/shard_map/cond/branch_6_fun/ppermute | solution.py:28
  34.1 1.4 %collective-permute-start.13 = (f32[64,1024]{1,0:T(8,128)S(1)}, f32[64,1024]{1,0:T(8,128)}, u32[]{:S(2)}, u32[]{:S(2)}) collective-permute-start(f32[64,1024]{1,0:T(8,128)S(1)} %param.6), channel_id=1, source_target_pairs={{48,24},{49,25},{50,26},{51,27},{52,28},{53,29},{54,30},{55,31},{1... | collective-permute-start | bytes 786440 | tf_op jit(solution)/shard_map/cond/branch_6_fun/ppermute | solution.py:29
  35.4 23.2 %collective-permute-start.20 = (f32[64,1024]{1,0:T(8,128)S(1)}, f32[64,1024]{1,0:T(8,128)S(1)}, u32[]{:S(2)}, u32[]{:S(2)}) collective-permute-start(f32[64,1024]{1,0:T(8,128)S(1)} %get-tuple-element.30), channel_id=1, source_target_pairs={{56,16},{57,17},{58,18},{59,19},{60,20},{61,21},{62,22},{63,23},{1... | collective-permute-start | bytes 786440 | tf_op jit(solution)/shard_map/ppermute | solution.py:28
  36.7 22.6 %collective-permute-start.21 = (f32[64,1024]{1,0:T(8,128)S(1)}, f32[64,1024]{1,0:T(8,128)}, u32[]{:S(2)}, u32[]{:S(2)}) collective-permute-start(f32[64,1024]{1,0:T(8,128)S(1)} %get-tuple-element.30), channel_id=1, source_target_pairs={{56,32},{57,33},{58,34},{59,35},{60,36},{61,37},{62,38},{63,39},{1... | collective-permute-start | bytes 786440 | tf_op jit(solution)/shard_map/ppermute | solution.py:29
  38.1 37.4 %copy-start.4 = (f32[64,4]{1,0:T(8,128)S(1)}, f32[64,4]{1,0:T(8,128)}, u32[]{:S(2)}) copy-start(f32[64,4]{1,0:T(8,128)} %constant.62.clone) | copy-start | bytes 3076
  39.1 31.0 %collective-permute-start.18 = (f32[64,1024]{1,0:T(8,128)S(1)}, f32[64,1024]{1,0:T(8,128)S(1)}, u32[]{:S(2)}, u32[]{:S(2)}) collective-permute-start(f32[64,1024]{1,0:T(8,128)S(1)} %select_select_fusion.3), channel_id=1, source_target_pairs={{0,8},{8,16},{16,24},{24,32},{32,40},{40,48},{48,56},{56,0},{1,9},... | collective-permute-start | bytes 786440 | tf_op jit(solution)/shard_map/ppermute | solution.py:43
  58.6 11.5 %collective-permute-start.19 = (f32[64,1024]{1,0:T(8,128)S(1)}, f32[64,1024]{1,0:T(8,128)S(1)}, u32[]{:S(2)}, u32[]{:S(2)}) collective-permute-start(f32[64,1024]{1,0:T(8,128)S(1)} %select_select_fusion.3), channel_id=1, source_target_pairs={{0,56},{8,0},{16,8},{24,16},{32,24},{40,32},{48,40},{56,48},{1,57}... | collective-permute-start | bytes 786440 | tf_op jit(solution)/shard_map/ppermute | solution.py:44
  60.3 12.0 %copy-start.2 = (f32[64,1024]{1,0:T(8,128)}, f32[64,1024]{1,0:T(8,128)S(1)}, u32[]{:S(2)}) copy-start(f32[64,1024]{1,0:T(8,128)S(1)} %select_select_fusion.1) | copy-start | bytes 786436
  60.4 11.9 %collective-permute-start.22 = (f32[64,1024]{1,0:T(8,128)S(1)}, f32[64,1024]{1,0:T(8,128)}, u32[]{:S(2)}, u32[]{:S(2)}) collective-permute-start(f32[64,1024]{1,0:T(8,128)S(1)} %select_select_fusion.1), channel_id=1, source_target_pairs={{56,0},{16,24},{32,40},{57,1},{17,25},{33,41},{58,2},{18,26},{34,4... | collective-permute-start | bytes 786440 | tf_op jit(solution)/shard_map/ppermute | solution.py:43
  65.0 7.3 %collective-permute-start.23 = (f32[64,1024]{1,0:T(8,128)S(1)}, f32[64,1024]{1,0:T(8,128)}, u32[]{:S(2)}, u32[]{:S(2)}) collective-permute-start(f32[64,1024]{1,0:T(8,128)S(1)} %select_select_fusion.1), channel_id=1, source_target_pairs={{56,48},{16,8},{57,49},{17,9},{58,50},{18,10},{59,51},{19,11},{60,... | collective-permute-start | bytes 786440 | tf_op jit(solution)/shard_map/ppermute | solution.py:44
  67.1 10.1 %collective-permute-start.17 = (f32[8,64,128]{2,1,0:T(8,128)}, f32[8,64,128]{2,1,0:T(8,128)}, u32[]{:S(2)}, u32[]{:S(2)}) collective-permute-start(f32[8,64,128]{2,1,0:T(8,128)} %broadcast_select_fusion), channel_id=1, source_target_pairs={{0,2},{2,0},{1,3},{3,1},{4,6},{6,4},{5,7},{7,5},{8,10},{10,8},{9,1... | collective-permute-start | bytes 786440 | tf_op jit(solution)/shard_map/ppermute | solution.py:63
  70.2 8.7 %collective-permute-start.24 = (f32[64,1024]{1,0:T(8,128)S(1)}, f32[64,1024]{1,0:T(8,128)S(1)}, u32[]{:S(2)}, u32[]{:S(2)}) collective-permute-start(f32[64,1024]{1,0:T(8,128)S(1)} %select_select_fusion.2.refs_0_), channel_id=1, source_target_pairs={{0,64},{64,128},{128,192},{192,0},{1,65},{65,129},{129,193},{193,1... | collective-permute-start | bytes 786440 | tf_op jit(solution)/shard_map/ppermute | solution.py:177
  72.2 9.8 %collective-permute-start.32 = (f32[64,1024]{1,0:T(8,128)S(1)}, f32[64,1024]{1,0:T(8,128)S(1)}, u32[]{:S(2)}, u32[]{:S(2)}) collective-permute-start(f32[64,1024]{1,0:T(8,128)S(1)} %select_select_fusion.2.refs_0_), channel_id=1, source_target_pairs={{0,4},{4,0},{1,5},{5,1},{2,6},{6,2},{3,7},{7,3},{8,12},{12,8},{9,1... | collective-permute-start | bytes 786440 | tf_op jit(solution)/shard_map/ppermute | solution.py:177
  72.3 10.7 %collective-permute-start.34 = (f32[64,1024]{1,0:T(8,128)S(1)}, f32[64,1024]{1,0:T(8,128)S(1)}, u32[]{:S(2)}, u32[]{:S(2)}) collective-permute-start(f32[64,1024]{1,0:T(8,128)S(1)} %select_select_fusion.2.refs_0_), channel_id=1, source_target_pairs={{0,192},{64,0},{128,64},{192,128},{1,193},{65,1},{129,65},{193,129... | collective-permute-start | bytes 786440 | tf_op jit(solution)/shard_map/ppermute | solution.py:177
  73.3 14.3 %collective-permute-start.27 = (f32[64,1024]{1,0:T(8,128)S(1)}, f32[64,1024]{1,0:T(8,128)}, u32[]{:S(2)}, u32[]{:S(2)}) collective-permute-start(f32[64,1024]{1,0:T(8,128)S(1)} %select_select_fusion.refs_1_), channel_id=1, source_target_pairs={{0,4},{4,0},{1,5},{5,1},{2,6},{6,2},{3,7},{7,3},{8,12},{12,8},{9,1... | collective-permute-start | bytes 786440 | tf_op jit(solution)/shard_map/ppermute | solution.py:177
  77.2 11.6 %collective-permute-start.30 = (f32[64,1024]{1,0:T(8,128)S(1)}, f32[64,1024]{1,0:T(8,128)}, u32[]{:S(2)}, u32[]{:S(2)}) collective-permute-start(f32[64,1024]{1,0:T(8,128)S(1)} %select_select_fusion.refs_1_), channel_id=1, source_target_pairs={{0,64},{64,128},{128,192},{192,0},{1,65},{65,129},{129,193},{193,1... | collective-permute-start | bytes 786440 | tf_op jit(solution)/shard_map/ppermute | solution.py:177
  78.9 12.9 %collective-permute-start.35 = (f32[64,1024]{1,0:T(8,128)S(1)}, f32[64,1024]{1,0:T(8,128)}, u32[]{:S(2)}, u32[]{:S(2)}) collective-permute-start(f32[64,1024]{1,0:T(8,128)S(1)} %select_select_fusion.refs_1_), channel_id=1, source_target_pairs={{0,192},{64,0},{128,64},{192,128},{1,193},{65,1},{129,65},{193,129... | collective-permute-start | bytes 786440 | tf_op jit(solution)/shard_map/ppermute | solution.py:177
  82.0 12.9 %collective-permute-start.25 = (f32[64,1024]{1,0:T(8,128)S(1)}, f32[64,1024]{1,0:T(8,128)}, u32[]{:S(2)}, u32[]{:S(2)}) collective-permute-start(f32[64,1024]{1,0:T(8,128)S(1)} %collective-permute-done.24.refs_4_), channel_id=1, source_target_pairs={{0,64},{64,128},{128,192},{192,0},{1,65},{65,129},{129,193},{193,1... | collective-permute-start | bytes 786440 | tf_op jit(solution)/shard_map/ppermute | solution.py:177
  83.0 12.1 %collective-permute-start.33 = (f32[64,1024]{1,0:T(8,128)S(1)}, f32[64,1024]{1,0:T(8,128)}, u32[]{:S(2)}, u32[]{:S(2)}) collective-permute-start(f32[64,1024]{1,0:T(8,128)S(1)} %collective-permute-done.32.refs_2_), channel_id=1, source_target_pairs={{0,192},{64,0},{128,64},{192,128},{1,193},{65,1},{129,65},{193,129... | collective-permute-start | bytes 786440 | tf_op jit(solution)/shard_map/ppermute | solution.py:177
  87.7 9.3 %collective-permute-start.28 = (f32[64,1024]{1,0:T(8,128)}, f32[64,1024]{1,0:T(8,128)}, u32[]{:S(2)}, u32[]{:S(2)}) collective-permute-start(f32[64,1024]{1,0:T(8,128)} %collective-permute-done.27.refs_3_), channel_id=1, source_target_pairs={{0,192},{64,0},{128,64},{192,128},{1,193},{65,1},{129,65},{193,129... | collective-permute-start | bytes 786440 | tf_op jit(solution)/shard_map/ppermute | solution.py:177
  88.9 8.3 %collective-permute-start.36 = (f32[64,1024]{1,0:T(8,128)S(1)}, f32[64,1024]{1,0:T(8,128)S(1)}, u32[]{:S(2)}, u32[]{:S(2)}) collective-permute-start(f32[64,1024]{1,0:T(8,128)S(1)} %collective-permute-done.24.refs_4_), channel_id=1, source_target_pairs={{0,4},{4,0},{1,5},{5,1},{2,6},{6,2},{3,7},{7,3},{8,12},{12,8},{9,1... | collective-permute-start | bytes 786440 | tf_op jit(solution)/shard_map/ppermute | solution.py:177
  91.7 7.4 %collective-permute-start.31 = (f32[64,1024]{1,0:T(8,128)}, f32[64,1024]{1,0:T(8,128)S(1)}, u32[]{:S(2)}, u32[]{:S(2)}) collective-permute-start(f32[64,1024]{1,0:T(8,128)} %collective-permute-done.30.refs_5_), channel_id=1, source_target_pairs={{0,64},{64,128},{128,192},{192,0},{1,65},{65,129},{129,193},{193,1... | collective-permute-start | bytes 786440 | tf_op jit(solution)/shard_map/ppermute | solution.py:177
  94.9 6.6 %collective-permute-start.37 = (f32[64,1024]{1,0:T(8,128)}, f32[64,1024]{1,0:T(8,128)S(1)}, u32[]{:S(2)}, u32[]{:S(2)}) collective-permute-start(f32[64,1024]{1,0:T(8,128)} %collective-permute-done.30.refs_5_), channel_id=1, source_target_pairs={{0,4},{4,0},{1,5},{5,1},{2,6},{6,2},{3,7},{7,3},{8,12},{12,8},{9,1... | collective-permute-start | bytes 786440 | tf_op jit(solution)/shard_map/ppermute | solution.py:177
  95.0 9.6 %collective-permute-start.26 = (f32[64,1024]{1,0:T(8,128)}, f32[64,1024]{1,0:T(8,128)S(1)}, u32[]{:S(2)}, u32[]{:S(2)}) collective-permute-start(f32[64,1024]{1,0:T(8,128)} %collective-permute-done.25.refs_0_), channel_id=1, source_target_pairs={{0,4},{4,0},{1,5},{5,1},{2,6},{6,2},{3,7},{7,3},{8,12},{12,8},{9,1... | collective-permute-start | bytes 786440 | tf_op jit(solution)/shard_map/ppermute | solution.py:177
  97.0 7.8 %collective-permute-start.29 = (f32[64,1024]{1,0:T(8,128)}, f32[64,1024]{1,0:T(8,128)S(1)}, u32[]{:S(2)}, u32[]{:S(2)}) collective-permute-start(f32[64,1024]{1,0:T(8,128)} %collective-permute-done.28.refs_7_), channel_id=1, source_target_pairs={{0,192},{64,0},{128,64},{192,128},{1,193},{65,1},{129,65},{193,129... | collective-permute-start | bytes 786440 | tf_op jit(solution)/shard_map/ppermute | solution.py:177
  (2 other events, 6.8 us)

commit v11 on v10

--- a/solution.py
+++ b/solution.py
@@ -57,10 +57,13 @@
     return block
 
 
-def swap(block, panel, axis):
+def opposite(block, axis):
+    return lax.ppermute(block, axis, [(0, 1), (1, 0)])
+
+
+def owned(block, other, panel, axis):
     is_first = lax.broadcasted_iota(jnp.int32, (1, 1, 2 * ROWS), 2) < ROWS
     bit = panel >> 4 & 1 if axis == "c" else panel >> 5
-    other = lax.ppermute(block, axis, [(0, 1), (1, 0)])
     keep = jnp.where(is_first, bit, 1) == lax.axis_index(axis)
     return jnp.where(keep, block, other)
 
@@ -193,19 +196,19 @@
     other = jnp.where(other_first, panels[0], panels[1])
     ox, oz, oy = place_of(other)
     lx, lz, ly = place_of(LAST)
-    strip = swap(strips(spectra, other), other, "c")
+    strip = strips(spectra, other)
+    strip = owned(strip, opposite(strip, "c"), other, "c")
     arrived = scatter(spectra.reshape(2 * FREQ, ROWS, COLS))
     arrived, strip = lax.optimization_barrier((arrived, strip))
     spot = (oy * 4 + ((ox + 2 * oy) & 3)).astype(jnp.uint32)
     mine = lax.dynamic_index_in_dim(arrived, spot, 0, keepdims=False)
+    branches = [lambda v, s, r=r: (leap(v, r), opposite(s, "yh")) for r in range(8)]
+    leapt, across = lax.switch(oz, branches, mine, strip)
+    leapt, across, arrived = lax.optimization_barrier((leapt, across, arrived))
+    mine = land(mine, leapt, oz, z)
     last = arrived[ly * 4 + (lx + 2 * ly) % 4]
-    branches = [lambda v, r=r: leap(v, r) for r in range(8)]
-    leapt = lax.switch(oz, branches, mine)
-    leapt, last = lax.optimization_barrier((leapt, last))
-    mine = land(mine, leapt, oz, z)
     last = land(last, leap(last, lz), lz, z)
-    mine, strip = lax.optimization_barrier((mine, strip))
-    strip = swap(strip, other, "yh").reshape(2, FREQ, ROWS, 2 * ROWS)
+    strip = owned(strip, across, other, "yh").reshape(2, FREQ, ROWS, 2 * ROWS)
     mine, last = exchange([steps(mine, oz, z, False), steps(last, lz, z, True)])
     blocks = [v for pair in zip(mine, last) for v in pair]
     bins = (x + 2 * yl + jnp.array([0, 2, 3, 1], jnp.int32)) & 3

time: 105 us -> 102 us (0.971)
  the two profiles are of different devices: /device:TPU:70 before, /device:TPU:16 now
where the time goes in v11:
time: 102 us; the launch traced here: 101 us
  starting transfers between devices  45.3 us (44%)
  waiting for transfers between devices  39.3 us (39%)
  other arithmetic  5.69 us (6%)
  Pallas kernels  5.33 us (5%)
  local copies, waits for them, and re-layouts  2.93 us (3%)
  between operations  2.33 us (2%)
    all_to_all x1, waiting for transfers between devices, scatter(): lax.all_to_all(rows, ('x', 'yl'), 0, 0, axis_index_groups=[members], tile...  21.9 us
    ppermute x14, starting transfers between devices, send(): return lax.ppermute(v, axis, pairs)  20.5 us
    ppermute x2, starting transfers between devices, leap(): up = lax.ppermute(v, 'z', [(root, (root + 3) % 8)])  7.92 us
    ppermute x2, waiting for transfers between devices, opposite(): return lax.ppermute(block, axis, [(0, 1), (1, 0)])  5.98 us
    ppermute x14, waiting for transfers between devices, send(): return lax.ppermute(v, axis, pairs)  5.53 us
    pallas_call x2, Pallas kernels, call(): pl.pallas_call(body, in_specs=[pl.BlockSpec(memory_space=pltpu.SMEM), *[v...  5.33 us
    all_to_all x1, starting transfers between devices, scatter(): lax.all_to_all(rows, ('x', 'yl'), 0, 0, axis_index_groups=[members], tile...  5.29 us
    ppermute x2, starting transfers between devices, leap(): down = lax.ppermute(v, 'z', [(root, (root - 3) % 8)])  4.87 us
  transfers between devices with their start and end apart: 25, of which 11 were waited for; matrix products, arithmetic and copies ran while one was open for 7% of the time, Pallas kernels for 3%

profile of v11, /device:TPU:16, one launch (start us, length us, event | category | flops | bytes accessed | tf_op | source)
XLA Modules:
  0.0 101.3 jit_solution(10265887806256399302)
XLA Ops:
  0.0 5.3 %all-to-all-start = ((f32[8,64,1024]{2,1,0:T(8,128)}), f32[8,64,1024]{2,1,0:T(8,128)}, u32[]{:S(2)}, u32[]{:S(2)}) async-start(f32[8,64,1024]{2,1,0:T(8,128)} %bitcast.16), calls=%async_computation | async-start | bytes 4194304 | tf_op jit(solution)/shard_map/all_to_all | solution.py:170
  8.8 1.2 %collective-permute-done.24 = f32[8,64,128]{2,1,0:T(8,128)S(1)} collective-permute-done((f32[8,64,128]{2,1,0:T(8,128)S(1)}, f32[8,64,128]{2,1,0:T(8,128)S(1)}, u32[]{:S(2)}, u32[]{:S(2)}) %collective-permute-start.24) | collective-permute-done | bytes 262176 | tf_op jit(solution)/shard_map/ppermute | solution.py:61
  10.9 21.9 %all-to-all-done = f32[8,64,1024]{2,1,0:T(8,128)} async-done(((f32[8,64,1024]{2,1,0:T(8,128)}), f32[8,64,1024]{2,1,0:T(8,128)}, u32[]{:S(2)}, u32[]{:S(2)}) %all-to-all-start) | async-done | bytes 2097184 | tf_op jit(solution)/shard_map/all_to_all | solution.py:170
  32.8 1.0 dynamic-slice_bitcast_fusion
  33.7 19.2 %conditional.1 = (f32[64,1024]{1,0:T(8,128)}, f32[64,1024]{1,0:T(8,128)}, f32[8,64,128]{2,1,0:T(8,128)}) conditional(s32[]{:T(128)} %clamp.3, (f32[64,1024]{1,0:T(8,128)S(1)}, f32[8,64,128]{2,1,0:T(8,128)}) %tuple.40, (f32[64,1024]{1,0:T(8,128)S(1)}, f32[8,64,128]{2,1,0:T(8,128)}) %tuple.40, ...), branch_computations={%region_0.1_spmd, %region_1.2_spmd, %region_2.3_spmd, %region_3.4_... | conditional | bytes 3145872 | solution.py:206
  33.7 7.2 %collective-permute-start = (f32[64,1024]{1,0:T(8,128)S(1)}, f32[64,1024]{1,0:T(8,128)}, u32[]{:S(2)}, u32[]{:S(2)}) collective-permute-start(f32[64,1024]{1,0:T(8,128)S(1)} %get-tuple-element.37), channel_id=1, source_target_pairs={{0,24},{1,25},{2,26},{3,27},{4,28},{5,29},{6,30},{7,31},{64,88},{6... | collective-permute-start | bytes 786440 | tf_op jit(solution)/shard_map/cond/branch_0_fun/ppermute | solution.py:28
  41.0 3.5 %collective-permute-start.1 = (f32[64,1024]{1,0:T(8,128)S(1)}, f32[64,1024]{1,0:T(8,128)}, u32[]{:S(2)}, u32[]{:S(2)}) collective-permute-start(f32[64,1024]{1,0:T(8,128)S(1)} %get-tuple-element.37), channel_id=1, source_target_pairs={{0,40},{1,41},{2,42},{3,43},{4,44},{5,45},{6,46},{7,47},{64,104},{... | collective-permute-start | bytes 786440 | tf_op jit(solution)/shard_map/cond/branch_0_fun/ppermute | solution.py:29
  45.1 3.1 %collective-permute-done.1 = f32[64,1024]{1,0:T(8,128)} collective-permute-done((f32[64,1024]{1,0:T(8,128)S(1)}, f32[64,1024]{1,0:T(8,128)}, u32[]{:S(2)}, u32[]{:S(2)}) %collective-permute-start.1) | collective-permute-done | bytes 262176 | tf_op jit(solution)/shard_map/cond/branch_0_fun/ppermute | solution.py:29
  48.2 4.7 %collective-permute-done.2 = f32[8,64,128]{2,1,0:T(8,128)} collective-permute-done((f32[8,64,128]{2,1,0:T(8,128)}, f32[8,64,128]{2,1,0:T(8,128)}, u32[]{:S(2)}, u32[]{:S(2)}) %collective-permute-start.2) | collective-permute-done | bytes 262176 | tf_op jit(solution)/shard_map/cond/branch_0_fun/ppermute | solution.py:61
  52.9 1.0 slice_bitcast_fusion
  54.6 1.4 %collective-permute-start.28 = (f32[64,1024]{1,0:T(8,128)S(1)}, f32[64,1024]{1,0:T(8,128)}, u32[]{:S(2)}, u32[]{:S(2)}) collective-permute-start(f32[64,1024]{1,0:T(8,128)S(1)} %slice_bitcast_fusion), channel_id=1, source_target_pairs={{56,32},{57,33},{58,34},{59,35},{60,36},{61,37},{62,38},{63,39},{1... | collective-permute-start | bytes 786440 | tf_op jit(solution)/shard_map/ppermute | solution.py:29
  56.0 1.1 %select_select_fusion.3 = f32[64,1024]{1,0:T(8,128)S(1)} fusion(f32[64,1024]{1,0:T(8,128)} %get-tuple-element.68, f32[64,1024]{1,0:T(8,128)} %get-tuple-element.69, pred[]{:T(512)S(6)} %eq.80, pred[]{:T(512)S(6)} %eq.79, f32[8,64,1024]{2,1,0:T(8,128)} %all-to-all-done, u32[]{:T(128)S(6)} %convert_element_type.21), kind=kLoop, calls=%fused_computation.6 | loop fusion | flops 131072 | bytes 1048582 | tf_op jit(solution)/shard_map/jit(_where)/select_n | solution.py:35
  57.1 3.2 %collective-permute-start.26 = (f32[64,1024]{1,0:T(8,128)S(1)}, f32[64,1024]{1,0:T(8,128)S(1)}, u32[]{:S(2)}, u32[]{:S(2)}) collective-permute-start(f32[64,1024]{1,0:T(8,128)S(1)} %select_select_fusion.3), channel_id=1, source_target_pairs={{0,56},{8,0},{16,8},{24,16},{32,24},{40,32},{48,40},{56,48},{1,57}... | collective-permute-start | bytes 786440 | tf_op jit(solution)/shard_map/ppermute | solution.py:44
  60.4 1.1 %select_select_fusion.1 = f32[64,1024]{1,0:T(8,128)S(1)} fusion(f32[64,1024]{1,0:T(8,128)S(1)} %collective-permute-done.27, f32[64,1024]{1,0:T(8,128)} %collective-permute-done.28, pred[]{:T(512)S(6)} %eq.87, pred[]{:T(512)S(6)} %eq.86, f32[8,64,1024]{2,1,0:T(8,128)} %all-to-all-done), kind=kLoop, calls=%fused_computation.3 | loop fusion | flops 131072 | bytes 1048578 | tf_op jit(solution)/shard_map/jit(_where)/select_n | solution.py:35
  61.5 1.3 %collective-permute-start.29 = (f32[64,1024]{1,0:T(8,128)S(1)}, f32[64,1024]{1,0:T(8,128)}, u32[]{:S(2)}, u32[]{:S(2)}) collective-permute-start(f32[64,1024]{1,0:T(8,128)S(1)} %select_select_fusion.1), channel_id=1, source_target_pairs={{56,0},{16,24},{32,40},{57,1},{17,25},{33,41},{58,2},{18,26},{34,4... | collective-permute-start | bytes 786440 | tf_op jit(solution)/shard_map/ppermute | solution.py:43
  62.8 1.4 %collective-permute-start.30 = (f32[64,1024]{1,0:T(8,128)S(1)}, f32[64,1024]{1,0:T(8,128)}, u32[]{:S(2)}, u32[]{:S(2)}) collective-permute-start(f32[64,1024]{1,0:T(8,128)S(1)} %select_select_fusion.1), channel_id=1, source_target_pairs={{56,48},{16,8},{57,49},{17,9},{58,50},{18,10},{59,51},{19,11},{60,... | collective-permute-start | bytes 786440 | tf_op jit(solution)/shard_map/ppermute | solution.py:44
  66.5 2.7 %collective-permute-start.41 = (f32[64,1024]{1,0:T(8,128)S(1)}, f32[64,1024]{1,0:T(8,128)S(1)}, u32[]{:S(2)}, u32[]{:S(2)}) collective-permute-start(f32[64,1024]{1,0:T(8,128)S(1)} %select_select_fusion.2.refs_0_), channel_id=1, source_target_pairs={{0,192},{64,0},{128,64},{192,128},{1,193},{65,1},{129,65},{193,129... | collective-permute-start | bytes 786440 | tf_op jit(solution)/shard_map/ppermute | solution.py:180
  69.2 1.9 %collective-permute-done.29 = f32[64,1024]{1,0:T(8,128)} collective-permute-done((f32[64,1024]{1,0:T(8,128)S(1)}, f32[64,1024]{1,0:T(8,128)}, u32[]{:S(2)}, u32[]{:S(2)}) %collective-permute-start.29) | collective-permute-done | bytes 262176 | tf_op jit(solution)/shard_map/ppermute | solution.py:43
  71.1 1.1 %select_select_fusion.refs_1_ = f32[64,1024]{1,0:T(8,128)S(1)} fusion(f32[64,1024]{1,0:T(8,128)} %collective-permute-done.29, f32[64,1024]{1,0:T(8,128)} %collective-permute-done.30, f32[64,1024]{1,0:T(8,128)} %copy-done.2, pred[]{:T(512)S(6)} %or.23, pred[]{:T(512)S(6)} %or.22), kind=kLoop, calls=%fused_computation.2 | loop fusion | flops 131072 | bytes 1048578 | tf_op jit(solution)/shard_map/jit(_where)/select_n | solution.py:48
  73.6 2.8 %collective-permute-start.42 = (f32[64,1024]{1,0:T(8,128)S(1)}, f32[64,1024]{1,0:T(8,128)}, u32[]{:S(2)}, u32[]{:S(2)}) collective-permute-start(f32[64,1024]{1,0:T(8,128)S(1)} %select_select_fusion.refs_1_), channel_id=1, source_target_pairs={{0,192},{64,0},{128,64},{192,128},{1,193},{65,1},{129,65},{193,129... | collective-permute-start | bytes 786440 | tf_op jit(solution)/shard_map/ppermute | solution.py:180
  76.4 3.2 %collective-permute-start.40 = (f32[64,1024]{1,0:T(8,128)S(1)}, f32[64,1024]{1,0:T(8,128)}, u32[]{:S(2)}, u32[]{:S(2)}) collective-permute-start(f32[64,1024]{1,0:T(8,128)S(1)} %collective-permute-done.39.refs_2_), channel_id=1, source_target_pairs={{0,192},{64,0},{128,64},{192,128},{1,193},{65,1},{129,65},{193,129... | collective-permute-start | bytes 786440 | tf_op jit(solution)/shard_map/ppermute | solution.py:180
  79.7 1.1 %collective-permute-start.35 = (f32[64,1024]{1,0:T(8,128)}, f32[64,1024]{1,0:T(8,128)}, u32[]{:S(2)}, u32[]{:S(2)}) collective-permute-start(f32[64,1024]{1,0:T(8,128)} %collective-permute-done.34.refs_3_), channel_id=1, source_target_pairs={{0,192},{64,0},{128,64},{192,128},{1,193},{65,1},{129,65},{193,129... | collective-permute-start | bytes 786440 | tf_op jit(solution)/shard_map/ppermute | solution.py:180
  80.8 1.1 %broadcast_select_fusion.1 = f32[8,64,128]{2,1,0:T(8,128)S(1)} fusion(f32[8,64,128]{2,1,0:T(8,128)} %broadcast_select_fusion, f32[8,64,128]{2,1,0:T(8,128)} %get-tuple-element.67, pred[128]{0:T(512)(128)(4,1)S(1)} %fusion.1), kind=kLoop, calls=%fused_computation.11 | loop fusion | flops 65536 | bytes 786560 | tf_op jit(solution)/shard_map/jit(_where)/select_n | solution.py:68
  81.9 1.2 %collective-permute-start.43 = (f32[64,1024]{1,0:T(8,128)S(1)}, f32[64,1024]{1,0:T(8,128)S(1)}, u32[]{:S(2)}, u32[]{:S(2)}) collective-permute-start(f32[64,1024]{1,0:T(8,128)S(1)} %collective-permute-done.31.refs_4_), channel_id=1, source_target_pairs={{0,4},{4,0},{1,5},{5,1},{2,6},{6,2},{3,7},{7,3},{8,12},{12,8},{9,1... | collective-permute-start | bytes 786440 | tf_op jit(solution)/shard_map/ppermute | solution.py:180
  83.2 1.2 %collective-permute-start.38 = (f32[64,1024]{1,0:T(8,128)}, f32[64,1024]{1,0:T(8,128)S(1)}, u32[]{:S(2)}, u32[]{:S(2)}) collective-permute-start(f32[64,1024]{1,0:T(8,128)} %collective-permute-done.37.refs_5_), channel_id=1, source_target_pairs={{0,64},{64,128},{128,192},{192,0},{1,65},{65,129},{129,193},{193,1... | collective-permute-start | bytes 786440 | tf_op jit(solution)/shard_map/ppermute | solution.py:180
  85.1 1.5 %collective-permute-start.44 = (f32[64,1024]{1,0:T(8,128)}, f32[64,1024]{1,0:T(8,128)S(1)}, u32[]{:S(2)}, u32[]{:S(2)}) collective-permute-start(f32[64,1024]{1,0:T(8,128)} %collective-permute-done.37.refs_5_), channel_id=1, source_target_pairs={{0,4},{4,0},{1,5},{5,1},{2,6},{6,2},{3,7},{7,3},{8,12},{12,8},{9,1... | collective-permute-start | bytes 786440 | tf_op jit(solution)/shard_map/ppermute | solution.py:180
  87.1 1.5 %collective-permute-start.33 = (f32[64,1024]{1,0:T(8,128)}, f32[64,1024]{1,0:T(8,128)S(1)}, u32[]{:S(2)}, u32[]{:S(2)}) collective-permute-start(f32[64,1024]{1,0:T(8,128)} %collective-permute-done.32.refs_0_), channel_id=1, source_target_pairs={{0,4},{4,0},{1,5},{5,1},{2,6},{6,2},{3,7},{7,3},{8,12},{12,8},{9,1... | collective-permute-start | bytes 786440 | tf_op jit(solution)/shard_map/ppermute | solution.py:180
  88.6 2.4 %collective-permute-done.35.refs_7_ = f32[64,1024]{1,0:T(8,128)} collective-permute-done((f32[64,1024]{1,0:T(8,128)}, f32[64,1024]{1,0:T(8,128)}, u32[]{:S(2)}, u32[]{:S(2)}) %collective-permute-start.35) | collective-permute-done | bytes 262176 | tf_op jit(solution)/shard_map/ppermute | solution.py:180
  91.0 3.0 %collective-permute-start.36 = (f32[64,1024]{1,0:T(8,128)}, f32[64,1024]{1,0:T(8,128)S(1)}, u32[]{:S(2)}, u32[]{:S(2)}) collective-permute-start(f32[64,1024]{1,0:T(8,128)} %collective-permute-done.35.refs_7_), channel_id=1, source_target_pairs={{0,192},{64,0},{128,64},{192,128},{1,193},{65,1},{129,65},{193,129... | collective-permute-start | bytes 786440 | tf_op jit(solution)/shard_map/ppermute | solution.py:180
  94.1 1.8 %collective-permute-done.44.refs_11_ = f32[64,1024]{1,0:T(8,128)S(1)} collective-permute-done((f32[64,1024]{1,0:T(8,128)}, f32[64,1024]{1,0:T(8,128)S(1)}, u32[]{:S(2)}, u32[]{:S(2)}) %collective-permute-start.44) | collective-permute-done | bytes 262176 | tf_op jit(solution)/shard_map/ppermute | solution.py:180
  95.9 3.1 %shard_map.73.refs_4_ = f32[8,64,1024]{2,1,0:T(8,128)S(1)} custom-call(s32[4]{0:T(128)S(1)} %get-tuple-element.79.bins, f32[2,4,64,1024]{3,2,1,0:T(8,128)S(1)} %copy-done.1, f32[4,128,256]{2,1,0:T(8,128)S(1)} %maximum_select_fusion.l_ref, f32[64,64]{1,0:T(8,128)S(1)} %copy.12.coef_ref, f32[64,1024]{1,0:T(8,128)} %collective-permute-done.32.refs_0_, ...), custom_call_target="tpu_custom_call" | custom-call | flops 603979776 | bytes 6291456 | tf_op jit(solution)/shard_map/pallas_call | solution.py:123
  99.1 2.2 %shard_map.74 = bf16[8,64,1024]{2,1,0:T(8,128)(2,1)} custom-call(s32[4]{0:T(128)S(1)} %get-tuple-element.79.bins, f32[2,4,64,1024]{3,2,1,0:T(8,128)S(1)} %copy-done.1, f32[4,128,256]{2,1,0:T(8,128)S(1)} %maximum_select_fusion.l_ref, f32[64,64]{1,0:T(8,128)S(1)} %copy.12.coef_ref, f32[64,1024]{1,0:T(8,128)S(1)} %select_select_fusion.2.refs_0_, ...), custom_call_target="tpu_custom_call" | custom-call | flops 201326592 | bytes 2097152 | tf_op jit(solution)/shard_map/pallas_call | solution.py:123
  (60 shorter events, 9.0 us)
Async XLA Ops:
  0.0 8.6 %copy-start = (f32[64,64]{1,0:T(8,128)S(1)}, f32[64,64]{1,0:T(8,128)}, u32[]{:S(2)}) copy-start(f32[64,64]{1,0:T(8,128)} %param.17) | copy-start | bytes 49156
  0.0 8.0 %copy-start.1 = (f32[2,4,64,1024]{3,2,1,0:T(8,128)S(1)}, f32[2,4,64,1024]{3,2,1,0:T(8,128)}, u32[]{:S(2)}) copy-start(f32[2,4,64,1024]{3,2,1,0:T(8,128)} %x_ref.3) | copy-start | bytes 6291460
  0.0 8.5 %copy-start.6 = (s32[64]{0:T(128)S(1)}, s32[64]{0:T(128)}, u32[]{:S(2)}) copy-start(s32[64]{0:T(128)} %param.18) | copy-start | bytes 772
  0.0 8.6 %copy-start.4 = (f32[64,4]{1,0:T(8,128)S(1)}, f32[64,4]{1,0:T(8,128)}, u32[]{:S(2)}) copy-start(f32[64,4]{1,0:T(8,128)} %constant.61.clone) | copy-start | bytes 3076
  0.0 32.7 %all-to-all-start = ((f32[8,64,1024]{2,1,0:T(8,128)}), f32[8,64,1024]{2,1,0:T(8,128)}, u32[]{:S(2)}, u32[]{:S(2)}) async-start(f32[8,64,1024]{2,1,0:T(8,128)} %bitcast.16), calls=%async_computation | async-start | bytes 4194304 | tf_op jit(solution)/shard_map/all_to_all | solution.py:170
  5.3 50.6 %copy-start.7 = (s32[4]{0:T(128)S(1)}, s32[4]{0:T(128)}, u32[]{:S(2)}) copy-start(s32[4]{0:T(128)} %constant.60.clone) | copy-start | bytes 52
  8.4 1.6 %collective-permute-start.24 = (f32[8,64,128]{2,1,0:T(8,128)S(1)}, f32[8,64,128]{2,1,0:T(8,128)S(1)}, u32[]{:S(2)}, u32[]{:S(2)}) collective-permute-start(f32[8,64,128]{2,1,0:T(8,128)S(1)} %pad_maximum_fusion), channel_id=1, source_target_pairs={{0,1},{1,0},{2,3},{3,2},{4,5},{5,4},{6,7},{7,6},{8,9},{9,8},{10,11... | collective-permute-start | bytes 786440 | tf_op jit(solution)/shard_map/ppermute | solution.py:61
  33.7 11.4 %collective-permute-start = (f32[64,1024]{1,0:T(8,128)S(1)}, f32[64,1024]{1,0:T(8,128)}, u32[]{:S(2)}, u32[]{:S(2)}) collective-permute-start(f32[64,1024]{1,0:T(8,128)S(1)} %get-tuple-element.37), channel_id=1, source_target_pairs={{0,24},{1,25},{2,26},{3,27},{4,28},{5,29},{6,30},{7,31},{64,88},{6... | collective-permute-start | bytes 786440 | tf_op jit(solution)/shard_map/cond/branch_0_fun/ppermute | solution.py:28
  41.0 7.2 %collective-permute-start.1 = (f32[64,1024]{1,0:T(8,128)S(1)}, f32[64,1024]{1,0:T(8,128)}, u32[]{:S(2)}, u32[]{:S(2)}) collective-permute-start(f32[64,1024]{1,0:T(8,128)S(1)} %get-tuple-element.37), channel_id=1, source_target_pairs={{0,40},{1,41},{2,42},{3,43},{4,44},{5,45},{6,46},{7,47},{64,104},{... | collective-permute-start | bytes 786440 | tf_op jit(solution)/shard_map/cond/branch_0_fun/ppermute | solution.py:29
  44.5 8.4 %collective-permute-start.2 = (f32[8,64,128]{2,1,0:T(8,128)}, f32[8,64,128]{2,1,0:T(8,128)}, u32[]{:S(2)}, u32[]{:S(2)}) collective-permute-start(f32[8,64,128]{2,1,0:T(8,128)} %get-tuple-element.38), channel_id=1, source_target_pairs={{0,2},{2,0},{1,3},{3,1},{4,6},{6,4},{5,7},{7,5},{8,10},{10,8},{9,1... | collective-permute-start | bytes 786440 | tf_op jit(solution)/shard_map/cond/branch_0_fun/ppermute | solution.py:61
  53.9 6.5 %collective-permute-start.27 = (f32[64,1024]{1,0:T(8,128)S(1)}, f32[64,1024]{1,0:T(8,128)S(1)}, u32[]{:S(2)}, u32[]{:S(2)}) collective-permute-start(f32[64,1024]{1,0:T(8,128)S(1)} %slice_bitcast_fusion), channel_id=1, source_target_pairs={{56,16},{57,17},{58,18},{59,19},{60,20},{61,21},{62,22},{63,23},{1... | collective-permute-start | bytes 786440 | tf_op jit(solution)/shard_map/ppermute | solution.py:28
  54.6 5.8 %collective-permute-start.28 = (f32[64,1024]{1,0:T(8,128)S(1)}, f32[64,1024]{1,0:T(8,128)}, u32[]{:S(2)}, u32[]{:S(2)}) collective-permute-start(f32[64,1024]{1,0:T(8,128)S(1)} %slice_bitcast_fusion), channel_id=1, source_target_pairs={{56,32},{57,33},{58,34},{59,35},{60,36},{61,37},{62,38},{63,39},{1... | collective-permute-start | bytes 786440 | tf_op jit(solution)/shard_map/ppermute | solution.py:29
  56.0 16.8 %copy-start.3 = (f32[64,4]{1,0:T(8,128)S(1)}, f32[64,4]{1,0:T(8,128)}, u32[]{:S(2)}) copy-start(f32[64,4]{1,0:T(8,128)} %constant.62.clone) | copy-start | bytes 3076
  57.0 8.2 %collective-permute-start.25 = (f32[64,1024]{1,0:T(8,128)S(1)}, f32[64,1024]{1,0:T(8,128)S(1)}, u32[]{:S(2)}, u32[]{:S(2)}) collective-permute-start(f32[64,1024]{1,0:T(8,128)S(1)} %select_select_fusion.3), channel_id=1, source_target_pairs={{0,8},{8,16},{16,24},{24,32},{32,40},{40,48},{48,56},{56,0},{1,9},... | collective-permute-start | bytes 786440 | tf_op jit(solution)/shard_map/ppermute | solution.py:43
  57.1 8.1 %collective-permute-start.26 = (f32[64,1024]{1,0:T(8,128)S(1)}, f32[64,1024]{1,0:T(8,128)S(1)}, u32[]{:S(2)}, u32[]{:S(2)}) collective-permute-start(f32[64,1024]{1,0:T(8,128)S(1)} %select_select_fusion.3), channel_id=1, source_target_pairs={{0,56},{8,0},{16,8},{24,16},{32,24},{40,32},{48,40},{56,48},{1,57}... | collective-permute-start | bytes 786440 | tf_op jit(solution)/shard_map/ppermute | solution.py:44
  61.5 9.6 %copy-start.2 = (f32[64,1024]{1,0:T(8,128)}, f32[64,1024]{1,0:T(8,128)S(1)}, u32[]{:S(2)}) copy-start(f32[64,1024]{1,0:T(8,128)S(1)} %select_select_fusion.1) | copy-start | bytes 786436
  61.5 9.6 %collective-permute-start.29 = (f32[64,1024]{1,0:T(8,128)S(1)}, f32[64,1024]{1,0:T(8,128)}, u32[]{:S(2)}, u32[]{:S(2)}) collective-permute-start(f32[64,1024]{1,0:T(8,128)S(1)} %select_select_fusion.1), channel_id=1, source_target_pairs={{56,0},{16,24},{32,40},{57,1},{17,25},{33,41},{58,2},{18,26},{34,4... | collective-permute-start | bytes 786440 | tf_op jit(solution)/shard_map/ppermute | solution.py:43
  62.8 8.3 %collective-permute-start.30 = (f32[64,1024]{1,0:T(8,128)S(1)}, f32[64,1024]{1,0:T(8,128)}, u32[]{:S(2)}, u32[]{:S(2)}) collective-permute-start(f32[64,1024]{1,0:T(8,128)S(1)} %select_select_fusion.1), channel_id=1, source_target_pairs={{56,48},{16,8},{57,49},{17,9},{58,50},{18,10},{59,51},{19,11},{60,... | collective-permute-start | bytes 786440 | tf_op jit(solution)/shard_map/ppermute | solution.py:44
  65.3 8.3 %collective-permute-start.31 = (f32[64,1024]{1,0:T(8,128)S(1)}, f32[64,1024]{1,0:T(8,128)S(1)}, u32[]{:S(2)}, u32[]{:S(2)}) collective-permute-start(f32[64,1024]{1,0:T(8,128)S(1)} %select_select_fusion.2.refs_0_), channel_id=1, source_target_pairs={{0,64},{64,128},{128,192},{192,0},{1,65},{65,129},{129,193},{193,1... | collective-permute-start | bytes 786440 | tf_op jit(solution)/shard_map/ppermute | solution.py:180
  65.9 10.5 %collective-permute-start.39 = (f32[64,1024]{1,0:T(8,128)S(1)}, f32[64,1024]{1,0:T(8,128)S(1)}, u32[]{:S(2)}, u32[]{:S(2)}) collective-permute-start(f32[64,1024]{1,0:T(8,128)S(1)} %select_select_fusion.2.refs_0_), channel_id=1, source_target_pairs={{0,4},{4,0},{1,5},{5,1},{2,6},{6,2},{3,7},{7,3},{8,12},{12,8},{9,1... | collective-permute-start | bytes 786440 | tf_op jit(solution)/shard_map/ppermute | solution.py:180
  66.5 10.0 %collective-permute-start.41 = (f32[64,1024]{1,0:T(8,128)S(1)}, f32[64,1024]{1,0:T(8,128)S(1)}, u32[]{:S(2)}, u32[]{:S(2)}) collective-permute-start(f32[64,1024]{1,0:T(8,128)S(1)} %select_select_fusion.2.refs_0_), channel_id=1, source_target_pairs={{0,192},{64,0},{128,64},{192,128},{1,193},{65,1},{129,65},{193,129... | collective-permute-start | bytes 786440 | tf_op jit(solution)/shard_map/ppermute | solution.py:180
  72.1 7.5 %collective-permute-start.34 = (f32[64,1024]{1,0:T(8,128)S(1)}, f32[64,1024]{1,0:T(8,128)}, u32[]{:S(2)}, u32[]{:S(2)}) collective-permute-start(f32[64,1024]{1,0:T(8,128)S(1)} %select_select_fusion.refs_1_), channel_id=1, source_target_pairs={{0,4},{4,0},{1,5},{5,1},{2,6},{6,2},{3,7},{7,3},{8,12},{12,8},{9,1... | collective-permute-start | bytes 786440 | tf_op jit(solution)/shard_map/ppermute | solution.py:180
  73.0 8.9 %collective-permute-start.37 = (f32[64,1024]{1,0:T(8,128)S(1)}, f32[64,1024]{1,0:T(8,128)}, u32[]{:S(2)}, u32[]{:S(2)}) collective-permute-start(f32[64,1024]{1,0:T(8,128)S(1)} %select_select_fusion.refs_1_), channel_id=1, source_target_pairs={{0,64},{64,128},{128,192},{192,0},{1,65},{65,129},{129,193},{193,1... | collective-permute-start | bytes 786440 | tf_op jit(solution)/shard_map/ppermute | solution.py:180
  73.6 9.5 %collective-permute-start.42 = (f32[64,1024]{1,0:T(8,128)S(1)}, f32[64,1024]{1,0:T(8,128)}, u32[]{:S(2)}, u32[]{:S(2)}) collective-permute-start(f32[64,1024]{1,0:T(8,128)S(1)} %select_select_fusion.refs_1_), channel_id=1, source_target_pairs={{0,192},{64,0},{128,64},{192,128},{1,193},{65,1},{129,65},{193,129... | collective-permute-start | bytes 786440 | tf_op jit(solution)/shard_map/ppermute | solution.py:180
  76.4 8.7 %collective-permute-start.32 = (f32[64,1024]{1,0:T(8,128)S(1)}, f32[64,1024]{1,0:T(8,128)}, u32[]{:S(2)}, u32[]{:S(2)}) collective-permute-start(f32[64,1024]{1,0:T(8,128)S(1)} %collective-permute-done.31.refs_4_), channel_id=1, source_target_pairs={{0,64},{64,128},{128,192},{192,0},{1,65},{65,129},{129,193},{193,1... | collective-permute-start | bytes 786440 | tf_op jit(solution)/shard_map/ppermute | solution.py:180
  76.4 10.7 %collective-permute-start.40 = (f32[64,1024]{1,0:T(8,128)S(1)}, f32[64,1024]{1,0:T(8,128)}, u32[]{:S(2)}, u32[]{:S(2)}) collective-permute-start(f32[64,1024]{1,0:T(8,128)S(1)} %collective-permute-done.39.refs_2_), channel_id=1, source_target_pairs={{0,192},{64,0},{128,64},{192,128},{1,193},{65,1},{129,65},{193,129... | collective-permute-start | bytes 786440 | tf_op jit(solution)/shard_map/ppermute | solution.py:180
  79.7 11.3 %collective-permute-start.35 = (f32[64,1024]{1,0:T(8,128)}, f32[64,1024]{1,0:T(8,128)}, u32[]{:S(2)}, u32[]{:S(2)}) collective-permute-start(f32[64,1024]{1,0:T(8,128)} %collective-permute-done.34.refs_3_), channel_id=1, source_target_pairs={{0,192},{64,0},{128,64},{192,128},{1,193},{65,1},{129,65},{193,129... | collective-permute-start | bytes 786440 | tf_op jit(solution)/shard_map/ppermute | solution.py:180
  81.9 12.2 %collective-permute-start.43 = (f32[64,1024]{1,0:T(8,128)S(1)}, f32[64,1024]{1,0:T(8,128)S(1)}, u32[]{:S(2)}, u32[]{:S(2)}) collective-permute-start(f32[64,1024]{1,0:T(8,128)S(1)} %collective-permute-done.31.refs_4_), channel_id=1, source_target_pairs={{0,4},{4,0},{1,5},{5,1},{2,6},{6,2},{3,7},{7,3},{8,12},{12,8},{9,1... | collective-permute-start | bytes 786440 | tf_op jit(solution)/shard_map/ppermute | solution.py:180
  83.2 10.9 %collective-permute-start.38 = (f32[64,1024]{1,0:T(8,128)}, f32[64,1024]{1,0:T(8,128)S(1)}, u32[]{:S(2)}, u32[]{:S(2)}) collective-permute-start(f32[64,1024]{1,0:T(8,128)} %collective-permute-done.37.refs_5_), channel_id=1, source_target_pairs={{0,64},{64,128},{128,192},{192,0},{1,65},{65,129},{129,193},{193,1... | collective-permute-start | bytes 786440 | tf_op jit(solution)/shard_map/ppermute | solution.py:180
  85.1 10.8 %collective-permute-start.44 = (f32[64,1024]{1,0:T(8,128)}, f32[64,1024]{1,0:T(8,128)S(1)}, u32[]{:S(2)}, u32[]{:S(2)}) collective-permute-start(f32[64,1024]{1,0:T(8,128)} %collective-permute-done.37.refs_5_), channel_id=1, source_target_pairs={{0,4},{4,0},{1,5},{5,1},{2,6},{6,2},{3,7},{7,3},{8,12},{12,8},{9,1... | collective-permute-start | bytes 786440 | tf_op jit(solution)/shard_map/ppermute | solution.py:180
  87.1 11.9 %collective-permute-start.33 = (f32[64,1024]{1,0:T(8,128)}, f32[64,1024]{1,0:T(8,128)S(1)}, u32[]{:S(2)}, u32[]{:S(2)}) collective-permute-start(f32[64,1024]{1,0:T(8,128)} %collective-permute-done.32.refs_0_), channel_id=1, source_target_pairs={{0,4},{4,0},{1,5},{5,1},{2,6},{6,2},{3,7},{7,3},{8,12},{12,8},{9,1... | collective-permute-start | bytes 786440 | tf_op jit(solution)/shard_map/ppermute | solution.py:180
  91.0 8.1 %collective-permute-start.36 = (f32[64,1024]{1,0:T(8,128)}, f32[64,1024]{1,0:T(8,128)S(1)}, u32[]{:S(2)}, u32[]{:S(2)}) collective-permute-start(f32[64,1024]{1,0:T(8,128)} %collective-permute-done.35.refs_7_), channel_id=1, source_target_pairs={{0,192},{64,0},{128,64},{192,128},{1,193},{65,1},{129,65},{193,129... | collective-permute-start | bytes 786440 | tf_op jit(solution)/shard_map/ppermute | solution.py:180
  (1 other events, 5.3 us)

commit v12 on v11

--- a/solution.py
+++ b/solution.py
@@ -202,12 +202,15 @@
     arrived, strip = lax.optimization_barrier((arrived, strip))
     spot = (oy * 4 + ((ox + 2 * oy) & 3)).astype(jnp.uint32)
     mine = lax.dynamic_index_in_dim(arrived, spot, 0, keepdims=False)
-    branches = [lambda v, s, r=r: (leap(v, r), opposite(s, "yh")) for r in range(8)]
-    leapt, across = lax.switch(oz, branches, mine, strip)
-    leapt, across, arrived = lax.optimization_barrier((leapt, across, arrived))
-    mine = land(mine, leapt, oz, z)
     last = arrived[ly * 4 + (lx + 2 * ly) % 4]
-    last = land(last, leap(last, lz), lz, z)
+
+    def branch(root):
+        return lambda a, b, block: (leap(a, root), leap(b, lz), opposite(block, "yh"))
+
+    leapt, last_leapt, across = lax.switch(
+        oz, [branch(r) for r in range(8)], mine, last, strip
+    )
+    mine, last = land(mine, leapt, oz, z), land(last, last_leapt, lz, z)
     strip = owned(strip, across, other, "yh").reshape(2, FREQ, ROWS, 2 * ROWS)
     mine, last = exchange([steps(mine, oz, z, False), steps(last, lz, z, True)])
     blocks = [v for pair in zip(mine, last) for v in pair]

time: 102 us -> 106 us (1.039)
  waiting for transfers between devices: 39.3 us -> 47.7 us
  starting transfers between devices: 45.3 us -> 42.9 us
    ppermute x2, starting transfers between devices: 4.61 us -> 13.6 us  [steps(): before = lax.ppermute(held, 'z', pairs(-1, (0, 3)))]
    ppermute x14, waiting for transfers between devices: 5.53 us -> 12.8 us  [send(): return lax.ppermute(v, axis, pairs)]
    ppermute x14, starting transfers between devices: 20.5 us -> 14.6 us  [send(): return lax.ppermute(v, axis, pairs)]
    ppermute x2, starting transfers between devices: 7.92 us -> 2.76 us  [leap(): up = lax.ppermute(v, 'z', [(root, (root + 3) % 8)])]
    ppermute x2, waiting for transfers between devices: 5.98 us -> 9.27 us  [opposite(): return lax.ppermute(block, axis, [(0, 1), (1, 0)])]
    ppermute x2, waiting for transfers between devices: 3.07 us -> 0.01 us  [leap(): down = lax.ppermute(v, 'z', [(root, (root - 3) % 8)])]
    ppermute x2, starting transfers between devices: 4.87 us -> 2.71 us  [leap(): down = lax.ppermute(v, 'z', [(root, (root - 3) % 8)])]
    ppermute x2, starting transfers between devices: 1.38 us -> 3.29 us  [steps(): after = lax.ppermute(held, 'z', pairs(1, (0, 3, 5)))]
  transfers between devices with their start and end apart: 25 -> 25, of which waited for: 11 -> 11; matrix products, arithmetic and copies ran while one was open for 7% -> 6% of each run, Pallas kernels for 3% -> 3%
where the time goes in v12:
time: 106 us
  waiting for transfers between devices  47.7 us (45%)
  starting transfers between devices  42.9 us (40%)
  other arithmetic  5.64 us (5%)
  Pallas kernels  5.37 us (5%)
  between operations  2.26 us (2%)
  local copies, waits for them, and re-layouts  2 us (2%)
    all_to_all x1, waiting for transfers between devices, scatter(): lax.all_to_all(rows, ('x', 'yl'), 0, 0, axis_index_groups=[members], tile...  22.1 us
    ppermute x14, starting transfers between devices, send(): return lax.ppermute(v, axis, pairs)  14.6 us
    ppermute x2, starting transfers between devices, steps(): before = lax.ppermute(held, 'z', pairs(-1, (0, 3)))  13.6 us
    ppermute x14, waiting for transfers between devices, send(): return lax.ppermute(v, axis, pairs)  12.8 us
    ppermute x2, waiting for transfers between devices, opposite(): return lax.ppermute(block, axis, [(0, 1), (1, 0)])  9.27 us
    pallas_call x2, Pallas kernels, call(): pl.pallas_call(body, in_specs=[pl.BlockSpec(memory_space=pltpu.SMEM), *[v...  5.37 us
    all_to_all x1, starting transfers between devices, scatter(): lax.all_to_all(rows, ('x', 'yl'), 0, 0, axis_index_groups=[members], tile...  5.29 us
    ppermute x2, waiting for transfers between devices, steps(): after = lax.ppermute(held, 'z', pairs(1, (0, 3, 5)))  3.52 us
  transfers between devices with their start and end apart: 25, of which 11 were waited for; matrix products, arithmetic and copies ran while one was open for 6% of the time, Pallas kernels for 3%

profile of v12, /device:TPU:16, one launch (start us, length us, event | category | flops | bytes accessed | tf_op | source)
XLA Modules:
  0.0 106.3 jit_solution(1670053993688809932)
XLA Ops:
  0.0 5.3 %all-to-all-start = ((f32[8,64,1024]{2,1,0:T(8,128)}), f32[8,64,1024]{2,1,0:T(8,128)}, u32[]{:S(2)}, u32[]{:S(2)}) async-start(f32[8,64,1024]{2,1,0:T(8,128)} %bitcast.14), calls=%async_computation | async-start | bytes 4194304 | tf_op jit(solution)/shard_map/all_to_all | solution.py:170
  8.6 1.2 %collective-permute-done.40 = f32[8,64,128]{2,1,0:T(8,128)S(1)} collective-permute-done((f32[8,64,128]{2,1,0:T(8,128)S(1)}, f32[8,64,128]{2,1,0:T(8,128)S(1)}, u32[]{:S(2)}, u32[]{:S(2)}) %collective-permute-start.40) | collective-permute-done | bytes 262176 | tf_op jit(solution)/shard_map/ppermute | solution.py:61
  10.7 22.1 %all-to-all-done = f32[8,64,1024]{2,1,0:T(8,128)} async-done(((f32[8,64,1024]{2,1,0:T(8,128)}), f32[8,64,1024]{2,1,0:T(8,128)}, u32[]{:S(2)}, u32[]{:S(2)}) %all-to-all-start) | async-done | bytes 2097184 | tf_op jit(solution)/shard_map/all_to_all | solution.py:170
  32.8 1.1 %slice_bitcast_fusion = (f32[64,1024]{1,0:T(8,128)S(1)}, f32[64,1024]{1,0:T(8,128)S(1)}) fusion(f32[8,64,1024]{2,1,0:T(8,128)} %all-to-all-done, u32[]{:T(128)S(6)} %convert_element_type.21), kind=kLoop, calls=%fused_computation.6 | loop fusion | bytes 1048580 | tf_op jit(solution)/shard_map/squeeze | solution.py:205
  33.8 14.2 %conditional.1 = (f32[64,1024]{1,0:T(8,128)}, f32[64,1024]{1,0:T(8,128)}, f32[64,1024]{1,0:T(8,128)}, f32[64,1024]{1,0:T(8,128)}, f32[8,64,128]{2,1,0:T(8,128)}) conditional(s32[]{:T(128)} %clamp.3, (f32[64,1024]{1,0:T(8,128)S(1)}, f32[64,1024]{1,0:T(8,128)S(1)}, f32[8,64,128]{2,1,0:T(8,128)}) %tuple.39, ...), branch_computations={%region_0.1_spmd, %region_1.2_spmd, %region_2.3_spmd, %region_3.4_... | conditional | bytes 5243120 | solution.py:210
  33.9 1.4 %collective-permute-start.10 = (f32[64,1024]{1,0:T(8,128)S(1)}, f32[64,1024]{1,0:T(8,128)}, u32[]{:S(2)}, u32[]{:S(2)}) collective-permute-start(f32[64,1024]{1,0:T(8,128)S(1)} %get-tuple-element.59), channel_id=1, source_target_pairs={{16,40},{17,41},{18,42},{19,43},{20,44},{21,45},{22,46},{23,47},{8... | collective-permute-start | bytes 786440 | tf_op jit(solution)/shard_map/cond/branch_2_fun/ppermute | solution.py:28
  35.2 1.4 %collective-permute-start.11 = (f32[64,1024]{1,0:T(8,128)S(1)}, f32[64,1024]{1,0:T(8,128)}, u32[]{:S(2)}, u32[]{:S(2)}) collective-permute-start(f32[64,1024]{1,0:T(8,128)S(1)} %get-tuple-element.59), channel_id=1, source_target_pairs={{16,56},{17,57},{18,58},{19,59},{20,60},{21,61},{22,62},{23,63},{8... | collective-permute-start | bytes 786440 | tf_op jit(solution)/shard_map/cond/branch_2_fun/ppermute | solution.py:29
  36.6 1.4 %collective-permute-start.12 = (f32[64,1024]{1,0:T(8,128)S(1)}, f32[64,1024]{1,0:T(8,128)}, u32[]{:S(2)}, u32[]{:S(2)}) collective-permute-start(f32[64,1024]{1,0:T(8,128)S(1)} %get-tuple-element.60), channel_id=1, source_target_pairs={{56,16},{57,17},{58,18},{59,19},{60,20},{61,21},{62,22},{63,23},{1... | collective-permute-start | bytes 786440 | tf_op jit(solution)/shard_map/cond/branch_2_fun/ppermute | solution.py:28
  38.0 1.3 %collective-permute-start.13 = (f32[64,1024]{1,0:T(8,128)S(1)}, f32[64,1024]{1,0:T(8,128)}, u32[]{:S(2)}, u32[]{:S(2)}) collective-permute-start(f32[64,1024]{1,0:T(8,128)S(1)} %get-tuple-element.60), channel_id=1, source_target_pairs={{56,32},{57,33},{58,34},{59,35},{60,36},{61,37},{62,38},{63,39},{1... | collective-permute-start | bytes 786440 | tf_op jit(solution)/shard_map/cond/branch_2_fun/ppermute | solution.py:29
  40.0 8.1 %collective-permute-done.14 = f32[8,64,128]{2,1,0:T(8,128)} collective-permute-done((f32[8,64,128]{2,1,0:T(8,128)}, f32[8,64,128]{2,1,0:T(8,128)}, u32[]{:S(2)}, u32[]{:S(2)}) %collective-permute-start.14) | collective-permute-done | bytes 262176 | tf_op jit(solution)/shard_map/cond/branch_2_fun/ppermute | solution.py:61
  48.1 1.1 %select_select_fusion.1 = f32[64,1024]{1,0:T(8,128)S(1)} fusion(f32[64,1024]{1,0:T(8,128)} %get-tuple-element.89, f32[64,1024]{1,0:T(8,128)} %get-tuple-element.90, pred[]{:T(512)S(6)} %eq.87, pred[]{:T(512)S(6)} %eq.86, f32[8,64,1024]{2,1,0:T(8,128)} %all-to-all-done), kind=kLoop, calls=%fused_computation.3 | loop fusion | flops 131072 | bytes 1048578 | tf_op jit(solution)/shard_map/jit(_where)/select_n | solution.py:35
  49.1 1.3 %collective-permute-start.43 = (f32[64,1024]{1,0:T(8,128)S(1)}, f32[64,1024]{1,0:T(8,128)S(1)}, u32[]{:S(2)}, u32[]{:S(2)}) collective-permute-start(f32[64,1024]{1,0:T(8,128)S(1)} %select_select_fusion.1), channel_id=1, source_target_pairs={{56,0},{16,24},{32,40},{57,1},{17,25},{33,41},{58,2},{18,26},{34,4... | collective-permute-start | bytes 786440 | tf_op jit(solution)/shard_map/ppermute | solution.py:43
  52.2 2.0 %collective-permute-start.41 = (f32[64,1024]{1,0:T(8,128)S(1)}, f32[64,1024]{1,0:T(8,128)}, u32[]{:S(2)}, u32[]{:S(2)}) collective-permute-start(f32[64,1024]{1,0:T(8,128)S(1)} %select_select_fusion.3), channel_id=1, source_target_pairs={{0,8},{8,16},{16,24},{24,32},{32,40},{40,48},{48,56},{56,0},{1,9},... | collective-permute-start | bytes 786440 | tf_op jit(solution)/shard_map/ppermute | solution.py:43
  54.2 12.9 %collective-permute-start.42 = (f32[64,1024]{1,0:T(8,128)S(1)}, f32[64,1024]{1,0:T(8,128)}, u32[]{:S(2)}, u32[]{:S(2)}) collective-permute-start(f32[64,1024]{1,0:T(8,128)S(1)} %select_select_fusion.3), channel_id=1, source_target_pairs={{0,56},{8,0},{16,8},{24,16},{32,24},{40,32},{48,40},{56,48},{1,57}... | collective-permute-start | bytes 786440 | tf_op jit(solution)/shard_map/ppermute | solution.py:44
  67.3 3.5 %collective-permute-done.43 = f32[64,1024]{1,0:T(8,128)S(1)} collective-permute-done((f32[64,1024]{1,0:T(8,128)S(1)}, f32[64,1024]{1,0:T(8,128)S(1)}, u32[]{:S(2)}, u32[]{:S(2)}) %collective-permute-start.43) | collective-permute-done | bytes 262176 | tf_op jit(solution)/shard_map/ppermute | solution.py:43
  71.9 2.8 %collective-permute-start.56 = (f32[64,1024]{1,0:T(8,128)S(1)}, f32[64,1024]{1,0:T(8,128)S(1)}, u32[]{:S(2)}, u32[]{:S(2)}) collective-permute-start(f32[64,1024]{1,0:T(8,128)S(1)} %select_select_fusion.refs_1_), channel_id=1, source_target_pairs={{0,192},{64,0},{128,64},{192,128},{1,193},{65,1},{129,65},{193,129... | collective-permute-start | bytes 786440 | tf_op jit(solution)/shard_map/ppermute | solution.py:180
  74.7 1.1 %select_select_fusion.2.refs_0_ = f32[64,1024]{1,0:T(8,128)S(1)} fusion(f32[64,1024]{1,0:T(8,128)} %collective-permute-done.41, f32[64,1024]{1,0:T(8,128)} %collective-permute-done.42, f32[64,1024]{1,0:T(8,128)} %copy-done.2, pred[]{:T(512)S(6)} %or.20, pred[]{:T(512)S(6)} %or.19), kind=kLoop, calls=%fused_computation.4 | loop fusion | flops 131072 | bytes 1048578 | tf_op jit(solution)/shard_map/jit(_where)/select_n | solution.py:48
  76.1 1.5 %collective-permute-start.53 = (f32[64,1024]{1,0:T(8,128)S(1)}, f32[64,1024]{1,0:T(8,128)}, u32[]{:S(2)}, u32[]{:S(2)}) collective-permute-start(f32[64,1024]{1,0:T(8,128)S(1)} %select_select_fusion.2.refs_0_), channel_id=1, source_target_pairs={{0,4},{4,0},{1,5},{5,1},{2,6},{6,2},{3,7},{7,3},{8,12},{12,8},{9,1... | collective-permute-start | bytes 786440 | tf_op jit(solution)/shard_map/ppermute | solution.py:180
  77.6 2.1 %collective-permute-done.48.refs_3_ = f32[64,1024]{1,0:T(8,128)S(1)} collective-permute-done((f32[64,1024]{1,0:T(8,128)S(1)}, f32[64,1024]{1,0:T(8,128)S(1)}, u32[]{:S(2)}, u32[]{:S(2)}) %collective-permute-start.48) | collective-permute-done | bytes 262176 | tf_op jit(solution)/shard_map/ppermute | solution.py:180
  79.7 1.1 %collective-permute-start.55 = (f32[64,1024]{1,0:T(8,128)S(1)}, f32[64,1024]{1,0:T(8,128)}, u32[]{:S(2)}, u32[]{:S(2)}) collective-permute-start(f32[64,1024]{1,0:T(8,128)S(1)} %select_select_fusion.2.refs_0_), channel_id=1, source_target_pairs={{0,192},{64,0},{128,64},{192,128},{1,193},{65,1},{129,65},{193,129... | collective-permute-start | bytes 786440 | tf_op jit(solution)/shard_map/ppermute | solution.py:180
  80.8 1.1 %collective-permute-done.51.refs_5_ = f32[64,1024]{1,0:T(8,128)S(1)} collective-permute-done((f32[64,1024]{1,0:T(8,128)S(1)}, f32[64,1024]{1,0:T(8,128)S(1)}, u32[]{:S(2)}, u32[]{:S(2)}) %collective-permute-start.51) | collective-permute-done | bytes 262176 | tf_op jit(solution)/shard_map/ppermute | solution.py:180
  82.0 2.0 %collective-permute-start.52 = (f32[64,1024]{1,0:T(8,128)S(1)}, f32[64,1024]{1,0:T(8,128)}, u32[]{:S(2)}, u32[]{:S(2)}) collective-permute-start(f32[64,1024]{1,0:T(8,128)S(1)} %collective-permute-done.51.refs_5_), channel_id=1, source_target_pairs={{0,64},{64,128},{128,192},{192,0},{1,65},{65,129},{129,193},{193,1... | collective-permute-start | bytes 786440 | tf_op jit(solution)/shard_map/ppermute | solution.py:180
  83.9 3.7 %collective-permute-done.45.refs_4_ = f32[64,1024]{1,0:T(8,128)} collective-permute-done((f32[64,1024]{1,0:T(8,128)S(1)}, f32[64,1024]{1,0:T(8,128)}, u32[]{:S(2)}, u32[]{:S(2)}) %collective-permute-start.45) | collective-permute-done | bytes 262176 | tf_op jit(solution)/shard_map/ppermute | solution.py:180
  87.8 1.1 %broadcast_select_fusion.1 = f32[8,64,128]{2,1,0:T(8,128)S(1)} fusion(f32[8,64,128]{2,1,0:T(8,128)} %broadcast_select_fusion, f32[8,64,128]{2,1,0:T(8,128)} %get-tuple-element.86, pred[128]{0:T(512)(128)(4,1)S(1)} %fusion.1), kind=kLoop, calls=%fused_computation.11 | loop fusion | flops 65536 | bytes 786560 | tf_op jit(solution)/shard_map/jit(_where)/select_n | solution.py:68
  89.4 1.5 %collective-permute-start.57 = (f32[64,1024]{1,0:T(8,128)}, f32[64,1024]{1,0:T(8,128)S(1)}, u32[]{:S(2)}, u32[]{:S(2)}) collective-permute-start(f32[64,1024]{1,0:T(8,128)} %collective-permute-done.45.refs_4_), channel_id=1, source_target_pairs={{0,4},{4,0},{1,5},{5,1},{2,6},{6,2},{3,7},{7,3},{8,12},{12,8},{9,1... | collective-permute-start | bytes 786440 | tf_op jit(solution)/shard_map/ppermute | solution.py:180
  91.0 3.2 %collective-permute-start.54 = (f32[64,1024]{1,0:T(8,128)}, f32[64,1024]{1,0:T(8,128)S(1)}, u32[]{:S(2)}, u32[]{:S(2)}) collective-permute-start(f32[64,1024]{1,0:T(8,128)} %collective-permute-done.53.refs_2_), channel_id=1, source_target_pairs={{0,192},{64,0},{128,64},{192,128},{1,193},{65,1},{129,65},{193,129... | collective-permute-start | bytes 786440 | tf_op jit(solution)/shard_map/ppermute | solution.py:180
  94.3 1.3 %collective-permute-done.46.refs_0_ = f32[64,1024]{1,0:T(8,128)} collective-permute-done((f32[64,1024]{1,0:T(8,128)}, f32[64,1024]{1,0:T(8,128)}, u32[]{:S(2)}, u32[]{:S(2)}) %collective-permute-start.46) | collective-permute-done | bytes 262176 | tf_op jit(solution)/shard_map/ppermute | solution.py:180
  96.2 1.0 collective-permute-done.58.refs_11_
  97.3 1.1 %collective-permute-done.54.refs_6_ = f32[64,1024]{1,0:T(8,128)S(1)} collective-permute-done((f32[64,1024]{1,0:T(8,128)}, f32[64,1024]{1,0:T(8,128)S(1)}, u32[]{:S(2)}, u32[]{:S(2)}) %collective-permute-start.54) | collective-permute-done | bytes 262176 | tf_op jit(solution)/shard_map/ppermute | solution.py:180
  98.4 2.5 %collective-permute-done.57.refs_10_ = f32[64,1024]{1,0:T(8,128)S(1)} collective-permute-done((f32[64,1024]{1,0:T(8,128)}, f32[64,1024]{1,0:T(8,128)S(1)}, u32[]{:S(2)}, u32[]{:S(2)}) %collective-permute-start.57) | collective-permute-done | bytes 262176 | tf_op jit(solution)/shard_map/ppermute | solution.py:180
  100.9 3.1 %shard_map.73.refs_4_ = f32[8,64,1024]{2,1,0:T(8,128)S(1)} custom-call(s32[4]{0:T(128)S(1)} %get-tuple-element.101.bins, f32[2,4,64,1024]{3,2,1,0:T(8,128)S(1)} %copy-done.1, f32[4,128,256]{2,1,0:T(8,128)S(1)} %maximum_select_fusion.l_ref, f32[64,64]{1,0:T(8,128)S(1)} %copy.12.coef_ref, f32[64,1024]{1,0:T(8,128)} %collective-permute-done.46.refs_0_, ...), custom_call_target="tpu_custom_call" | custom-call | flops 603979776 | bytes 6291456 | tf_op jit(solution)/shard_map/pallas_call | solution.py:123
  104.1 2.2 %shard_map.74 = bf16[8,64,1024]{2,1,0:T(8,128)(2,1)} custom-call(s32[4]{0:T(128)S(1)} %get-tuple-element.101.bins, f32[2,4,64,1024]{3,2,1,0:T(8,128)S(1)} %copy-done.1, f32[4,128,256]{2,1,0:T(8,128)S(1)} %maximum_select_fusion.l_ref, f32[64,64]{1,0:T(8,128)S(1)} %copy.12.coef_ref, f32[64,1024]{1,0:T(8,128)S(1)} %select_select_fusion.2.refs_0_, ...), custom_call_target="tpu_custom_call" | custom-call | flops 201326592 | bytes 2097152 | tf_op jit(solution)/shard_map/pallas_call | solution.py:123
  (59 shorter events, 7.6 us)
Async XLA Ops:
  0.0 8.4 %copy-start = (f32[64,64]{1,0:T(8,128)S(1)}, f32[64,64]{1,0:T(8,128)}, u32[]{:S(2)}) copy-start(f32[64,64]{1,0:T(8,128)} %param.17) | copy-start | bytes 49156
  0.0 7.9 %copy-start.1 = (f32[2,4,64,1024]{3,2,1,0:T(8,128)S(1)}, f32[2,4,64,1024]{3,2,1,0:T(8,128)}, u32[]{:S(2)}) copy-start(f32[2,4,64,1024]{3,2,1,0:T(8,128)} %x_ref.3) | copy-start | bytes 6291460
  0.0 8.3 %copy-start.7 = (s32[4]{0:T(128)S(1)}, s32[4]{0:T(128)}, u32[]{:S(2)}) copy-start(s32[4]{0:T(128)} %constant.60.clone) | copy-start | bytes 52
  0.0 8.3 %copy-start.6 = (s32[64]{0:T(128)S(1)}, s32[64]{0:T(128)}, u32[]{:S(2)}) copy-start(s32[64]{0:T(128)} %param.18) | copy-start | bytes 772
  0.0 8.4 %copy-start.4 = (f32[64,4]{1,0:T(8,128)S(1)}, f32[64,4]{1,0:T(8,128)}, u32[]{:S(2)}) copy-start(f32[64,4]{1,0:T(8,128)} %constant.61.clone) | copy-start | bytes 3076
  0.0 32.7 %all-to-all-start = ((f32[8,64,1024]{2,1,0:T(8,128)}), f32[8,64,1024]{2,1,0:T(8,128)}, u32[]{:S(2)}, u32[]{:S(2)}) async-start(f32[8,64,1024]{2,1,0:T(8,128)} %bitcast.14), calls=%async_computation | async-start | bytes 4194304 | tf_op jit(solution)/shard_map/all_to_all | solution.py:170
  8.2 1.6 %collective-permute-start.40 = (f32[8,64,128]{2,1,0:T(8,128)S(1)}, f32[8,64,128]{2,1,0:T(8,128)S(1)}, u32[]{:S(2)}, u32[]{:S(2)}) collective-permute-start(f32[8,64,128]{2,1,0:T(8,128)S(1)} %pad_maximum_fusion), channel_id=1, source_target_pairs={{0,1},{1,0},{2,3},{3,2},{4,5},{5,4},{6,7},{7,6},{8,9},{9,8},{10,11... | collective-permute-start | bytes 786440 | tf_op jit(solution)/shard_map/ppermute | solution.py:61
  33.9 6.1 %collective-permute-start.10 = (f32[64,1024]{1,0:T(8,128)S(1)}, f32[64,1024]{1,0:T(8,128)}, u32[]{:S(2)}, u32[]{:S(2)}) collective-permute-start(f32[64,1024]{1,0:T(8,128)S(1)} %get-tuple-element.59), channel_id=1, source_target_pairs={{16,40},{17,41},{18,42},{19,43},{20,44},{21,45},{22,46},{23,47},{8... | collective-permute-start | bytes 786440 | tf_op jit(solution)/shard_map/cond/branch_2_fun/ppermute | solution.py:28
  35.2 4.7 %collective-permute-start.11 = (f32[64,1024]{1,0:T(8,128)S(1)}, f32[64,1024]{1,0:T(8,128)}, u32[]{:S(2)}, u32[]{:S(2)}) collective-permute-start(f32[64,1024]{1,0:T(8,128)S(1)} %get-tuple-element.59), channel_id=1, source_target_pairs={{16,56},{17,57},{18,58},{19,59},{20,60},{21,61},{22,62},{23,63},{8... | collective-permute-start | bytes 786440 | tf_op jit(solution)/shard_map/cond/branch_2_fun/ppermute | solution.py:29
  36.6 3.4 %collective-permute-start.12 = (f32[64,1024]{1,0:T(8,128)S(1)}, f32[64,1024]{1,0:T(8,128)}, u32[]{:S(2)}, u32[]{:S(2)}) collective-permute-start(f32[64,1024]{1,0:T(8,128)S(1)} %get-tuple-element.60), channel_id=1, source_target_pairs={{56,16},{57,17},{58,18},{59,19},{60,20},{61,21},{62,22},{63,23},{1... | collective-permute-start | bytes 786440 | tf_op jit(solution)/shard_map/cond/branch_2_fun/ppermute | solution.py:28
  38.0 2.0 %collective-permute-start.13 = (f32[64,1024]{1,0:T(8,128)S(1)}, f32[64,1024]{1,0:T(8,128)}, u32[]{:S(2)}, u32[]{:S(2)}) collective-permute-start(f32[64,1024]{1,0:T(8,128)S(1)} %get-tuple-element.60), channel_id=1, source_target_pairs={{56,32},{57,33},{58,34},{59,35},{60,36},{61,37},{62,38},{63,39},{1... | collective-permute-start | bytes 786440 | tf_op jit(solution)/shard_map/cond/branch_2_fun/ppermute | solution.py:29
  39.3 8.7 %collective-permute-start.14 = (f32[8,64,128]{2,1,0:T(8,128)}, f32[8,64,128]{2,1,0:T(8,128)}, u32[]{:S(2)}, u32[]{:S(2)}) collective-permute-start(f32[8,64,128]{2,1,0:T(8,128)} %get-tuple-element.61), channel_id=1, source_target_pairs={{0,2},{2,0},{1,3},{3,1},{4,6},{6,4},{5,7},{7,5},{8,10},{10,8},{9,1... | collective-permute-start | bytes 786440 | tf_op jit(solution)/shard_map/cond/branch_2_fun/ppermute | solution.py:61
  48.1 27.9 %copy-start.3 = (f32[64,4]{1,0:T(8,128)S(1)}, f32[64,4]{1,0:T(8,128)}, u32[]{:S(2)}) copy-start(f32[64,4]{1,0:T(8,128)} %constant.62.clone) | copy-start | bytes 3076
  49.1 21.6 %collective-permute-start.43 = (f32[64,1024]{1,0:T(8,128)S(1)}, f32[64,1024]{1,0:T(8,128)S(1)}, u32[]{:S(2)}, u32[]{:S(2)}) collective-permute-start(f32[64,1024]{1,0:T(8,128)S(1)} %select_select_fusion.1), channel_id=1, source_target_pairs={{56,0},{16,24},{32,40},{57,1},{17,25},{33,41},{58,2},{18,26},{34,4... | collective-permute-start | bytes 786440 | tf_op jit(solution)/shard_map/ppermute | solution.py:43
  50.4 20.3 %collective-permute-start.44 = (f32[64,1024]{1,0:T(8,128)S(1)}, f32[64,1024]{1,0:T(8,128)S(1)}, u32[]{:S(2)}, u32[]{:S(2)}) collective-permute-start(f32[64,1024]{1,0:T(8,128)S(1)} %select_select_fusion.1), channel_id=1, source_target_pairs={{56,48},{16,8},{57,49},{17,9},{58,50},{18,10},{59,51},{19,11},{60,... | collective-permute-start | bytes 786440 | tf_op jit(solution)/shard_map/ppermute | solution.py:44
  52.2 22.6 %copy-start.2 = (f32[64,1024]{1,0:T(8,128)}, f32[64,1024]{1,0:T(8,128)S(1)}, u32[]{:S(2)}) copy-start(f32[64,1024]{1,0:T(8,128)S(1)} %select_select_fusion.3) | copy-start | bytes 786436
  52.2 22.5 %collective-permute-start.41 = (f32[64,1024]{1,0:T(8,128)S(1)}, f32[64,1024]{1,0:T(8,128)}, u32[]{:S(2)}, u32[]{:S(2)}) collective-permute-start(f32[64,1024]{1,0:T(8,128)S(1)} %select_select_fusion.3), channel_id=1, source_target_pairs={{0,8},{8,16},{16,24},{24,32},{32,40},{40,48},{48,56},{56,0},{1,9},... | collective-permute-start | bytes 786440 | tf_op jit(solution)/shard_map/ppermute | solution.py:43
  54.2 20.6 %collective-permute-start.42 = (f32[64,1024]{1,0:T(8,128)S(1)}, f32[64,1024]{1,0:T(8,128)}, u32[]{:S(2)}, u32[]{:S(2)}) collective-permute-start(f32[64,1024]{1,0:T(8,128)S(1)} %select_select_fusion.3), channel_id=1, source_target_pairs={{0,56},{8,0},{16,8},{24,16},{32,24},{40,32},{48,40},{56,48},{1,57}... | collective-permute-start | bytes 786440 | tf_op jit(solution)/shard_map/ppermute | solution.py:44
  70.8 8.9 %collective-permute-start.48 = (f32[64,1024]{1,0:T(8,128)S(1)}, f32[64,1024]{1,0:T(8,128)S(1)}, u32[]{:S(2)}, u32[]{:S(2)}) collective-permute-start(f32[64,1024]{1,0:T(8,128)S(1)} %select_select_fusion.refs_1_), channel_id=1, source_target_pairs={{0,4},{4,0},{1,5},{5,1},{2,6},{6,2},{3,7},{7,3},{8,12},{12,8},{9,1... | collective-permute-start | bytes 786440 | tf_op jit(solution)/shard_map/ppermute | solution.py:180
  71.5 10.4 %collective-permute-start.51 = (f32[64,1024]{1,0:T(8,128)S(1)}, f32[64,1024]{1,0:T(8,128)S(1)}, u32[]{:S(2)}, u32[]{:S(2)}) collective-permute-start(f32[64,1024]{1,0:T(8,128)S(1)} %select_select_fusion.refs_1_), channel_id=1, source_target_pairs={{0,64},{64,128},{128,192},{192,0},{1,65},{65,129},{129,193},{193,1... | collective-permute-start | bytes 786440 | tf_op jit(solution)/shard_map/ppermute | solution.py:180
  71.9 10.0 %collective-permute-start.56 = (f32[64,1024]{1,0:T(8,128)S(1)}, f32[64,1024]{1,0:T(8,128)S(1)}, u32[]{:S(2)}, u32[]{:S(2)}) collective-permute-start(f32[64,1024]{1,0:T(8,128)S(1)} %select_select_fusion.refs_1_), channel_id=1, source_target_pairs={{0,192},{64,0},{128,64},{192,128},{1,193},{65,1},{129,65},{193,129... | collective-permute-start | bytes 786440 | tf_op jit(solution)/shard_map/ppermute | solution.py:180
  75.8 11.8 %collective-permute-start.45 = (f32[64,1024]{1,0:T(8,128)S(1)}, f32[64,1024]{1,0:T(8,128)}, u32[]{:S(2)}, u32[]{:S(2)}) collective-permute-start(f32[64,1024]{1,0:T(8,128)S(1)} %select_select_fusion.2.refs_0_), channel_id=1, source_target_pairs={{0,64},{64,128},{128,192},{192,0},{1,65},{65,129},{129,193},{193,1... | collective-permute-start | bytes 786440 | tf_op jit(solution)/shard_map/ppermute | solution.py:180
  76.1 12.7 %collective-permute-start.53 = (f32[64,1024]{1,0:T(8,128)S(1)}, f32[64,1024]{1,0:T(8,128)}, u32[]{:S(2)}, u32[]{:S(2)}) collective-permute-start(f32[64,1024]{1,0:T(8,128)S(1)} %select_select_fusion.2.refs_0_), channel_id=1, source_target_pairs={{0,4},{4,0},{1,5},{5,1},{2,6},{6,2},{3,7},{7,3},{8,12},{12,8},{9,1... | collective-permute-start | bytes 786440 | tf_op jit(solution)/shard_map/ppermute | solution.py:180
  79.7 9.8 %collective-permute-start.55 = (f32[64,1024]{1,0:T(8,128)S(1)}, f32[64,1024]{1,0:T(8,128)}, u32[]{:S(2)}, u32[]{:S(2)}) collective-permute-start(f32[64,1024]{1,0:T(8,128)S(1)} %select_select_fusion.2.refs_0_), channel_id=1, source_target_pairs={{0,192},{64,0},{128,64},{192,128},{1,193},{65,1},{129,65},{193,129... | collective-permute-start | bytes 786440 | tf_op jit(solution)/shard_map/ppermute | solution.py:180
  81.9 9.0 %collective-permute-start.49 = (f32[64,1024]{1,0:T(8,128)S(1)}, f32[64,1024]{1,0:T(8,128)}, u32[]{:S(2)}, u32[]{:S(2)}) collective-permute-start(f32[64,1024]{1,0:T(8,128)S(1)} %collective-permute-done.48.refs_3_), channel_id=1, source_target_pairs={{0,192},{64,0},{128,64},{192,128},{1,193},{65,1},{129,65},{193,129... | collective-permute-start | bytes 786440 | tf_op jit(solution)/shard_map/ppermute | solution.py:180
  82.0 12.2 %collective-permute-start.52 = (f32[64,1024]{1,0:T(8,128)S(1)}, f32[64,1024]{1,0:T(8,128)}, u32[]{:S(2)}, u32[]{:S(2)}) collective-permute-start(f32[64,1024]{1,0:T(8,128)S(1)} %collective-permute-done.51.refs_5_), channel_id=1, source_target_pairs={{0,64},{64,128},{128,192},{192,0},{1,65},{65,129},{129,193},{193,1... | collective-permute-start | bytes 786440 | tf_op jit(solution)/shard_map/ppermute | solution.py:180
  87.6 7.9 %collective-permute-start.46 = (f32[64,1024]{1,0:T(8,128)}, f32[64,1024]{1,0:T(8,128)}, u32[]{:S(2)}, u32[]{:S(2)}) collective-permute-start(f32[64,1024]{1,0:T(8,128)} %collective-permute-done.45.refs_4_), channel_id=1, source_target_pairs={{0,64},{64,128},{128,192},{192,0},{1,65},{65,129},{129,193},{193,1... | collective-permute-start | bytes 786440 | tf_op jit(solution)/shard_map/ppermute | solution.py:180
  88.8 8.4 %collective-permute-start.58 = (f32[64,1024]{1,0:T(8,128)S(1)}, f32[64,1024]{1,0:T(8,128)S(1)}, u32[]{:S(2)}, u32[]{:S(2)}) collective-permute-start(f32[64,1024]{1,0:T(8,128)S(1)} %collective-permute-done.51.refs_5_), channel_id=1, source_target_pairs={{0,4},{4,0},{1,5},{5,1},{2,6},{6,2},{3,7},{7,3},{8,12},{12,8},{9,1... | collective-permute-start | bytes 786440 | tf_op jit(solution)/shard_map/ppermute | solution.py:180
  89.4 11.5 %collective-permute-start.57 = (f32[64,1024]{1,0:T(8,128)}, f32[64,1024]{1,0:T(8,128)S(1)}, u32[]{:S(2)}, u32[]{:S(2)}) collective-permute-start(f32[64,1024]{1,0:T(8,128)} %collective-permute-done.45.refs_4_), channel_id=1, source_target_pairs={{0,4},{4,0},{1,5},{5,1},{2,6},{6,2},{3,7},{7,3},{8,12},{12,8},{9,1... | collective-permute-start | bytes 786440 | tf_op jit(solution)/shard_map/ppermute | solution.py:180
  91.0 7.4 %collective-permute-start.54 = (f32[64,1024]{1,0:T(8,128)}, f32[64,1024]{1,0:T(8,128)S(1)}, u32[]{:S(2)}, u32[]{:S(2)}) collective-permute-start(f32[64,1024]{1,0:T(8,128)} %collective-permute-done.53.refs_2_), channel_id=1, source_target_pairs={{0,192},{64,0},{128,64},{192,128},{1,193},{65,1},{129,65},{193,129... | collective-permute-start | bytes 786440 | tf_op jit(solution)/shard_map/ppermute | solution.py:180
  94.2 9.9 %collective-permute-start.50 = (f32[64,1024]{1,0:T(8,128)}, f32[64,1024]{1,0:T(8,128)S(1)}, u32[]{:S(2)}, u32[]{:S(2)}) collective-permute-start(f32[64,1024]{1,0:T(8,128)} %collective-permute-done.49.refs_7_), channel_id=1, source_target_pairs={{0,192},{64,0},{128,64},{192,128},{1,193},{65,1},{129,65},{193,129... | collective-permute-start | bytes 786440 | tf_op jit(solution)/shard_map/ppermute | solution.py:180
  95.5 8.5 %collective-permute-start.47 = (f32[64,1024]{1,0:T(8,128)}, f32[64,1024]{1,0:T(8,128)S(1)}, u32[]{:S(2)}, u32[]{:S(2)}) collective-permute-start(f32[64,1024]{1,0:T(8,128)} %collective-permute-done.46.refs_0_), channel_id=1, source_target_pairs={{0,4},{4,0},{1,5},{5,1},{2,6},{6,2},{3,7},{7,3},{8,12},{12,8},{9,1... | collective-permute-start | bytes 786440 | tf_op jit(solution)/shard_map/ppermute | solution.py:180
  (1 other events, 5.3 us)

commit v13 on v12

--- a/solution.py
+++ b/solution.py
@@ -68,75 +68,87 @@
     return jnp.where(keep, block, other)
 
 
-def partial(sets, bins, x_ref, l_ref, coef_ref, block_refs, before_ref, d_ref, store):
-    for n, i in enumerate(sets):
-        b = jnp.concatenate([r[...] for r in block_refs[4 * n : 4 * n + 4]], axis=0)
-        high = b.astype(jnp.bfloat16)
-        low = (b - high.astype(jnp.float32)).astype(jnp.bfloat16)
-        f = bins[i]
-        left = l_ref[f]
-        left_high = left.astype(jnp.bfloat16)
-        left_low = (left - left_high.astype(jnp.float32)).astype(jnp.bfloat16)
-        both = jnp.dot(
-            jnp.concatenate([left_high, left_low], axis=0),
-            high,
-            preferred_element_type=jnp.float32,
-        )
-        rest = jnp.dot(left_high, low, preferred_element_type=jnp.float32)
-        product = both[: 2 * ROWS] + (both[2 * ROWS :] + rest)
-        d_ref[2 * n] = x_ref[0, f] - product[:ROWS]
-        d_ref[2 * n + 1] = x_ref[1, f] - product[ROWS:]
+def product(left, part, block_refs):
+    left = left[:, part * 2 * ROWS : (part + 1) * 2 * ROWS]
+    b = jnp.concatenate([r[...] for r in block_refs], axis=0)
+    high = b.astype(jnp.bfloat16)
+    low = (b - high.astype(jnp.float32)).astype(jnp.bfloat16)
+    left_high = left.astype(jnp.bfloat16)
+    left_low = (left - left_high.astype(jnp.float32)).astype(jnp.bfloat16)
+    both = jnp.dot(
+        jnp.concatenate([left_high, left_low], axis=0),
+        high,
+        preferred_element_type=jnp.float32,
+    )
+    rest = jnp.dot(left_high, low, preferred_element_type=jnp.float32)
+    return both[: 2 * ROWS] + (both[2 * ROWS :] + rest)
+
+
+def synthesis(planes_ref, first_plane, count, coef_ref, before_ref, o_ref):
     for first in range(0, ROWS, GROUP):
         rows = slice(first, first + GROUP)
-        spectrum = [d_ref[k, rows, :] for k in range(2 * len(sets))]
+        planes = [planes_ref[k, rows, :] for k in range(count)]
         for u in range(TWIN):
             total = None if before_ref is None else before_ref[u, rows, :]
-            for k, value in enumerate(spectrum):
-                at = u * 8 + 2 * sets[0] + k
+            for k, value in enumerate(planes):
+                at = u * 8 + first_plane + k
                 term = value * coef_ref[rows, at : at + 1]
                 total = term if total is None else total + term
-            store(u, rows, total)
-
-
-def early_kernel(bins, x_ref, l_ref, coef_ref, *refs):
-    block_refs, o_ref, d_ref = refs[:12], refs[12], refs[13]
-
-    def store(u, rows, total):
-        o_ref[u, rows, :] = total
-
-    partial((1, 2, 3), bins, x_ref, l_ref, coef_ref, block_refs, None, d_ref, store)
-
-
-def late_kernel(bins, x_ref, l_ref, coef_ref, *refs):
-    block_refs, before_ref, o_ref, d_ref = refs[:4], refs[4], refs[5], refs[6]
-
-    def store(u, rows, total):
-        o_ref[u, rows, :] = total.astype(o_ref.dtype)
-
-    partial((0,), bins, x_ref, l_ref, coef_ref, block_refs, before_ref, d_ref, store)
-
-
-def synthesise(bins, spectra, left, coefs, blocks):
+            o_ref[u, rows, :] = total.astype(o_ref.dtype)
+
+
+def first_kernel(bins, x_ref, l_ref, *refs):
+    block_refs, d_ref = refs[:8], refs[8]
+    for i, part in enumerate((0, 1, 0, 0)):
+        f = bins[i]
+        p = product(l_ref[f], part, block_refs[2 * i : 2 * i + 2])
+        d_ref[2 * i] = x_ref[0, f] - p[:ROWS]
+        d_ref[2 * i + 1] = x_ref[1, f] - p[ROWS:]
+
+
+def second_kernel(bins, d_ref, l_ref, coef_ref, *refs):
+    block_refs, o_ref, e_ref = refs[:6], refs[6], refs[7]
+    for n, part in enumerate((0, 1, 1)):
+        p = product(l_ref[bins[n + 1]], part, block_refs[2 * n : 2 * n + 2])
+        e_ref[2 * n] = d_ref[2 * n + 2] - p[:ROWS]
+        e_ref[2 * n + 1] = d_ref[2 * n + 3] - p[ROWS:]
+    synthesis(e_ref, 2, 6, coef_ref, None, o_ref)
+
+
+def third_kernel(bins, d_ref, l_ref, coef_ref, mine_ref, last_ref, before_ref, o_ref, e_ref):
+    p = product(l_ref[bins[0]], 1, (mine_ref, last_ref))
+    e_ref[0] = d_ref[0] - p[:ROWS]
+    e_ref[1] = d_ref[1] - p[ROWS:]
+    synthesis(e_ref, 0, 2, coef_ref, before_ref, o_ref)
+
+
+def synthesise(bins, spectra, left, coefs, mine, last):
     vmem = pl.BlockSpec(memory_space=pltpu.VMEM)
 
-    def call(body, sets, dtype, operands):
+    def call(body, halves, dtype, scratch, operands):
         return pl.pallas_call(
             body,
             in_specs=[pl.BlockSpec(memory_space=pltpu.SMEM), *[vmem] * len(operands)],
             out_specs=vmem,
             out_shape=jax.ShapeDtypeStruct((TWIN, ROWS, COLS), dtype),
-            scratch_shapes=[pltpu.VMEM((2 * sets, ROWS, COLS), jnp.float32)],
+            scratch_shapes=[pltpu.VMEM((n, ROWS, COLS), jnp.float32) for n in scratch],
             compiler_params=pltpu.CompilerParams(vmem_limit_bytes=24 * 1024 * 1024),
             cost_estimate=pl.CostEstimate(
-                flops=2 * 3 * sets * 128 * 256 * COLS,
-                bytes_accessed=2 * 2**20 * sets,
+                flops=2 * 3 * halves * 128 * 128 * COLS,
+                bytes_accessed=2**20 * halves,
                 transcendentals=0,
             ),
         )(bins, *operands)
 
-    early = call(early_kernel, 3, jnp.float32, [spectra, left, coefs, *blocks[4:]])
+    def pick(*places):
+        return [v[k] for k in places for v in (mine, last)]
+
+    planes = call(first_kernel, 4, jnp.float32, [], [spectra, left, *pick(0, 3, 4, 6)])
+    totals = call(
+        second_kernel, 3, jnp.float32, [6], [planes, left, coefs, *pick(2, 5, 7)]
+    )
     return call(
-        late_kernel, 1, jnp.bfloat16, [spectra, left, coefs, *blocks[:4], early]
+        third_kernel, 1, jnp.bfloat16, [2], [planes, left, coefs, *pick(1), totals]
     )
 
 
@@ -213,10 +225,9 @@
     mine, last = land(mine, leapt, oz, z), land(last, last_leapt, lz, z)
     strip = owned(strip, across, other, "yh").reshape(2, FREQ, ROWS, 2 * ROWS)
     mine, last = exchange([steps(mine, oz, z, False), steps(last, lz, z, True)])
-    blocks = [v for pair in zip(mine, last) for v in pair]
     bins = (x + 2 * yl + jnp.array([0, 2, 3, 1], jnp.int32)) & 3
     left, coefs = tables(filters, offsets, strip, bins, yl)
-    return synthesise(bins, spectra, left, coefs, blocks)
+    return synthesise(bins, spectra, left, coefs, mine, last)
 
 
 def solution(mesh):

time: 106 us -> 103 us (0.972); the launches traced: 106 us -> 101 us
  starting transfers between devices: 42.9 us -> 37.7 us
  waiting for transfers between devices: 47.7 us -> 45.9 us
  Pallas kernels: 5.37 us -> 7.08 us
    ppermute x2, starting transfers between devices: 13.6 us -> 8.37 us  [steps(): before = lax.ppermute(held, 'z', pairs(-1, (0, 3)))]
    ppermute x14, waiting for transfers between devices: 12.8 us -> 10.6 us  [send(): return lax.ppermute(v, axis, pairs)]
    pallas_call x2 -> x3, Pallas kernels: 5.37 us -> 7.08 us  [call(): pl.pallas_call(body, in_specs=[pl.BlockSpec(memory_space=pltpu.SMEM), *[v...]
  transfers between devices with their start and end apart: 25 -> 25, of which waited for: 11 -> 9; matrix products, arithmetic and copies ran while one was open for 6% -> 6% of each run, Pallas kernels for 3% -> 5%
where the time goes in v13:
time: 103 us; the launch traced here: 101 us
  waiting for transfers between devices  45.9 us (45%)
  starting transfers between devices  37.7 us (37%)
  Pallas kernels  7.08 us (7%)
  other arithmetic  5.56 us (5%)
  between operations  2.27 us (2%)
  local copies, waits for them, and re-layouts  2 us (2%)
    all_to_all x1, waiting for transfers between devices, scatter(): lax.all_to_all(rows, ('x', 'yl'), 0, 0, axis_index_groups=[members], tile...  22.1 us
    ppermute x14, starting transfers between devices, send(): return lax.ppermute(v, axis, pairs)  14.6 us
    ppermute x14, waiting for transfers between devices, send(): return lax.ppermute(v, axis, pairs)  10.6 us
    ppermute x2, waiting for transfers between devices, opposite(): return lax.ppermute(block, axis, [(0, 1), (1, 0)])  9.27 us
    ppermute x2, starting transfers between devices, steps(): before = lax.ppermute(held, 'z', pairs(-1, (0, 3)))  8.37 us
    pallas_call x3, Pallas kernels, call(): pl.pallas_call(body, in_specs=[pl.BlockSpec(memory_space=pltpu.SMEM), *[v...  7.08 us
    all_to_all x1, starting transfers between devices, scatter(): lax.all_to_all(rows, ('x', 'yl'), 0, 0, axis_index_groups=[members], tile...  5.29 us
    ppermute x2, waiting for transfers between devices, steps(): after = lax.ppermute(held, 'z', pairs(1, (0, 3, 5)))  3.94 us
  transfers between devices with their start and end apart: 25, of which 9 were waited for; matrix products, arithmetic and copies ran while one was open for 6% of the time, Pallas kernels for 5%

profile of v13, /device:TPU:16, one launch (start us, length us, event | category | flops | bytes accessed | tf_op | source)
XLA Modules:
  0.0 101.0 jit_solution(7979367691630149625)
XLA Ops:
  0.0 5.3 %all-to-all-start = ((f32[8,64,1024]{2,1,0:T(8,128)}), f32[8,64,1024]{2,1,0:T(8,128)}, u32[]{:S(2)}, u32[]{:S(2)}) async-start(f32[8,64,1024]{2,1,0:T(8,128)} %bitcast.14), calls=%async_computation | async-start | bytes 4194304 | tf_op jit(solution)/shard_map/all_to_all | solution.py:182
  8.6 1.2 %collective-permute-done.40 = f32[8,64,128]{2,1,0:T(8,128)S(1)} collective-permute-done((f32[8,64,128]{2,1,0:T(8,128)S(1)}, f32[8,64,128]{2,1,0:T(8,128)S(1)}, u32[]{:S(2)}, u32[]{:S(2)}) %collective-permute-start.40) | collective-permute-done | bytes 262176 | tf_op jit(solution)/shard_map/ppermute | solution.py:61
  10.7 22.1 %all-to-all-done = f32[8,64,1024]{2,1,0:T(8,128)} async-done(((f32[8,64,1024]{2,1,0:T(8,128)}), f32[8,64,1024]{2,1,0:T(8,128)}, u32[]{:S(2)}, u32[]{:S(2)}) %all-to-all-start) | async-done | bytes 2097184 | tf_op jit(solution)/shard_map/all_to_all | solution.py:182
  32.8 1.1 %slice_bitcast_fusion = (f32[64,1024]{1,0:T(8,128)S(1)}, f32[64,1024]{1,0:T(8,128)S(1)}) fusion(f32[8,64,1024]{2,1,0:T(8,128)} %all-to-all-done, u32[]{:T(128)S(6)} %convert_element_type.21), kind=kLoop, calls=%fused_computation.6 | loop fusion | bytes 1048580 | tf_op jit(solution)/shard_map/squeeze | solution.py:217
  33.8 14.2 %conditional.1 = (f32[64,1024]{1,0:T(8,128)}, f32[64,1024]{1,0:T(8,128)}, f32[64,1024]{1,0:T(8,128)}, f32[64,1024]{1,0:T(8,128)}, f32[8,64,128]{2,1,0:T(8,128)}) conditional(s32[]{:T(128)} %clamp.3, (f32[64,1024]{1,0:T(8,128)S(1)}, f32[64,1024]{1,0:T(8,128)S(1)}, f32[8,64,128]{2,1,0:T(8,128)}) %tuple.39, ...), branch_computations={%region_0.1_spmd, %region_1.2_spmd, %region_2.3_spmd, %region_3.4_... | conditional | bytes 5243120 | solution.py:222
  33.9 1.4 %collective-permute-start.30 = (f32[64,1024]{1,0:T(8,128)S(1)}, f32[64,1024]{1,0:T(8,128)}, u32[]{:S(2)}, u32[]{:S(2)}) collective-permute-start(f32[64,1024]{1,0:T(8,128)S(1)} %get-tuple-element.71), channel_id=1, source_target_pairs={{48,8},{49,9},{50,10},{51,11},{52,12},{53,13},{54,14},{55,15},{112... | collective-permute-start | bytes 786440 | tf_op jit(solution)/shard_map/cond/branch_6_fun/ppermute | solution.py:28
  35.3 1.4 %collective-permute-start.31 = (f32[64,1024]{1,0:T(8,128)S(1)}, f32[64,1024]{1,0:T(8,128)}, u32[]{:S(2)}, u32[]{:S(2)}) collective-permute-start(f32[64,1024]{1,0:T(8,128)S(1)} %get-tuple-element.71), channel_id=1, source_target_pairs={{48,24},{49,25},{50,26},{51,27},{52,28},{53,29},{54,30},{55,31},{1... | collective-permute-start | bytes 786440 | tf_op jit(solution)/shard_map/cond/branch_6_fun/ppermute | solution.py:29
  36.6 1.4 %collective-permute-start.32 = (f32[64,1024]{1,0:T(8,128)S(1)}, f32[64,1024]{1,0:T(8,128)}, u32[]{:S(2)}, u32[]{:S(2)}) collective-permute-start(f32[64,1024]{1,0:T(8,128)S(1)} %get-tuple-element.72), channel_id=1, source_target_pairs={{56,16},{57,17},{58,18},{59,19},{60,20},{61,21},{62,22},{63,23},{1... | collective-permute-start | bytes 786440 | tf_op jit(solution)/shard_map/cond/branch_6_fun/ppermute | solution.py:28
  38.0 1.3 %collective-permute-start.33 = (f32[64,1024]{1,0:T(8,128)S(1)}, f32[64,1024]{1,0:T(8,128)}, u32[]{:S(2)}, u32[]{:S(2)}) collective-permute-start(f32[64,1024]{1,0:T(8,128)S(1)} %get-tuple-element.72), channel_id=1, source_target_pairs={{56,32},{57,33},{58,34},{59,35},{60,36},{61,37},{62,38},{63,39},{1... | collective-permute-start | bytes 786440 | tf_op jit(solution)/shard_map/cond/branch_6_fun/ppermute | solution.py:29
  40.0 8.1 %collective-permute-done.34 = f32[8,64,128]{2,1,0:T(8,128)} collective-permute-done((f32[8,64,128]{2,1,0:T(8,128)}, f32[8,64,128]{2,1,0:T(8,128)}, u32[]{:S(2)}, u32[]{:S(2)}) %collective-permute-start.34) | collective-permute-done | bytes 262176 | tf_op jit(solution)/shard_map/cond/branch_6_fun/ppermute | solution.py:61
  48.1 1.1 %select_select_fusion.1 = f32[64,1024]{1,0:T(8,128)S(1)} fusion(f32[64,1024]{1,0:T(8,128)} %get-tuple-element.89, f32[64,1024]{1,0:T(8,128)} %get-tuple-element.90, pred[]{:T(512)S(6)} %eq.87, pred[]{:T(512)S(6)} %eq.86, f32[8,64,1024]{2,1,0:T(8,128)} %all-to-all-done), kind=kLoop, calls=%fused_computation.3 | loop fusion | flops 131072 | bytes 1048578 | tf_op jit(solution)/shard_map/jit(_where)/select_n | solution.py:35
  49.2 1.3 %collective-permute-start.43 = (f32[64,1024]{1,0:T(8,128)S(1)}, f32[64,1024]{1,0:T(8,128)S(1)}, u32[]{:S(2)}, u32[]{:S(2)}) collective-permute-start(f32[64,1024]{1,0:T(8,128)S(1)} %select_select_fusion.1), channel_id=1, source_target_pairs={{56,0},{16,24},{32,40},{57,1},{17,25},{33,41},{58,2},{18,26},{34,4... | collective-permute-start | bytes 786440 | tf_op jit(solution)/shard_map/ppermute | solution.py:43
  51.1 1.0 %select_select_fusion.3 = f32[64,1024]{1,0:T(8,128)S(1)} fusion(f32[64,1024]{1,0:T(8,128)S(1)} %get-tuple-element.94, f32[64,1024]{1,0:T(8,128)} %get-tuple-element.87, f32[64,1024]{1,0:T(8,128)} %get-tuple-element.88, pred[]{:T(512)S(6)} %eq.80, pred[]{:T(512)S(6)} %eq.79), kind=kLoop, calls=%fused_computation.5 | loop fusion | flops 131072 | bytes 1048578 | tf_op jit(solution)/shard_map/jit(_where)/select_n | solution.py:35
  52.2 1.9 %collective-permute-start.41 = (f32[64,1024]{1,0:T(8,128)S(1)}, f32[64,1024]{1,0:T(8,128)}, u32[]{:S(2)}, u32[]{:S(2)}) collective-permute-start(f32[64,1024]{1,0:T(8,128)S(1)} %select_select_fusion.3), channel_id=1, source_target_pairs={{0,8},{8,16},{16,24},{24,32},{32,40},{40,48},{48,56},{56,0},{1,9},... | collective-permute-start | bytes 786440 | tf_op jit(solution)/shard_map/ppermute | solution.py:43
  54.1 7.7 %collective-permute-start.42 = (f32[64,1024]{1,0:T(8,128)S(1)}, f32[64,1024]{1,0:T(8,128)}, u32[]{:S(2)}, u32[]{:S(2)}) collective-permute-start(f32[64,1024]{1,0:T(8,128)S(1)} %select_select_fusion.3), channel_id=1, source_target_pairs={{0,56},{8,0},{16,8},{24,16},{32,24},{40,32},{48,40},{56,48},{1,57}... | collective-permute-start | bytes 786440 | tf_op jit(solution)/shard_map/ppermute | solution.py:44
  62.0 3.9 %collective-permute-done.43 = f32[64,1024]{1,0:T(8,128)S(1)} collective-permute-done((f32[64,1024]{1,0:T(8,128)S(1)}, f32[64,1024]{1,0:T(8,128)S(1)}, u32[]{:S(2)}, u32[]{:S(2)}) %collective-permute-start.43) | collective-permute-done | bytes 262176 | tf_op jit(solution)/shard_map/ppermute | solution.py:43
  67.0 2.8 %collective-permute-start.50 = (f32[64,1024]{1,0:T(8,128)S(1)}, f32[64,1024]{1,0:T(8,128)S(1)}, u32[]{:S(2)}, u32[]{:S(2)}) collective-permute-start(f32[64,1024]{1,0:T(8,128)S(1)} %select_select_fusion.refs_1_), channel_id=1, source_target_pairs={{0,192},{64,0},{128,64},{192,128},{1,193},{65,1},{129,65},{193,129... | collective-permute-start | bytes 786440 | tf_op jit(solution)/shard_map/ppermute | solution.py:192
  69.9 1.0 select_select_fusion.2.refs_0_
  71.2 1.5 %collective-permute-start.45 = (f32[64,1024]{1,0:T(8,128)S(1)}, f32[64,1024]{1,0:T(8,128)}, u32[]{:S(2)}, u32[]{:S(2)}) collective-permute-start(f32[64,1024]{1,0:T(8,128)S(1)} %select_select_fusion.2.refs_0_), channel_id=1, source_target_pairs={{0,4},{4,0},{1,5},{5,1},{2,6},{6,2},{3,7},{7,3},{8,12},{12,8},{9,1... | collective-permute-start | bytes 786440 | tf_op jit(solution)/shard_map/ppermute | solution.py:192
  72.7 2.5 %collective-permute-done.46.refs_3_ = f32[64,1024]{1,0:T(8,128)S(1)} collective-permute-done((f32[64,1024]{1,0:T(8,128)S(1)}, f32[64,1024]{1,0:T(8,128)S(1)}, u32[]{:S(2)}, u32[]{:S(2)}) %collective-permute-start.46) | collective-permute-done | bytes 262176 | tf_op jit(solution)/shard_map/ppermute | solution.py:192
  75.9 1.1 %collective-permute-done.48.refs_5_ = f32[64,1024]{1,0:T(8,128)S(1)} collective-permute-done((f32[64,1024]{1,0:T(8,128)S(1)}, f32[64,1024]{1,0:T(8,128)S(1)}, u32[]{:S(2)}, u32[]{:S(2)}) %collective-permute-start.48) | collective-permute-done | bytes 262176 | tf_op jit(solution)/shard_map/ppermute | solution.py:192
  77.0 2.0 %collective-permute-start.55 = (f32[64,1024]{1,0:T(8,128)S(1)}, f32[64,1024]{1,0:T(8,128)}, u32[]{:S(2)}, u32[]{:S(2)}) collective-permute-start(f32[64,1024]{1,0:T(8,128)S(1)} %collective-permute-done.48.refs_5_), channel_id=1, source_target_pairs={{0,64},{64,128},{128,192},{192,0},{1,65},{65,129},{129,193},{193,1... | collective-permute-start | bytes 786440 | tf_op jit(solution)/shard_map/ppermute | solution.py:192
  79.0 3.7 %collective-permute-done.47.refs_4_ = f32[64,1024]{1,0:T(8,128)} collective-permute-done((f32[64,1024]{1,0:T(8,128)S(1)}, f32[64,1024]{1,0:T(8,128)}, u32[]{:S(2)}, u32[]{:S(2)}) %collective-permute-start.47) | collective-permute-done | bytes 262176 | tf_op jit(solution)/shard_map/ppermute | solution.py:192
  82.8 1.1 %broadcast_select_fusion.1 = f32[8,64,128]{2,1,0:T(8,128)S(1)} fusion(f32[8,64,128]{2,1,0:T(8,128)} %broadcast_select_fusion, f32[8,64,128]{2,1,0:T(8,128)} %get-tuple-element.86, pred[128]{0:T(512)(128)(4,1)S(1)} %fusion.1), kind=kLoop, calls=%fused_computation.11 | loop fusion | flops 65536 | bytes 786560 | tf_op jit(solution)/shard_map/jit(_where)/select_n | solution.py:68
  83.9 1.1 %collective-permute-start.58 = (f32[64,1024]{1,0:T(8,128)S(1)}, f32[64,1024]{1,0:T(8,128)S(1)}, u32[]{:S(2)}, u32[]{:S(2)}) collective-permute-start(f32[64,1024]{1,0:T(8,128)S(1)} %collective-permute-done.48.refs_5_), channel_id=1, source_target_pairs={{0,4},{4,0},{1,5},{5,1},{2,6},{6,2},{3,7},{7,3},{8,12},{12,8},{9,1... | collective-permute-start | bytes 786440 | tf_op jit(solution)/shard_map/ppermute | solution.py:192
  85.0 1.0 %collective-permute-start.57 = (f32[64,1024]{1,0:T(8,128)}, f32[64,1024]{1,0:T(8,128)S(1)}, u32[]{:S(2)}, u32[]{:S(2)}) collective-permute-start(f32[64,1024]{1,0:T(8,128)} %collective-permute-done.47.refs_4_), channel_id=1, source_target_pairs={{0,4},{4,0},{1,5},{5,1},{2,6},{6,2},{3,7},{7,3},{8,12},{12,8},{9,1... | collective-permute-start | bytes 786440 | tf_op jit(solution)/shard_map/ppermute | solution.py:192
  86.0 3.2 %collective-permute-start.56 = (f32[64,1024]{1,0:T(8,128)}, f32[64,1024]{1,0:T(8,128)S(1)}, u32[]{:S(2)}, u32[]{:S(2)}) collective-permute-start(f32[64,1024]{1,0:T(8,128)} %collective-permute-done.45.refs_2_), channel_id=1, source_target_pairs={{0,192},{64,0},{128,64},{192,128},{1,193},{65,1},{129,65},{193,129... | collective-permute-start | bytes 786440 | tf_op jit(solution)/shard_map/ppermute | solution.py:192
  89.3 1.3 %collective-permute-done.51.refs_0_ = f32[64,1024]{1,0:T(8,128)} collective-permute-done((f32[64,1024]{1,0:T(8,128)}, f32[64,1024]{1,0:T(8,128)}, u32[]{:S(2)}, u32[]{:S(2)}) %collective-permute-start.51) | collective-permute-done | bytes 262176 | tf_op jit(solution)/shard_map/ppermute | solution.py:192
  91.8 2.1 %shard_map.73.d_ref = f32[8,64,1024]{2,1,0:T(8,128)S(1)} custom-call(s32[4]{0:T(128)S(1)} %get-tuple-element.101.bins, f32[2,4,64,1024]{3,2,1,0:T(8,128)S(1)} %copy-done.1, f32[4,128,256]{2,1,0:T(8,128)S(1)} %maximum_select_fusion.l_ref, f32[64,1024]{1,0:T(8,128)S(1)} %select_select_fusion.2.refs_0_, f32[64,1024]{1,0:T(8,128)S(1)} %select_select_fusion.refs_1_, ...), custom_call_target="tpu_custom_call" | custom-call | flops 402653184 | bytes 4194304 | tf_op jit(solution)/shard_map/pallas_call | solution.py:129
  94.0 2.0 %collective-permute-done.57.refs_4_ = f32[64,1024]{1,0:T(8,128)S(1)} collective-permute-done((f32[64,1024]{1,0:T(8,128)}, f32[64,1024]{1,0:T(8,128)S(1)}, u32[]{:S(2)}, u32[]{:S(2)}) %collective-permute-start.57) | collective-permute-done | bytes 262176 | tf_op jit(solution)/shard_map/ppermute | solution.py:192
  96.0 2.7 %shard_map.74.before_ref = f32[8,64,1024]{2,1,0:T(8,128)S(1)} custom-call(s32[4]{0:T(128)S(1)} %get-tuple-element.101.bins, f32[8,64,1024]{2,1,0:T(8,128)S(1)} %shard_map.73.d_ref, f32[4,128,256]{2,1,0:T(8,128)S(1)} %maximum_select_fusion.l_ref, f32[64,64]{1,0:T(8,128)S(1)} %copy.12.coef_ref, f32[64,1024]{1,0:T(8,128)} %collective-permute-done.51.refs_0_, ...), custom_call_target="tpu_custom_call" | custom-call | flops 301989888 | bytes 3145728 | tf_op jit(solution)/shard_map/pallas_call | solution.py:129
  98.8 2.2 %shard_map.75 = bf16[8,64,1024]{2,1,0:T(8,128)(2,1)} custom-call(s32[4]{0:T(128)S(1)} %get-tuple-element.101.bins, f32[8,64,1024]{2,1,0:T(8,128)S(1)} %shard_map.73.d_ref, f32[4,128,256]{2,1,0:T(8,128)S(1)} %maximum_select_fusion.l_ref, f32[64,64]{1,0:T(8,128)S(1)} %copy.12.coef_ref, f32[64,1024]{1,0:T(8,128)S(1)} %collective-permute-done.52.mine_ref, ...), custom_call_target="tpu_custom_call" | custom-call | flops 100663296 | bytes 1048576 | tf_op jit(solution)/shard_map/pallas_call | solution.py:129
  (60 shorter events, 7.1 us)
Async XLA Ops:
  0.0 8.4 %copy-start = (f32[64,64]{1,0:T(8,128)S(1)}, f32[64,64]{1,0:T(8,128)}, u32[]{:S(2)}) copy-start(f32[64,64]{1,0:T(8,128)} %param.17) | copy-start | bytes 49156
  0.0 7.9 %copy-start.1 = (f32[2,4,64,1024]{3,2,1,0:T(8,128)S(1)}, f32[2,4,64,1024]{3,2,1,0:T(8,128)}, u32[]{:S(2)}) copy-start(f32[2,4,64,1024]{3,2,1,0:T(8,128)} %x_ref.1) | copy-start | bytes 6291460
  0.0 8.3 %copy-start.7 = (s32[4]{0:T(128)S(1)}, s32[4]{0:T(128)}, u32[]{:S(2)}) copy-start(s32[4]{0:T(128)} %constant.60.clone) | copy-start | bytes 52
  0.0 8.3 %copy-start.6 = (s32[64]{0:T(128)S(1)}, s32[64]{0:T(128)}, u32[]{:S(2)}) copy-start(s32[64]{0:T(128)} %param.18) | copy-start | bytes 772
  0.0 8.4 %copy-start.4 = (f32[64,4]{1,0:T(8,128)S(1)}, f32[64,4]{1,0:T(8,128)}, u32[]{:S(2)}) copy-start(f32[64,4]{1,0:T(8,128)} %constant.61.clone) | copy-start | bytes 3076
  0.0 32.7 %all-to-all-start = ((f32[8,64,1024]{2,1,0:T(8,128)}), f32[8,64,1024]{2,1,0:T(8,128)}, u32[]{:S(2)}, u32[]{:S(2)}) async-start(f32[8,64,1024]{2,1,0:T(8,128)} %bitcast.14), calls=%async_computation | async-start | bytes 4194304 | tf_op jit(solution)/shard_map/all_to_all | solution.py:182
  8.2 1.6 %collective-permute-start.40 = (f32[8,64,128]{2,1,0:T(8,128)S(1)}, f32[8,64,128]{2,1,0:T(8,128)S(1)}, u32[]{:S(2)}, u32[]{:S(2)}) collective-permute-start(f32[8,64,128]{2,1,0:T(8,128)S(1)} %pad_maximum_fusion), channel_id=1, source_target_pairs={{0,1},{1,0},{2,3},{3,2},{4,5},{5,4},{6,7},{7,6},{8,9},{9,8},{10,11... | collective-permute-start | bytes 786440 | tf_op jit(solution)/shard_map/ppermute | solution.py:61
  33.9 6.1 %collective-permute-start.30 = (f32[64,1024]{1,0:T(8,128)S(1)}, f32[64,1024]{1,0:T(8,128)}, u32[]{:S(2)}, u32[]{:S(2)}) collective-permute-start(f32[64,1024]{1,0:T(8,128)S(1)} %get-tuple-element.71), channel_id=1, source_target_pairs={{48,8},{49,9},{50,10},{51,11},{52,12},{53,13},{54,14},{55,15},{112... | collective-permute-start | bytes 786440 | tf_op jit(solution)/shard_map/cond/branch_6_fun/ppermute | solution.py:28
  35.3 4.7 %collective-permute-start.31 = (f32[64,1024]{1,0:T(8,128)S(1)}, f32[64,1024]{1,0:T(8,128)}, u32[]{:S(2)}, u32[]{:S(2)}) collective-permute-start(f32[64,1024]{1,0:T(8,128)S(1)} %get-tuple-element.71), channel_id=1, source_target_pairs={{48,24},{49,25},{50,26},{51,27},{52,28},{53,29},{54,30},{55,31},{1... | collective-permute-start | bytes 786440 | tf_op jit(solution)/shard_map/cond/branch_6_fun/ppermute | solution.py:29
  36.6 3.4 %collective-permute-start.32 = (f32[64,1024]{1,0:T(8,128)S(1)}, f32[64,1024]{1,0:T(8,128)}, u32[]{:S(2)}, u32[]{:S(2)}) collective-permute-start(f32[64,1024]{1,0:T(8,128)S(1)} %get-tuple-element.72), channel_id=1, source_target_pairs={{56,16},{57,17},{58,18},{59,19},{60,20},{61,21},{62,22},{63,23},{1... | collective-permute-start | bytes 786440 | tf_op jit(solution)/shard_map/cond/branch_6_fun/ppermute | solution.py:28
  38.0 2.0 %collective-permute-start.33 = (f32[64,1024]{1,0:T(8,128)S(1)}, f32[64,1024]{1,0:T(8,128)}, u32[]{:S(2)}, u32[]{:S(2)}) collective-permute-start(f32[64,1024]{1,0:T(8,128)S(1)} %get-tuple-element.72), channel_id=1, source_target_pairs={{56,32},{57,33},{58,34},{59,35},{60,36},{61,37},{62,38},{63,39},{1... | collective-permute-start | bytes 786440 | tf_op jit(solution)/shard_map/cond/branch_6_fun/ppermute | solution.py:29
  39.3 8.7 %collective-permute-start.34 = (f32[8,64,128]{2,1,0:T(8,128)}, f32[8,64,128]{2,1,0:T(8,128)}, u32[]{:S(2)}, u32[]{:S(2)}) collective-permute-start(f32[8,64,128]{2,1,0:T(8,128)} %get-tuple-element.73), channel_id=1, source_target_pairs={{0,2},{2,0},{1,3},{3,1},{4,6},{6,4},{5,7},{7,5},{8,10},{10,8},{9,1... | collective-permute-start | bytes 786440 | tf_op jit(solution)/shard_map/cond/branch_6_fun/ppermute | solution.py:61
  48.1 22.9 %copy-start.3 = (f32[64,4]{1,0:T(8,128)S(1)}, f32[64,4]{1,0:T(8,128)}, u32[]{:S(2)}) copy-start(f32[64,4]{1,0:T(8,128)} %constant.62.clone) | copy-start | bytes 3076
  49.2 16.8 %collective-permute-start.43 = (f32[64,1024]{1,0:T(8,128)S(1)}, f32[64,1024]{1,0:T(8,128)S(1)}, u32[]{:S(2)}, u32[]{:S(2)}) collective-permute-start(f32[64,1024]{1,0:T(8,128)S(1)} %select_select_fusion.1), channel_id=1, source_target_pairs={{56,0},{16,24},{32,40},{57,1},{17,25},{33,41},{58,2},{18,26},{34,4... | collective-permute-start | bytes 786440 | tf_op jit(solution)/shard_map/ppermute | solution.py:43
  50.5 15.5 %collective-permute-start.44 = (f32[64,1024]{1,0:T(8,128)S(1)}, f32[64,1024]{1,0:T(8,128)S(1)}, u32[]{:S(2)}, u32[]{:S(2)}) collective-permute-start(f32[64,1024]{1,0:T(8,128)S(1)} %select_select_fusion.1), channel_id=1, source_target_pairs={{56,48},{16,8},{57,49},{17,9},{58,50},{18,10},{59,51},{19,11},{60,... | collective-permute-start | bytes 786440 | tf_op jit(solution)/shard_map/ppermute | solution.py:44
  52.2 17.7 %copy-start.2 = (f32[64,1024]{1,0:T(8,128)}, f32[64,1024]{1,0:T(8,128)S(1)}, u32[]{:S(2)}) copy-start(f32[64,1024]{1,0:T(8,128)S(1)} %select_select_fusion.3) | copy-start | bytes 786436
  52.2 17.7 %collective-permute-start.41 = (f32[64,1024]{1,0:T(8,128)S(1)}, f32[64,1024]{1,0:T(8,128)}, u32[]{:S(2)}, u32[]{:S(2)}) collective-permute-start(f32[64,1024]{1,0:T(8,128)S(1)} %select_select_fusion.3), channel_id=1, source_target_pairs={{0,8},{8,16},{16,24},{24,32},{32,40},{40,48},{48,56},{56,0},{1,9},... | collective-permute-start | bytes 786440 | tf_op jit(solution)/shard_map/ppermute | solution.py:43
  54.1 15.8 %collective-permute-start.42 = (f32[64,1024]{1,0:T(8,128)S(1)}, f32[64,1024]{1,0:T(8,128)}, u32[]{:S(2)}, u32[]{:S(2)}) collective-permute-start(f32[64,1024]{1,0:T(8,128)S(1)} %select_select_fusion.3), channel_id=1, source_target_pairs={{0,56},{8,0},{16,8},{24,16},{32,24},{40,32},{48,40},{56,48},{1,57}... | collective-permute-start | bytes 786440 | tf_op jit(solution)/shard_map/ppermute | solution.py:44
  66.0 9.2 %collective-permute-start.46 = (f32[64,1024]{1,0:T(8,128)S(1)}, f32[64,1024]{1,0:T(8,128)S(1)}, u32[]{:S(2)}, u32[]{:S(2)}) collective-permute-start(f32[64,1024]{1,0:T(8,128)S(1)} %select_select_fusion.refs_1_), channel_id=1, source_target_pairs={{0,4},{4,0},{1,5},{5,1},{2,6},{6,2},{3,7},{7,3},{8,12},{12,8},{9,1... | collective-permute-start | bytes 786440 | tf_op jit(solution)/shard_map/ppermute | solution.py:192
  66.6 10.4 %collective-permute-start.48 = (f32[64,1024]{1,0:T(8,128)S(1)}, f32[64,1024]{1,0:T(8,128)S(1)}, u32[]{:S(2)}, u32[]{:S(2)}) collective-permute-start(f32[64,1024]{1,0:T(8,128)S(1)} %select_select_fusion.refs_1_), channel_id=1, source_target_pairs={{0,64},{64,128},{128,192},{192,0},{1,65},{65,129},{129,193},{193,1... | collective-permute-start | bytes 786440 | tf_op jit(solution)/shard_map/ppermute | solution.py:192
  67.0 10.0 %collective-permute-start.50 = (f32[64,1024]{1,0:T(8,128)S(1)}, f32[64,1024]{1,0:T(8,128)S(1)}, u32[]{:S(2)}, u32[]{:S(2)}) collective-permute-start(f32[64,1024]{1,0:T(8,128)S(1)} %select_select_fusion.refs_1_), channel_id=1, source_target_pairs={{0,192},{64,0},{128,64},{192,128},{1,193},{65,1},{129,65},{193,129... | collective-permute-start | bytes 786440 | tf_op jit(solution)/shard_map/ppermute | solution.py:192
  70.9 11.8 %collective-permute-start.47 = (f32[64,1024]{1,0:T(8,128)S(1)}, f32[64,1024]{1,0:T(8,128)}, u32[]{:S(2)}, u32[]{:S(2)}) collective-permute-start(f32[64,1024]{1,0:T(8,128)S(1)} %select_select_fusion.2.refs_0_), channel_id=1, source_target_pairs={{0,64},{64,128},{128,192},{192,0},{1,65},{65,129},{129,193},{193,1... | collective-permute-start | bytes 786440 | tf_op jit(solution)/shard_map/ppermute | solution.py:192
  71.2 12.7 %collective-permute-start.45 = (f32[64,1024]{1,0:T(8,128)S(1)}, f32[64,1024]{1,0:T(8,128)}, u32[]{:S(2)}, u32[]{:S(2)}) collective-permute-start(f32[64,1024]{1,0:T(8,128)S(1)} %select_select_fusion.2.refs_0_), channel_id=1, source_target_pairs={{0,4},{4,0},{1,5},{5,1},{2,6},{6,2},{3,7},{7,3},{8,12},{12,8},{9,1... | collective-permute-start | bytes 786440 | tf_op jit(solution)/shard_map/ppermute | solution.py:192
  75.2 9.8 %collective-permute-start.49 = (f32[64,1024]{1,0:T(8,128)S(1)}, f32[64,1024]{1,0:T(8,128)}, u32[]{:S(2)}, u32[]{:S(2)}) collective-permute-start(f32[64,1024]{1,0:T(8,128)S(1)} %select_select_fusion.2.refs_0_), channel_id=1, source_target_pairs={{0,192},{64,0},{128,64},{192,128},{1,193},{65,1},{129,65},{193,129... | collective-permute-start | bytes 786440 | tf_op jit(solution)/shard_map/ppermute | solution.py:192
  77.0 9.0 %collective-permute-start.53 = (f32[64,1024]{1,0:T(8,128)S(1)}, f32[64,1024]{1,0:T(8,128)}, u32[]{:S(2)}, u32[]{:S(2)}) collective-permute-start(f32[64,1024]{1,0:T(8,128)S(1)} %collective-permute-done.46.refs_3_), channel_id=1, source_target_pairs={{0,192},{64,0},{128,64},{192,128},{1,193},{65,1},{129,65},{193,129... | collective-permute-start | bytes 786440 | tf_op jit(solution)/shard_map/ppermute | solution.py:192
  77.0 12.3 %collective-permute-start.55 = (f32[64,1024]{1,0:T(8,128)S(1)}, f32[64,1024]{1,0:T(8,128)}, u32[]{:S(2)}, u32[]{:S(2)}) collective-permute-start(f32[64,1024]{1,0:T(8,128)S(1)} %collective-permute-done.48.refs_5_), channel_id=1, source_target_pairs={{0,64},{64,128},{128,192},{192,0},{1,65},{65,129},{129,193},{193,1... | collective-permute-start | bytes 786440 | tf_op jit(solution)/shard_map/ppermute | solution.py:192
  82.7 7.9 %collective-permute-start.51 = (f32[64,1024]{1,0:T(8,128)}, f32[64,1024]{1,0:T(8,128)}, u32[]{:S(2)}, u32[]{:S(2)}) collective-permute-start(f32[64,1024]{1,0:T(8,128)} %collective-permute-done.47.refs_4_), channel_id=1, source_target_pairs={{0,64},{64,128},{128,192},{192,0},{1,65},{65,129},{129,193},{193,1... | collective-permute-start | bytes 786440 | tf_op jit(solution)/shard_map/ppermute | solution.py:192
  83.9 10.0 %collective-permute-start.58 = (f32[64,1024]{1,0:T(8,128)S(1)}, f32[64,1024]{1,0:T(8,128)S(1)}, u32[]{:S(2)}, u32[]{:S(2)}) collective-permute-start(f32[64,1024]{1,0:T(8,128)S(1)} %collective-permute-done.48.refs_5_), channel_id=1, source_target_pairs={{0,4},{4,0},{1,5},{5,1},{2,6},{6,2},{3,7},{7,3},{8,12},{12,8},{9,1... | collective-permute-start | bytes 786440 | tf_op jit(solution)/shard_map/ppermute | solution.py:192
  85.0 11.0 %collective-permute-start.57 = (f32[64,1024]{1,0:T(8,128)}, f32[64,1024]{1,0:T(8,128)S(1)}, u32[]{:S(2)}, u32[]{:S(2)}) collective-permute-start(f32[64,1024]{1,0:T(8,128)} %collective-permute-done.47.refs_4_), channel_id=1, source_target_pairs={{0,4},{4,0},{1,5},{5,1},{2,6},{6,2},{3,7},{7,3},{8,12},{12,8},{9,1... | collective-permute-start | bytes 786440 | tf_op jit(solution)/shard_map/ppermute | solution.py:192
  86.0 7.9 %collective-permute-start.56 = (f32[64,1024]{1,0:T(8,128)}, f32[64,1024]{1,0:T(8,128)S(1)}, u32[]{:S(2)}, u32[]{:S(2)}) collective-permute-start(f32[64,1024]{1,0:T(8,128)} %collective-permute-done.45.refs_2_), channel_id=1, source_target_pairs={{0,192},{64,0},{128,64},{192,128},{1,193},{65,1},{129,65},{193,129... | collective-permute-start | bytes 786440 | tf_op jit(solution)/shard_map/ppermute | solution.py:192
  89.3 9.5 %collective-permute-start.54 = (f32[64,1024]{1,0:T(8,128)}, f32[64,1024]{1,0:T(8,128)S(1)}, u32[]{:S(2)}, u32[]{:S(2)}) collective-permute-start(f32[64,1024]{1,0:T(8,128)} %collective-permute-done.53.refs_3_), channel_id=1, source_target_pairs={{0,192},{64,0},{128,64},{192,128},{1,193},{65,1},{129,65},{193,129... | collective-permute-start | bytes 786440 | tf_op jit(solution)/shard_map/ppermute | solution.py:192
  90.6 8.2 %collective-permute-start.52 = (f32[64,1024]{1,0:T(8,128)}, f32[64,1024]{1,0:T(8,128)S(1)}, u32[]{:S(2)}, u32[]{:S(2)}) collective-permute-start(f32[64,1024]{1,0:T(8,128)} %collective-permute-done.51.refs_0_), channel_id=1, source_target_pairs={{0,4},{4,0},{1,5},{5,1},{2,6},{6,2},{3,7},{7,3},{8,12},{12,8},{9,1... | collective-permute-start | bytes 786440 | tf_op jit(solution)/shard_map/ppermute | solution.py:192
  (1 other events, 5.3 us)
